TPU v7x, 32 devices: a whole 2x2x4 slice. The times are simulated.
32 devices in a mesh: groups: 2 (over x), pool: 4 (over y, core), tp: 4 (over z).
Axes of the slice: x: 2, y: 2, z: 4, core: 2. Of those that a mesh axis runs over, the one named last changes fastest.
Arguments:
- tokens: bfloat16 [1024, 8192], P(('groups', 'pool')), parts along dimension 0, may hold values from -6 to 6
- input_norm_gain: bfloat16 [8192], replicated, may hold values from 0.25 to 1.75
- query_matrix: bfloat16 [8192, 8192], P('pool', 'tp'), may hold values from -0.0625 to 0.0625
- key_matrix: bfloat16 [8192, 1024], P('pool', 'tp'), may hold values from -0.0625 to 0.0625
- value_matrix: bfloat16 [8192, 1024], P('pool', 'tp'), may hold values from -0.0625 to 0.0625
- output_matrix: bfloat16 [8192, 8192], P('tp', 'pool'), may hold values from -0.0625 to 0.0625
- rotated_key_cache: bfloat16 [1024, 8, 64, 128], P(('groups', 'pool'), 'tp'), parts along dimension 0, may hold values from -105 to 105
- cached_value_rows: bfloat16 [1024, 8, 64, 128], P(('groups', 'pool'), 'tp'), parts along dimension 0, may hold values from -6 to 6
- cache_length_per_row: int32 [1024], P(('groups', 'pool')), parts along dimension 0, may hold values from 1 to 64, as said below
- row_adapter_index: int32 [1024], P(('groups', 'pool')), parts along dimension 0, may hold values from 0 to 127, as said below
- query_down_maps: bfloat16 [128, 16, 8192], P('pool', None, 'tp'), may hold values from -0.0625 to 0.0625
- query_up_maps: bfloat16 [128, 16, 8192], P('pool', None, 'tp'), may hold values from -1.5 to 1.5
- value_down_maps: bfloat16 [128, 16, 8192], P('pool', None, 'tp'), may hold values from -0.0625 to 0.0625
- value_up_maps: bfloat16 [128, 16, 1024], P('pool', None, 'tp'), may hold values from -1.5 to 1.5
Outputs:
- attn_out: bfloat16 [1024, 8192], P(('groups', 'tp'), 'pool'), parts along dimension 0
- new_key: bfloat16 [1024, 1024], P(('groups', 'pool'), 'tp'), parts along dimension 0
- new_value: bfloat16 [1024, 1024], P(('groups', 'pool'), 'tp'), parts along dimension 0
There are 2 independent parts, one for each index of `groups`. A program takes and returns all parts, laid end to end along the dimension named above; an argument that names none is the same for every part. Nothing has to cross between parts.
Inputs may be any that keep to these rules, and one draw needn't show every extreme that they name: `row_adapter_index`: adapter i is held by pool index i // 32. The rows of one pool index name adapters held by any one pool index at most 64 times. Positions 0 to cache_length_per_row - 1 of a row's cache hold its keys and values; the new token sits at position cache_length_per_row.
All inputs are finite; a program needn't handle non-finite values.
Results may differ from a plain program's by a relative error of at most 0.0099.
Values may be sent and summed in bfloat16 or wider, within the bound.
No kernel may reach another device: no remote copies, remote signals or barrier semaphores. Data moves between devices by JAX's collectives and lax.ppermute only.
A program may use at most 128 MiB of HBM per device.

v0:
```python
import math

import jax
import jax.numpy as jnp
from jax import lax
from jax.sharding import PartitionSpec as P

epsilon = 1e-05
adapter_scale = 0.5
rope_base = 500000.0


def rms_norm(tokens, input_norm_gain):
    values = tokens.astype(jnp.float32)
    mean_square = jnp.mean(values * values, axis=-1, keepdims=True)
    return (values * lax.rsqrt(mean_square + epsilon) * input_norm_gain.astype(jnp.float32)).astype(
        jnp.bfloat16
    )


def rotate(values, positions):
    head_dim = values.shape[-1]
    half_dim = head_dim // 2
    frequency = jnp.power(
        jnp.float32(rope_base), jnp.arange(half_dim, dtype=jnp.float32) * (-2.0 / head_dim)
    )
    angles = positions.astype(jnp.float32)[:, None] * frequency[None, :]
    cosines = jnp.cos(angles)[:, None, :]
    sine_terms = jnp.sin(angles)[:, None, :]
    first_half = values[..., :half_dim]
    second_half = values[..., half_dim:]
    return jnp.concatenate(
        [
            first_half * cosines - second_half * sine_terms,
            second_half * cosines + first_half * sine_terms,
        ],
        axis=-1,
    )


def holder_updates(
    received_row_values,
    received_index,
    query_down_maps,
    query_up_maps,
    value_down_maps,
    value_up_maps,
):
    adapters_per_device, reduced_rank_rows, piece_width = query_down_maps.shape
    flattened = received_row_values.reshape(-1, piece_width)
    labels = received_index.reshape(-1).astype(jnp.float32)
    chosen = labels[:, None] == jnp.arange(adapters_per_device, dtype=jnp.float32)[None, :]
    selector = chosen.astype(jnp.float32)[:, :, None]

    def reduction_piece(down_map_table):
        all_terms = lax.dot_general(
            flattened,
            down_map_table.reshape(adapters_per_device * reduced_rank_rows, piece_width),
            (((1,), (1,)), ((), ())),
            preferred_element_type=jnp.float32,
        )
        return jnp.sum(
            all_terms.reshape(-1, adapters_per_device, reduced_rank_rows) * selector, axis=1
        )

    reduced_query, reduced_value = lax.psum(
        (reduction_piece(query_down_maps), reduction_piece(value_down_maps)), "tp"
    )
    picker = chosen.astype(jnp.bfloat16)[:, :, None]

    def expansion_piece(shrink, up_map_table):
        spread_low = (picker * shrink.astype(jnp.bfloat16)[:, None, :]).reshape(
            -1, adapters_per_device * reduced_rank_rows
        )
        expanded_rows = jnp.dot(
            spread_low,
            up_map_table.reshape(adapters_per_device * reduced_rank_rows, up_map_table.shape[2]),
            preferred_element_type=jnp.float32,
        )
        return (expanded_rows * adapter_scale).astype(jnp.bfloat16)

    return (
        expansion_piece(reduced_query, query_up_maps),
        expansion_piece(reduced_value, value_up_maps),
    )


def shards(
    tokens,
    input_norm_gain,
    query_matrix,
    key_matrix,
    value_matrix,
    output_matrix,
    rotated_key_cache,
    cached_value_rows,
    cache_length_per_row,
    row_adapter_index,
    query_down_maps,
    query_up_maps,
    value_down_maps,
    value_up_maps,
):
    pool_count = lax.axis_size("pool")
    rows_here = tokens.shape[0]
    capacity = 2 * rows_here // pool_count
    slot_count = pool_count * capacity
    adapters_per_device = query_down_maps.shape[0]
    piece_width = query_down_maps.shape[2]
    query_cols = query_matrix.shape[1]
    kv_cols = key_matrix.shape[1]
    normed = rms_norm(tokens, input_norm_gain)
    gathered = lax.all_to_all(normed, "pool", split_axis=1, concat_axis=0, tiled=True)
    local_cols = lax.dynamic_slice_in_dim(
        normed, lax.axis_index("tp") * piece_width, piece_width, 1
    )
    owner_of = row_adapter_index // adapters_per_device
    local_id = row_adapter_index - owner_of * adapters_per_device
    member = (owner_of[:, None] == jnp.arange(pool_count, dtype=jnp.int32)[None, :]).astype(
        jnp.int32
    )
    earlier = jnp.cumsum(member, axis=0) - member
    position = owner_of * capacity + jnp.sum(earlier * member, axis=1)
    send_rows = (
        jnp.zeros((slot_count, piece_width), jnp.bfloat16)
        .at[position]
        .set(local_cols)
        .reshape(pool_count, capacity, piece_width)
    )
    send_ids = (
        jnp.full((slot_count,), -1.0, jnp.float32)
        .at[position]
        .set(local_id.astype(jnp.float32))
        .astype(jnp.bfloat16)
        .reshape(pool_count, capacity)
    )
    received_row_values, received_index = (
        lax.all_to_all(send_rows, "pool", split_axis=0, concat_axis=0, tiled=True),
        lax.all_to_all(send_ids, "pool", split_axis=0, concat_axis=0, tiled=True),
    )
    delta_query, delta_value = holder_updates(
        received_row_values,
        received_index,
        query_down_maps,
        query_up_maps,
        value_down_maps,
        value_up_maps,
    )
    returned_parts = (
        lax.all_to_all(
            delta_query.reshape(pool_count, capacity, query_cols),
            "pool",
            split_axis=0,
            concat_axis=0,
            tiled=True,
        ),
        lax.all_to_all(
            delta_value.reshape(pool_count, capacity, kv_cols),
            "pool",
            split_axis=0,
            concat_axis=0,
            tiled=True,
        ),
    )
    products = jnp.concatenate(
        [
            jnp.dot(gathered, weights, preferred_element_type=jnp.float32)
            for weights in (query_matrix, key_matrix, value_matrix)
        ],
        axis=1,
    )
    projected = lax.psum_scatter(products, "pool", scatter_dimension=0, tiled=True)
    query_full = projected[:, :query_cols]
    key_full = projected[:, query_cols : query_cols + kv_cols]
    value_full = projected[:, query_cols + kv_cols :]
    query_full = query_full + jnp.take(
        returned_parts[0].reshape(slot_count, query_cols), position, axis=0
    ).astype(jnp.float32)
    value_full = value_full + jnp.take(
        returned_parts[1].reshape(slot_count, kv_cols), position, axis=0
    ).astype(jnp.float32)
    kv_local = rotated_key_cache.shape[1]
    head_dim = rotated_key_cache.shape[3]
    group_size = query_cols // (kv_local * head_dim)
    query = (
        rotate(query_full.reshape(rows_here, kv_local * group_size, head_dim), cache_length_per_row)
        .astype(jnp.bfloat16)
        .reshape(rows_here, kv_local, group_size, head_dim)
    )
    new_key = rotate(key_full.reshape(rows_here, kv_local, head_dim), cache_length_per_row).astype(
        jnp.bfloat16
    )
    new_value = value_full.astype(jnp.bfloat16).reshape(rows_here, kv_local, head_dim)
    score_scale = 1.0 / math.sqrt(head_dim)
    scores = (
        jnp.einsum("rgid,rgjd->rgij", query, rotated_key_cache, preferred_element_type=jnp.float32)
        * score_scale
    )
    own_score = (
        jnp.einsum("rgid,rgd->rgi", query, new_key, preferred_element_type=jnp.float32)
        * score_scale
    )
    in_range = (
        jnp.arange(rotated_key_cache.shape[2], dtype=jnp.int32)[None, :]
        < cache_length_per_row[:, None]
    )
    masked = jnp.where(in_range[:, None, None, :], scores, -jnp.inf)
    peak_score = jnp.maximum(jnp.max(masked, axis=-1), own_score)
    weights = jnp.exp(masked - peak_score[..., None])
    own_weight = jnp.exp(own_score - peak_score)
    denominator = jnp.sum(weights, axis=-1) + own_weight
    probability = (weights / denominator[..., None]).astype(jnp.bfloat16)
    own_prob = (own_weight / denominator).astype(jnp.bfloat16)
    attended = jnp.einsum(
        "rgij,rgjd->rgid", probability, cached_value_rows, preferred_element_type=jnp.float32
    )
    attended = (
        attended
        + own_prob.astype(jnp.float32)[..., None] * new_value.astype(jnp.float32)[:, :, None, :]
    )
    attended = attended.astype(jnp.bfloat16).reshape(rows_here, query_cols)
    partial_out = jnp.dot(
        lax.all_gather(attended, "pool", axis=0, tiled=True),
        output_matrix,
        preferred_element_type=jnp.float32,
    )
    attn_out = lax.psum_scatter(partial_out, "tp", scatter_dimension=0, tiled=True).astype(
        jnp.bfloat16
    )
    return (
        attn_out,
        new_key.reshape(rows_here, kv_local * head_dim),
        new_value.reshape(rows_here, kv_local * head_dim),
    )


def solution(mesh):
    return jax.shard_map(
        shards,
        mesh=mesh,
        in_specs=(
            P(("groups", "pool"), None),
            P(),
            P("pool", "tp"),
            P("pool", "tp"),
            P("pool", "tp"),
            P("tp", "pool"),
            P(("groups", "pool"), "tp", None, None),
            P(("groups", "pool"), "tp", None, None),
            P(("groups", "pool")),
            P(("groups", "pool")),
            P("pool", None, "tp"),
            P("pool", None, "tp"),
            P("pool", None, "tp"),
            P("pool", None, "tp"),
        ),
        out_specs=(
            P(("groups", "tp"), "pool"),
            P(("groups", "pool"), "tp"),
            P(("groups", "pool"), "tp"),
        ),
        check_vma=False,
    )
```

profile of v0, /device:TPU:0, one launch (start us, length us, event | category | flops | bytes accessed | tf_op | source)
XLA Modules:
  0.0 281.7 jit_solution(13445133421522892129)
XLA Ops:
  7.2 0.0 reduce-scatter.3.cloned.1.call-start
  7.2 4.2 %copy.59 = bf16[128,8192]{0,1:T(8,128)(2,1)} copy(bf16[128,8192]{1,0:T(8,128)(2,1)} %param.14) | data formatting | bytes 4194304 | tf_op args[0]
  11.4 2.8 %fusion = f32[128]{0:T(128)S(1)} fusion(bf16[128,8192]{0,1:T(8,128)(2,1)} %copy.59), kind=kLoop, calls=%fused_computation.7 | loop fusion | flops 3145600 | bytes 2097664 | tf_op jit(solution)/shard_map/reduce_sum | solution.py:15
  14.3 3.5 %fusion.2 = bf16[128,8192]{0,1:T(8,128)(2,1)S(1)} fusion(bf16[128,8192]{0,1:T(8,128)(2,1)S(1)} %copy-done.2, f32[8192]{0:T(1024)S(1)} %convert_element_type.102, f32[128]{0:T(128)S(1)} %add_rsqrt_fusion), kind=kLoop, calls=%fused_computation.9 | loop fusion | flops 4194304 | bytes 4227584 | tf_op jit(solution)/shard_map/convert_element_type | solution.py:16
  17.8 29.8 %all_to_all.44 = bf16[128,4,2048]{0,2,1:T(8,128)(2,1)} all-to-all(bf16[128,4,2048]{0,2,1:T(8,128)(2,1)S(1)} %bitcast.70), channel_id=1, replica_groups=mesh['groups'=2,'pool'=4,'tp'=4] {'pool'}, dimensions={1} | all-to-all | bytes 4194304 | tf_op jit(solution)/shard_map/all_to_all | solution.py:113
  47.7 4.0 %copy.60 = bf16[4,128,2048]{2,1,0:T(8,128)(2,1)} copy(bf16[4,128,2048]{1,2,0:T(8,128)(2,1)} %bitcast.72) | data formatting | bytes 4194304 | tf_op jit(solution)/shard_map/all_to_all | solution.py:113
  51.7 7.7 %fusion.56 = f32[512,2048]{1,0:T(8,128)S(1)} fusion(bf16[512,2048]{1,0:T(8,128)(2,1)} %bitcast.74, bf16[2048,2048]{1,0:T(8,128)(2,1)} %param.16), kind=kOutput, calls=%fused_computation.92 | convolution fusion | flops 4294967296 | bytes 14680064 | tf_op jit(solution)/shard_map/dot_general | solution.py:167
  59.4 0.7 fusion.57
  60.1 0.5 copy-done.10
  60.6 0.7 fusion.58
  61.4 2.8 pad_maximum_fusion
  64.2 0.6 copy-done.12
  64.8 0.1 fusion.44
  64.9 0.2 reduce_window_sum.11
  65.1 0.2 select_reduce_fusion
  65.3 1.0 scatter_custom_fusion
  66.3 0.7 all_to_all.38
  66.9 3.2 %all-to-all-start.1 = ((bf16[4,1,64]{2,1,0:T(2,128)(2,1)}), bf16[4,1,64]{2,1,0:T(2,128)(2,1)S(1)}, u32[]{:S(2)}, u32[]{:S(2)}) async-start(bf16[4,1,64]{2,1,0:T(2,128)(2,1)} %all_to_all.38), calls=%async_computation.2 | async-start | bytes 4096 | tf_op jit(solution)/shard_map/all_to_all | solution.py:139
  70.2 1.2 constant_dynamic-slice_fusion
  71.4 0.2 copy.64
  71.6 2.5 scatter_custom_fusion.1
  74.1 3.5 %all-to-all-start.2 = ((bf16[4,64,2048]{2,1,0:T(8,128)(2,1)}), bf16[4,64,2048]{2,1,0:T(8,128)(2,1)S(1)}, u32[]{:S(2)}, u32[]{:S(2)}) async-start(bf16[4,64,2048]{2,1,0:T(8,128)(2,1)} %bitcast.3), calls=%async_computation.3 | async-start | bytes 2097152 | tf_op jit(solution)/shard_map/all_to_all | solution.py:138
  77.7 0.1 reshape.213
  77.8 19.8 %all-to-all-done.2 = bf16[4,64,2048]{2,1,0:T(8,128)(2,1)S(1)} async-done(((bf16[4,64,2048]{2,1,0:T(8,128)(2,1)}), bf16[4,64,2048]{2,1,0:T(8,128)(2,1)S(1)}, u32[]{:S(2)}, u32[]{:S(2)}) %all-to-all-start.2) | async-done | bytes 1048608 | tf_op jit(solution)/shard_map/all_to_all | solution.py:138
  97.6 3.3 %fusion.18 = f32[256,16]{0,1:T(8,128)S(1)} fusion(bf16[256,2048,1]{1,0,2:T(8,128)(2,1)S(1)} %bitcast.78, bf16[32,16,2048]{2,1,0:T(8,128)(2,1)} %param.26, f32[256,32]{0,1:T(8,128)S(1)} %get-tuple-element.20), kind=kOutput, calls=%fused_computation.24 | convolution fusion | flops 537128960 | bytes 3194880 | tf_op jit(solution)/shard_map/dot_general | solution.py:56
  100.9 1.6 fusion.21
  102.5 20.4 %all-reduce = (bf16[256,16]{0,1:T(8,128)(2,1)S(1)}, bf16[256,16]{0,1:T(8,128)(2,1)S(1)}) all-reduce(f32[256,16]{0,1:T(8,128)S(1)} %fusion.21, f32[256,16]{0,1:T(8,128)S(1)} %fusion.18), channel_id=1, replica_groups=mesh['groups'=2,'pool'=4,'tp'=4] {'tp'}, use_global_device_ids=true, to_apply=%region_7.8 | all-reduce | flops 8192 | bytes 49152 | tf_op jit(solution)/shard_map/psum | solution.py:66
  122.9 1.0 fusion.25
  123.9 3.3 %all-to-all-start.4 = ((bf16[4,64,256]{2,1,0:T(8,128)(2,1)}), bf16[4,64,256]{2,1,0:T(8,128)(2,1)S(1)}, u32[]{:S(2)}, u32[]{:S(2)}) async-start(bf16[4,64,256]{2,1,0:T(8,128)(2,1)} %bitcast.15), calls=%async_computation.5 | async-start | bytes 262144 | tf_op jit(solution)/shard_map/all_to_all | solution.py:157
  127.2 2.5 fusion.4
  129.7 2.1 all-to-all-done.4
  131.8 3.5 %all-to-all-start.3 = ((bf16[4,64,2048]{2,1,0:T(8,128)(2,1)}), bf16[4,64,2048]{2,1,0:T(8,128)(2,1)S(1)}, u32[]{:S(2)}, u32[]{:S(2)}) async-start(bf16[4,64,2048]{2,1,0:T(8,128)(2,1)} %bitcast.7), calls=%async_computation.4 | async-start | bytes 2097152 | tf_op jit(solution)/shard_map/all_to_all | solution.py:150
  135.3 0.0 all-gather.2.cloned.1.call-start
  135.4 0.1 iota_compare_fusion.1
  135.5 0.3 multiply_cosine_fusion
  135.8 0.8 gather_fusion.1
  136.7 13.1 %all-to-all-done.3 = bf16[4,64,2048]{2,1,0:T(8,128)(2,1)S(1)} async-done(((bf16[4,64,2048]{2,1,0:T(8,128)(2,1)}), bf16[4,64,2048]{2,1,0:T(8,128)(2,1)S(1)}, u32[]{:S(2)}, u32[]{:S(2)}) %all-to-all-start.3) | async-done | bytes 1048608 | tf_op jit(solution)/shard_map/all_to_all | solution.py:150
  149.8 0.9 gather_fusion
  150.7 1.1 fusion.54
  151.8 0.1 reshape.209
  151.9 1.4 fusion.26
  153.3 0.2 copy.78
  153.5 0.3 multiply_subtract_fusion
  153.8 0.5 fusion.28
  154.3 0.2 fusion.72
  154.4 0.5 fusion.42
  154.9 0.1 copy.77
  155.0 4.7 %fusion.55 = (f32[128,2,8]{2,1,0:T(2,128)S(1)}, f32[128,2,8,64]{3,2,1,0:T(8,128)S(1)}) fusion(bf16[128,2,64,128]{3,2,1,0:T(8,128)(2,1)} %param.20, bf16[128,2,8,64]{3,2,1,0:T(8,128)(2,1)S(1)} %get-tuple-element.12, bf16[128,2,8,64]{3,2,1,0:T(8,128)(2,1)S(1)} %get-tuple-element.11, pred[128,64]{1,0:T(8,128)(4,1)S(1)} %iota_compare_fusion.1), kind=kOutput, calls=%fused_computation.91 | convolution fusion | flops 34994176 | bytes 5259264 | tf_op jit(solution)/shard_map/rgid,rgjd->rgij/dot_general | solution.py:196
  159.7 0.1 copy.67
  159.8 0.2 copy.68
  159.9 0.8 fusion.27
  160.7 0.1 copy.69
  160.8 0.1 copy.70
  161.0 0.1 copy.71
  161.1 0.1 reshape.214
  161.2 3.5 %fusion.11 = bf16[128,2,8,128]{3,2,1,0:T(8,128)(2,1)S(1)} fusion(bf16[128,2,64,128]{3,2,1,0:T(8,128)(2,1)} %param.21, f32[128,2,8,64]{3,2,1,0:T(8,128)S(1)} %get-tuple-element.22, f32[128,2,128]{2,1,0:T(2,128)S(1)} %reshape.214, f32[128,2,8]{2,1,0:T(2,128)S(1)} %copy.71, f32[128,2,8]{2,1,0:T(2,128)S(1)} %copy.70, f32[128,2,8]{2,1,0:T(2,128)S(1)} %copy.68), kind=kOutput, calls=%fused_computation.21 | convolution fusion | flops 34734080 | bytes 5398528 | tf_op jit(solution)/shard_map/rgij,rgjd->rgid/dot_general | solution.py:214
  164.7 0.9 copy.101
  165.6 0.3 reduce-scatter.5.cloned.1.call-start
  165.9 19.8 %all-gather.2.cloned.1.call-done = bf16[512,2048]{1,0:T(8,128)(2,1)} async-done(((bf16[128,2048]{1,0:T(8,128)(2,1)}), bf16[512,2048]{1,0:T(8,128)(2,1)}) %all-gather.2.cloned.1.call-update) | async-done | bytes 2097168 | tf_op jit(solution)/shard_map/all_gather | solution.py:223
  185.7 10.5 %fusion.59 = f32[512,2048]{1,0:T(8,128)} fusion(bf16[512,2048]{1,0:T(8,128)(2,1)} %all-gather.2.cloned.1.call-done, bf16[2048,2048]{1,0:T(8,128)(2,1)} %param.19), kind=kOutput, calls=%fused_computation.95 | convolution fusion | flops 4294967296 | bytes 14680064 | tf_op jit(solution)/shard_map/dot_general | solution.py:222
  196.2 0.2 maximum_convert_fusion
  196.4 0.6 copy.102
  197.0 76.1 %reduce-scatter.5.cloned.1.call-done = f32[128,2048]{1,0:T(8,128)} async-done(((f32[512,2048]{1,0:T(8,128)}), f32[128,2048]{1,0:T(8,128)}) %reduce-scatter.5.cloned.1.call-update) | async-done | bytes 1048592 | tf_op jit(solution)/shard_map/reduce_scatter | solution.py:227
  273.1 2.1 convert_element_type.126
  (41 shorter events, 0.3 us)
Async XLA Ops:
  7.2 120.1 %copy-start = (bf16[32,16,2048]{2,1,0:T(8,128)(2,1)S(1)}, bf16[32,16,2048]{2,1,0:T(8,128)(2,1)}, u32[]{:S(2)}) copy-start(bf16[32,16,2048]{2,1,0:T(8,128)(2,1)} %param.25) | copy-start | bytes 6291460
  7.2 143.5 %reduce-scatter.3.cloned.1.call-start = ((), (), s32[]{:S(2)}) async-start(), calls=%async_computation.7 | async-start | bytes 6553600 | tf_op jit(solution)/shard_map/reduce_scatter | solution.py:172
  7.2 7.1 %copy-start.6 = (bf16[8192]{0:T(1024)(128)(2,1)S(1)}, bf16[8192]{0:T(1024)(128)(2,1)}, u32[]{:S(2)}) copy-start(bf16[8192]{0:T(1024)(128)(2,1)} %param.15) | copy-start | bytes 49156
  11.4 2.9 %copy-start.2 = (bf16[128,8192]{0,1:T(8,128)(2,1)S(1)}, bf16[128,8192]{0,1:T(8,128)(2,1)}, u32[]{:S(2)}) copy-start(bf16[128,8192]{0,1:T(8,128)(2,1)} %copy.59) | copy-start | bytes 6291460
  17.8 29.9 %copy-start.3 = (bf16[128,8192]{0,1:T(8,128)(2,1)}, bf16[128,8192]{0,1:T(8,128)(2,1)S(1)}, u32[]{:S(2)}) copy-start(bf16[128,8192]{0,1:T(8,128)(2,1)S(1)} %fusion.2) | copy-start | bytes 6291460
  51.7 7.7 %copy-start.4 = (bf16[4,128,2048]{2,1,0:T(8,128)(2,1)S(1)}, bf16[4,128,2048]{2,1,0:T(8,128)(2,1)}, u32[]{:S(2)}) copy-start(bf16[4,128,2048]{2,1,0:T(8,128)(2,1)} %copy.60) | copy-start | bytes 6291460
  51.7 7.7 %copy-start.9 = (bf16[2048,256]{1,0:T(8,128)(2,1)S(1)}, bf16[2048,256]{1,0:T(8,128)(2,1)}, u32[]{:S(2)}) copy-start(bf16[2048,256]{1,0:T(8,128)(2,1)} %param.17) | copy-start | bytes 3145732
  59.4 1.2 copy-start.10
  64.2 0.7 copy-start.12
  66.9 7.2 %all-to-all-start.1 = ((bf16[4,1,64]{2,1,0:T(2,128)(2,1)}), bf16[4,1,64]{2,1,0:T(2,128)(2,1)S(1)}, u32[]{:S(2)}, u32[]{:S(2)}) async-start(bf16[4,1,64]{2,1,0:T(2,128)(2,1)} %all_to_all.38), calls=%async_computation.2 | async-start | bytes 4096 | tf_op jit(solution)/shard_map/all_to_all | solution.py:139
  74.1 23.5 %all-to-all-start.2 = ((bf16[4,64,2048]{2,1,0:T(8,128)(2,1)}), bf16[4,64,2048]{2,1,0:T(8,128)(2,1)S(1)}, u32[]{:S(2)}, u32[]{:S(2)}) async-start(bf16[4,64,2048]{2,1,0:T(8,128)(2,1)} %bitcast.3), calls=%async_computation.3 | async-start | bytes 2097152 | tf_op jit(solution)/shard_map/all_to_all | solution.py:138
  97.6 3.4 %copy-start.8 = (bf16[32,16,2048]{2,1,0:T(8,128)(2,1)S(1)}, bf16[32,16,2048]{2,1,0:T(8,128)(2,1)}, u32[]{:S(2)}) copy-start(bf16[32,16,2048]{2,1,0:T(8,128)(2,1)} %param.24) | copy-start | bytes 6291460
  100.9 22.0 %copy-start.11 = (bf16[32,16,256]{2,1,0:T(8,128)(2,1)S(1)}, bf16[32,16,256]{2,1,0:T(8,128)(2,1)}, u32[]{:S(2)}) copy-start(bf16[32,16,256]{2,1,0:T(8,128)(2,1)} %param.27) | copy-start | bytes 786436
  123.9 7.9 %all-to-all-start.4 = ((bf16[4,64,256]{2,1,0:T(8,128)(2,1)}), bf16[4,64,256]{2,1,0:T(8,128)(2,1)S(1)}, u32[]{:S(2)}, u32[]{:S(2)}) async-start(bf16[4,64,256]{2,1,0:T(8,128)(2,1)} %bitcast.15), calls=%async_computation.5 | async-start | bytes 262144 | tf_op jit(solution)/shard_map/all_to_all | solution.py:157
  129.7 5.7 %copy-start.7 = (s32[128]{0:T(128)S(1)}, s32[128]{0:T(128)}, u32[]{:S(2)}) copy-start(s32[128]{0:T(128)} %param.22) | copy-start | bytes 1540
  131.8 18.0 %all-to-all-start.3 = ((bf16[4,64,2048]{2,1,0:T(8,128)(2,1)}), bf16[4,64,2048]{2,1,0:T(8,128)(2,1)S(1)}, u32[]{:S(2)}, u32[]{:S(2)}) async-start(bf16[4,64,2048]{2,1,0:T(8,128)(2,1)} %bitcast.7), calls=%async_computation.4 | async-start | bytes 2097152 | tf_op jit(solution)/shard_map/all_to_all | solution.py:150
  135.3 50.3 %all-gather.2.cloned.1.call-start = ((), (), s32[]{:S(2)}) async-start(), calls=%async_computation.8 | async-start | bytes 2621440 | tf_op jit(solution)/shard_map/all_gather | solution.py:223
  151.8 9.3 %copy-start.5 = (bf16[128,256]{1,0:T(8,128)(2,1)}, bf16[128,256]{1,0:T(8,128)(2,1)S(1)}, u32[]{:S(2)}) copy-start(bf16[128,256]{1,0:T(8,128)(2,1)S(1)} %get-tuple-element.10) | copy-start | bytes 196612
  165.6 107.5 %reduce-scatter.5.cloned.1.call-start = ((), (), s32[]{:S(2)}) async-start(), calls=%async_computation.9 | async-start | bytes 5242880 | tf_op jit(solution)/shard_map/reduce_scatter | solution.py:227
  196.1 79.0 %copy-start.1 = (bf16[32,16,2048]{2,1,0:T(8,128)(2,1)S(1)}, bf16[32,16,2048]{2,1,0:T(8,128)(2,1)}, u32[]{:S(2)}) copy-start(bf16[32,16,2048]{2,1,0:T(8,128)(2,1)} %param.25) | copy-start | bytes 6291460
Sparse Core Ops, SparseCore 0:
  64.3 57.3 reduce-scatter.2
  165.7 19.8 all-gather.1
  196.3 76.7 reduce-scatter.4
where the time goes:
time: 283 us; the launch traced here: 282 us
  waiting for transfers between devices  131 us (46%)
  blocking collectives  50.2 us (18%)
  matrix products  36.6 us (13%)
  local copies, waits for them, and re-layouts  19.4 us (7%)
  other arithmetic  16.5 us (6%)
  between operations  14.2 us (5%)
  starting transfers between devices  13.9 us (5%)
    reduce_scatter x1, waiting for transfers between devices, shards(): lax.psum_scatter(partial_out, 'tp', scatter_dimension=0, tiled=True)  76.1 us
    all_to_all x1, blocking collectives, shards(): lax.all_to_all(normed, 'pool', split_axis=1, concat_axis=0, tiled=True)  29.8 us
    psum x1, blocking collectives, holder_updates(): lax.psum((reduction_piece(query_down_maps), reduction_piece(value_down_ma...  20.4 us
    all_to_all x1, waiting for transfers between devices, shards(): lax.all_to_all(send_rows, 'pool', split_axis=0, concat_axis=0, tiled=True)  19.8 us
    all_gather x1, waiting for transfers between devices, shards(): lax.all_gather(attended, 'pool', axis=0, tiled=True)  19.8 us
    all_to_all x1, waiting for transfers between devices, shards(): lax.all_to_all(delta_query.reshape(pool_count, capacity, query_cols), 'po...  13.1 us
    dot_general x1, matrix products, shards(): jnp.dot(lax.all_gather(attended, 'pool', axis=0, tiled=True), output_matr...  10.5 us
    dot_general x3, matrix products, shards(): jnp.dot(gathered, weights, preferred_element_type=jnp.float32)  9.11 us
  transfers between devices with their start and end apart: 7, of which 5 were waited for; matrix products, arithmetic and copies ran while one was open for 6% of the time, Pallas kernels for 0%

commit v1 on v0

v1 whole, which is shorter than its diff:
```python
import functools
import math

import jax
import jax.numpy as jnp
from jax import lax
from jax.experimental import pallas as pl
from jax.experimental.pallas import tpu as pltpu
from jax.sharding import PartitionSpec as P

epsilon = 1e-05
adapter_scale = 0.5
rope_base = 500000.0
tile = 256
masked_score = -1e30


def params(mib):
    return pltpu.CompilerParams(vmem_limit_bytes=mib * 1024 * 1024)


def core_swap(x, pool_count):
    return lax.ppermute(x, "pool", [(p, p ^ 1) for p in range(pool_count)])


def chip_move(x, pool_count, d, e=0):
    chips = pool_count // 2
    return lax.ppermute(
        x,
        "pool",
        [(p, (p // 2 + d) % chips * 2 + ((p % 2) ^ e)) for p in range(pool_count)],
    )


def shrink_kernel(*refs):
    ids, *blocks, query_down, value_down, out = refs
    adapters = query_down.shape[0] // 16
    rows = blocks[0].shape[0]
    per = 2 if len(blocks) % 2 == 0 else 1
    for first in range(0, len(blocks), per):
        x = jnp.concatenate([b[...] for b in blocks[first : first + per]], axis=0)
        span = slice(first * rows, (first + per) * rows)
        label = ids[:, span].reshape(1, 1, per * rows)
        chosen = lax.broadcasted_iota(jnp.int32, (adapters, 1, per * rows), 0) == label
        for at, table in enumerate((query_down, value_down)):
            terms = lax.dot_general(
                table[...], x, (((1,), (1,)), ((), ())), preferred_element_type=jnp.float32
            ).reshape(adapters, 16, per * rows)
            out[at * 16 : (at + 1) * 16, span] = jnp.sum(jnp.where(chosen, terms, 0.0), axis=0)


def project_kernel(parts, block_count, *refs):
    ids = refs[0]
    lows = refs[1 : 1 + parts]
    blocks = refs[1 + parts : 1 + parts + block_count]
    wq, wk, wv, uq, uv, keep, send, xs, spread_q, spread_v = refs[1 + parts + block_count :]
    step = pl.program_id(0)
    last = pl.num_programs(0) - 1
    rows = blocks[0].shape[0]
    adapters = uq.shape[0] // 16
    total = rows * block_count

    @pl.when(step == 0)
    def _():
        for at, block in enumerate(blocks):
            xs[at * rows : (at + 1) * rows, :] = block[...]
        low = lows[0][...]
        for other in lows[1:]:
            low = low + other[...]
        low = low.astype(jnp.bfloat16).astype(jnp.float32) * adapter_scale
        chosen = lax.broadcasted_iota(jnp.int32, (adapters, 1, total), 0) == ids[...].reshape(
            1, 1, total
        )
        for at, spread in enumerate((spread_q, spread_v)):
            wide = jnp.where(chosen, low[at * 16 : (at + 1) * 16][None], 0.0)
            spread[...] = wide.reshape(adapters * 16, total).T.astype(jnp.bfloat16)

    def write(acc):
        for d in range(block_count // 2):
            at = 2 * d * rows
            keep[d] = acc[at : at + rows]
            send[d] = acc[at + rows : at + 2 * rows].astype(jnp.bfloat16)

    @pl.when(step < last)
    def _():
        write(
            jnp.dot(xs[...], wq[...], preferred_element_type=jnp.float32)
            + jnp.dot(spread_q[...], uq[...], preferred_element_type=jnp.float32)
        )

    @pl.when(step == last)
    def _():
        both = jnp.concatenate([wk[...], wv[...]], axis=1)
        acc = jnp.dot(xs[...], both, preferred_element_type=jnp.float32)
        extra = jnp.dot(spread_v[...], uv[...], preferred_element_type=jnp.float32)
        write(jnp.concatenate([acc[:, : wk.shape[1]], acc[:, wk.shape[1] :] + extra], axis=1))


def project(g, kv_heads, ids, lows, blocks, wq, wk, wv, uq, uv):
    rows, width = blocks[0].shape
    block_count = len(blocks)
    total = rows * block_count
    query_cols = wq.shape[1] // kv_heads
    head = wk.shape[1] // kv_heads
    steps = query_cols // tile
    columns = query_cols + 2 * head
    slots = uq.shape[0]

    def whole(x):
        return pl.BlockSpec(x.shape, lambda i: (0,) * x.ndim)

    def query_block(i):
        return (0, g * steps + jnp.minimum(i, steps - 1))

    def out_spec():
        return pl.BlockSpec((block_count // 2, rows, tile), lambda i: (0, 0, i))

    return pl.pallas_call(
        functools.partial(project_kernel, len(lows), block_count),
        grid=(steps + 1,),
        in_specs=[
            whole(ids),
            *[whole(x) for x in lows],
            *[whole(x) for x in blocks],
            pl.BlockSpec((width, tile), query_block),
            pl.BlockSpec((width, head), lambda i: (0, g)),
            pl.BlockSpec((width, head), lambda i: (0, g)),
            pl.BlockSpec((slots, tile), query_block),
            pl.BlockSpec((slots, head), lambda i: (0, g)),
        ],
        out_specs=[out_spec(), out_spec()],
        out_shape=[
            jax.ShapeDtypeStruct((block_count // 2, rows, columns), jnp.float32),
            jax.ShapeDtypeStruct((block_count // 2, rows, columns), jnp.bfloat16),
        ],
        scratch_shapes=[
            pltpu.VMEM((total, width), jnp.bfloat16),
            pltpu.VMEM((total, slots), jnp.bfloat16),
            pltpu.VMEM((total, slots), jnp.bfloat16),
        ],
        compiler_params=params(40),
        cost_estimate=pl.CostEstimate(
            flops=2 * total * (width + slots) * columns,
            bytes_accessed=2 * (width + slots) * columns + 6 * total * columns // 2,
            transcendentals=0,
        ),
        name=f"project_{g}",
    )(ids, *lows, *blocks, wq, wk, wv, uq, uv)


def attend_kernel(arrived, *refs):
    keep, swapped = refs[:2]
    moved = refs[2 : 2 + arrived]
    scale, cosines, sines, lengths, keys, values, out, key_out, value_out = refs[2 + arrived :]
    head = cosines.shape[1]
    rows_block = out.shape[0]
    group = out.shape[1] // head
    cache = keys.shape[2]
    score_scale = 1.0 / math.sqrt(head)
    sub = 8
    for pair in range(rows_block // 16):
        attended, new_keys, new_values = [], [], []
        for half in range(2):
            at = pair * 16 + half * sub
            r = slice(at, at + sub)
            x = keep[0, r] + swapped[0, r].astype(jnp.float32)
            for m in moved:
                x = x + m[r].astype(jnp.float32)
            x = x * scale[r]
            cos, sin = cosines[r], sines[r]

            def turn(v):
                return v * cos + pltpu.roll(v, head // 2, 1) * sin

            query = jnp.concatenate(
                [turn(x[:, h * head : (h + 1) * head]) for h in range(group)], axis=0
            ).astype(jnp.bfloat16)
            new_key = turn(x[:, group * head : (group + 1) * head]).astype(jnp.bfloat16)
            new_value = x[:, (group + 1) * head :].astype(jnp.bfloat16)
            k = keys[r, 0].reshape(sub * cache, head)
            v = values[r, 0].reshape(sub * cache, head)
            scores = (
                lax.dot_general(
                    query, k, (((1,), (1,)), ((), ())), preferred_element_type=jnp.float32
                )
                * score_scale
            )
            column = lax.broadcasted_iota(jnp.int32, (sub, sub * cache), 1)
            row = lax.broadcasted_iota(jnp.int32, (sub, sub * cache), 0)
            start = row * cache
            inside = (column >= start) & (column < start + lengths[r])
            own_key = jnp.concatenate([new_key.astype(jnp.float32)] * group, axis=0)
            own = (
                jnp.sum(query.astype(jnp.float32) * own_key, axis=1, keepdims=True) * score_scale
            )
            scores = jnp.where(
                inside[None], scores.reshape(group, sub, sub * cache), masked_score
            ).reshape(group * sub, sub * cache)
            peak = jnp.maximum(jnp.max(scores, axis=1, keepdims=True), own)
            weights = jnp.exp(scores - peak)
            own_weight = jnp.exp(own - peak)
            inverse = 1.0 / (jnp.sum(weights, axis=1, keepdims=True) + own_weight)
            mixed = jnp.dot(weights.astype(jnp.bfloat16), v, preferred_element_type=jnp.float32)
            own_value = jnp.concatenate([new_value.astype(jnp.float32)] * group, axis=0)
            mixed = (mixed + own_weight * own_value) * inverse
            attended.append(
                jnp.concatenate([mixed[h * sub : (h + 1) * sub] for h in range(group)], axis=1)
            )
            new_keys.append(new_key.astype(jnp.float32))
            new_values.append(new_value.astype(jnp.float32))
        r = slice(pair * 16, pair * 16 + 16)
        out[r] = jnp.concatenate(attended, axis=0).astype(jnp.bfloat16)
        key_out[r] = jnp.concatenate(new_keys, axis=0).astype(jnp.bfloat16)
        value_out[r] = jnp.concatenate(new_values, axis=0).astype(jnp.bfloat16)


def attend(g, keep, swapped, moved, scale, cosines, sines, lengths, keys, values):
    _, rows, columns = keep.shape
    head = keys.shape[3]
    cache = keys.shape[2]
    query_cols = columns - 2 * head
    block = 32 if rows % 32 == 0 else 16

    def by_rows(x):
        return pl.BlockSpec((block, x.shape[1]), lambda i: (i, 0))

    first = pl.BlockSpec((1, block, columns), lambda i: (0, i, 0))
    cached = pl.BlockSpec((block, 1, cache, head), lambda i: (i, g, 0, 0))
    return pl.pallas_call(
        functools.partial(attend_kernel, len(moved)),
        grid=(rows // block,),
        in_specs=[
            first,
            first,
            *[by_rows(x) for x in moved],
            by_rows(scale),
            by_rows(cosines),
            by_rows(sines),
            by_rows(lengths),
            cached,
            cached,
        ],
        out_specs=[
            pl.BlockSpec((block, query_cols), lambda i: (i, 0)),
            pl.BlockSpec((block, head), lambda i: (i, 0)),
            pl.BlockSpec((block, head), lambda i: (i, 0)),
        ],
        out_shape=[
            jax.ShapeDtypeStruct((rows, query_cols), jnp.bfloat16),
            jax.ShapeDtypeStruct((rows, head), jnp.bfloat16),
            jax.ShapeDtypeStruct((rows, head), jnp.bfloat16),
        ],
        compiler_params=params(32),
        cost_estimate=pl.CostEstimate(
            flops=4 * rows * 8 * cache * query_cols,
            bytes_accessed=4 * rows * cache * head + 8 * rows * columns,
            transcendentals=rows * 8 * cache * query_cols // head,
        ),
        name=f"attend_{g}",
    )(keep, swapped, *moved, scale, cosines, sines, lengths, keys, values)


def output_kernel(heads, *refs):
    order = refs[0]
    weights, out, xs = refs[-3:]
    blocks = refs[1:-3]
    rows, width = blocks[0].shape

    @pl.when(pl.program_id(0) == 0)
    def _():
        for at, block in enumerate(blocks):
            b, g = at // heads, at % heads
            xs[b * rows : (b + 1) * rows, g * width : (g + 1) * width] = block[...]

    acc = jnp.dot(xs[...], weights[...], preferred_element_type=jnp.float32).astype(jnp.bfloat16)
    for b in range(len(blocks) // heads):
        to = pl.multiple_of(order[b] * rows, rows)
        out[pl.ds(to, rows), :] = acc[b * rows : (b + 1) * rows]


def output_part(half, halves, heads, order, blocks, weights):
    rows, width = blocks[0].shape
    depth, columns = weights.shape
    steps = columns // halves // tile
    total = rows * len(blocks) // heads
    return pl.pallas_call(
        functools.partial(output_kernel, heads),
        grid=(steps,),
        in_specs=[
            pl.BlockSpec(memory_space=pltpu.SMEM),
            *[pl.BlockSpec(x.shape, lambda i: (0, 0)) for x in blocks],
            pl.BlockSpec((depth, tile), lambda i: (0, half * steps + i)),
        ],
        out_specs=pl.BlockSpec((total, tile), lambda i: (0, i)),
        out_shape=jax.ShapeDtypeStruct((total, columns // halves), jnp.bfloat16),
        scratch_shapes=[pltpu.VMEM((total, depth), jnp.bfloat16)],
        compiler_params=params(40),
        cost_estimate=pl.CostEstimate(
            flops=2 * total * depth * columns // halves,
            bytes_accessed=2 * depth * columns // halves + 2 * total * depth,
            transcendentals=0,
        ),
        name=f"output_{half}",
    )(order, *blocks, weights)


def line_sum(partial, n):
    z = lax.axis_index("tp")
    rows = partial.shape[0] // n

    def block(b):
        return lax.dynamic_slice_in_dim(partial, jnp.clip(b, 0, n - 1) * rows, rows, 0).astype(
            jnp.float32
        )

    right = left = None
    for s in range(1, n):
        go_right = block(n - s + z)
        go_left = block(z + s - n)
        if s > 1:
            go_right = go_right + right.astype(jnp.float32)
            go_left = go_left + left.astype(jnp.float32)
        right = lax.ppermute(
            go_right.astype(jnp.bfloat16), "tp", [(i, i + 1) for i in range(s)]
        )
        left = lax.ppermute(
            go_left.astype(jnp.bfloat16), "tp", [(n - 1 - i, n - 2 - i) for i in range(s)]
        )
    own = block(z)
    return (own + right.astype(jnp.float32) + left.astype(jnp.float32)).astype(jnp.bfloat16)


def shards(
    tokens,
    input_norm_gain,
    query_matrix,
    key_matrix,
    value_matrix,
    output_matrix,
    rotated_key_cache,
    cached_value_rows,
    cache_length_per_row,
    row_adapter_index,
    query_down_maps,
    query_up_maps,
    value_down_maps,
    value_up_maps,
):
    pool_count = lax.axis_size("pool")
    tp_count = lax.axis_size("tp")
    chips = pool_count // 2
    pool_at = lax.axis_index("pool")
    tp_at = lax.axis_index("tp")
    chip, core = pool_at // 2, pool_at % 2
    rows = tokens.shape[0]
    adapters, rank, piece = query_down_maps.shape
    base = query_matrix.shape[0]
    kv_heads = rotated_key_cache.shape[1]
    head = rotated_key_cache.shape[3]

    def scaled(start, width):
        x = lax.dynamic_slice_in_dim(tokens, start, width, 1).astype(jnp.float32)
        gain = lax.dynamic_slice_in_dim(input_norm_gain, start, width, 0).astype(jnp.float32)
        return (x * gain[None, :]).astype(jnp.bfloat16)

    def gather_pool(x):
        same = [x] + [chip_move(x, pool_count, d) for d in range(1, chips)]
        return [b for s in same for b in (s, core_swap(s, pool_count))]

    adapter_rows = gather_pool(scaled(tp_at * piece, piece))
    local_ids = (
        jnp.concatenate(gather_pool(row_adapter_index.reshape(1, rows)), axis=1)
        - pool_at * adapters
    )

    blocks = []
    for d in range(chips):
        for e in range(2):
            target = (chip + d) % chips * 2 + (core + e) % 2
            x = scaled(target * base, base)
            blocks.append(x if d == e == 0 else chip_move(x, pool_count, d, e))

    shrunk = pl.pallas_call(
        shrink_kernel,
        out_shape=jax.ShapeDtypeStruct((2 * rank, rows * pool_count), jnp.float32),
        compiler_params=params(40),
        cost_estimate=pl.CostEstimate(
            flops=4 * adapters * rank * piece * rows * pool_count,
            bytes_accessed=4 * adapters * rank * piece + 2 * piece * rows * pool_count,
            transcendentals=0,
        ),
        name="shrink",
    )(
        local_ids,
        *adapter_rows,
        query_down_maps.reshape(adapters * rank, piece),
        value_down_maps.reshape(adapters * rank, piece),
    )
    lows = [shrunk] + [
        lax.ppermute(shrunk, "tp", [(i, (i + d) % tp_count) for i in range(tp_count)])
        for d in range(1, tp_count)
    ]

    values = tokens.astype(jnp.float32)
    scale = lax.rsqrt(jnp.mean(values * values, axis=-1, keepdims=True) + epsilon)
    half_dim = head // 2
    frequency = jnp.power(
        jnp.float32(rope_base), jnp.arange(half_dim, dtype=jnp.float32) * (-2.0 / head)
    )
    angles = cache_length_per_row.astype(jnp.float32)[:, None] * frequency[None, :]
    cosines = jnp.concatenate([jnp.cos(angles)] * 2, axis=1)
    sines = jnp.concatenate([-jnp.sin(angles), jnp.sin(angles)], axis=1)
    lengths = cache_length_per_row.reshape(rows, 1)

    up_q = query_up_maps.reshape(adapters * rank, query_up_maps.shape[2])
    up_v = value_up_maps.reshape(adapters * rank, value_up_maps.shape[2])
    attended, new_keys, new_values = [], [], []
    for g in range(kv_heads):
        keep, send = project(
            g,
            kv_heads,
            local_ids,
            lows,
            blocks,
            query_matrix,
            key_matrix,
            value_matrix,
            up_q,
            up_v,
        )
        moved = []
        for d in range(1, chips):
            both = keep[d] + core_swap(send[d], pool_count).astype(jnp.float32)
            moved.append(chip_move(both.astype(jnp.bfloat16), pool_count, -d))
        swapped = core_swap(send[:1], pool_count)
        out, new_key, new_value = attend(
            g,
            keep,
            swapped,
            moved,
            scale,
            cosines,
            sines,
            lengths,
            rotated_key_cache,
            cached_value_rows,
        )
        attended.append(gather_pool(out))
        new_keys.append(new_key)
        new_values.append(new_value)

    order = jnp.stack(
        [(chip - d) % chips * 2 + (core + e) % 2 for d in range(chips) for e in range(2)]
    ).astype(jnp.int32)
    halves = 2
    columns = []
    for half in range(halves):
        partial = output_part(
            half,
            halves,
            kv_heads,
            order,
            [attended[g][b] for b in range(pool_count) for g in range(kv_heads)],
            output_matrix,
        )
        columns.append(line_sum(partial, tp_count))
    return (
        jnp.concatenate(columns, axis=1),
        jnp.concatenate(new_keys, axis=1),
        jnp.concatenate(new_values, axis=1),
    )


def solution(mesh):
    return jax.shard_map(
        shards,
        mesh=mesh,
        in_specs=(
            P(("groups", "pool"), None),
            P(),
            P("pool", "tp"),
            P("pool", "tp"),
            P("pool", "tp"),
            P("tp", "pool"),
            P(("groups", "pool"), "tp", None, None),
            P(("groups", "pool"), "tp", None, None),
            P(("groups", "pool")),
            P(("groups", "pool")),
            P("pool", None, "tp"),
            P("pool", None, "tp"),
            P("pool", None, "tp"),
            P("pool", None, "tp"),
        ),
        out_specs=(
            P(("groups", "tp"), "pool"),
            P(("groups", "pool"), "tp"),
            P(("groups", "pool"), "tp"),
        ),
        check_vma=False,
    )
```

time: 283 us -> 157 us (0.55)
  waiting for transfers between devices: 131 us -> 49.5 us
  blocking collectives: 50.2 us -> 0 us
  Pallas kernels: 0 us -> 36.7 us
  matrix products: 36.6 us -> 0 us
  starting transfers between devices: 13.9 us -> 46.2 us
  between operations: 14.2 us -> 1.22 us
  local copies, waits for them, and re-layouts: 19.4 us -> 10.7 us
  other arithmetic: 16.5 us -> 11.7 us
    reduce_scatter x2 -> x0, waiting for transfers between devices: 76.1 us -> none  [the longest x1 76.1 us: shards(): lax.psum_scatter(partial_out, 'tp', scatter_dimension=0, tiled=True)]
    ppermute x0 -> x36, waiting for transfers between devices: none -> 49.5 us  [the longest x9 33.9 us: chip_move(): lax.ppermute(x, 'pool', [(p, (p // 2 + d) % chips * 2 + (p % 2 ^ e)) for...]
    ppermute x0 -> x36, starting transfers between devices: none -> 46.2 us  [the longest x6 21.6 us: line_sum(): lax.ppermute(go_right.astype(jnp.bfloat16), 'tp', [(i, i + 1) for i in ra...]
    pallas_call x0 -> x7, Pallas kernels: none -> 36.7 us  [the longest x2 13.6 us: project(): pl.pallas_call(functools.partial(project_kernel, len(lows), block_count),...]
    dot_general x11 -> x0, matrix products: 36.6 us -> none  [the longest x1 10.5 us: shards(): jnp.dot(lax.all_gather(attended, 'pool', axis=0, tiled=True), output_matr...]
    all_to_all x4 -> x0, waiting for transfers between devices: 35 us -> none  [the longest x1 19.8 us: shards(): lax.all_to_all(send_rows, 'pool', split_axis=0, concat_axis=0, tiled=True)]
    all_to_all x1 -> x0, blocking collectives: 29.8 us -> none  [shards(): lax.all_to_all(normed, 'pool', split_axis=1, concat_axis=0, tiled=True)]
    psum x1 -> x0, blocking collectives: 20.4 us -> none  [holder_updates(): lax.psum((reduction_piece(query_down_maps), reduction_piece(value_down_ma...]
  transfers between devices with their start and end apart: 7 -> 36, of which waited for: 5 -> 10; matrix products, arithmetic and copies ran while one was open for 6% -> 4% of each run, Pallas kernels for 0% -> 17%
where the time goes in v1:
time: 157 us; the launch traced here: 156 us
  waiting for transfers between devices  49.5 us (32%)
  starting transfers between devices  46.2 us (29%)
  Pallas kernels  36.7 us (23%)
  other arithmetic  11.7 us (7%)
  local copies, waits for them, and re-layouts  10.7 us (7%)
    ppermute x9, waiting for transfers between devices, chip_move(): lax.ppermute(x, 'pool', [(p, (p // 2 + d) % chips * 2 + (p % 2 ^ e)) for...  33.9 us
    ppermute x6, starting transfers between devices, line_sum(): lax.ppermute(go_right.astype(jnp.bfloat16), 'tp', [(i, i + 1) for i in ra...  21.6 us
    pallas_call x2, Pallas kernels, project(): pl.pallas_call(functools.partial(project_kernel, len(lows), block_count),...  13.6 us
    ppermute x9, starting transfers between devices, chip_move(): lax.ppermute(x, 'pool', [(p, (p // 2 + d) % chips * 2 + (p % 2 ^ e)) for...  11.1 us
    pallas_call x2, Pallas kernels, attend(): pl.pallas_call(functools.partial(attend_kernel, len(moved)), grid=(rows /...  11 us
    unnamed x36, local copies, waits for them, and re-layouts  9.45 us
    ppermute x6, waiting for transfers between devices, line_sum(): lax.ppermute(go_left.astype(jnp.bfloat16), 'tp', [(n - 1 - i, n - 2 - i)...  9.01 us
    pallas_call x2, Pallas kernels, output_part(): pl.pallas_call(functools.partial(output_kernel, heads), grid=(steps,), in...  8.37 us
  transfers between devices with their start and end apart: 36, of which 10 were waited for; matrix products, arithmetic and copies ran while one was open for 4% of the time, Pallas kernels for 17%

profile of v1, /device:TPU:0, one launch (start us, length us, event | category | flops | bytes accessed | tf_op | source)
XLA Modules:
  0.0 156.0 jit_solution(15248213852627171209)
XLA Ops:
  0.7 0.8 dynamic-slice_convert_fusion
  1.5 3.4 %multiply_convert_fusion = (bf16[128,2048]{1,0:T(8,128)(2,1)}, bf16[128,2048]{1,0:T(8,128)(2,1)}, bf16[128,2048]{1,0:T(8,128)(2,1)}, bf16[128,2048]{1,0:T(8,128)(2,1)S(1)}, bf16[128,2048]{1,0:T(8,128)(2,1)S(1)}) fusion(f32[2048]{0:T(1024)S(1)} %get-tuple-element.40, bf16[128,8192]{1,0:T(8,128)(2,1)} %param.14, s32[]{:T(128)S(6)} %select_n.112, ...), kind=kLoop, calls=%fused_computation.1 | loop fusion | flops 3932160 | bytes 5283860 | tf_op jit(solution)/shard_map/convert_element_type | solution.py:364
  5.0 3.0 %collective-permute-start.4 = (bf16[128,2048]{1,0:T(8,128)(2,1)S(1)}, bf16[128,2048]{1,0:T(8,128)(2,1)S(1)}, u32[]{:S(2)}, u32[]{:S(2)}) collective-permute-start(bf16[128,2048]{1,0:T(8,128)(2,1)S(1)} %get-tuple-element.27.refs_1_), channel_id=1, source_target_pairs={{0,8},{4,12},{8,0},{12,4},{1,9},{5,13},{9,1},{13,5},{2,10},{6,14},... | collective-permute-start | bytes 1572872 | tf_op jit(solution)/shard_map/ppermute | solution.py:28
  8.0 0.5 collective-permute-start.3
  8.5 11.4 %collective-permute-done.1 = s32[1,128]{1,0:T(1,128)S(1)} collective-permute-done((s32[1,128]{1,0:T(1,128)S(1)}, s32[1,128]{1,0:T(1,128)S(1)}, u32[]{:S(2)}, u32[]{:S(2)}) %collective-permute-start.1) | collective-permute-done | bytes 544 | tf_op jit(solution)/shard_map/ppermute | solution.py:28
  19.9 0.5 collective-permute-start.5
  20.4 0.5 multiply_reduce_fusion
  20.9 1.8 %collective-permute-start.10 = (bf16[128,2048]{1,0:T(8,128)(2,1)}, bf16[128,2048]{1,0:T(8,128)(2,1)S(1)}, u32[]{:S(2)}, u32[]{:S(2)}) collective-permute-start(bf16[128,2048]{1,0:T(8,128)(2,1)} %get-tuple-element.24), channel_id=1, source_target_pairs={{0,8},{4,12},{8,0},{12,4},{1,9},{5,13},{9,1},{13,5},{2,10},{6,14},... | collective-permute-start | bytes 1572872 | tf_op jit(solution)/shard_map/ppermute | solution.py:28
  22.7 0.1 copy.17.refs_3_
  23.0 1.6 %copy-done.13 = bf16[32,16,2048]{2,1,0:T(8,128)(2,1)S(1)} copy-done((bf16[32,16,2048]{2,1,0:T(8,128)(2,1)S(1)}, bf16[32,16,2048]{2,1,0:T(8,128)(2,1)}, u32[]{:S(2)}) %copy-start.13) | copy-done | bytes 2097176
  24.6 1.6 %copy-done.14 = bf16[32,16,2048]{2,1,0:T(8,128)(2,1)S(1)} copy-done((bf16[32,16,2048]{2,1,0:T(8,128)(2,1)S(1)}, bf16[32,16,2048]{2,1,0:T(8,128)(2,1)}, u32[]{:S(2)}) %copy-start.14) | copy-done | bytes 2097176
  26.2 3.7 %shrink.1.refs_1_ = f32[32,512]{1,0:T(8,128)S(1)} custom-call(s32[1,512]{1,0:T(1,128)S(1)} %add_subtract_fusion.refs_0_, bf16[128,2048]{1,0:T(8,128)(2,1)S(1)} %get-tuple-element.27.refs_1_, bf16[128,2048]{1,0:T(8,128)(2,1)} %collective-permute-done.3.refs_2_, bf16[128,2048]{1,0:T(8,128)(2,1)S(1)} %collective-permute-done.4.refs_3_, ...), custom_call_target="tpu_custom_call" | custom-call | flops 2147483648 | bytes 6291456 | tf_op jit(solution)/shard_map/shrink/pallas_call | solution.py:383
  29.9 1.6 %collective-permute-start.6 = (f32[32,512]{1,0:T(8,128)S(1)}, f32[32,512]{1,0:T(8,128)S(1)}, u32[]{:S(2)}, u32[]{:S(2)}) collective-permute-start(f32[32,512]{1,0:T(8,128)S(1)} %shrink.1.refs_1_), channel_id=1, source_target_pairs={{0,1},{1,2},{2,3},{3,0},{4,5},{5,6},{6,7},{7,4},{8,9},{9,10},{10,1... | collective-permute-start | bytes 196616 | tf_op jit(solution)/shard_map/ppermute | solution.py:400
  31.6 2.6 %collective-permute-start.7 = (f32[32,512]{1,0:T(8,128)S(1)}, f32[32,512]{1,0:T(8,128)S(1)}, u32[]{:S(2)}, u32[]{:S(2)}) collective-permute-start(f32[32,512]{1,0:T(8,128)S(1)} %shrink.1.refs_1_), channel_id=1, source_target_pairs={{0,2},{1,3},{2,0},{3,1},{4,6},{5,7},{6,4},{7,5},{8,10},{9,11},{10,... | collective-permute-start | bytes 196616 | tf_op jit(solution)/shard_map/ppermute | solution.py:400
  34.2 1.3 collective-permute-start.8
  35.5 0.5 collective-permute-done.10.refs_7_
  36.0 9.6 %collective-permute-done.11.refs_8_ = bf16[128,2048]{1,0:T(8,128)(2,1)S(1)} collective-permute-done((bf16[128,2048]{1,0:T(8,128)(2,1)}, bf16[128,2048]{1,0:T(8,128)(2,1)S(1)}, u32[]{:S(2)}, u32[]{:S(2)}) %collective-permute-start.11) | collective-permute-done | bytes 524320 | tf_op jit(solution)/shard_map/ppermute | solution.py:28
  45.7 6.7 %project_0.1 = (f32[2,128,1280]{2,1,0:T(8,128)S(1)}, bf16[2,128,1280]{2,1,0:T(8,128)(2,1)S(1)}) custom-call(s32[1,512]{1,0:T(1,128)S(1)} %add_subtract_fusion.refs_0_, f32[32,512]{1,0:T(8,128)S(1)} %shrink.1.refs_1_, f32[32,512]{1,0:T(8,128)S(1)} %collective-permute-done.6.refs_2_, f32[32,512]{1,0:T(8,128)S(1)} %collective-permute-done.7.refs_3_, ...), custom_call_target="tpu_custom_call" | custom-call | flops 3355443200 | bytes 8519680 | tf_op jit(solution)/shard_map/project_0/pallas_call | solution.py:118
  52.5 0.5 collective-permute-start.12
  53.1 6.8 %project_1.1 = (f32[2,128,1280]{2,1,0:T(8,128)S(1)}, bf16[2,128,1280]{2,1,0:T(8,128)(2,1)S(1)}) custom-call(s32[1,512]{1,0:T(1,128)S(1)} %add_subtract_fusion.refs_0_, f32[32,512]{1,0:T(8,128)S(1)} %shrink.1.refs_1_, f32[32,512]{1,0:T(8,128)S(1)} %collective-permute-done.6.refs_2_, f32[32,512]{1,0:T(8,128)S(1)} %collective-permute-done.7.refs_3_, ...), custom_call_target="tpu_custom_call" | custom-call | flops 3355443200 | bytes 8519680 | tf_op jit(solution)/shard_map/project_1/pallas_call | solution.py:118
  60.0 0.5 collective-permute-start.15
  60.7 1.8 %collective-permute-start.14 = (bf16[128,1280]{1,0:T(8,128)(2,1)S(1)}, bf16[128,1280]{1,0:T(8,128)(2,1)S(1)}, u32[]{:S(2)}, u32[]{:S(2)}) collective-permute-start(bf16[128,1280]{1,0:T(8,128)(2,1)S(1)} %fusion.1), channel_id=1, source_target_pairs={{0,8},{4,12},{8,0},{12,4},{1,9},{5,13},{9,1},{13,5},{2,10},{6,14},... | collective-permute-start | bytes 983048 | tf_op jit(solution)/shard_map/ppermute | solution.py:28
  62.5 1.6 %collective-permute-start.17 = (bf16[128,1280]{1,0:T(8,128)(2,1)S(1)}, bf16[128,1280]{1,0:T(8,128)(2,1)S(1)}, u32[]{:S(2)}, u32[]{:S(2)}) collective-permute-start(bf16[128,1280]{1,0:T(8,128)(2,1)S(1)} %fusion), channel_id=1, source_target_pairs={{0,8},{4,12},{8,0},{12,4},{1,9},{5,13},{9,1},{13,5},{2,10},{6,14},... | collective-permute-start | bytes 983048 | tf_op jit(solution)/shard_map/ppermute | solution.py:28
  64.1 0.3 fusion.2
  64.5 6.7 %collective-permute-done.14.refs_2_ = bf16[128,1280]{1,0:T(8,128)(2,1)S(1)} collective-permute-done((bf16[128,1280]{1,0:T(8,128)(2,1)S(1)}, bf16[128,1280]{1,0:T(8,128)(2,1)S(1)}, u32[]{:S(2)}, u32[]{:S(2)}) %collective-permute-start.14) | collective-permute-done | bytes 327712 | tf_op jit(solution)/shard_map/ppermute | solution.py:28
  71.2 5.5 %attend_0.1 = (bf16[128,1024]{1,0:T(8,128)(2,1)S(1)}, bf16[128,128]{1,0:T(8,128)(2,1)S(1)}, bf16[128,128]{1,0:T(8,128)(2,1)S(1)}) custom-call(f32[2,128,1280]{2,1,0:T(8,128)S(1)} %get-tuple-element.13.refs_0_, bf16[1,128,1280]{2,1,0:T(8,128)(2,1)S(1)} %collective-permute-done.12.refs_1_, bf16[128,1280]{1,0:T(8,128)(2,1)S(1)} %collective-permute-done.14.refs_2_, ...), custom_call_target="tpu_custom_call" | custom-call | flops 268435456 | bytes 5505024 | tf_op jit(solution)/shard_map/attend_0/pallas_call | solution.py:229
  76.8 1.8 %collective-permute-start.20 = (bf16[128,1024]{1,0:T(8,128)(2,1)S(1)}, bf16[128,1024]{1,0:T(8,128)(2,1)S(1)}, u32[]{:S(2)}, u32[]{:S(2)}) collective-permute-start(bf16[128,1024]{1,0:T(8,128)(2,1)S(1)} %get-tuple-element.15.refs_1_), channel_id=1, source_target_pairs={{0,8},{4,12},{8,0},{12,4},{1,9},{5,13},{9,1},{13,5},{2,10},{6,14},... | collective-permute-start | bytes 786440 | tf_op jit(solution)/shard_map/ppermute | solution.py:28
  78.6 5.5 %attend_1.1 = (bf16[128,1024]{1,0:T(8,128)(2,1)S(1)}, bf16[128,128]{1,0:T(8,128)(2,1)S(1)}, bf16[128,128]{1,0:T(8,128)(2,1)S(1)}) custom-call(f32[2,128,1280]{2,1,0:T(8,128)S(1)} %get-tuple-element.16.refs_0_, bf16[1,128,1280]{2,1,0:T(8,128)(2,1)S(1)} %collective-permute-done.15.refs_1_, bf16[128,1280]{1,0:T(8,128)(2,1)S(1)} %collective-permute-done.17.refs_2_, ...), custom_call_target="tpu_custom_call" | custom-call | flops 268435456 | bytes 5505024 | tf_op jit(solution)/shard_map/attend_1/pallas_call | solution.py:229
  84.1 1.0 collective-permute-start.21
  85.1 0.5 collective-permute-start.19
  85.7 5.7 %collective-permute-done.21.refs_6_ = bf16[128,1024]{1,0:T(8,128)(2,1)S(1)} collective-permute-done((bf16[128,1024]{1,0:T(8,128)(2,1)S(1)}, bf16[128,1024]{1,0:T(8,128)(2,1)S(1)}, u32[]{:S(2)}, u32[]{:S(2)}) %collective-permute-start.21) | collective-permute-done | bytes 262176 | tf_op jit(solution)/shard_map/ppermute | solution.py:28
  91.4 1.4 collective-permute-done.23.refs_8_
  92.8 3.4 %copy-done = bf16[2048,2048]{1,0:T(8,128)(2,1)S(1)} copy-done((bf16[2048,2048]{1,0:T(8,128)(2,1)S(1)}, bf16[2048,2048]{1,0:T(8,128)(2,1)}, u32[]{:S(2)}) %copy-start) | copy-done | bytes 8388632
  96.2 4.2 %output_1.1 = bf16[512,1024]{1,0:T(8,128)(2,1)S(1)} custom-call(s32[4]{0:T(128)S(1)} %pad_add_fusion.refs_0_, bf16[128,1024]{1,0:T(8,128)(2,1)S(1)} %get-tuple-element.15.refs_1_, bf16[128,1024]{1,0:T(8,128)(2,1)S(1)} %get-tuple-element.18.refs_2_, bf16[128,1024]{1,0:T(8,128)(2,1)S(1)} %collective-permute-done.18.refs_3_, ...), custom_call_target="tpu_custom_call" | custom-call | flops 2147483648 | bytes 6291456 | tf_op jit(solution)/shard_map/output_1/pallas_call | solution.py:286
  100.5 0.9 constant_dynamic-slice_fusion.1
  101.3 4.4 %collective-permute-start.30 = (bf16[128,1024]{1,0:T(8,128)(2,1)}, bf16[128,1024]{1,0:T(8,128)(2,1)}, u32[]{:S(2)}, u32[]{:S(2)}) collective-permute-start(bf16[128,1024]{1,0:T(8,128)(2,1)} %get-tuple-element.34), channel_id=1, source_target_pairs={{0,1},{4,5},{8,9},{12,13},{16,17},{20,21},{24,25},{28,29}} | collective-permute-start | bytes 786440 | tf_op jit(solution)/shard_map/ppermute | solution.py:323
  105.7 0.9 copy-done.8
  106.6 0.9 copy-done.10
  107.6 0.9 copy-done.12
  108.5 4.2 %output_0.1 = bf16[512,1024]{1,0:T(8,128)(2,1)S(1)} custom-call(s32[4]{0:T(128)S(1)} %pad_add_fusion.refs_0_, bf16[128,1024]{1,0:T(8,128)(2,1)S(1)} %get-tuple-element.15.refs_1_, bf16[128,1024]{1,0:T(8,128)(2,1)S(1)} %get-tuple-element.18.refs_2_, bf16[128,1024]{1,0:T(8,128)(2,1)S(1)} %collective-permute-done.18.refs_3_, bf16[128,1024]{1,0:T(8,128)(2,1)S(1)} %copy-done.8, ...), custom_call_target="tpu_custom_call" | custom-call | flops 2147483648 | bytes 6291456 | tf_op jit(solution)/shard_map/output_0/pallas_call | solution.py:286
  112.8 2.0 %collective-permute-start.24 = (bf16[128,1024]{1,0:T(8,128)(2,1)S(1)}, bf16[128,1024]{1,0:T(8,128)(2,1)}, u32[]{:S(2)}, u32[]{:S(2)}) collective-permute-start(bf16[128,1024]{1,0:T(8,128)(2,1)S(1)} %get-tuple-element.30), channel_id=1, source_target_pairs={{0,1},{4,5},{8,9},{12,13},{16,17},{20,21},{24,25},{28,29}} | collective-permute-start | bytes 786440 | tf_op jit(solution)/shard_map/ppermute | solution.py:323
  114.8 0.7 collective-permute-start.33
  115.4 1.7 %add_convert_fusion.4 = bf16[128,1024]{1,0:T(8,128)(2,1)} fusion(bf16[128,1024]{1,0:T(8,128)(2,1)} %collective-permute-done.30, bf16[512,1024]{1,0:T(8,128)(2,1)S(1)} %output_1.1, s32[]{:T(128)S(6)} %select_n.115), kind=kLoop, calls=%fused_computation.15 | loop fusion | flops 524288 | bytes 786436 | tf_op jit(solution)/shard_map/convert_element_type | solution.py:324
  117.2 1.3 collective-permute-start.31
  118.5 0.7 collective-permute-start.27
  119.2 1.6 collective-permute-done.24
  120.7 1.7 %add_convert_fusion.9 = bf16[128,1024]{1,0:T(8,128)(2,1)} fusion(bf16[128,1024]{1,0:T(8,128)(2,1)} %collective-permute-done.24, bf16[512,1024]{1,0:T(8,128)(2,1)S(1)} %output_0.1, s32[]{:T(128)S(6)} %select_n.115), kind=kLoop, calls=%fused_computation.20 | loop fusion | flops 524288 | bytes 786436 | tf_op jit(solution)/shard_map/convert_element_type | solution.py:324
  122.4 4.5 %collective-permute-start.25 = (bf16[128,1024]{1,0:T(8,128)(2,1)}, bf16[128,1024]{1,0:T(8,128)(2,1)S(1)}, u32[]{:S(2)}, u32[]{:S(2)}) collective-permute-start(bf16[128,1024]{1,0:T(8,128)(2,1)} %add_convert_fusion.9), channel_id=1, source_target_pairs={{0,1},{1,2},{4,5},{5,6},{8,9},{9,10},{12,13},{13,14},{16,17},{17,1... | collective-permute-start | bytes 786440 | tf_op jit(solution)/shard_map/ppermute | solution.py:323
  127.0 0.2 add_convert_fusion.3
  127.2 0.7 collective-permute-start.34
  127.9 3.6 %collective-permute-done.25 = bf16[128,1024]{1,0:T(8,128)(2,1)S(1)} collective-permute-done((bf16[128,1024]{1,0:T(8,128)(2,1)}, bf16[128,1024]{1,0:T(8,128)(2,1)S(1)}, u32[]{:S(2)}, u32[]{:S(2)}) %collective-permute-start.25) | collective-permute-done | bytes 262176 | tf_op jit(solution)/shard_map/ppermute | solution.py:323
  131.5 0.2 add_convert_fusion.8
  131.7 0.7 collective-permute-start.28
  132.4 0.6 pad_maximum_fusion.3
  133.0 4.9 %collective-permute-start.32 = (bf16[128,1024]{1,0:T(8,128)(2,1)S(1)}, bf16[128,1024]{1,0:T(8,128)(2,1)S(1)}, u32[]{:S(2)}, u32[]{:S(2)}) collective-permute-start(bf16[128,1024]{1,0:T(8,128)(2,1)S(1)} %get-tuple-element.32), channel_id=1, source_target_pairs={{0,1},{1,2},{2,3},{4,5},{5,6},{6,7},{8,9},{9,10},{10,11},{12,13},{... | collective-permute-start | bytes 786440 | tf_op jit(solution)/shard_map/ppermute | solution.py:323
  137.9 4.6 %collective-permute-start.26 = (bf16[128,1024]{1,0:T(8,128)(2,1)S(1)}, bf16[128,1024]{1,0:T(8,128)(2,1)S(1)}, u32[]{:S(2)}, u32[]{:S(2)}) collective-permute-start(bf16[128,1024]{1,0:T(8,128)(2,1)S(1)} %get-tuple-element.28), channel_id=1, source_target_pairs={{0,1},{1,2},{2,3},{4,5},{5,6},{6,7},{8,9},{9,10},{10,11},{12,13},{... | collective-permute-start | bytes 786440 | tf_op jit(solution)/shard_map/ppermute | solution.py:323
  142.6 1.3 collective-permute-start.35
  143.9 1.3 collective-permute-start.29
  145.2 0.6 pad_maximum_fusion.4
  145.9 6.3 %collective-permute-done.35 = bf16[128,1024]{1,0:T(8,128)(2,1)S(1)} collective-permute-done((bf16[128,1024]{1,0:T(8,128)(2,1)S(1)}, bf16[128,1024]{1,0:T(8,128)(2,1)S(1)}, u32[]{:S(2)}, u32[]{:S(2)}) %collective-permute-start.35) | collective-permute-done | bytes 262176 | tf_op jit(solution)/shard_map/ppermute | solution.py:326
  152.2 0.1 add_convert_fusion
  152.4 2.7 %collective-permute-done.29 = bf16[128,1024]{1,0:T(8,128)(2,1)S(1)} collective-permute-done((bf16[128,1024]{1,0:T(8,128)(2,1)S(1)}, bf16[128,1024]{1,0:T(8,128)(2,1)S(1)}, u32[]{:S(2)}, u32[]{:S(2)}) %collective-permute-start.29) | collective-permute-done | bytes 262176 | tf_op jit(solution)/shard_map/ppermute | solution.py:326
  155.0 0.1 add_convert_fusion.5
  155.2 0.8 pad_maximum_fusion
  (80 shorter events, 1.1 us)
Async XLA Ops:
  1.5 6.4 %copy-start.17 = (s32[128]{0:T(128)S(1)}, s32[128]{0:T(128)}, u32[]{:S(2)}) copy-start(s32[128]{0:T(128)} %param.23) | copy-start | bytes 1540
  1.5 18.9 %copy-start.15 = (bf16[128,8192]{1,0:T(8,128)(2,1)S(1)}, bf16[128,8192]{1,0:T(8,128)(2,1)}, u32[]{:S(2)}) copy-start(bf16[128,8192]{1,0:T(8,128)(2,1)} %param.14) | copy-start | bytes 6291460
  4.9 17.9 %copy-start.16 = (s32[128]{0:T(128)S(1)}, s32[128]{0:T(128)}, u32[]{:S(2)}) copy-start(s32[128]{0:T(128)} %param.22) | copy-start | bytes 1540
  5.0 15.0 %collective-permute-start.4 = (bf16[128,2048]{1,0:T(8,128)(2,1)S(1)}, bf16[128,2048]{1,0:T(8,128)(2,1)S(1)}, u32[]{:S(2)}, u32[]{:S(2)}) collective-permute-start(bf16[128,2048]{1,0:T(8,128)(2,1)S(1)} %get-tuple-element.27.refs_1_), channel_id=1, source_target_pairs={{0,8},{4,12},{8,0},{12,4},{1,9},{5,13},{9,1},{13,5},{2,10},{6,14},... | collective-permute-start | bytes 1572872 | tf_op jit(solution)/shard_map/ppermute | solution.py:28
  7.9 12.0 %collective-permute-start.1 = (s32[1,128]{1,0:T(1,128)S(1)}, s32[1,128]{1,0:T(1,128)S(1)}, u32[]{:S(2)}, u32[]{:S(2)}) collective-permute-start(s32[1,128]{1,0:T(1,128)S(1)} %bitcast.31), channel_id=1, source_target_pairs={{0,8},{4,12},{8,0},{12,4},{1,9},{5,13},{9,1},{13,5},{2,10},{6,14},... | collective-permute-start | bytes 1544 | tf_op jit(solution)/shard_map/ppermute | solution.py:28
  8.0 12.9 %collective-permute-start = (s32[1,128]{1,0:T(1,128)S(1)}, s32[1,128]{1,0:T(1,128)S(1)}, u32[]{:S(2)}, u32[]{:S(2)}) collective-permute-start(s32[1,128]{1,0:T(1,128)S(1)} %bitcast.32), channel_id=1, source_target_pairs={{0,4},{4,0},{8,12},{12,8},{1,5},{5,1},{9,13},{13,9},{2,6},{6,2},{1... | collective-permute-start | bytes 1544 | tf_op jit(solution)/shard_map/ppermute | solution.py:23
  8.0 15.0 %collective-permute-start.3 = (bf16[128,2048]{1,0:T(8,128)(2,1)S(1)}, bf16[128,2048]{1,0:T(8,128)(2,1)}, u32[]{:S(2)}, u32[]{:S(2)}) collective-permute-start(bf16[128,2048]{1,0:T(8,128)(2,1)S(1)} %get-tuple-element.27.refs_1_), channel_id=1, source_target_pairs={{0,4},{4,0},{8,12},{12,8},{1,5},{5,1},{9,13},{13,9},{2,6},{6,2},{1... | collective-permute-start | bytes 1572872 | tf_op jit(solution)/shard_map/ppermute | solution.py:23
  8.5 25.7 %collective-permute-start.9 = (bf16[128,2048]{1,0:T(8,128)(2,1)}, bf16[128,2048]{1,0:T(8,128)(2,1)S(1)}, u32[]{:S(2)}, u32[]{:S(2)}) collective-permute-start(bf16[128,2048]{1,0:T(8,128)(2,1)} %get-tuple-element.25), channel_id=1, source_target_pairs={{0,4},{4,0},{8,12},{12,8},{1,5},{5,1},{9,13},{13,9},{2,6},{6,2},{1... | collective-permute-start | bytes 1572872 | tf_op jit(solution)/shard_map/ppermute | solution.py:28
  19.9 2.8 %collective-permute-start.2 = (s32[1,128]{1,0:T(1,128)S(1)}, s32[1,128]{1,0:T(1,128)S(1)}, u32[]{:S(2)}, u32[]{:S(2)}) collective-permute-start(s32[1,128]{1,0:T(1,128)S(1)} %collective-permute-done.1), channel_id=1, source_target_pairs={{0,4},{4,0},{8,12},{12,8},{1,5},{5,1},{9,13},{13,9},{2,6},{6,2},{1... | collective-permute-start | bytes 1544 | tf_op jit(solution)/shard_map/ppermute | solution.py:23
  19.9 3.1 %collective-permute-start.5 = (bf16[128,2048]{1,0:T(8,128)(2,1)S(1)}, bf16[128,2048]{1,0:T(8,128)(2,1)}, u32[]{:S(2)}, u32[]{:S(2)}) collective-permute-start(bf16[128,2048]{1,0:T(8,128)(2,1)S(1)} %collective-permute-done.4.refs_3_), channel_id=1, source_target_pairs={{0,4},{4,0},{8,12},{12,8},{1,5},{5,1},{9,13},{13,9},{2,6},{6,2},{1... | collective-permute-start | bytes 1572872 | tf_op jit(solution)/shard_map/ppermute | solution.py:23
  20.9 15.1 %collective-permute-start.10 = (bf16[128,2048]{1,0:T(8,128)(2,1)}, bf16[128,2048]{1,0:T(8,128)(2,1)S(1)}, u32[]{:S(2)}, u32[]{:S(2)}) collective-permute-start(bf16[128,2048]{1,0:T(8,128)(2,1)} %get-tuple-element.24), channel_id=1, source_target_pairs={{0,8},{4,12},{8,0},{12,4},{1,9},{5,13},{9,1},{13,5},{2,10},{6,14},... | collective-permute-start | bytes 1572872 | tf_op jit(solution)/shard_map/ppermute | solution.py:28
  22.7 22.9 %collective-permute-start.11 = (bf16[128,2048]{1,0:T(8,128)(2,1)}, bf16[128,2048]{1,0:T(8,128)(2,1)S(1)}, u32[]{:S(2)}, u32[]{:S(2)}) collective-permute-start(bf16[128,2048]{1,0:T(8,128)(2,1)} %get-tuple-element.23), channel_id=1, source_target_pairs={{0,12},{4,8},{8,4},{12,0},{1,13},{5,9},{9,5},{13,1},{2,14},{6,10},... | collective-permute-start | bytes 1572872 | tf_op jit(solution)/shard_map/ppermute | solution.py:28
  23.0 1.6 %copy-start.13 = (bf16[32,16,2048]{2,1,0:T(8,128)(2,1)S(1)}, bf16[32,16,2048]{2,1,0:T(8,128)(2,1)}, u32[]{:S(2)}) copy-start(bf16[32,16,2048]{2,1,0:T(8,128)(2,1)} %param.24) | copy-start | bytes 6291460
  24.6 1.6 %copy-start.14 = (bf16[32,16,2048]{2,1,0:T(8,128)(2,1)S(1)}, bf16[32,16,2048]{2,1,0:T(8,128)(2,1)}, u32[]{:S(2)}) copy-start(bf16[32,16,2048]{2,1,0:T(8,128)(2,1)} %param.26) | copy-start | bytes 6291460
  26.2 19.4 %copy-start.3 = (bf16[32,16,2048]{2,1,0:T(8,128)(2,1)S(1)}, bf16[32,16,2048]{2,1,0:T(8,128)(2,1)}, u32[]{:S(2)}) copy-start(bf16[32,16,2048]{2,1,0:T(8,128)(2,1)} %param.25) | copy-start | bytes 6291460
  26.2 19.4 %copy-start.4 = (bf16[2048,256]{1,0:T(8,128)(2,1)S(1)}, bf16[2048,256]{1,0:T(8,128)(2,1)}, u32[]{:S(2)}) copy-start(bf16[2048,256]{1,0:T(8,128)(2,1)} %refs_10_.3) | copy-start | bytes 3145732
  26.2 19.5 %copy-start.5 = (bf16[2048,256]{1,0:T(8,128)(2,1)S(1)}, bf16[2048,256]{1,0:T(8,128)(2,1)}, u32[]{:S(2)}) copy-start(bf16[2048,256]{1,0:T(8,128)(2,1)} %refs_11_.3) | copy-start | bytes 3145732
  26.2 19.5 %copy-start.6 = (bf16[32,16,256]{2,1,0:T(8,128)(2,1)S(1)}, bf16[32,16,256]{2,1,0:T(8,128)(2,1)}, u32[]{:S(2)}) copy-start(bf16[32,16,256]{2,1,0:T(8,128)(2,1)} %param.27) | copy-start | bytes 786436
  29.9 15.7 %collective-permute-start.6 = (f32[32,512]{1,0:T(8,128)S(1)}, f32[32,512]{1,0:T(8,128)S(1)}, u32[]{:S(2)}, u32[]{:S(2)}) collective-permute-start(f32[32,512]{1,0:T(8,128)S(1)} %shrink.1.refs_1_), channel_id=1, source_target_pairs={{0,1},{1,2},{2,3},{3,0},{4,5},{5,6},{6,7},{7,4},{8,9},{9,10},{10,1... | collective-permute-start | bytes 196616 | tf_op jit(solution)/shard_map/ppermute | solution.py:400
  31.6 14.1 %collective-permute-start.7 = (f32[32,512]{1,0:T(8,128)S(1)}, f32[32,512]{1,0:T(8,128)S(1)}, u32[]{:S(2)}, u32[]{:S(2)}) collective-permute-start(f32[32,512]{1,0:T(8,128)S(1)} %shrink.1.refs_1_), channel_id=1, source_target_pairs={{0,2},{1,3},{2,0},{3,1},{4,6},{5,7},{6,4},{7,5},{8,10},{9,11},{10,... | collective-permute-start | bytes 196616 | tf_op jit(solution)/shard_map/ppermute | solution.py:400
  34.2 11.5 %collective-permute-start.8 = (f32[32,512]{1,0:T(8,128)S(1)}, f32[32,512]{1,0:T(8,128)S(1)}, u32[]{:S(2)}, u32[]{:S(2)}) collective-permute-start(f32[32,512]{1,0:T(8,128)S(1)} %shrink.1.refs_1_), channel_id=1, source_target_pairs={{0,3},{1,0},{2,1},{3,2},{4,7},{5,4},{6,5},{7,6},{8,11},{9,8},{10,9... | collective-permute-start | bytes 196616 | tf_op jit(solution)/shard_map/ppermute | solution.py:400
  52.5 12.1 %collective-permute-start.12 = (bf16[1,128,1280]{2,1,0:T(8,128)(2,1)S(1)}, bf16[1,128,1280]{2,1,0:T(8,128)(2,1)S(1)}, u32[]{:S(2)}, u32[]{:S(2)}) collective-permute-start(bf16[1,128,1280]{2,1,0:T(8,128)(2,1)S(1)} %get-tuple-element.39), channel_id=1, source_target_pairs={{0,4},{4,0},{8,12},{12,8},{1,5},{5,1},{9,13},{13,9},{2,6},{6,2},{1... | collective-permute-start | bytes 983048 | tf_op jit(solution)/shard_map/ppermute | solution.py:23
  53.0 7.6 %collective-permute-start.13 = (bf16[128,1280]{1,0:T(8,128)(2,1)S(1)}, bf16[128,1280]{1,0:T(8,128)(2,1)S(1)}, u32[]{:S(2)}, u32[]{:S(2)}) collective-permute-start(bf16[128,1280]{1,0:T(8,128)(2,1)S(1)} %get-tuple-element.38), channel_id=1, source_target_pairs={{0,4},{4,0},{8,12},{12,8},{1,5},{5,1},{9,13},{13,9},{2,6},{6,2},{1... | collective-permute-start | bytes 983048 | tf_op jit(solution)/shard_map/ppermute | solution.py:23
  53.1 18.2 %copy-start.2 = (bf16[128,2,64,128]{3,2,1,0:T(8,128)(2,1)S(1)}, bf16[128,2,64,128]{3,2,1,0:T(8,128)(2,1)}, u32[]{:S(2)}) copy-start(bf16[128,2,64,128]{3,2,1,0:T(8,128)(2,1)} %refs_8_.3) | copy-start | bytes 12582916
  59.9 11.3 %copy-start.1 = (bf16[128,2,64,128]{3,2,1,0:T(8,128)(2,1)S(1)}, bf16[128,2,64,128]{3,2,1,0:T(8,128)(2,1)}, u32[]{:S(2)}) copy-start(bf16[128,2,64,128]{3,2,1,0:T(8,128)(2,1)} %refs_7_.3) | copy-start | bytes 12582916
  60.0 18.6 %collective-permute-start.15 = (bf16[1,128,1280]{2,1,0:T(8,128)(2,1)S(1)}, bf16[1,128,1280]{2,1,0:T(8,128)(2,1)S(1)}, u32[]{:S(2)}, u32[]{:S(2)}) collective-permute-start(bf16[1,128,1280]{2,1,0:T(8,128)(2,1)S(1)} %get-tuple-element.37), channel_id=1, source_target_pairs={{0,4},{4,0},{8,12},{12,8},{1,5},{5,1},{9,13},{13,9},{2,6},{6,2},{1... | collective-permute-start | bytes 983048 | tf_op jit(solution)/shard_map/ppermute | solution.py:23
  60.5 2.0 %collective-permute-start.16 = (bf16[128,1280]{1,0:T(8,128)(2,1)S(1)}, bf16[128,1280]{1,0:T(8,128)(2,1)S(1)}, u32[]{:S(2)}, u32[]{:S(2)}) collective-permute-start(bf16[128,1280]{1,0:T(8,128)(2,1)S(1)} %get-tuple-element.36), channel_id=1, source_target_pairs={{0,4},{4,0},{8,12},{12,8},{1,5},{5,1},{9,13},{13,9},{2,6},{6,2},{1... | collective-permute-start | bytes 983048 | tf_op jit(solution)/shard_map/ppermute | solution.py:23
  60.7 10.6 %collective-permute-start.14 = (bf16[128,1280]{1,0:T(8,128)(2,1)S(1)}, bf16[128,1280]{1,0:T(8,128)(2,1)S(1)}, u32[]{:S(2)}, u32[]{:S(2)}) collective-permute-start(bf16[128,1280]{1,0:T(8,128)(2,1)S(1)} %fusion.1), channel_id=1, source_target_pairs={{0,8},{4,12},{8,0},{12,4},{1,9},{5,13},{9,1},{13,5},{2,10},{6,14},... | collective-permute-start | bytes 983048 | tf_op jit(solution)/shard_map/ppermute | solution.py:28
  62.5 16.0 %collective-permute-start.17 = (bf16[128,1280]{1,0:T(8,128)(2,1)S(1)}, bf16[128,1280]{1,0:T(8,128)(2,1)S(1)}, u32[]{:S(2)}, u32[]{:S(2)}) collective-permute-start(bf16[128,1280]{1,0:T(8,128)(2,1)S(1)} %fusion), channel_id=1, source_target_pairs={{0,8},{4,12},{8,0},{12,4},{1,9},{5,13},{9,1},{13,5},{2,10},{6,14},... | collective-permute-start | bytes 983048 | tf_op jit(solution)/shard_map/ppermute | solution.py:28
  76.8 8.9 %collective-permute-start.20 = (bf16[128,1024]{1,0:T(8,128)(2,1)S(1)}, bf16[128,1024]{1,0:T(8,128)(2,1)S(1)}, u32[]{:S(2)}, u32[]{:S(2)}) collective-permute-start(bf16[128,1024]{1,0:T(8,128)(2,1)S(1)} %get-tuple-element.15.refs_1_), channel_id=1, source_target_pairs={{0,8},{4,12},{8,0},{12,4},{1,9},{5,13},{9,1},{13,5},{2,10},{6,14},... | collective-permute-start | bytes 786440 | tf_op jit(solution)/shard_map/ppermute | solution.py:28
  84.1 7.2 %collective-permute-start.21 = (bf16[128,1024]{1,0:T(8,128)(2,1)S(1)}, bf16[128,1024]{1,0:T(8,128)(2,1)S(1)}, u32[]{:S(2)}, u32[]{:S(2)}) collective-permute-start(bf16[128,1024]{1,0:T(8,128)(2,1)S(1)} %get-tuple-element.18.refs_2_), channel_id=1, source_target_pairs={{0,8},{4,12},{8,0},{12,4},{1,9},{5,13},{9,1},{13,5},{2,10},{6,14},... | collective-permute-start | bytes 786440 | tf_op jit(solution)/shard_map/ppermute | solution.py:28
  85.1 6.3 %collective-permute-start.18 = (bf16[128,1024]{1,0:T(8,128)(2,1)S(1)}, bf16[128,1024]{1,0:T(8,128)(2,1)S(1)}, u32[]{:S(2)}, u32[]{:S(2)}) collective-permute-start(bf16[128,1024]{1,0:T(8,128)(2,1)S(1)} %get-tuple-element.15.refs_1_), channel_id=1, source_target_pairs={{0,4},{4,0},{8,12},{12,8},{1,5},{5,1},{9,13},{13,9},{2,6},{6,2},{1... | collective-permute-start | bytes 786440 | tf_op jit(solution)/shard_map/ppermute | solution.py:23
  85.1 6.3 %collective-permute-start.19 = (bf16[128,1024]{1,0:T(8,128)(2,1)S(1)}, bf16[128,1024]{1,0:T(8,128)(2,1)S(1)}, u32[]{:S(2)}, u32[]{:S(2)}) collective-permute-start(bf16[128,1024]{1,0:T(8,128)(2,1)S(1)} %get-tuple-element.18.refs_2_), channel_id=1, source_target_pairs={{0,4},{4,0},{8,12},{12,8},{1,5},{5,1},{9,13},{13,9},{2,6},{6,2},{1... | collective-permute-start | bytes 786440 | tf_op jit(solution)/shard_map/ppermute | solution.py:23
  85.7 5.8 %collective-permute-start.22 = (bf16[128,1024]{1,0:T(8,128)(2,1)S(1)}, bf16[128,1024]{1,0:T(8,128)(2,1)S(1)}, u32[]{:S(2)}, u32[]{:S(2)}) collective-permute-start(bf16[128,1024]{1,0:T(8,128)(2,1)S(1)} %collective-permute-done.20.refs_5_), channel_id=1, source_target_pairs={{0,4},{4,0},{8,12},{12,8},{1,5},{5,1},{9,13},{13,9},{2,6},{6,2},{1... | collective-permute-start | bytes 786440 | tf_op jit(solution)/shard_map/ppermute | solution.py:23
  91.3 1.5 collective-permute-start.23
  91.4 9.0 %copy-start.7 = (bf16[128,1024]{1,0:T(8,128)(2,1)}, bf16[128,1024]{1,0:T(8,128)(2,1)S(1)}, u32[]{:S(2)}) copy-start(bf16[128,1024]{1,0:T(8,128)(2,1)S(1)} %collective-permute-done.19.refs_4_) | copy-start | bytes 786436
  91.4 9.0 %copy-start.9 = (bf16[128,1024]{1,0:T(8,128)(2,1)}, bf16[128,1024]{1,0:T(8,128)(2,1)S(1)}, u32[]{:S(2)}) copy-start(bf16[128,1024]{1,0:T(8,128)(2,1)S(1)} %collective-permute-done.22.refs_7_) | copy-start | bytes 786436
  92.8 3.4 %copy-start = (bf16[2048,2048]{1,0:T(8,128)(2,1)S(1)}, bf16[2048,2048]{1,0:T(8,128)(2,1)}, u32[]{:S(2)}) copy-start(bf16[2048,2048]{1,0:T(8,128)(2,1)} %refs_9_.7) | copy-start | bytes 25165828
  96.2 4.2 %copy-start.11 = (bf16[128,1024]{1,0:T(8,128)(2,1)}, bf16[128,1024]{1,0:T(8,128)(2,1)S(1)}, u32[]{:S(2)}) copy-start(bf16[128,1024]{1,0:T(8,128)(2,1)S(1)} %collective-permute-done.23.refs_8_) | copy-start | bytes 786436
  101.3 14.1 %collective-permute-start.30 = (bf16[128,1024]{1,0:T(8,128)(2,1)}, bf16[128,1024]{1,0:T(8,128)(2,1)}, u32[]{:S(2)}, u32[]{:S(2)}) collective-permute-start(bf16[128,1024]{1,0:T(8,128)(2,1)} %get-tuple-element.34), channel_id=1, source_target_pairs={{0,1},{4,5},{8,9},{12,13},{16,17},{20,21},{24,25},{28,29}} | collective-permute-start | bytes 786440 | tf_op jit(solution)/shard_map/ppermute | solution.py:323
  105.7 0.9 copy-start.8
  106.6 0.9 copy-start.10
  107.6 0.9 copy-start.12
  112.8 7.9 %collective-permute-start.24 = (bf16[128,1024]{1,0:T(8,128)(2,1)S(1)}, bf16[128,1024]{1,0:T(8,128)(2,1)}, u32[]{:S(2)}, u32[]{:S(2)}) collective-permute-start(bf16[128,1024]{1,0:T(8,128)(2,1)S(1)} %get-tuple-element.30), channel_id=1, source_target_pairs={{0,1},{4,5},{8,9},{12,13},{16,17},{20,21},{24,25},{28,29}} | collective-permute-start | bytes 786440 | tf_op jit(solution)/shard_map/ppermute | solution.py:323
  114.8 12.2 %collective-permute-start.33 = (bf16[128,1024]{1,0:T(8,128)(2,1)}, bf16[128,1024]{1,0:T(8,128)(2,1)S(1)}, u32[]{:S(2)}, u32[]{:S(2)}) collective-permute-start(bf16[128,1024]{1,0:T(8,128)(2,1)} %get-tuple-element.35), channel_id=1, source_target_pairs={{3,2},{7,6},{11,10},{15,14},{19,18},{23,22},{27,26},{31,30}} | collective-permute-start | bytes 786440 | tf_op jit(solution)/shard_map/ppermute | solution.py:326
  117.2 9.8 %collective-permute-start.31 = (bf16[128,1024]{1,0:T(8,128)(2,1)}, bf16[128,1024]{1,0:T(8,128)(2,1)S(1)}, u32[]{:S(2)}, u32[]{:S(2)}) collective-permute-start(bf16[128,1024]{1,0:T(8,128)(2,1)} %add_convert_fusion.4), channel_id=1, source_target_pairs={{0,1},{1,2},{4,5},{5,6},{8,9},{9,10},{12,13},{13,14},{16,17},{17,1... | collective-permute-start | bytes 786440 | tf_op jit(solution)/shard_map/ppermute | solution.py:323
  118.5 9.4 %collective-permute-start.27 = (bf16[128,1024]{1,0:T(8,128)(2,1)S(1)}, bf16[128,1024]{1,0:T(8,128)(2,1)S(1)}, u32[]{:S(2)}, u32[]{:S(2)}) collective-permute-start(bf16[128,1024]{1,0:T(8,128)(2,1)S(1)} %get-tuple-element.31), channel_id=1, source_target_pairs={{3,2},{7,6},{11,10},{15,14},{19,18},{23,22},{27,26},{31,30}} | collective-permute-start | bytes 786440 | tf_op jit(solution)/shard_map/ppermute | solution.py:326
  122.4 9.0 %collective-permute-start.25 = (bf16[128,1024]{1,0:T(8,128)(2,1)}, bf16[128,1024]{1,0:T(8,128)(2,1)S(1)}, u32[]{:S(2)}, u32[]{:S(2)}) collective-permute-start(bf16[128,1024]{1,0:T(8,128)(2,1)} %add_convert_fusion.9), channel_id=1, source_target_pairs={{0,1},{1,2},{4,5},{5,6},{8,9},{9,10},{12,13},{13,14},{16,17},{17,1... | collective-permute-start | bytes 786440 | tf_op jit(solution)/shard_map/ppermute | solution.py:323
  127.2 15.3 %collective-permute-start.34 = (bf16[128,1024]{1,0:T(8,128)(2,1)S(1)}, bf16[128,1024]{1,0:T(8,128)(2,1)S(1)}, u32[]{:S(2)}, u32[]{:S(2)}) collective-permute-start(bf16[128,1024]{1,0:T(8,128)(2,1)S(1)} %get-tuple-element.33), channel_id=1, source_target_pairs={{3,2},{2,1},{7,6},{6,5},{11,10},{10,9},{15,14},{14,13},{19,18},{18... | collective-permute-start | bytes 786440 | tf_op jit(solution)/shard_map/ppermute | solution.py:326
  131.7 12.2 %collective-permute-start.28 = (bf16[128,1024]{1,0:T(8,128)(2,1)S(1)}, bf16[128,1024]{1,0:T(8,128)(2,1)S(1)}, u32[]{:S(2)}, u32[]{:S(2)}) collective-permute-start(bf16[128,1024]{1,0:T(8,128)(2,1)S(1)} %get-tuple-element.29), channel_id=1, source_target_pairs={{3,2},{2,1},{7,6},{6,5},{11,10},{10,9},{15,14},{14,13},{19,18},{18... | collective-permute-start | bytes 786440 | tf_op jit(solution)/shard_map/ppermute | solution.py:326
  133.0 12.9 %collective-permute-start.32 = (bf16[128,1024]{1,0:T(8,128)(2,1)S(1)}, bf16[128,1024]{1,0:T(8,128)(2,1)S(1)}, u32[]{:S(2)}, u32[]{:S(2)}) collective-permute-start(bf16[128,1024]{1,0:T(8,128)(2,1)S(1)} %get-tuple-element.32), channel_id=1, source_target_pairs={{0,1},{1,2},{2,3},{4,5},{5,6},{6,7},{8,9},{9,10},{10,11},{12,13},{... | collective-permute-start | bytes 786440 | tf_op jit(solution)/shard_map/ppermute | solution.py:323
  137.9 14.4 %collective-permute-start.26 = (bf16[128,1024]{1,0:T(8,128)(2,1)S(1)}, bf16[128,1024]{1,0:T(8,128)(2,1)S(1)}, u32[]{:S(2)}, u32[]{:S(2)}) collective-permute-start(bf16[128,1024]{1,0:T(8,128)(2,1)S(1)} %get-tuple-element.28), channel_id=1, source_target_pairs={{0,1},{1,2},{2,3},{4,5},{5,6},{6,7},{8,9},{9,10},{10,11},{12,13},{... | collective-permute-start | bytes 786440 | tf_op jit(solution)/shard_map/ppermute | solution.py:323
  142.6 9.7 %collective-permute-start.35 = (bf16[128,1024]{1,0:T(8,128)(2,1)S(1)}, bf16[128,1024]{1,0:T(8,128)(2,1)S(1)}, u32[]{:S(2)}, u32[]{:S(2)}) collective-permute-start(bf16[128,1024]{1,0:T(8,128)(2,1)S(1)} %add_convert_fusion.1), channel_id=1, source_target_pairs={{3,2},{2,1},{1,0},{7,6},{6,5},{5,4},{11,10},{10,9},{9,8},{15,14},{... | collective-permute-start | bytes 786440 | tf_op jit(solution)/shard_map/ppermute | solution.py:326
  143.9 11.1 %collective-permute-start.29 = (bf16[128,1024]{1,0:T(8,128)(2,1)S(1)}, bf16[128,1024]{1,0:T(8,128)(2,1)S(1)}, u32[]{:S(2)}, u32[]{:S(2)}) collective-permute-start(bf16[128,1024]{1,0:T(8,128)(2,1)S(1)} %add_convert_fusion.6), channel_id=1, source_target_pairs={{3,2},{2,1},{1,0},{7,6},{6,5},{5,4},{11,10},{10,9},{9,8},{15,14},{... | collective-permute-start | bytes 786440 | tf_op jit(solution)/shard_map/ppermute | solution.py:326

commit v2 on v1

v2 whole, which is shorter than its diff:
```python
import functools
import math

import jax
import jax.numpy as jnp
from jax import lax
from jax.experimental import pallas as pl
from jax.experimental.pallas import tpu as pltpu
from jax.sharding import PartitionSpec as P

epsilon = 1e-05
adapter_scale = 0.5
rope_base = 500000.0
masked_score = -1e30


def params(mib):
    return pltpu.CompilerParams(vmem_limit_bytes=mib * 1024 * 1024)


def core_swap(x, pool_count):
    return lax.ppermute(x, "pool", [(p, p ^ 1) for p in range(pool_count)])


def chip_move(x, pool_count, d, e=0):
    chips = pool_count // 2
    return lax.ppermute(
        x,
        "pool",
        [(p, (p // 2 + d) % chips * 2 + ((p % 2) ^ e)) for p in range(pool_count)],
    )


def shrink_kernel(*refs):
    ids, *blocks, query_down, value_down, out = refs
    adapters = query_down.shape[0] // 16
    rows = blocks[0].shape[0]
    per = 2 if len(blocks) % 2 == 0 else 1
    for first in range(0, len(blocks), per):
        x = jnp.concatenate([b[...] for b in blocks[first : first + per]], axis=0)
        span = slice(first * rows, (first + per) * rows)
        label = ids[:, span].reshape(1, 1, per * rows)
        chosen = lax.broadcasted_iota(jnp.int32, (adapters, 1, per * rows), 0) == label
        for at, table in enumerate((query_down, value_down)):
            terms = lax.dot_general(
                table[...], x, (((1,), (1,)), ((), ())), preferred_element_type=jnp.float32
            ).reshape(adapters, 16, per * rows)
            out[at * 16 : (at + 1) * 16, span] = jnp.sum(jnp.where(chosen, terms, 0.0), axis=0)


def project_kernel(parts, chunks, *refs):
    ids = refs[0]
    lows = refs[1 : 1 + parts]
    blocks = refs[1 + parts : 3 + parts]
    wq, wk, wv, uq, uv, keep, *sends, xs, spread_q, spread_v = refs[3 + parts :]
    step = pl.program_id(0)
    last = pl.num_programs(0) - 1
    rows = blocks[0].shape[0]
    adapters = uq.shape[0] // 16
    total = 2 * rows

    @pl.when(step == 0)
    def _():
        for at, block in enumerate(blocks):
            xs[at * rows : (at + 1) * rows, :] = block[...]
        low = lows[0][...]
        for other in lows[1:]:
            low = low + other[...]
        low = low.astype(jnp.bfloat16).astype(jnp.float32) * adapter_scale
        chosen = lax.broadcasted_iota(jnp.int32, (adapters, 1, total), 0) == ids[...].reshape(
            1, 1, total
        )
        for at, spread in enumerate((spread_q, spread_v)):
            wide = jnp.where(chosen, low[at * 16 : (at + 1) * 16][None], 0.0)
            spread[...] = wide.reshape(adapters * 16, total).T.astype(jnp.bfloat16)

    def write(acc, columns):
        keep[:, columns] = acc[:rows]
        part = rows // chunks
        for c, send in enumerate(sends):
            at = rows + c * part
            send[:, columns] = acc[at : at + part].astype(jnp.bfloat16)

    @pl.when(step < last)
    def _():
        write(
            jnp.dot(xs[...], wq[...], preferred_element_type=jnp.float32)
            + jnp.dot(spread_q[...], uq[...], preferred_element_type=jnp.float32),
            slice(None),
        )

    @pl.when(step == last)
    def _():
        kv = wk.shape[1]
        write(jnp.dot(xs[...], wk[...], preferred_element_type=jnp.float32), slice(0, kv))
        write(
            jnp.dot(xs[...], wv[...], preferred_element_type=jnp.float32)
            + jnp.dot(spread_v[...], uv[...], preferred_element_type=jnp.float32),
            slice(kv, 2 * kv),
        )


def project(d, chunks, ids, lows, blocks, wq, wk, wv, uq, uv):
    rows, width = blocks[0].shape
    total = 2 * rows
    query_cols, kv_cols = wq.shape[1], wk.shape[1]
    tile = 2 * kv_cols
    steps = query_cols // tile
    columns = query_cols + tile
    slots = uq.shape[0]
    part = rows // chunks

    def whole(x):
        return pl.BlockSpec(x.shape, lambda i: (0, 0))

    def lanes(x):
        return pl.BlockSpec((x.shape[0], total), lambda i: (0, d))

    def query_block(i):
        return (0, jnp.minimum(i, steps - 1))

    keep, *sends = pl.pallas_call(
        functools.partial(project_kernel, len(lows), chunks),
        grid=(steps + 1,),
        in_specs=[
            lanes(ids),
            *[lanes(x) for x in lows],
            *[whole(x) for x in blocks],
            pl.BlockSpec((width, tile), query_block),
            whole(wk),
            whole(wv),
            pl.BlockSpec((slots, tile), query_block),
            whole(uv),
        ],
        out_specs=[
            pl.BlockSpec((rows, tile), lambda i: (0, i)),
            *[pl.BlockSpec((part, tile), lambda i: (0, i))] * chunks,
        ],
        out_shape=[
            jax.ShapeDtypeStruct((rows, columns), jnp.float32),
            *[jax.ShapeDtypeStruct((part, columns), jnp.bfloat16)] * chunks,
        ],
        scratch_shapes=[
            pltpu.VMEM((total, width), jnp.bfloat16),
            pltpu.VMEM((total, slots), jnp.bfloat16),
            pltpu.VMEM((total, slots), jnp.bfloat16),
        ],
        compiler_params=params(40),
        cost_estimate=pl.CostEstimate(
            flops=2 * total * (width + slots) * columns,
            bytes_accessed=2 * (width + slots) * columns + 6 * rows * columns,
            transcendentals=0,
        ),
        name=f"project_{d}",
    )(ids, *lows, *blocks, wq, wk, wv, uq, uv)
    return keep, sends


def attend_kernel(arrived, *refs):
    keep, swapped = refs[:2]
    moved = refs[2 : 2 + arrived]
    scale, cosines, sines, lengths, keys, values, out, key_out, value_out = refs[2 + arrived :]
    head = cosines.shape[1]
    rows_block = out.shape[0]
    _, kv_heads, cache, _ = keys.shape
    heads = out.shape[1] // head
    group = heads // kv_heads
    score_scale = 1.0 / math.sqrt(head)
    sub = 8
    column = lax.broadcasted_iota(jnp.int32, (sub, sub * cache), 1)
    start = lax.broadcasted_iota(jnp.int32, (sub, sub * cache), 0) * cache
    for pair in range(rows_block // 16):
        attended, new_keys, new_values = [], [], []
        for half in range(2):
            at = pair * 16 + half * sub
            r = slice(at, at + sub)
            x = keep[r] + swapped[r].astype(jnp.float32)
            for m in moved:
                x = x + m[r].astype(jnp.float32)
            x = x * scale[r]
            cos, sin = cosines[r], sines[r]
            inside = (column >= start) & (column < start + lengths[r])

            def piece(i):
                return x[:, i * head : (i + 1) * head]

            def turn(v):
                return v * cos + pltpu.roll(v, head // 2, 1) * sin

            for g in range(kv_heads):
                query = jnp.concatenate(
                    [turn(piece(g * group + h)) for h in range(group)], axis=0
                ).astype(jnp.bfloat16)
                new_key = turn(piece(heads + g)).astype(jnp.bfloat16).astype(jnp.float32)
                new_value = piece(heads + kv_heads + g).astype(jnp.bfloat16).astype(jnp.float32)
                k = keys[r, g].reshape(sub * cache, head)
                v = values[r, g].reshape(sub * cache, head)
                scores = (
                    lax.dot_general(
                        query, k, (((1,), (1,)), ((), ())), preferred_element_type=jnp.float32
                    )
                    * score_scale
                )
                own_key = jnp.concatenate([new_key] * group, axis=0)
                own = (
                    jnp.sum(query.astype(jnp.float32) * own_key, axis=1, keepdims=True)
                    * score_scale
                )
                scores = jnp.where(
                    inside[None], scores.reshape(group, sub, sub * cache), masked_score
                ).reshape(group * sub, sub * cache)
                peak = jnp.maximum(jnp.max(scores, axis=1, keepdims=True), own)
                weights = jnp.exp(scores - peak)
                own_weight = jnp.exp(own - peak)
                inverse = 1.0 / (jnp.sum(weights, axis=1, keepdims=True) + own_weight)
                mixed = jnp.dot(weights.astype(jnp.bfloat16), v, preferred_element_type=jnp.float32)
                own_value = jnp.concatenate([new_value] * group, axis=0)
                mixed = (mixed + own_weight * own_value) * inverse
                attended += [mixed[h * sub : (h + 1) * sub] for h in range(group)]
                new_keys.append(new_key)
                new_values.append(new_value)
        r = slice(pair * 16, pair * 16 + 16)

        def both(pieces):
            n = len(pieces) // 2
            return jnp.concatenate(
                [jnp.concatenate([pieces[i], pieces[n + i]], axis=0) for i in range(n)], axis=1
            ).astype(jnp.bfloat16)

        out[r] = both(attended)
        key_out[r] = both(new_keys)
        value_out[r] = both(new_values)


def attend(c, chunks, keep, swapped, moved, scale, cosines, sines, lengths, keys, values):
    rows, columns = keep.shape
    _, kv_heads, cache, head = keys.shape
    kv_cols = kv_heads * head
    query_cols = columns - 2 * kv_cols
    part = rows // chunks
    block = 32 if part % 32 == 0 else 16
    steps = part // block

    def own(x):
        return pl.BlockSpec((block, x.shape[1]), lambda i: (c * steps + i, 0))

    cached = pl.BlockSpec((block, kv_heads, cache, head), lambda i: (c * steps + i, 0, 0, 0))
    widths = (query_cols, kv_cols, kv_cols)
    return pl.pallas_call(
        functools.partial(attend_kernel, len(moved)),
        grid=(steps,),
        in_specs=[
            own(keep),
            pl.BlockSpec((block, columns), lambda i: (i, 0)),
            *[pl.BlockSpec((block, columns), lambda i: (i, 0)) for _ in moved],
            own(scale),
            own(cosines),
            own(sines),
            own(lengths),
            cached,
            cached,
        ],
        out_specs=[pl.BlockSpec((block, w), lambda i: (i, 0)) for w in widths],
        out_shape=[jax.ShapeDtypeStruct((part, w), jnp.bfloat16) for w in widths],
        compiler_params=params(32),
        cost_estimate=pl.CostEstimate(
            flops=4 * part * 8 * cache * query_cols,
            bytes_accessed=4 * part * cache * kv_cols + 8 * part * columns,
            transcendentals=part * 8 * cache * query_cols // head,
        ),
        name=f"attend_{c}",
    )(keep, swapped, *moved, scale, cosines, sines, lengths, keys, values)


def output_kernel(*refs):
    order, *blocks, weights, out, xs = refs
    rows = blocks[0].shape[0]

    @pl.when(pl.program_id(0) == 0)
    def _():
        for b, block in enumerate(blocks):
            xs[b * rows : (b + 1) * rows, :] = block[...]

    acc = jnp.dot(xs[...], weights[...], preferred_element_type=jnp.float32).astype(jnp.bfloat16)
    for b in range(len(blocks)):
        to = pl.multiple_of(order[b] * rows, rows)
        out[pl.ds(to, rows), :] = acc[b * rows : (b + 1) * rows]


def output_part(c, order, blocks, weights):
    rows = blocks[0].shape[0]
    depth, columns = weights.shape
    tile = 512 if columns % 512 == 0 else columns
    total = rows * len(blocks)
    return pl.pallas_call(
        output_kernel,
        grid=(columns // tile,),
        in_specs=[
            pl.BlockSpec(memory_space=pltpu.SMEM),
            *[pl.BlockSpec(x.shape, lambda i: (0, 0)) for x in blocks],
            pl.BlockSpec((depth, tile), lambda i: (0, i)),
        ],
        out_specs=pl.BlockSpec((total, tile), lambda i: (0, i)),
        out_shape=jax.ShapeDtypeStruct((total, columns), jnp.bfloat16),
        scratch_shapes=[pltpu.VMEM((total, depth), jnp.bfloat16)],
        compiler_params=params(40),
        cost_estimate=pl.CostEstimate(
            flops=2 * total * depth * columns,
            bytes_accessed=2 * depth * columns + 2 * total * (depth + columns),
            transcendentals=0,
        ),
        name=f"output_{c}",
    )(order, *blocks, weights)


def shards(
    tokens,
    input_norm_gain,
    query_matrix,
    key_matrix,
    value_matrix,
    output_matrix,
    rotated_key_cache,
    cached_value_rows,
    cache_length_per_row,
    row_adapter_index,
    query_down_maps,
    query_up_maps,
    value_down_maps,
    value_up_maps,
):
    pool_count = lax.axis_size("pool")
    tp_count = lax.axis_size("tp")
    chips = pool_count // 2
    pool_at = lax.axis_index("pool")
    tp_at = lax.axis_index("tp")
    chip, core = pool_at // 2, pool_at % 2
    rows = tokens.shape[0]
    adapters, rank, piece = query_down_maps.shape
    base = query_matrix.shape[0]
    kv_heads = rotated_key_cache.shape[1]
    head = rotated_key_cache.shape[3]

    def scaled(start, width):
        x = lax.dynamic_slice_in_dim(tokens, start, width, 1).astype(jnp.float32)
        gain = lax.dynamic_slice_in_dim(input_norm_gain, start, width, 0).astype(jnp.float32)
        return (x * gain[None, :]).astype(jnp.bfloat16)

    def gather_pool(x):
        same = [x] + [chip_move(x, pool_count, d) for d in range(1, chips)]
        return [b for s in same for b in (s, core_swap(s, pool_count))]

    first = scaled(tp_at * piece, piece)
    first, tokens, input_norm_gain = lax.optimization_barrier((first, tokens, input_norm_gain))
    adapter_rows = gather_pool(first)
    local_ids = (
        jnp.concatenate(gather_pool(row_adapter_index.reshape(1, rows)), axis=1)
        - pool_at * adapters
    )

    blocks = []
    for d in range(chips):
        for e in range(2):
            target = (chip + d) % chips * 2 + (core + e) % 2
            x = scaled(target * base, base)
            blocks.append(x if d == e == 0 else chip_move(x, pool_count, d, e))

    shrunk = pl.pallas_call(
        shrink_kernel,
        out_shape=jax.ShapeDtypeStruct((2 * rank, rows * pool_count), jnp.float32),
        compiler_params=params(40),
        cost_estimate=pl.CostEstimate(
            flops=4 * adapters * rank * piece * rows * pool_count,
            bytes_accessed=4 * adapters * rank * piece + 2 * piece * rows * pool_count,
            transcendentals=0,
        ),
        name="shrink",
    )(
        local_ids,
        *adapter_rows,
        query_down_maps.reshape(adapters * rank, piece),
        value_down_maps.reshape(adapters * rank, piece),
    )
    lows = [shrunk] + [
        lax.ppermute(shrunk, "tp", [(i, (i + d) % tp_count) for i in range(tp_count)])
        for d in range(1, tp_count)
    ]

    values = tokens.astype(jnp.float32)
    scale = lax.rsqrt(jnp.mean(values * values, axis=-1, keepdims=True) + epsilon)
    half_dim = head // 2
    frequency = jnp.power(
        jnp.float32(rope_base), jnp.arange(half_dim, dtype=jnp.float32) * (-2.0 / head)
    )
    angles = cache_length_per_row.astype(jnp.float32)[:, None] * frequency[None, :]
    cosines = jnp.concatenate([jnp.cos(angles)] * 2, axis=1)
    sines = jnp.concatenate([-jnp.sin(angles), jnp.sin(angles)], axis=1)
    lengths = cache_length_per_row.reshape(rows, 1)

    up_q = query_up_maps.reshape(adapters * rank, query_up_maps.shape[2])
    up_v = value_up_maps.reshape(adapters * rank, value_up_maps.shape[2])
    weights = (query_matrix, key_matrix, value_matrix, up_q, up_v)
    chunks = 2
    own_sums, own_sends = project(0, chunks, local_ids, lows, blocks[:2], *weights)
    swapped = [core_swap(x, pool_count) for x in own_sends]
    moved = [[] for _ in range(chunks)]
    part = rows // chunks
    for d in range(1, chips):
        keep, sends = project(d, chunks, local_ids, lows, blocks[2 * d : 2 * d + 2], *weights)
        for c in range(chunks):
            both = keep[c * part : (c + 1) * part] + core_swap(sends[c], pool_count).astype(
                jnp.float32
            )
            moved[c].append(chip_move(both.astype(jnp.bfloat16), pool_count, -d))

    order = jnp.stack(
        [(chip - d) % chips * 2 + (core + e) % 2 for d in range(chips) for e in range(2)]
    ).astype(jnp.int32)
    outputs = []
    for c in range(chunks):
        attended, new_key, new_value = attend(
            c,
            chunks,
            own_sums,
            swapped[c],
            moved[c],
            scale,
            cosines,
            sines,
            lengths,
            rotated_key_cache,
            cached_value_rows,
        )
        partial = output_part(c, order, gather_pool(attended), output_matrix)
        summed = lax.psum_scatter(partial, "tp", scatter_dimension=0, tiled=True)
        outputs.append((summed.reshape(-1, part, summed.shape[1]), new_key, new_value))
    attn_out = jnp.concatenate([o[0] for o in outputs], axis=1)
    return (
        attn_out.reshape(-1, attn_out.shape[2]),
        jnp.concatenate([o[1] for o in outputs], axis=0),
        jnp.concatenate([o[2] for o in outputs], axis=0),
    )


def solution(mesh):
    return jax.shard_map(
        shards,
        mesh=mesh,
        in_specs=(
            P(("groups", "pool"), None),
            P(),
            P("pool", "tp"),
            P("pool", "tp"),
            P("pool", "tp"),
            P("tp", "pool"),
            P(("groups", "pool"), "tp", None, None),
            P(("groups", "pool"), "tp", None, None),
            P(("groups", "pool")),
            P(("groups", "pool")),
            P("pool", None, "tp"),
            P("pool", None, "tp"),
            P("pool", None, "tp"),
            P("pool", None, "tp"),
        ),
        out_specs=(
            P(("groups", "tp"), "pool"),
            P(("groups", "pool"), "tp"),
            P(("groups", "pool"), "tp"),
        ),
        check_vma=False,
    )
```

time: 157 us -> 188 us (1.20)
  starting transfers between devices: 46.2 us -> 19.9 us
  waiting for transfers between devices: 49.5 us -> 75.5 us
  local copies, waits for them, and re-layouts: 10.7 us -> 28.2 us
  between operations: 1.22 us -> 14.3 us
    reduce_scatter x0 -> x2, waiting for transfers between devices: none -> 27.6 us  [shards(): summed = lax.psum_scatter(partial, 'tp', scatter_dimension=0, tiled=True)]
    ppermute x12 -> x0, starting transfers between devices: 26.9 us -> none  [the longest x6 21.6 us: line_sum(): lax.ppermute(go_right.astype(jnp.bfloat16), 'tp', [(i, i + 1) for i in ra...]
    unnamed x36 -> x74, local copies, waits for them, and re-layouts: 9.45 us -> 28 us
    ppermute x12 -> x0, waiting for transfers between devices: 14.2 us -> none  [the longest x6 9.01 us: line_sum(): lax.ppermute(go_left.astype(jnp.bfloat16), 'tp', [(n - 1 - i, n - 2 - i)...]
    ppermute x9, waiting for transfers between devices: 33.9 us -> 44.7 us  [chip_move(): lax.ppermute(x, 'pool', [(p, (p // 2 + d) % chips * 2 + (p % 2 ^ e)) for...]
    convert_element_type x10 -> x1, other arithmetic: 4.38 us -> 1.21 us  [shards(): moved[c].append(chip_move(both.astype(jnp.bfloat16), pool_count, -d))]
    pallas_call x6, Pallas kernels: 33 us -> 35.2 us  [the longest x2 16.5 us: project(): pl.pallas_call(functools.partial(project_kernel, len(lows), chunks), grid...]
    convert_element_type x1 -> x2, other arithmetic: 3.42 us -> 4.52 us  [scaled(): return (x * gain[None, :]).astype(jnp.bfloat16)]
  transfers between devices with their start and end apart: 36 -> 26, of which waited for: 10 -> 10; matrix products, arithmetic and copies ran while one was open for 4% -> 4% of each run, Pallas kernels for 17% -> 15%
where the time goes in v2:
time: 188 us; the launch traced here: 187 us
  waiting for transfers between devices  75.5 us (40%)
  Pallas kernels  37.6 us (20%)
  local copies, waits for them, and re-layouts  28.2 us (15%)
  starting transfers between devices  19.9 us (11%)
  between operations  14.3 us (8%)
  other arithmetic  11.3 us (6%)
    ppermute x9, waiting for transfers between devices, chip_move(): lax.ppermute(x, 'pool', [(p, (p // 2 + d) % chips * 2 + (p % 2 ^ e)) for...  44.7 us
    unnamed x74, local copies, waits for them, and re-layouts  28 us
    reduce_scatter x2, waiting for transfers between devices, shards(): summed = lax.psum_scatter(partial, 'tp', scatter_dimension=0, tiled=True)  27.6 us
    pallas_call x2, Pallas kernels, project(): pl.pallas_call(functools.partial(project_kernel, len(lows), chunks), grid...  16.5 us
    ppermute x9, starting transfers between devices, chip_move(): lax.ppermute(x, 'pool', [(p, (p // 2 + d) % chips * 2 + (p % 2 ^ e)) for...  12.6 us
    pallas_call x2, Pallas kernels, output_part(): pl.pallas_call(output_kernel, grid=(columns // tile,), in_specs=[pl.Block...  9.49 us
    pallas_call x2, Pallas kernels, attend(): pl.pallas_call(functools.partial(attend_kernel, len(moved)), grid=(steps,...  9.22 us
    ppermute x3, starting transfers between devices, shards(): lax.ppermute(shrunk, 'tp', [(i, (i + d) % tp_count) for i in range(tp_cou...  5.6 us
  transfers between devices with their start and end apart: 26, of which 10 were waited for; matrix products, arithmetic and copies ran while one was open for 4% of the time, Pallas kernels for 15%

profile of v2, /device:TPU:0, one launch (start us, length us, event | category | flops | bytes accessed | tf_op | source)
XLA Modules:
  0.0 186.8 jit_solution(6974340070113467294)
XLA Ops:
  7.2 0.7 dynamic-slice_convert_fusion.4
  7.9 1.1 multiply_convert_fusion.4.refs_1_
  9.1 3.0 %collective-permute-start.4 = (bf16[128,2048]{1,0:T(8,128)(2,1)S(1)}, bf16[128,2048]{1,0:T(8,128)(2,1)S(1)}, u32[]{:S(2)}, u32[]{:S(2)}) collective-permute-start(bf16[128,2048]{1,0:T(8,128)(2,1)S(1)} %multiply_convert_fusion.4.refs_1_), channel_id=1, source_target_pairs={{0,8},{4,12},{8,0},{12,4},{1,9},{5,13},{9,1},{13,5},{2,10},{6,14},... | collective-permute-start | bytes 1572872 | tf_op jit(solution)/shard_map/ppermute | solution.py:27
  12.1 0.2 collective-permute-start.1
  12.2 0.4 collective-permute-start
  12.6 0.7 dynamic-slice_convert_fusion
  13.3 10.7 %collective-permute-done.4.refs_3_ = bf16[128,2048]{1,0:T(8,128)(2,1)S(1)} collective-permute-done((bf16[128,2048]{1,0:T(8,128)(2,1)S(1)}, bf16[128,2048]{1,0:T(8,128)(2,1)S(1)}, u32[]{:S(2)}, u32[]{:S(2)}) %collective-permute-start.4) | collective-permute-done | bytes 524320 | tf_op jit(solution)/shard_map/ppermute | solution.py:27
  24.0 3.4 %multiply_convert_fusion = (bf16[128,2048]{1,0:T(8,128)(2,1)}, bf16[128,2048]{1,0:T(8,128)(2,1)}, bf16[128,2048]{1,0:T(8,128)(2,1)}, bf16[128,2048]{1,0:T(8,128)(2,1)}) fusion(f32[2048]{0:T(1024)S(1)} %get-tuple-element.39, bf16[128,8192]{1,0:T(8,128)(2,1)} %param.14, s32[]{:T(128)S(6)} %select_n.84, f32[2048]{0:T(1024)S(1)} %get-tuple-element.40, ...), kind=kLoop, calls=%fused_computation.1 | loop fusion | flops 3145728 | bytes 4227088 | tf_op jit(solution)/shard_map/convert_element_type | solution.py:347
  27.4 1.8 collective-permute-start.11
  29.3 0.5 multiply_reduce_fusion
  29.8 0.3 collective-permute-start.12
  30.1 0.2 collective-permute-done.2
  30.3 0.2 collective-permute-start.9
  30.5 0.8 copy-done.28
  31.3 0.8 copy-done.30
  32.1 1.6 copy-done.24
  33.7 1.6 copy-done.25
  35.3 1.0 copy-done.27
  36.3 1.0 copy-done.29
  37.4 1.0 copy-done.31
  38.4 2.4 %shrink.1.refs_1_ = f32[32,512]{1,0:T(8,128)S(1)} custom-call(s32[1,512]{1,0:T(1,128)S(1)} %add_subtract_fusion.refs_0_, bf16[128,2048]{1,0:T(8,128)(2,1)S(1)} %multiply_convert_fusion.4.refs_1_, bf16[128,2048]{1,0:T(8,128)(2,1)S(1)} %copy-done.29, bf16[128,2048]{1,0:T(8,128)(2,1)S(1)} %copy-done.27, bf16[128,2048]{1,0:T(8,128)(2,1)S(1)} %copy-done.31, ...), custom_call_target="tpu_custom_call" | custom-call | flops 2147483648 | bytes 6291456 | tf_op jit(solution)/shard_map/shrink/pallas_call | solution.py:368
  40.8 1.7 collective-permute-start.6
  42.5 2.6 %collective-permute-start.7 = (f32[32,512]{1,0:T(8,128)S(1)}, f32[32,512]{1,0:T(8,128)S(1)}, u32[]{:S(2)}, u32[]{:S(2)}) collective-permute-start(f32[32,512]{1,0:T(8,128)S(1)} %shrink.1.refs_1_), channel_id=1, source_target_pairs={{0,2},{1,3},{2,0},{3,1},{4,6},{5,7},{6,4},{7,5},{8,10},{9,11},{10,... | collective-permute-start | bytes 196616 | tf_op jit(solution)/shard_map/ppermute | solution.py:385
  45.1 1.3 collective-permute-start.8
  46.4 6.2 %collective-permute-done.12.refs_6_ = bf16[128,2048]{1,0:T(8,128)(2,1)S(1)} collective-permute-done((bf16[128,2048]{1,0:T(8,128)(2,1)}, bf16[128,2048]{1,0:T(8,128)(2,1)S(1)}, u32[]{:S(2)}, u32[]{:S(2)}) %collective-permute-start.12) | collective-permute-done | bytes 524320 | tf_op jit(solution)/shard_map/ppermute | solution.py:27
  52.8 7.9 %project_1.1 = (f32[128,2560]{1,0:T(8,128)S(1)}, bf16[64,2560]{1,0:T(8,128)(2,1)}, bf16[64,2560]{1,0:T(8,128)(2,1)}) custom-call(s32[1,512]{1,0:T(1,128)S(1)} %add_subtract_fusion.refs_0_, f32[32,512]{1,0:T(8,128)S(1)} %shrink.1.refs_1_, f32[32,512]{1,0:T(8,128)S(1)} %collective-permute-done.6.refs_2_, f32[32,512]{1,0:T(8,128)S(1)} %collective-permute-done.7.refs_3_, ...), custom_call_target="tpu_custom_call" | custom-call | flops 3355443200 | bytes 15073280 | tf_op jit(solution)/shard_map/project_1/pallas_call | solution.py:122
  60.7 1.1 copy-done.12
  61.8 0.3 collective-permute-start.13
  62.1 0.2 collective-permute-start.19
  62.5 1.2 copy-done.8
  63.8 1.2 copy-done.10
  65.0 1.0 copy-done.11
  66.0 0.9 copy-done.15
  67.0 0.8 copy-done.17
  67.8 0.8 copy-done.19
  68.7 0.8 copy-done.21
  69.5 0.8 copy-done.23
  70.3 8.6 %project_0.1 = (f32[128,2560]{1,0:T(8,128)S(1)}, bf16[64,2560]{1,0:T(8,128)(2,1)S(1)}, bf16[64,2560]{1,0:T(8,128)(2,1)S(1)}) custom-call(s32[1,512]{1,0:T(1,128)S(1)} %add_subtract_fusion.refs_0_, f32[32,512]{1,0:T(8,128)S(1)} %copy-done.17, f32[32,512]{1,0:T(8,128)S(1)} %copy-done.19, f32[32,512]{1,0:T(8,128)S(1)} %copy-done.21, f32[32,512]{1,0:T(8,128)S(1)} %copy-done.23, ...), custom_call_target="tpu_custom_call" | custom-call | flops 3355443200 | bytes 15073280 | tf_op jit(solution)/shard_map/project_0/pallas_call | solution.py:122
  78.9 0.4 collective-permute-start.10
  79.3 1.2 add_convert_fusion.1
  80.5 1.8 collective-permute-start.14
  82.3 0.3 fusion
  82.8 7.7 %collective-permute-done.14.refs_2_ = bf16[64,2560]{1,0:T(8,128)(2,1)S(1)} collective-permute-done((bf16[64,2560]{1,0:T(8,128)(2,1)S(1)}, bf16[64,2560]{1,0:T(8,128)(2,1)S(1)}, u32[]{:S(2)}, u32[]{:S(2)}) %collective-permute-start.14) | collective-permute-done | bytes 327712 | tf_op jit(solution)/shard_map/ppermute | solution.py:27
  90.4 4.6 %attend_0.1 = (bf16[64,2048]{1,0:T(8,128)(2,1)S(1)}, bf16[64,256]{1,0:T(8,128)(2,1)S(1)}, bf16[64,256]{1,0:T(8,128)(2,1)S(1)}) custom-call(f32[128,2560]{1,0:T(8,128)S(1)} %get-tuple-element.21.refs_0_, bf16[64,2560]{1,0:T(8,128)(2,1)S(1)} %collective-permute-done.10.refs_1_, bf16[64,2560]{1,0:T(8,128)(2,1)S(1)} %collective-permute-done.14.refs_2_, ...), custom_call_target="tpu_custom_call" | custom-call | flops 268435456 | bytes 5505024 | tf_op jit(solution)/shard_map/attend_0/pallas_call | solution.py:249
  95.1 1.8 collective-permute-start.16
  96.9 5.9 %collective-permute-done.16.refs_3_ = bf16[64,2048]{1,0:T(8,128)(2,1)S(1)} collective-permute-done((bf16[64,2048]{1,0:T(8,128)(2,1)S(1)}, bf16[64,2048]{1,0:T(8,128)(2,1)S(1)}, u32[]{:S(2)}, u32[]{:S(2)}) %collective-permute-start.16) | collective-permute-done | bytes 262176 | tf_op jit(solution)/shard_map/ppermute | solution.py:27
  102.8 1.5 collective-permute-done.17.refs_4_
  104.3 3.4 %copy-done = bf16[2048,2048]{1,0:T(8,128)(2,1)S(1)} copy-done((bf16[2048,2048]{1,0:T(8,128)(2,1)S(1)}, bf16[2048,2048]{1,0:T(8,128)(2,1)}, u32[]{:S(2)}) %copy-start) | copy-done | bytes 8388632
  107.7 4.8 %output_0.1 = bf16[256,2048]{1,0:T(8,128)(2,1)} custom-call(s32[4]{0:T(128)S(1)} %pad_add_fusion.refs_0_, bf16[64,2048]{1,0:T(8,128)(2,1)S(1)} %get-tuple-element.25.refs_1_, bf16[64,2048]{1,0:T(8,128)(2,1)S(1)} %collective-permute-done.15.refs_2_, bf16[64,2048]{1,0:T(8,128)(2,1)S(1)} %collective-permute-done.16.refs_3_, ...), custom_call_target="tpu_custom_call" | custom-call | flops 2147483648 | bytes 10485760 | tf_op jit(solution)/shard_map/output_0/pallas_call | solution.py:295
  112.5 0.2 collective-permute-start.18
  112.7 1.8 collective-permute-start.20
  114.5 8.2 %collective-permute-done.20.refs_2_ = bf16[64,2560]{1,0:T(8,128)(2,1)S(1)} collective-permute-done((bf16[64,2560]{1,0:T(8,128)(2,1)S(1)}, bf16[64,2560]{1,0:T(8,128)(2,1)S(1)}, u32[]{:S(2)}, u32[]{:S(2)}) %collective-permute-start.20) | collective-permute-done | bytes 327712 | tf_op jit(solution)/shard_map/ppermute | solution.py:27
  122.7 2.2 %copy-done.3 = bf16[128,2,64,128]{3,2,1,0:T(8,128)(2,1)S(1)} copy-done((bf16[128,2,64,128]{3,2,1,0:T(8,128)(2,1)S(1)}, bf16[128,2,64,128]{3,2,1,0:T(8,128)(2,1)}, u32[]{:S(2)}) %copy-start.3) | copy-done | bytes 4194328
  124.9 2.2 %copy-done.5 = bf16[128,2,64,128]{3,2,1,0:T(8,128)(2,1)S(1)} copy-done((bf16[128,2,64,128]{3,2,1,0:T(8,128)(2,1)S(1)}, bf16[128,2,64,128]{3,2,1,0:T(8,128)(2,1)}, u32[]{:S(2)}) %copy-start.5) | copy-done | bytes 4194328
  127.1 4.6 %attend_1.1 = (bf16[64,2048]{1,0:T(8,128)(2,1)S(1)}, bf16[64,256]{1,0:T(8,128)(2,1)S(1)}, bf16[64,256]{1,0:T(8,128)(2,1)S(1)}) custom-call(f32[128,2560]{1,0:T(8,128)S(1)} %get-tuple-element.21.refs_0_, bf16[64,2560]{1,0:T(8,128)(2,1)S(1)} %collective-permute-done.18.refs_1_, bf16[64,2560]{1,0:T(8,128)(2,1)S(1)} %collective-permute-done.20.refs_2_, ...), custom_call_target="tpu_custom_call" | custom-call | flops 268435456 | bytes 5505024 | tf_op jit(solution)/shard_map/attend_1/pallas_call | solution.py:249
  131.7 1.8 collective-permute-start.22
  133.5 6.0 %collective-permute-done.22.refs_3_ = bf16[64,2048]{1,0:T(8,128)(2,1)S(1)} collective-permute-done((bf16[64,2048]{1,0:T(8,128)(2,1)S(1)}, bf16[64,2048]{1,0:T(8,128)(2,1)S(1)}, u32[]{:S(2)}, u32[]{:S(2)}) %collective-permute-start.22) | collective-permute-done | bytes 262176 | tf_op jit(solution)/shard_map/ppermute | solution.py:27
  139.5 1.5 collective-permute-done.23.refs_4_
  141.1 3.4 %copy-done.1 = bf16[2048,2048]{1,0:T(8,128)(2,1)S(1)} copy-done((bf16[2048,2048]{1,0:T(8,128)(2,1)S(1)}, bf16[2048,2048]{1,0:T(8,128)(2,1)}, u32[]{:S(2)}) %copy-start.1) | copy-done | bytes 8388632
  144.5 4.7 %output_1.1 = bf16[256,2048]{1,0:T(8,128)(2,1)} custom-call(s32[4]{0:T(128)S(1)} %pad_add_fusion.refs_0_, bf16[64,2048]{1,0:T(8,128)(2,1)S(1)} %get-tuple-element.28.refs_1_, bf16[64,2048]{1,0:T(8,128)(2,1)S(1)} %collective-permute-done.21.refs_2_, bf16[64,2048]{1,0:T(8,128)(2,1)S(1)} %collective-permute-done.22.refs_3_, ...), custom_call_target="tpu_custom_call" | custom-call | flops 2147483648 | bytes 10485760 | tf_op jit(solution)/shard_map/output_1/pallas_call | solution.py:295
  149.2 0.6 pad_maximum_fusion.3
  149.8 0.6 pad_maximum_fusion.2
  150.5 27.6 %reduce-scatter.5.cloned.1.call-done = bf16[64,2048]{1,0:T(8,128)(2,1)} async-done(((bf16[256,2048]{1,0:T(8,128)(2,1)}), bf16[64,2048]{1,0:T(8,128)(2,1)}) %reduce-scatter.5.cloned.1.call-update) | async-done | bytes 262160 | tf_op jit(solution)/shard_map/reduce_scatter | solution.py:435
  178.1 1.9 %maximum_bitcast_fusion = bf16[128,2048]{1,0:T(8,128)(2,1)} fusion(bf16[1,64,2048]{2,1,0:T(8,128)(2,1)} %bitcast.23, bf16[1,64,2048]{2,1,0:T(8,128)(2,1)} %bitcast.22), kind=kLoop, calls=%fused_computation.8 | loop fusion | flops 1048576 | bytes 1048576 | tf_op jit(solution)/shard_map/reshape | solution.py:439
  (89 shorter events, 0.9 us)
Async XLA Ops:
  7.2 143.3 %reduce-scatter.3.cloned.1.call-start = ((), (), s32[]{:S(2)}) async-start(), calls=%async_computation.2 | async-start | bytes 1310720 | tf_op jit(solution)/shard_map/reduce_scatter | solution.py:435
  9.1 15.0 %collective-permute-start.4 = (bf16[128,2048]{1,0:T(8,128)(2,1)S(1)}, bf16[128,2048]{1,0:T(8,128)(2,1)S(1)}, u32[]{:S(2)}, u32[]{:S(2)}) collective-permute-start(bf16[128,2048]{1,0:T(8,128)(2,1)S(1)} %multiply_convert_fusion.4.refs_1_), channel_id=1, source_target_pairs={{0,8},{4,12},{8,0},{12,4},{1,9},{5,13},{9,1},{13,5},{2,10},{6,14},... | collective-permute-start | bytes 1572872 | tf_op jit(solution)/shard_map/ppermute | solution.py:27
  12.1 18.4 %collective-permute-start.3 = (bf16[128,2048]{1,0:T(8,128)(2,1)S(1)}, bf16[128,2048]{1,0:T(8,128)(2,1)S(1)}, u32[]{:S(2)}, u32[]{:S(2)}) collective-permute-start(bf16[128,2048]{1,0:T(8,128)(2,1)S(1)} %multiply_convert_fusion.4.refs_1_), channel_id=1, source_target_pairs={{0,4},{4,0},{8,12},{12,8},{1,5},{5,1},{9,13},{13,9},{2,6},{6,2},{1... | collective-permute-start | bytes 1572872 | tf_op jit(solution)/shard_map/ppermute | solution.py:22
  12.1 17.1 %collective-permute-start.1 = (s32[1,128]{1,0:T(1,128)}, s32[1,128]{1,0:T(1,128)S(1)}, u32[]{:S(2)}, u32[]{:S(2)}) collective-permute-start(s32[1,128]{1,0:T(1,128)} %bitcast.25), channel_id=1, source_target_pairs={{0,8},{4,12},{8,0},{12,4},{1,9},{5,13},{9,1},{13,5},{2,10},{6,14},... | collective-permute-start | bytes 1544 | tf_op jit(solution)/shard_map/ppermute | solution.py:27
  12.2 17.6 %collective-permute-start = (s32[1,128]{1,0:T(1,128)}, s32[1,128]{1,0:T(1,128)S(1)}, u32[]{:S(2)}, u32[]{:S(2)}) collective-permute-start(s32[1,128]{1,0:T(1,128)} %bitcast.26), channel_id=1, source_target_pairs={{0,4},{4,0},{8,12},{12,8},{1,5},{5,1},{9,13},{13,9},{2,6},{6,2},{1... | collective-permute-start | bytes 1544 | tf_op jit(solution)/shard_map/ppermute | solution.py:22
  24.0 3.4 %copy-start.26 = (bf16[128,2048]{1,0:T(8,128)(2,1)}, bf16[128,2048]{1,0:T(8,128)(2,1)S(1)}, u32[]{:S(2)}) copy-start(bf16[128,2048]{1,0:T(8,128)(2,1)S(1)} %collective-permute-done.4.refs_3_) | copy-start | bytes 1572868
  24.0 7.3 %collective-permute-start.5 = (bf16[128,2048]{1,0:T(8,128)(2,1)S(1)}, bf16[128,2048]{1,0:T(8,128)(2,1)S(1)}, u32[]{:S(2)}, u32[]{:S(2)}) collective-permute-start(bf16[128,2048]{1,0:T(8,128)(2,1)S(1)} %collective-permute-done.4.refs_3_), channel_id=1, source_target_pairs={{0,4},{4,0},{8,12},{12,8},{1,5},{5,1},{9,13},{13,9},{2,6},{6,2},{1... | collective-permute-start | bytes 1572872 | tf_op jit(solution)/shard_map/ppermute | solution.py:22
  24.0 5.3 %copy-start.34 = (bf16[128,8192]{1,0:T(8,128)(2,1)S(1)}, bf16[128,8192]{1,0:T(8,128)(2,1)}, u32[]{:S(2)}) copy-start(bf16[128,8192]{1,0:T(8,128)(2,1)} %param.14) | copy-start | bytes 6291460
  27.4 3.1 %copy-start.36 = (s32[128]{0:T(128)S(1)}, s32[128]{0:T(128)}, u32[]{:S(2)}) copy-start(s32[128]{0:T(128)} %param.23) | copy-start | bytes 1540
  27.4 17.7 %collective-permute-start.11 = (bf16[128,2048]{1,0:T(8,128)(2,1)}, bf16[128,2048]{1,0:T(8,128)(2,1)S(1)}, u32[]{:S(2)}, u32[]{:S(2)}) collective-permute-start(bf16[128,2048]{1,0:T(8,128)(2,1)} %get-tuple-element.34), channel_id=1, source_target_pairs={{0,8},{4,12},{8,0},{12,4},{1,9},{5,13},{9,1},{13,5},{2,10},{6,14},... | collective-permute-start | bytes 1572872 | tf_op jit(solution)/shard_map/ppermute | solution.py:27
  29.2 1.1 collective-permute-start.2
  29.8 22.8 %collective-permute-start.12 = (bf16[128,2048]{1,0:T(8,128)(2,1)}, bf16[128,2048]{1,0:T(8,128)(2,1)S(1)}, u32[]{:S(2)}, u32[]{:S(2)}) collective-permute-start(bf16[128,2048]{1,0:T(8,128)(2,1)} %get-tuple-element.33), channel_id=1, source_target_pairs={{0,12},{4,8},{8,4},{12,0},{1,13},{5,9},{9,5},{13,1},{2,14},{6,10},... | collective-permute-start | bytes 1572872 | tf_op jit(solution)/shard_map/ppermute | solution.py:27
  30.3 32.2 %collective-permute-start.9 = (bf16[128,2048]{1,0:T(8,128)(2,1)}, bf16[128,2048]{1,0:T(8,128)(2,1)}, u32[]{:S(2)}, u32[]{:S(2)}) collective-permute-start(bf16[128,2048]{1,0:T(8,128)(2,1)} %get-tuple-element.35), channel_id=1, source_target_pairs={{0,4},{4,0},{8,12},{12,8},{1,5},{5,1},{9,13},{13,9},{2,6},{6,2},{1... | collective-permute-start | bytes 1572872 | tf_op jit(solution)/shard_map/ppermute | solution.py:27
  30.5 0.8 copy-start.28
  31.3 0.8 copy-start.30
  32.1 1.6 copy-start.24
  33.7 1.6 copy-start.25
  35.3 1.0 copy-start.27
  36.3 1.0 copy-start.29
  37.4 1.0 copy-start.31
  38.4 14.3 %copy-start.6 = (bf16[32,16,2048]{2,1,0:T(8,128)(2,1)S(1)}, bf16[32,16,2048]{2,1,0:T(8,128)(2,1)}, u32[]{:S(2)}) copy-start(bf16[32,16,2048]{2,1,0:T(8,128)(2,1)} %param.25) | copy-start | bytes 6291460
  38.4 14.3 %copy-start.7 = (bf16[2048,256]{1,0:T(8,128)(2,1)S(1)}, bf16[2048,256]{1,0:T(8,128)(2,1)}, u32[]{:S(2)}) copy-start(bf16[2048,256]{1,0:T(8,128)(2,1)} %refs_8_.5) | copy-start | bytes 3145732
  38.4 14.3 %copy-start.9 = (bf16[2048,256]{1,0:T(8,128)(2,1)S(1)}, bf16[2048,256]{1,0:T(8,128)(2,1)}, u32[]{:S(2)}) copy-start(bf16[2048,256]{1,0:T(8,128)(2,1)} %refs_9_.3) | copy-start | bytes 3145732
  38.4 14.3 %copy-start.14 = (bf16[32,16,256]{2,1,0:T(8,128)(2,1)S(1)}, bf16[32,16,256]{2,1,0:T(8,128)(2,1)}, u32[]{:S(2)}) copy-start(bf16[32,16,256]{2,1,0:T(8,128)(2,1)} %param.27) | copy-start | bytes 786436
  40.8 19.8 %copy-start.16 = (f32[32,512]{1,0:T(8,128)}, f32[32,512]{1,0:T(8,128)S(1)}, u32[]{:S(2)}) copy-start(f32[32,512]{1,0:T(8,128)S(1)} %shrink.1.refs_1_) | copy-start | bytes 196612
  40.8 11.8 %collective-permute-start.6 = (f32[32,512]{1,0:T(8,128)S(1)}, f32[32,512]{1,0:T(8,128)S(1)}, u32[]{:S(2)}, u32[]{:S(2)}) collective-permute-start(f32[32,512]{1,0:T(8,128)S(1)} %shrink.1.refs_1_), channel_id=1, source_target_pairs={{0,1},{1,2},{2,3},{3,0},{4,5},{5,6},{6,7},{7,4},{8,9},{9,10},{10,1... | collective-permute-start | bytes 196616 | tf_op jit(solution)/shard_map/ppermute | solution.py:385
  42.5 10.2 %collective-permute-start.7 = (f32[32,512]{1,0:T(8,128)S(1)}, f32[32,512]{1,0:T(8,128)S(1)}, u32[]{:S(2)}, u32[]{:S(2)}) collective-permute-start(f32[32,512]{1,0:T(8,128)S(1)} %shrink.1.refs_1_), channel_id=1, source_target_pairs={{0,2},{1,3},{2,0},{3,1},{4,6},{5,7},{6,4},{7,5},{8,10},{9,11},{10,... | collective-permute-start | bytes 196616 | tf_op jit(solution)/shard_map/ppermute | solution.py:385
  45.1 7.6 %collective-permute-start.8 = (f32[32,512]{1,0:T(8,128)S(1)}, f32[32,512]{1,0:T(8,128)S(1)}, u32[]{:S(2)}, u32[]{:S(2)}) collective-permute-start(f32[32,512]{1,0:T(8,128)S(1)} %shrink.1.refs_1_), channel_id=1, source_target_pairs={{0,3},{1,0},{2,1},{3,2},{4,7},{5,4},{6,5},{7,6},{8,11},{9,8},{10,9... | collective-permute-start | bytes 196616 | tf_op jit(solution)/shard_map/ppermute | solution.py:385
  52.7 8.0 %copy-start.18 = (f32[32,512]{1,0:T(8,128)}, f32[32,512]{1,0:T(8,128)S(1)}, u32[]{:S(2)}) copy-start(f32[32,512]{1,0:T(8,128)S(1)} %collective-permute-done.6.refs_2_) | copy-start | bytes 196612
  52.7 8.0 %copy-start.20 = (f32[32,512]{1,0:T(8,128)}, f32[32,512]{1,0:T(8,128)S(1)}, u32[]{:S(2)}) copy-start(f32[32,512]{1,0:T(8,128)S(1)} %collective-permute-done.7.refs_3_) | copy-start | bytes 196612
  52.7 8.0 %copy-start.22 = (f32[32,512]{1,0:T(8,128)}, f32[32,512]{1,0:T(8,128)S(1)}, u32[]{:S(2)}) copy-start(f32[32,512]{1,0:T(8,128)S(1)} %collective-permute-done.8.refs_4_) | copy-start | bytes 196612
  52.7 9.6 %copy-start.35 = (s32[128]{0:T(128)S(1)}, s32[128]{0:T(128)}, u32[]{:S(2)}) copy-start(s32[128]{0:T(128)} %param.22) | copy-start | bytes 1540
  60.7 1.1 copy-start.12
  61.8 17.6 %collective-permute-start.13 = (bf16[64,2560]{1,0:T(8,128)(2,1)}, bf16[64,2560]{1,0:T(8,128)(2,1)}, u32[]{:S(2)}, u32[]{:S(2)}) collective-permute-start(bf16[64,2560]{1,0:T(8,128)(2,1)} %get-tuple-element.24), channel_id=1, source_target_pairs={{0,4},{4,0},{8,12},{12,8},{1,5},{5,1},{9,13},{13,9},{2,6},{6,2},{1... | collective-permute-start | bytes 983048 | tf_op jit(solution)/shard_map/ppermute | solution.py:22
  62.1 17.3 %collective-permute-start.19 = (bf16[64,2560]{1,0:T(8,128)(2,1)}, bf16[64,2560]{1,0:T(8,128)(2,1)}, u32[]{:S(2)}, u32[]{:S(2)}) collective-permute-start(bf16[64,2560]{1,0:T(8,128)(2,1)} %get-tuple-element.27), channel_id=1, source_target_pairs={{0,4},{4,0},{8,12},{12,8},{1,5},{5,1},{9,13},{13,9},{2,6},{6,2},{1... | collective-permute-start | bytes 983048 | tf_op jit(solution)/shard_map/ppermute | solution.py:22
  62.5 1.2 copy-start.8
  63.8 1.2 copy-start.10
  65.0 1.0 copy-start.11
  66.0 0.9 copy-start.15
  67.0 0.8 copy-start.17
  67.8 0.8 copy-start.19
  68.7 0.8 copy-start.21
  69.5 0.8 copy-start.23
  70.3 9.0 %copy-start.13 = (f32[128,2560]{1,0:T(8,128)S(1)}, f32[128,2560]{1,0:T(8,128)}, u32[]{:S(2)}) copy-start(f32[128,2560]{1,0:T(8,128)} %copy-done.12) | copy-start | bytes 3932164
  70.3 20.1 %copy-start.2 = (bf16[128,2,64,128]{3,2,1,0:T(8,128)(2,1)S(1)}, bf16[128,2,64,128]{3,2,1,0:T(8,128)(2,1)}, u32[]{:S(2)}) copy-start(bf16[128,2,64,128]{3,2,1,0:T(8,128)(2,1)} %refs_7_.7) | copy-start | bytes 12582916
  70.3 20.1 %copy-start.4 = (bf16[128,2,64,128]{3,2,1,0:T(8,128)(2,1)S(1)}, bf16[128,2,64,128]{3,2,1,0:T(8,128)(2,1)}, u32[]{:S(2)}) copy-start(bf16[128,2,64,128]{3,2,1,0:T(8,128)(2,1)} %refs_8_.7) | copy-start | bytes 12582916
  78.9 16.1 %copy-start.32 = (bf16[64,2560]{1,0:T(8,128)(2,1)}, bf16[64,2560]{1,0:T(8,128)(2,1)S(1)}, u32[]{:S(2)}) copy-start(bf16[64,2560]{1,0:T(8,128)(2,1)S(1)} %get-tuple-element.26) | copy-start | bytes 983044
  78.9 3.8 %collective-permute-start.10 = (bf16[64,2560]{1,0:T(8,128)(2,1)S(1)}, bf16[64,2560]{1,0:T(8,128)(2,1)S(1)}, u32[]{:S(2)}, u32[]{:S(2)}) collective-permute-start(bf16[64,2560]{1,0:T(8,128)(2,1)S(1)} %get-tuple-element.22), channel_id=1, source_target_pairs={{0,4},{4,0},{8,12},{12,8},{1,5},{5,1},{9,13},{13,9},{2,6},{6,2},{1... | collective-permute-start | bytes 983048 | tf_op jit(solution)/shard_map/ppermute | solution.py:22
  80.5 9.9 %collective-permute-start.14 = (bf16[64,2560]{1,0:T(8,128)(2,1)S(1)}, bf16[64,2560]{1,0:T(8,128)(2,1)S(1)}, u32[]{:S(2)}, u32[]{:S(2)}) collective-permute-start(bf16[64,2560]{1,0:T(8,128)(2,1)S(1)} %get-tuple-element.37), channel_id=1, source_target_pairs={{0,8},{4,12},{8,0},{12,4},{1,9},{5,13},{9,1},{13,5},{2,10},{6,14},... | collective-permute-start | bytes 983048 | tf_op jit(solution)/shard_map/ppermute | solution.py:27
  95.1 7.7 %collective-permute-start.16 = (bf16[64,2048]{1,0:T(8,128)(2,1)S(1)}, bf16[64,2048]{1,0:T(8,128)(2,1)S(1)}, u32[]{:S(2)}, u32[]{:S(2)}) collective-permute-start(bf16[64,2048]{1,0:T(8,128)(2,1)S(1)} %get-tuple-element.25.refs_1_), channel_id=1, source_target_pairs={{0,8},{4,12},{8,0},{12,4},{1,9},{5,13},{9,1},{13,5},{2,10},{6,14},... | collective-permute-start | bytes 786440 | tf_op jit(solution)/shard_map/ppermute | solution.py:27
  96.9 5.9 %collective-permute-start.15 = (bf16[64,2048]{1,0:T(8,128)(2,1)S(1)}, bf16[64,2048]{1,0:T(8,128)(2,1)S(1)}, u32[]{:S(2)}, u32[]{:S(2)}) collective-permute-start(bf16[64,2048]{1,0:T(8,128)(2,1)S(1)} %get-tuple-element.25.refs_1_), channel_id=1, source_target_pairs={{0,4},{4,0},{8,12},{12,8},{1,5},{5,1},{9,13},{13,9},{2,6},{6,2},{1... | collective-permute-start | bytes 786440 | tf_op jit(solution)/shard_map/ppermute | solution.py:22
  102.7 1.5 collective-permute-start.17
  104.3 3.4 %copy-start = (bf16[2048,2048]{1,0:T(8,128)(2,1)S(1)}, bf16[2048,2048]{1,0:T(8,128)(2,1)}, u32[]{:S(2)}) copy-start(bf16[2048,2048]{1,0:T(8,128)(2,1)} %refs_5_.3) | copy-start | bytes 25165828
  107.7 4.8 %copy-start.33 = (bf16[64,2560]{1,0:T(8,128)(2,1)S(1)}, bf16[64,2560]{1,0:T(8,128)(2,1)}, u32[]{:S(2)}) copy-start(bf16[64,2560]{1,0:T(8,128)(2,1)} %copy-done.32) | copy-start | bytes 983044
  112.4 65.7 %reduce-scatter.5.cloned.1.call-start = ((), (), s32[]{:S(2)}) async-start(), calls=%async_computation.3 | async-start | bytes 1310720 | tf_op jit(solution)/shard_map/reduce_scatter | solution.py:435
  112.5 2.0 %collective-permute-start.18 = (bf16[64,2560]{1,0:T(8,128)(2,1)S(1)}, bf16[64,2560]{1,0:T(8,128)(2,1)S(1)}, u32[]{:S(2)}, u32[]{:S(2)}) collective-permute-start(bf16[64,2560]{1,0:T(8,128)(2,1)S(1)} %copy-done.33), channel_id=1, source_target_pairs={{0,4},{4,0},{8,12},{12,8},{1,5},{5,1},{9,13},{13,9},{2,6},{6,2},{1... | collective-permute-start | bytes 983048 | tf_op jit(solution)/shard_map/ppermute | solution.py:22
  112.7 10.0 %collective-permute-start.20 = (bf16[64,2560]{1,0:T(8,128)(2,1)S(1)}, bf16[64,2560]{1,0:T(8,128)(2,1)S(1)}, u32[]{:S(2)}, u32[]{:S(2)}) collective-permute-start(bf16[64,2560]{1,0:T(8,128)(2,1)S(1)} %get-tuple-element.38), channel_id=1, source_target_pairs={{0,8},{4,12},{8,0},{12,4},{1,9},{5,13},{9,1},{13,5},{2,10},{6,14},... | collective-permute-start | bytes 983048 | tf_op jit(solution)/shard_map/ppermute | solution.py:27
  122.7 2.2 %copy-start.3 = (bf16[128,2,64,128]{3,2,1,0:T(8,128)(2,1)S(1)}, bf16[128,2,64,128]{3,2,1,0:T(8,128)(2,1)}, u32[]{:S(2)}) copy-start(bf16[128,2,64,128]{3,2,1,0:T(8,128)(2,1)} %refs_7_.7) | copy-start | bytes 12582916
  124.9 2.2 %copy-start.5 = (bf16[128,2,64,128]{3,2,1,0:T(8,128)(2,1)S(1)}, bf16[128,2,64,128]{3,2,1,0:T(8,128)(2,1)}, u32[]{:S(2)}) copy-start(bf16[128,2,64,128]{3,2,1,0:T(8,128)(2,1)} %refs_8_.7) | copy-start | bytes 12582916
  131.7 7.8 %collective-permute-start.22 = (bf16[64,2048]{1,0:T(8,128)(2,1)S(1)}, bf16[64,2048]{1,0:T(8,128)(2,1)S(1)}, u32[]{:S(2)}, u32[]{:S(2)}) collective-permute-start(bf16[64,2048]{1,0:T(8,128)(2,1)S(1)} %get-tuple-element.28.refs_1_), channel_id=1, source_target_pairs={{0,8},{4,12},{8,0},{12,4},{1,9},{5,13},{9,1},{13,5},{2,10},{6,14},... | collective-permute-start | bytes 786440 | tf_op jit(solution)/shard_map/ppermute | solution.py:27
  133.5 6.0 %collective-permute-start.21 = (bf16[64,2048]{1,0:T(8,128)(2,1)S(1)}, bf16[64,2048]{1,0:T(8,128)(2,1)S(1)}, u32[]{:S(2)}, u32[]{:S(2)}) collective-permute-start(bf16[64,2048]{1,0:T(8,128)(2,1)S(1)} %get-tuple-element.28.refs_1_), channel_id=1, source_target_pairs={{0,4},{4,0},{8,12},{12,8},{1,5},{5,1},{9,13},{13,9},{2,6},{6,2},{1... | collective-permute-start | bytes 786440 | tf_op jit(solution)/shard_map/ppermute | solution.py:22
  139.5 1.5 collective-permute-start.23
  141.1 3.4 %copy-start.1 = (bf16[2048,2048]{1,0:T(8,128)(2,1)S(1)}, bf16[2048,2048]{1,0:T(8,128)(2,1)}, u32[]{:S(2)}) copy-start(bf16[2048,2048]{1,0:T(8,128)(2,1)} %refs_5_.3) | copy-start | bytes 25165828
Sparse Core Ops, SparseCore 0:
  112.6 28.5 reduce-scatter.2
  149.3 28.7 reduce-scatter.4

commit v3 on v2

v3 whole, which is shorter than its diff:
```python
import functools
import math

import jax
import jax.numpy as jnp
from jax import lax
from jax.experimental import pallas as pl
from jax.experimental.pallas import tpu as pltpu
from jax.sharding import PartitionSpec as P

epsilon = 1e-05
adapter_scale = 0.5
rope_base = 500000.0
masked_score = -1e30


def params():
    return pltpu.CompilerParams(vmem_limit_bytes=28 * 1024 * 1024)


VMEM = pl.BlockSpec(memory_space=pltpu.VMEM)
HBM = pl.BlockSpec(memory_space=pltpu.HBM)


def columns_of(ref, i, width):
    return ref.at[:, pl.ds(pl.multiple_of(i * width, width), width)]


def small_cost():
    return pl.CostEstimate(flops=1000, bytes_accessed=1000, transcendentals=0)


def after(x, *earlier):
    return lax.optimization_barrier((x, *earlier))[0]


def core_swap(x, pool_count):
    return lax.ppermute(x, "pool", [(p, p ^ 1) for p in range(pool_count)])


def chip_move(x, pool_count, d, e=0):
    chips = pool_count // 2
    return lax.ppermute(
        x,
        "pool",
        [(p, (p // 2 + d) % chips * 2 + ((p % 2) ^ e)) for p in range(pool_count)],
    )


def shrink_kernel(*refs):
    ids, *blocks, query_down, value_down, out, query_held, value_held, sems = refs
    tables = ((query_down, query_held), (value_down, value_held))
    copies = [
        pltpu.make_async_copy(far, near, sems.at[i]) for i, (far, near) in enumerate(tables)
    ]
    for copy in copies:
        copy.start()
    adapters = query_down.shape[0] // 16
    rows = blocks[0].shape[0]
    per = 2
    for at, (_, table) in enumerate(tables):
        copies[at].wait()
        for first in range(0, len(blocks), per):
            x = jnp.concatenate([b[...] for b in blocks[first : first + per]], axis=0)
            span = slice(first * rows, (first + per) * rows)
            label = ids[:, span].reshape(1, 1, per * rows)
            chosen = lax.broadcasted_iota(jnp.int32, (adapters, 1, per * rows), 0) == label
            terms = lax.dot_general(
                table[...], x, (((1,), (1,)), ((), ())), preferred_element_type=jnp.float32
            ).reshape(adapters, 16, per * rows)
            out[at * 16 : (at + 1) * 16, span] = jnp.sum(jnp.where(chosen, terms, 0.0), axis=0)


def spread_lows(low, ids, adapters):
    total = ids.shape[1]
    low = low.astype(jnp.bfloat16).astype(jnp.float32) * adapter_scale
    chosen = lax.broadcasted_iota(jnp.int32, (adapters, 1, total), 0) == ids.reshape(1, 1, total)
    return [
        jnp.where(chosen, low[at : at + 16][None], 0.0)
        .reshape(adapters * 16, total)
        .T.astype(jnp.bfloat16)
        for at in (0, 16)
    ]


def project_kernel(parts, n, spans, tile, window, *refs):
    ids = refs[0] if parts else None
    lows = refs[1 : 1 + parts]
    refs = refs[1 + parts :] if parts else refs
    count = 5 if parts else 3
    blocks, far, refs = refs[:n], refs[n : n + count], refs[n + count :]
    (keep, *sends), near, refs = refs[:4], refs[4 : 4 + count], refs[4 + count :]
    xs, sem_q, sem_v, *spreads = refs
    wq, wk, wv, *up = near
    steps = wq.shape[1] // tile
    first, rows = window
    wide = [(0, 0)] + ([(3, 1)] if parts else [])
    narrow = [(1, 0), (2, 1)] + ([(4, 2)] if parts else [])

    def wide_copy(which, slot, i):
        return pltpu.make_async_copy(
            columns_of(far[which], i, tile), columns_of(near[which], i, tile), sem_q.at[slot, i]
        )

    def narrow_copy(which, slot):
        return pltpu.make_async_copy(far[which], near[which], sem_v.at[slot])

    for i in range(steps):
        for which, slot in wide:
            wide_copy(which, slot, i).start()
    for which, slot in narrow:
        narrow_copy(which, slot).start()

    xs[:rows, :] = blocks[0][first : first + rows, :]
    at = rows
    for block in blocks[1:]:
        size = min(rows, block.shape[0])
        xs[at : at + size, :] = block[first : first + size, :]
        at += size
    if parts:
        low = lows[0][...]
        for other in lows[1:]:
            low = low + other[...]
        low = jnp.concatenate([low[:, at : at + rows] for at in spans], axis=1)
        label = jnp.concatenate([ids[:, at : at + rows] for at in spans], axis=1)
        for ref, value in zip(spreads, spread_lows(low, label, up[0].shape[0] // 16)):
            ref[...] = value

    def sums(w, spread=None, u=None):
        acc = jnp.dot(xs[...], w, preferred_element_type=jnp.float32)
        if u is not None:
            acc = acc + jnp.dot(spread[...], u, preferred_element_type=jnp.float32)
        return acc

    for half in range(2):

        @pl.loop(0, steps // 2)
        def _(j):
            i = half * (steps // 2) + j
            for which, slot in wide:
                wide_copy(which, slot, i).wait()
            columns = pl.ds(pl.multiple_of(i * tile, tile), tile)
            extra = (spreads[0], up[0][:, columns]) if parts else ()
            acc = sums(wq[:, columns], *extra)
            keep[:, columns] = acc[:rows]
            columns = pl.ds(pl.multiple_of(j * tile, tile), tile)
            sends[half][:, columns] = acc[rows:].astype(sends[half].dtype)

    for which, slot in narrow:
        narrow_copy(which, slot).wait()
    start, kv = wq.shape[1], wk.shape[1]
    for at, w in enumerate((wk, wv)):
        extra = (spreads[1], up[1][...]) if parts and at else ()
        acc = sums(w[...], *extra)
        keep[:, start + at * kv : start + (at + 1) * kv] = acc[:rows]
        sends[2][:, at * kv : (at + 1) * kv] = acc[rows:].astype(sends[2].dtype)


def project(name, blocks, wq, wk, wv, adapter=None, spans=None, window=None):
    rows, width = blocks[0].shape
    window = window or (0, rows)
    rows = window[1]
    tile = min(512, wq.shape[1] // 2)
    columns = wq.shape[1] + 2 * wk.shape[1]
    ids, lows, *up = adapter if adapter else (None, [])
    front = [ids, *lows] if adapter else []
    far = [wq, wk, wv, *up]
    send_type = jnp.bfloat16 if adapter else jnp.float32
    spreads = [pltpu.VMEM((2 * rows, u.shape[0]), jnp.bfloat16) for u in up]
    return pl.pallas_call(
        functools.partial(project_kernel, len(lows), len(blocks), spans, tile, window),
        in_specs=[VMEM] * (len(front) + len(blocks)) + [HBM] * len(far),
        out_specs=[VMEM] * 4,
        out_shape=[
            jax.ShapeDtypeStruct((rows, columns), jnp.float32),
            *[jax.ShapeDtypeStruct((rows, wq.shape[1] // 2), send_type)] * 2,
            jax.ShapeDtypeStruct((rows, 2 * wk.shape[1]), send_type),
        ],
        scratch_shapes=[
            *[pltpu.VMEM(x.shape, x.dtype) for x in far],
            pltpu.VMEM((2 * rows, width), jnp.bfloat16),
            pltpu.SemaphoreType.DMA((2, wq.shape[1] // tile)),
            pltpu.SemaphoreType.DMA((3,)),
            *spreads,
        ],
        compiler_params=params(),
        cost_estimate=small_cost(),
        name=name,
    )(*front, *blocks, *far)


def add_adapters_kernel(parts, tile, *refs):
    ids, *refs = refs
    lows, refs = refs[:parts], refs[parts:]
    keep0, low0, high0, kv0, far_q, far_v, keep, send, uq, uv, spread_q, spread_v, sems = refs
    copies = [
        pltpu.make_async_copy(far_q, uq, sems.at[0]),
        pltpu.make_async_copy(far_v, uv, sems.at[1]),
    ]
    for copy in copies:
        copy.start()
    rows = keep.shape[0]
    low = lows[0][:, : 2 * rows]
    for other in lows[1:]:
        low = low + other[:, : 2 * rows]
    both = spread_lows(low, ids[:, : 2 * rows], uq.shape[0] // 16)
    spread_q[...], spread_v[...] = both
    wide, kv = uq.shape[1], uv.shape[1]

    def write(extra, columns, at, at_columns):
        keep[:, columns] = keep0[:, columns] + extra[:rows]
        send[:, columns] = (at[:, at_columns] + extra[rows:]).astype(send.dtype)

    keep[:, wide : wide + kv] = keep0[:, wide : wide + kv]
    send[:, wide : wide + kv] = kv0[:, :kv].astype(send.dtype)
    copies[0].wait()

    for half, at in enumerate((low0, high0)):

        @pl.loop(0, wide // 2 // tile)
        def _(j):
            columns = pl.ds(pl.multiple_of(half * (wide // 2) + j * tile, tile), tile)
            extra = jnp.dot(spread_q[...], uq[:, columns], preferred_element_type=jnp.float32)
            write(extra, columns, at, pl.ds(pl.multiple_of(j * tile, tile), tile))

    copies[1].wait()
    extra = jnp.dot(spread_v[...], uv[...], preferred_element_type=jnp.float32)
    write(extra, slice(wide + kv, wide + 2 * kv), kv0, slice(kv, 2 * kv))


def add_adapters(keep, sends, adapter):
    ids, lows, uq, uv = adapter
    rows = keep.shape[0]
    spread = pltpu.VMEM((2 * rows, uq.shape[0]), jnp.bfloat16)
    return pl.pallas_call(
        functools.partial(add_adapters_kernel, len(lows), min(512, uq.shape[1] // 2)),
        in_specs=[VMEM] * (len(lows) + 5) + [HBM] * 2,
        out_specs=[VMEM] * 2,
        out_shape=[
            jax.ShapeDtypeStruct(keep.shape, jnp.float32),
            jax.ShapeDtypeStruct(keep.shape, jnp.bfloat16),
        ],
        scratch_shapes=[
            pltpu.VMEM(uq.shape, uq.dtype),
            pltpu.VMEM(uv.shape, uv.dtype),
            spread,
            spread,
            pltpu.SemaphoreType.DMA((2,)),
        ],
        compiler_params=params(),
        cost_estimate=small_cost(),
        name="add_adapters",
    )(ids, *lows, keep, *sends, uq, uv)


def attend_kernel(arrived, first_row, block, *refs):
    keep, swapped = refs[:2]
    moved = refs[2 : 2 + arrived]
    scale, cosines, sines, lengths, far_keys, far_values, *refs = refs[2 + arrived :]
    out, key_out, value_out, keys, values, sems = refs
    head = cosines.shape[1]
    rows = out.shape[0]
    _, kv_heads, cache, _ = keys.shape
    heads = out.shape[1] // head
    group = heads // kv_heads
    score_scale = 1.0 / math.sqrt(head)
    sub = 8

    def copies(i):
        to = pl.ds(pl.multiple_of(i * block, block), block)
        at = pl.ds(pl.multiple_of(first_row + i * block, block), block)
        return [
            pltpu.make_async_copy(far.at[at], near.at[to], sems.at[which, i])
            for which, (far, near) in enumerate(((far_keys, keys), (far_values, values)))
        ]

    for i in range(rows // block):
        for copy in copies(i):
            copy.start()

    column = lax.broadcasted_iota(jnp.int32, (sub, sub * cache), 1)
    start = lax.broadcasted_iota(jnp.int32, (sub, sub * cache), 0) * cache

    @pl.loop(0, rows // block)
    def _(i):
        for copy in copies(i):
            copy.wait()
        attended, new_keys, new_values = [], [], []
        for half in range(block // sub):
            here = pl.ds(pl.multiple_of(i * block + half * sub, sub), sub)
            whole = pl.ds(pl.multiple_of(first_row + i * block + half * sub, sub), sub)
            x = keep[whole] + swapped[whole].astype(jnp.float32)
            for m in moved:
                x = x + m[here].astype(jnp.float32)
            x = x * scale[whole]
            cos, sin = cosines[whole], sines[whole]
            inside = (column >= start) & (column < start + lengths[whole])

            def piece(i):
                return x[:, i * head : (i + 1) * head]

            def turn(v):
                return v * cos + pltpu.roll(v, head // 2, 1) * sin

            for g in range(kv_heads):
                query = jnp.concatenate(
                    [turn(piece(g * group + h)) for h in range(group)], axis=0
                ).astype(jnp.bfloat16)
                new_key = turn(piece(heads + g)).astype(jnp.bfloat16).astype(jnp.float32)
                new_value = piece(heads + kv_heads + g).astype(jnp.bfloat16).astype(jnp.float32)
                k = keys[here, g].reshape(sub * cache, head)
                v = values[here, g].reshape(sub * cache, head)
                scores = (
                    lax.dot_general(
                        query, k, (((1,), (1,)), ((), ())), preferred_element_type=jnp.float32
                    )
                    * score_scale
                )
                own_key = jnp.concatenate([new_key] * group, axis=0)
                own = (
                    jnp.sum(query.astype(jnp.float32) * own_key, axis=1, keepdims=True)
                    * score_scale
                )
                scores = jnp.where(
                    inside[None], scores.reshape(group, sub, sub * cache), masked_score
                ).reshape(group * sub, sub * cache)
                peak = jnp.maximum(jnp.max(scores, axis=1, keepdims=True), own)
                weights = jnp.exp(scores - peak)
                own_weight = jnp.exp(own - peak)
                inverse = 1.0 / (jnp.sum(weights, axis=1, keepdims=True) + own_weight)
                mixed = jnp.dot(weights.astype(jnp.bfloat16), v, preferred_element_type=jnp.float32)
                own_value = jnp.concatenate([new_value] * group, axis=0)
                mixed = (mixed + own_weight * own_value) * inverse
                attended += [mixed[h * sub : (h + 1) * sub] for h in range(group)]
                new_keys.append(new_key)
                new_values.append(new_value)
        r = pl.ds(pl.multiple_of(i * block, block), block)

        def joined(pieces):
            n = len(pieces) * sub // block
            return jnp.concatenate(
                [jnp.concatenate(pieces[j::n], axis=0) for j in range(n)], axis=1
            ).astype(jnp.bfloat16)

        out[r] = joined(attended)
        key_out[r] = joined(new_keys)
        value_out[r] = joined(new_values)


def attend(c, window, keep, swapped, moved, scale, cosines, sines, lengths, keys, values):
    rows, columns = keep.shape
    _, kv_heads, cache, head = keys.shape
    kv_cols = kv_heads * head
    first, part = window
    block = 16
    widths = (columns - 2 * kv_cols, kv_cols, kv_cols)
    held = pltpu.VMEM((part, kv_heads, cache, head), jnp.bfloat16)
    return pl.pallas_call(
        functools.partial(attend_kernel, len(moved), first, block),
        in_specs=[VMEM] * (len(moved) + 6) + [HBM] * 2,
        out_specs=[VMEM] * 3,
        out_shape=[jax.ShapeDtypeStruct((part, w), jnp.bfloat16) for w in widths],
        scratch_shapes=[held, held, pltpu.SemaphoreType.DMA((2, part // block))],
        compiler_params=params(),
        cost_estimate=small_cost(),
        name=f"attend_{c}",
    )(keep, swapped, *moved, scale, cosines, sines, lengths, keys, values)


def output_kernel(tile, *refs):
    order, *blocks, far, keep, send, weights, xs, sems = refs
    rows = blocks[0].shape[0]
    steps = far.shape[1] // tile

    def copy(i):
        return pltpu.make_async_copy(
            columns_of(far, i, tile), columns_of(weights, i, tile), sems.at[i]
        )

    for i in range(steps):
        copy(i).start()
    for b, block in enumerate(blocks):
        to = pl.multiple_of(order[b] * rows, rows)
        xs[pl.ds(to, rows), :] = block[...]
    half = keep.shape[0]

    @pl.loop(0, steps)
    def _(i):
        copy(i).wait()
        columns = pl.ds(pl.multiple_of(i * tile, tile), tile)
        acc = jnp.dot(xs[...], weights[:, columns], preferred_element_type=jnp.float32)
        keep[:, columns] = acc[:half].astype(jnp.bfloat16)
        send[:, columns] = acc[half:].astype(jnp.bfloat16)


def output_part(c, order, blocks, weights):
    rows = blocks[0].shape[0]
    depth, columns = weights.shape
    tile = min(512, columns)
    total = rows * len(blocks)
    half = jax.ShapeDtypeStruct((total // 2, columns), jnp.bfloat16)
    return pl.pallas_call(
        functools.partial(output_kernel, tile),
        in_specs=[pl.BlockSpec(memory_space=pltpu.SMEM), *[VMEM] * len(blocks), HBM],
        out_specs=[VMEM] * 2,
        out_shape=[half, half],
        scratch_shapes=[
            pltpu.VMEM(weights.shape, weights.dtype),
            pltpu.VMEM((total, depth), jnp.bfloat16),
            pltpu.SemaphoreType.DMA((columns // tile,)),
        ],
        compiler_params=params(),
        cost_estimate=small_cost(),
        name=f"output_{c}",
    )(order, *blocks, weights)


def reversed_bits(x, count):
    out, bit = 0, 1
    while bit < count:
        out = out * 2 + (x // bit) % 2
        bit *= 2
    return out


def halving_sum(keep, send, count, earlier):
    step, totals = 1, []
    while True:
        got = lax.ppermute(send, "tp", [(z, z ^ step) for z in range(count)])
        if earlier:
            got = after(got, earlier[len(totals)])
        total = keep.astype(jnp.float32) + got.astype(jnp.float32)
        totals.append(total)
        step *= 2
        if step == count:
            return total.astype(jnp.bfloat16), totals
        half = total.shape[0] // 2
        keep, send = total[:half], total[half:].astype(jnp.bfloat16)


def shards(
    tokens,
    input_norm_gain,
    query_matrix,
    key_matrix,
    value_matrix,
    output_matrix,
    rotated_key_cache,
    cached_value_rows,
    cache_length_per_row,
    row_adapter_index,
    query_down_maps,
    query_up_maps,
    value_down_maps,
    value_up_maps,
):
    pool_count = lax.axis_size("pool")
    tp_count = lax.axis_size("tp")
    chips = pool_count // 2
    pool_at = lax.axis_index("pool")
    tp_at = lax.axis_index("tp")
    chip, core = pool_at // 2, pool_at % 2
    rows = tokens.shape[0]
    adapters, rank, piece = query_down_maps.shape
    base = query_matrix.shape[0]
    kv_heads = rotated_key_cache.shape[1]
    head = rotated_key_cache.shape[3]

    def scaled(start, width):
        x = lax.dynamic_slice_in_dim(tokens, start, width, 1).astype(jnp.float32)
        gain = lax.dynamic_slice_in_dim(input_norm_gain, start, width, 0).astype(jnp.float32)
        return (x * gain[None, :]).astype(jnp.bfloat16)

    def gather_pool(x):
        same = [x] + [chip_move(x, pool_count, d) for d in range(1, chips)]
        return [b for s in same for b in (s, core_swap(s, pool_count))]

    first = scaled(tp_at * piece, piece)
    first, tokens, input_norm_gain = lax.optimization_barrier((first, tokens, input_norm_gain))
    same_core = [first] + [chip_move(first, pool_count, d) for d in range(1, chips)]
    local_ids = (
        jnp.concatenate(gather_pool(row_adapter_index.reshape(1, rows)), axis=1)
        - pool_at * adapters
    )

    cut = rows * 3 // 8
    chunks = [(0, cut), (cut, rows - cut)]
    own = scaled(pool_at * base, base)
    partner = scaled((pool_at // 2 * 2 + 1 - core) * base, base)
    partner = [
        core_swap(partner[at : at + rows // 2], pool_count) for at in range(0, rows, rows // 2)
    ]
    weights = (query_matrix, key_matrix, value_matrix)
    own_base, *own_sends = project("project_own", [own, *partner], *weights)
    same_core[1:] = [after(x, own_base) for x in same_core[1:]]
    adapter_rows = [b for x in same_core for b in (x, core_swap(x, pool_count))]
    tokens, input_norm_gain = lax.optimization_barrier((tokens, input_norm_gain, own_base))[:2]

    remote = [[] for _ in range(chips)]
    for d in range(1, chips):
        for e in range(2):
            target = (chip + d) % chips * 2 + (core + e) % 2
            x = after(scaled(target * base, base), same_core[-1])
            remote[d].append(chip_move(x, pool_count, d, e))

    down = [x.reshape(adapters * rank, piece) for x in (query_down_maps, value_down_maps)]
    shrunk = pl.pallas_call(
        shrink_kernel,
        in_specs=[VMEM] * (len(adapter_rows) + 1) + [HBM] * 2,
        out_specs=VMEM,
        out_shape=jax.ShapeDtypeStruct((2 * rank, rows * pool_count), jnp.float32),
        scratch_shapes=[
            *[pltpu.VMEM(x.shape, x.dtype) for x in down],
            pltpu.SemaphoreType.DMA((2,)),
        ],
        compiler_params=params(),
        cost_estimate=small_cost(),
        name="shrink",
    )(local_ids, *adapter_rows, *down)
    lows = [shrunk] + [
        lax.ppermute(shrunk, "tp", [(i, (i + d) % tp_count) for i in range(tp_count)])
        for d in range(1, tp_count)
    ]

    values = tokens.astype(jnp.float32)
    scale = lax.rsqrt(jnp.mean(values * values, axis=-1, keepdims=True) + epsilon)
    half_dim = head // 2
    frequency = jnp.power(
        jnp.float32(rope_base), jnp.arange(half_dim, dtype=jnp.float32) * (-2.0 / head)
    )
    angles = cache_length_per_row.astype(jnp.float32)[:, None] * frequency[None, :]
    cosines = jnp.concatenate([jnp.cos(angles)] * 2, axis=1)
    sines = jnp.concatenate([-jnp.sin(angles), jnp.sin(angles)], axis=1)
    lengths = cache_length_per_row.reshape(rows, 1)

    up_q = query_up_maps.reshape(adapters * rank, query_up_maps.shape[2])
    up_v = value_up_maps.reshape(adapters * rank, value_up_maps.shape[2])
    adapter = (local_ids, lows, up_q, up_v)
    own_sums, own_send = add_adapters(own_base, own_sends, adapter)
    swapped = core_swap(own_send, pool_count)
    adapter = (after(local_ids, own_sums), lows, up_q, up_v)
    moved = [[] for _ in chunks]
    both = None
    for c, (at, part) in enumerate(chunks):
        for d in range(1, chips):
            spans = [(2 * d + e) * rows + at for e in range(2)]
            if both is not None:
                remote[d][0] = after(remote[d][0], both)
            keep, *sends = project(
                f"project_{c}_{d}",
                remote[d],
                *weights,
                adapter=adapter,
                spans=spans,
                window=(at, part),
            )
            swaps = [core_swap(x, pool_count) for x in sends]
            if c:
                keep = after(keep, moved[c - 1][-1])
            swaps = jnp.concatenate(swaps, axis=1)
            both = (keep + swaps.astype(jnp.float32)).astype(jnp.bfloat16)
            moved[c].append(chip_move(both, pool_count, -d))
    moved[0][0] = after(moved[0][0], both)

    share = pool_count // tp_count
    order = []
    for d in range(chips):
        for e in range(2):
            p = (chip - d) % chips * 2 + (core + e) % 2
            order.append(
                reversed_bits(jnp.bitwise_xor(p // share, tp_at), tp_count) * share + p % share
            )
    order = jnp.stack(order).astype(jnp.int32)
    gathered, new_keys, new_values = [], [], []
    for c, window in enumerate(chunks):
        attended, new_key, new_value = attend(
            c,
            window,
            own_sums,
            swapped,
            moved[c],
            scale,
            cosines,
            sines,
            lengths,
            rotated_key_cache,
            cached_value_rows,
        )
        if c + 1 < len(chunks):
            attended, *moved[c + 1] = lax.optimization_barrier((attended, *moved[c + 1]))
        if c:
            attended = after(attended, gathered[-1][-2])
        gathered.append(gather_pool(attended))
        new_keys.append(new_key)
        new_values.append(new_value)
    gathered[0][0] = after(gathered[0][0], *new_keys)
    outputs, totals = [], []
    for c, (_, part) in enumerate(chunks):
        if c:
            gathered[c][0] = after(gathered[c][0], keep)
        keep, send = output_part(c, order, gathered[c], output_matrix)
        summed, totals = halving_sum(keep, send, tp_count, totals)
        outputs.append(summed.reshape(-1, part, summed.shape[1]))
    attn_out = jnp.concatenate(outputs, axis=1)
    return (
        attn_out.reshape(-1, attn_out.shape[2]),
        jnp.concatenate(new_keys, axis=0),
        jnp.concatenate(new_values, axis=0),
    )


def solution(mesh):
    return jax.shard_map(
        shards,
        mesh=mesh,
        in_specs=(
            P(("groups", "pool"), None),
            P(),
            P("pool", "tp"),
            P("pool", "tp"),
            P("pool", "tp"),
            P("tp", "pool"),
            P(("groups", "pool"), "tp", None, None),
            P(("groups", "pool"), "tp", None, None),
            P(("groups", "pool")),
            P(("groups", "pool")),
            P("pool", None, "tp"),
            P("pool", None, "tp"),
            P("pool", None, "tp"),
            P("pool", None, "tp"),
        ),
        out_specs=(
            P(("groups", "tp"), "pool"),
            P(("groups", "pool"), "tp"),
            P(("groups", "pool"), "tp"),
        ),
        check_vma=False,
    )
```

time: 188 us -> 184 us (0.979)
  between operations: 14.3 us -> 1.04 us
  Pallas kernels: 37.6 us -> 46.4 us
  starting transfers between devices: 19.9 us -> 21.9 us
    ppermute x0 -> x4, waiting for transfers between devices: none -> 33.9 us  [halving_sum(): got = lax.ppermute(send, 'tp', [(z, z ^ step) for z in range(count)])]
    reduce_scatter x2 -> x0, waiting for transfers between devices: 27.6 us -> none  [shards(): summed = lax.psum_scatter(partial, 'tp', scatter_dimension=0, tiled=True)]
    ppermute x9 -> x8, waiting for transfers between devices: 44.7 us -> 30.5 us  [chip_move(): lax.ppermute(x, 'pool', [(p, (p // 2 + d) % chips * 2 + (p % 2 ^ e)) for...]
    pallas_call x7 -> x9, Pallas kernels: 37.6 us -> 46.4 us  [the longest x3 19.2 us: project(): pl.pallas_call(functools.partial(project_kernel, len(lows), len(blocks),...]
    ppermute x3, waiting for transfers between devices: 0.01 us -> 3.7 us  [shards(): lax.ppermute(shrunk, 'tp', [(i, (i + d) % tp_count) for i in range(tp_cou...]
    ppermute x0 -> x4, starting transfers between devices: none -> 3.63 us  [halving_sum(): got = lax.ppermute(send, 'tp', [(z, z ^ step) for z in range(count)])]
    ppermute x9 -> x8, starting transfers between devices: 12.6 us -> 9.27 us  [chip_move(): lax.ppermute(x, 'pool', [(p, (p // 2 + d) % chips * 2 + (p % 2 ^ e)) for...]
    ppermute x12 -> x17, waiting for transfers between devices: 3.16 us -> 5.69 us  [core_swap(): return lax.ppermute(x, 'pool', [(p, p ^ 1) for p in range(pool_count)])]
  transfers between devices with their start and end apart: 26 -> 32, of which waited for: 10 -> 15; matrix products, arithmetic and copies ran while one was open for 4% -> 6% of each run, Pallas kernels for 15% -> 22%
where the time goes in v3:
time: 184 us
  waiting for transfers between devices  73.8 us (40%)
  Pallas kernels  46.4 us (25%)
  local copies, waits for them, and re-layouts  27.3 us (15%)
  starting transfers between devices  21.9 us (12%)
  other arithmetic  13.1 us (7%)
    ppermute x4, waiting for transfers between devices, halving_sum(): got = lax.ppermute(send, 'tp', [(z, z ^ step) for z in range(count)])  33.9 us
    ppermute x8, waiting for transfers between devices, chip_move(): lax.ppermute(x, 'pool', [(p, (p // 2 + d) % chips * 2 + (p % 2 ^ e)) for...  30.5 us
    unnamed x54, local copies, waits for them, and re-layouts  26.2 us
    pallas_call x3, Pallas kernels, project(): pl.pallas_call(functools.partial(project_kernel, len(lows), len(blocks),...  19.2 us
    pallas_call x2, Pallas kernels, attend(): pl.pallas_call(functools.partial(attend_kernel, len(moved), first, block)...  11.9 us
    ppermute x8, starting transfers between devices, chip_move(): lax.ppermute(x, 'pool', [(p, (p // 2 + d) % chips * 2 + (p % 2 ^ e)) for...  9.27 us
    pallas_call x2, Pallas kernels, output_part(): pl.pallas_call(functools.partial(output_kernel, tile), in_specs=[pl.Block...  9.25 us
    ppermute x17, waiting for transfers between devices, core_swap(): return lax.ppermute(x, 'pool', [(p, p ^ 1) for p in range(pool_count)])  5.69 us
  transfers between devices with their start and end apart: 32, of which 15 were waited for; matrix products, arithmetic and copies ran while one was open for 6% of the time, Pallas kernels for 22%

profile of v3, /device:TPU:0, one launch (start us, length us, event | category | flops | bytes accessed | tf_op | source)
XLA Modules:
  0.0 183.6 jit_solution(3905168375814590066)
XLA Ops:
  0.6 0.7 dynamic-slice_convert_fusion.4
  1.3 1.3 multiply_convert_fusion.4.refs_1_
  2.6 3.0 %collective-permute-start.4 = (bf16[128,2048]{1,0:T(8,128)(2,1)S(1)}, bf16[128,2048]{1,0:T(8,128)(2,1)}, u32[]{:S(2)}, u32[]{:S(2)}) collective-permute-start(bf16[128,2048]{1,0:T(8,128)(2,1)S(1)} %multiply_convert_fusion.4.refs_1_), channel_id=1, source_target_pairs={{0,8},{4,12},{8,0},{12,4},{1,9},{5,13},{9,1},{13,5},{2,10},{6,14},... | collective-permute-start | bytes 1572872 | tf_op jit(solution)/shard_map/ppermute | solution.py:43
  5.7 0.7 dynamic-slice_convert_fusion.2
  6.4 1.4 multiply_convert_fusion.2
  7.8 0.8 fusion.3
  8.6 0.5 collective-permute-start.6
  9.2 1.6 collective-permute-done.5.refs_1_
  11.0 3.4 %copy-done = bf16[2048,2048]{1,0:T(8,128)(2,1)S(1)} copy-done((bf16[2048,2048]{1,0:T(8,128)(2,1)S(1)}, bf16[2048,2048]{1,0:T(8,128)(2,1)}, u32[]{:S(2)}) %copy-start) | copy-done | bytes 8388632
  14.4 7.1 %project_own.1 = (f32[128,2560]{1,0:T(8,128)S(1)}, f32[128,1024]{1,0:T(8,128)S(1)}, f32[128,1024]{1,0:T(8,128)S(1)}, f32[128,512]{1,0:T(8,128)S(1)}) custom-call(bf16[128,2048]{1,0:T(8,128)(2,1)S(1)} %get-tuple-element.92.refs_0_, bf16[64,2048]{1,0:T(8,128)(2,1)S(1)} %collective-permute-done.5.refs_1_, bf16[64,2048]{1,0:T(8,128)(2,1)} %collective-permute-done.6.refs_2_, ...), custom_call_target="tpu_custom_call" | custom-call | flops 1000 | bytes 1000 | tf_op jit(solution)/shard_map/project_own/pallas_call | solution.py:170
  21.5 1.1 copy-done.13
  22.6 0.8 copy-done.16
  23.4 0.8 copy-done.18
  24.2 0.7 copy-done.20
  25.3 1.2 multiply_convert_fusion
  26.6 1.4 collective-permute-start.13
  28.0 0.6 collective-permute-start.1
  28.6 23.3 %collective-permute-done.1 = s32[1,128]{1,0:T(1,128)S(1)} collective-permute-done((s32[1,128]{1,0:T(1,128)S(1)}, s32[1,128]{1,0:T(1,128)S(1)}, u32[]{:S(2)}, u32[]{:S(2)}) %collective-permute-start.1) | collective-permute-done | bytes 544 | tf_op jit(solution)/shard_map/ppermute | solution.py:43
  51.9 1.1 collective-permute-done
  53.3 0.9 collective-permute-done.2
  54.2 1.6 copy-done.11
  55.8 1.6 copy-done.12
  57.4 4.2 %shrink.1.refs_1_ = f32[32,512]{1,0:T(8,128)S(1)} custom-call(s32[1,512]{1,0:T(1,128)S(1)} %add_subtract_fusion.refs_0_, bf16[128,2048]{1,0:T(8,128)(2,1)S(1)} %multiply_convert_fusion.4.refs_1_, bf16[128,2048]{1,0:T(8,128)(2,1)} %collective-permute-done.3.refs_2_, bf16[128,2048]{1,0:T(8,128)(2,1)} %collective-permute-done.4.refs_3_, ...), custom_call_target="tpu_custom_call" | custom-call | flops 1000 | bytes 1000 | tf_op jit(solution)/shard_map/shrink/pallas_call | solution.py:507
  61.7 1.6 collective-permute-start.8
  63.3 2.6 %collective-permute-start.9 = (f32[32,512]{1,0:T(8,128)S(1)}, f32[32,512]{1,0:T(8,128)S(1)}, u32[]{:S(2)}, u32[]{:S(2)}) collective-permute-start(f32[32,512]{1,0:T(8,128)S(1)} %shrink.1.refs_1_), channel_id=1, source_target_pairs={{0,2},{1,3},{2,0},{3,1},{4,6},{5,7},{6,4},{7,5},{8,10},{9,11},{10,... | collective-permute-start | bytes 196616 | tf_op jit(solution)/shard_map/ppermute | solution.py:521
  65.9 1.3 collective-permute-start.10
  67.2 0.7 collective-permute-done.8.refs_2_
  68.0 2.7 %collective-permute-done.9.refs_3_ = f32[32,512]{1,0:T(8,128)S(1)} collective-permute-done((f32[32,512]{1,0:T(8,128)S(1)}, f32[32,512]{1,0:T(8,128)S(1)}, u32[]{:S(2)}, u32[]{:S(2)}) %collective-permute-start.9) | collective-permute-done | bytes 65568 | tf_op jit(solution)/shard_map/ppermute | solution.py:521
  71.0 1.8 %add_adapters.1 = (f32[128,2560]{1,0:T(8,128)S(1)}, bf16[128,2560]{1,0:T(8,128)(2,1)S(1)}) custom-call(s32[1,512]{1,0:T(1,128)S(1)} %add_subtract_fusion.refs_0_, f32[32,512]{1,0:T(8,128)S(1)} %shrink.1.refs_1_, f32[32,512]{1,0:T(8,128)S(1)} %collective-permute-done.8.refs_2_, f32[32,512]{1,0:T(8,128)S(1)} %collective-permute-done.9.refs_3_, ...), custom_call_target="tpu_custom_call" | custom-call | flops 1000 | bytes 1000 | tf_op jit(solution)/shard_map/add_adapters/pallas_call | solution.py:235
  72.8 0.8 copy-done.22
  73.7 3.4 %copy-done.1 = bf16[2048,2048]{1,0:T(8,128)(2,1)S(1)} copy-done((bf16[2048,2048]{1,0:T(8,128)(2,1)S(1)}, bf16[2048,2048]{1,0:T(8,128)(2,1)}, u32[]{:S(2)}) %copy-start.1) | copy-done | bytes 8388632
  77.0 5.8 %project_0_1.1 = (f32[48,2560]{1,0:T(8,128)S(1)}, bf16[48,1024]{1,0:T(8,128)(2,1)S(1)}, bf16[48,1024]{1,0:T(8,128)(2,1)S(1)}, bf16[48,512]{1,0:T(8,128)(2,1)S(1)}) custom-call(s32[1,512]{1,0:T(1,128)S(1)} %add_subtract_fusion.refs_0_, f32[32,512]{1,0:T(8,128)S(1)} %shrink.1.refs_1_, f32[32,512]{1,0:T(8,128)S(1)} %collective-permute-done.8.refs_2_, ...), custom_call_target="tpu_custom_call" | custom-call | flops 1000 | bytes 1000 | tf_op jit(solution)/shard_map/project_0_1/pallas_call | solution.py:170
  82.9 0.5 collective-permute-start.15
  83.5 0.6 collective-permute-done.16
  84.7 0.7 add_convert_fusion.1
  85.4 0.5 collective-permute-start.17
  85.9 6.3 %project_1_1.1 = (f32[80,2560]{1,0:T(8,128)S(1)}, bf16[80,1024]{1,0:T(8,128)(2,1)}, bf16[80,1024]{1,0:T(8,128)(2,1)}, bf16[80,512]{1,0:T(8,128)(2,1)S(1)}) custom-call(s32[1,512]{1,0:T(1,128)S(1)} %add_subtract_fusion.refs_0_, f32[32,512]{1,0:T(8,128)S(1)} %shrink.1.refs_1_, f32[32,512]{1,0:T(8,128)S(1)} %collective-permute-done.8.refs_2_, ...), custom_call_target="tpu_custom_call" | custom-call | flops 1000 | bytes 1000 | tf_op jit(solution)/shard_map/project_1_1/pallas_call | solution.py:170
  92.3 0.9 copy-done.15
  93.2 0.5 collective-permute-start.18
  94.3 0.6 collective-permute-start.11
  94.9 0.6 collective-permute-done.20
  95.5 2.0 %add_convert_fusion = bf16[80,2560]{1,0:T(8,128)(2,1)} fusion(f32[80,2560]{1,0:T(8,128)} %copy-done.15, bf16[80,512]{1,0:T(8,128)(2,1)S(1)} %collective-permute-done.20, bf16[80,1024]{1,0:T(8,128)(2,1)S(1)} %collective-permute-done.19, bf16[80,1024]{1,0:T(8,128)(2,1)S(1)} %collective-permute-done.18), kind=kLoop, calls=%fused_computation.7 | loop fusion | flops 1638400 | bytes 1638400 | tf_op jit(solution)/shard_map/convert_element_type | solution.py:561
  97.4 1.5 collective-permute-start.21
  99.0 2.1 %multiply_reduce_fusion = f32[128]{0:T(128)S(1)} fusion(bf16[128,8192]{1,0:T(8,128)(2,1)} %param.14), kind=kLoop, calls=%fused_computation | loop fusion | flops 3145600 | bytes 2097664 | tf_op jit(solution)/shard_map/reduce_sum | solution.py:526
  101.2 2.2 %copy-done.5 = bf16[128,2,64,128]{3,2,1,0:T(8,128)(2,1)S(1)} copy-done((bf16[128,2,64,128]{3,2,1,0:T(8,128)(2,1)S(1)}, bf16[128,2,64,128]{3,2,1,0:T(8,128)(2,1)}, u32[]{:S(2)}) %copy-start.5) | copy-done | bytes 4194328
  103.4 2.2 %copy-done.7 = bf16[128,2,64,128]{3,2,1,0:T(8,128)(2,1)S(1)} copy-done((bf16[128,2,64,128]{3,2,1,0:T(8,128)(2,1)S(1)}, bf16[128,2,64,128]{3,2,1,0:T(8,128)(2,1)}, u32[]{:S(2)}) %copy-start.7) | copy-done | bytes 4194328
  105.6 5.1 %attend_0.1 = (bf16[48,2048]{1,0:T(8,128)(2,1)S(1)}, bf16[48,256]{1,0:T(8,128)(2,1)S(1)}, bf16[48,256]{1,0:T(8,128)(2,1)S(1)}) custom-call(f32[128,2560]{1,0:T(8,128)S(1)} %get-tuple-element.54.refs_0_, bf16[128,2560]{1,0:T(8,128)(2,1)S(1)} %collective-permute-done.11.refs_1_, bf16[48,2560]{1,0:T(8,128)(2,1)} %collective-permute-done.17.refs_2_, ...), custom_call_target="tpu_custom_call" | custom-call | flops 1000 | bytes 1000 | tf_op jit(solution)/shard_map/attend_0/pallas_call | solution.py:358
  110.7 0.6 collective-permute-start.23
  111.3 6.8 %attend_1.1 = (bf16[80,2048]{1,0:T(8,128)(2,1)S(1)}, bf16[80,256]{1,0:T(8,128)(2,1)S(1)}, bf16[80,256]{1,0:T(8,128)(2,1)S(1)}) custom-call(f32[128,2560]{1,0:T(8,128)S(1)} %get-tuple-element.54.refs_0_, bf16[128,2560]{1,0:T(8,128)(2,1)S(1)} %collective-permute-done.11.refs_1_, bf16[80,2560]{1,0:T(8,128)(2,1)S(1)} %collective-permute-done.21.refs_2_, ...), custom_call_target="tpu_custom_call" | custom-call | flops 1000 | bytes 1000 | tf_op jit(solution)/shard_map/attend_1/pallas_call | solution.py:358
  118.1 1.6 collective-permute-start.28
  119.7 0.5 collective-permute-start.24
  120.2 7.2 %collective-permute-done.28.refs_3_ = bf16[80,2048]{1,0:T(8,128)(2,1)S(1)} collective-permute-done((bf16[80,2048]{1,0:T(8,128)(2,1)S(1)}, bf16[80,2048]{1,0:T(8,128)(2,1)S(1)}, u32[]{:S(2)}, u32[]{:S(2)}) %collective-permute-start.28) | collective-permute-done | bytes 327712 | tf_op jit(solution)/shard_map/ppermute | solution.py:43
  127.5 3.4 %copy-done.2 = bf16[2048,2048]{1,0:T(8,128)(2,1)S(1)} copy-done((bf16[2048,2048]{1,0:T(8,128)(2,1)S(1)}, bf16[2048,2048]{1,0:T(8,128)(2,1)}, u32[]{:S(2)}) %copy-start.2) | copy-done | bytes 8388632
  130.8 4.1 %output_0.1 = (bf16[96,2048]{1,0:T(8,128)(2,1)S(1)}, bf16[96,2048]{1,0:T(8,128)(2,1)S(1)}) custom-call(s32[4]{0:T(128)S(1)} %pad_add_fusion.refs_0_, bf16[48,2048]{1,0:T(8,128)(2,1)S(1)} %get-tuple-element.77.refs_1_, bf16[48,2048]{1,0:T(8,128)(2,1)S(1)} %collective-permute-done.22.refs_2_, bf16[48,2048]{1,0:T(8,128)(2,1)S(1)} %collective-permute-done.23.refs_3_, ...), custom_call_target="tpu_custom_call" | custom-call | flops 1000 | bytes 1000 | tf_op jit(solution)/shard_map/output_0/pallas_call | solution.py:402
  134.9 1.7 collective-permute-start.25
  136.7 3.4 %copy-done.3 = bf16[2048,2048]{1,0:T(8,128)(2,1)S(1)} copy-done((bf16[2048,2048]{1,0:T(8,128)(2,1)S(1)}, bf16[2048,2048]{1,0:T(8,128)(2,1)}, u32[]{:S(2)}) %copy-start.3) | copy-done | bytes 8388632
  140.0 5.2 %output_1.1 = (bf16[160,2048]{1,0:T(8,128)(2,1)S(1)}, bf16[160,2048]{1,0:T(8,128)(2,1)S(1)}) custom-call(s32[4]{0:T(128)S(1)} %pad_add_fusion.refs_0_, bf16[80,2048]{1,0:T(8,128)(2,1)S(1)} %get-tuple-element.82.refs_1_, bf16[80,2048]{1,0:T(8,128)(2,1)S(1)} %collective-permute-done.27.refs_2_, bf16[80,2048]{1,0:T(8,128)(2,1)S(1)} %collective-permute-done.28.refs_3_, ...), custom_call_target="tpu_custom_call" | custom-call | flops 1000 | bytes 1000 | tf_op jit(solution)/shard_map/output_1/pallas_call | solution.py:402
  145.2 0.5 collective-permute-start.30
  145.7 0.6 pad_maximum_fusion.2
  146.3 0.6 pad_maximum_fusion.3
  147.1 1.4 collective-permute-start.26
  148.5 17.9 %collective-permute-done.30 = bf16[160,2048]{1,0:T(8,128)(2,1)S(1)} collective-permute-done((bf16[160,2048]{1,0:T(8,128)(2,1)S(1)}, bf16[160,2048]{1,0:T(8,128)(2,1)S(1)}, u32[]{:S(2)}, u32[]{:S(2)}) %collective-permute-start.30) | collective-permute-done | bytes 655392 | tf_op jit(solution)/shard_map/ppermute | solution.py:429
  166.7 16.0 %collective-permute-done.31 = bf16[80,2048]{1,0:T(8,128)(2,1)S(1)} collective-permute-done((bf16[80,2048]{1,0:T(8,128)(2,1)S(1)}, bf16[80,2048]{1,0:T(8,128)(2,1)S(1)}, u32[]{:S(2)}, u32[]{:S(2)}) %collective-permute-start.31) | collective-permute-done | bytes 327712 | tf_op jit(solution)/shard_map/ppermute | solution.py:429
  182.8 0.8 maximum_bitcast_fusion
  (91 shorter events, 3.4 us)
Async XLA Ops:
  1.3 9.7 %copy-start.8 = (bf16[2048,256]{1,0:T(8,128)(2,1)S(1)}, bf16[2048,256]{1,0:T(8,128)(2,1)}, u32[]{:S(2)}) copy-start(bf16[2048,256]{1,0:T(8,128)(2,1)} %refs_8_.5) | copy-start | bytes 3145732
  1.3 9.7 %copy-start.9 = (bf16[2048,256]{1,0:T(8,128)(2,1)S(1)}, bf16[2048,256]{1,0:T(8,128)(2,1)}, u32[]{:S(2)}) copy-start(bf16[2048,256]{1,0:T(8,128)(2,1)} %refs_9_.3) | copy-start | bytes 3145732
  2.6 22.2 %collective-permute-start.4 = (bf16[128,2048]{1,0:T(8,128)(2,1)S(1)}, bf16[128,2048]{1,0:T(8,128)(2,1)}, u32[]{:S(2)}, u32[]{:S(2)}) collective-permute-start(bf16[128,2048]{1,0:T(8,128)(2,1)S(1)} %multiply_convert_fusion.4.refs_1_), channel_id=1, source_target_pairs={{0,8},{4,12},{8,0},{12,4},{1,9},{5,13},{9,1},{13,5},{2,10},{6,14},... | collective-permute-start | bytes 1572872 | tf_op jit(solution)/shard_map/ppermute | solution.py:43
  8.6 2.1 %collective-permute-start.5 = (bf16[64,2048]{1,0:T(8,128)(2,1)}, bf16[64,2048]{1,0:T(8,128)(2,1)S(1)}, u32[]{:S(2)}, u32[]{:S(2)}) collective-permute-start(bf16[64,2048]{1,0:T(8,128)(2,1)} %get-tuple-element.94), channel_id=1, source_target_pairs={{0,4},{4,0},{8,12},{12,8},{1,5},{5,1},{9,13},{13,9},{2,6},{6,2},{1... | collective-permute-start | bytes 786440 | tf_op jit(solution)/shard_map/ppermute | solution.py:38
  8.6 2.4 %collective-permute-start.6 = (bf16[64,2048]{1,0:T(8,128)(2,1)}, bf16[64,2048]{1,0:T(8,128)(2,1)}, u32[]{:S(2)}, u32[]{:S(2)}) collective-permute-start(bf16[64,2048]{1,0:T(8,128)(2,1)} %get-tuple-element.93), channel_id=1, source_target_pairs={{0,4},{4,0},{8,12},{12,8},{1,5},{5,1},{9,13},{13,9},{2,6},{6,2},{1... | collective-permute-start | bytes 786440 | tf_op jit(solution)/shard_map/ppermute | solution.py:38
  9.1 45.0 %collective-permute-start.3 = (bf16[128,2048]{1,0:T(8,128)(2,1)S(1)}, bf16[128,2048]{1,0:T(8,128)(2,1)}, u32[]{:S(2)}, u32[]{:S(2)}) collective-permute-start(bf16[128,2048]{1,0:T(8,128)(2,1)S(1)} %multiply_convert_fusion.4.refs_1_), channel_id=1, source_target_pairs={{0,4},{4,0},{8,12},{12,8},{1,5},{5,1},{9,13},{13,9},{2,6},{6,2},{1... | collective-permute-start | bytes 1572872 | tf_op jit(solution)/shard_map/ppermute | solution.py:38
  11.0 3.4 %copy-start = (bf16[2048,2048]{1,0:T(8,128)(2,1)S(1)}, bf16[2048,2048]{1,0:T(8,128)(2,1)}, u32[]{:S(2)}) copy-start(bf16[2048,2048]{1,0:T(8,128)(2,1)} %refs_7_.5) | copy-start | bytes 25165828
  14.4 10.5 %copy-start.24 = (bf16[8192]{0:T(1024)(128)(2,1)S(1)}, bf16[8192]{0:T(1024)(128)(2,1)}, u32[]{:S(2)}) copy-start(bf16[8192]{0:T(1024)(128)(2,1)} %param.15) | copy-start | bytes 49156
  14.4 10.9 %copy-start.23 = (bf16[128,8192]{1,0:T(8,128)(2,1)S(1)}, bf16[128,8192]{1,0:T(8,128)(2,1)}, u32[]{:S(2)}) copy-start(bf16[128,8192]{1,0:T(8,128)(2,1)} %param.14) | copy-start | bytes 6291460
  21.5 1.1 copy-start.13
  22.6 0.8 copy-start.16
  23.4 0.8 copy-start.18
  24.2 0.7 copy-start.20
  24.9 3.2 %copy-start.26 = (s32[128]{0:T(128)S(1)}, s32[128]{0:T(128)}, u32[]{:S(2)}) copy-start(s32[128]{0:T(128)} %param.23) | copy-start | bytes 1540
  24.9 29.3 %collective-permute-start.7 = (bf16[128,2048]{1,0:T(8,128)(2,1)}, bf16[128,2048]{1,0:T(8,128)(2,1)S(1)}, u32[]{:S(2)}, u32[]{:S(2)}) collective-permute-start(bf16[128,2048]{1,0:T(8,128)(2,1)} %collective-permute-done.4.refs_3_), channel_id=1, source_target_pairs={{0,4},{4,0},{8,12},{12,8},{1,5},{5,1},{9,13},{13,9},{2,6},{6,2},{1... | collective-permute-start | bytes 1572872 | tf_op jit(solution)/shard_map/ppermute | solution.py:38
  26.6 46.3 %collective-permute-start.12 = (bf16[128,2048]{1,0:T(8,128)(2,1)}, bf16[128,2048]{1,0:T(8,128)(2,1)}, u32[]{:S(2)}, u32[]{:S(2)}) collective-permute-start(bf16[128,2048]{1,0:T(8,128)(2,1)} %get-tuple-element.59), channel_id=1, source_target_pairs={{0,8},{4,12},{8,0},{12,4},{1,9},{5,13},{9,1},{13,5},{2,10},{6,14},... | collective-permute-start | bytes 1572872 | tf_op jit(solution)/shard_map/ppermute | solution.py:43
  26.6 47.0 %collective-permute-start.13 = (bf16[128,2048]{1,0:T(8,128)(2,1)}, bf16[128,2048]{1,0:T(8,128)(2,1)}, u32[]{:S(2)}, u32[]{:S(2)}) collective-permute-start(bf16[128,2048]{1,0:T(8,128)(2,1)} %get-tuple-element.60), channel_id=1, source_target_pairs={{0,12},{4,8},{8,4},{12,0},{1,13},{5,9},{9,5},{13,1},{2,14},{6,10},... | collective-permute-start | bytes 1572872 | tf_op jit(solution)/shard_map/ppermute | solution.py:43
  28.0 23.9 %collective-permute-start.1 = (s32[1,128]{1,0:T(1,128)S(1)}, s32[1,128]{1,0:T(1,128)S(1)}, u32[]{:S(2)}, u32[]{:S(2)}) collective-permute-start(s32[1,128]{1,0:T(1,128)S(1)} %bitcast.29), channel_id=1, source_target_pairs={{0,8},{4,12},{8,0},{12,4},{1,9},{5,13},{9,1},{13,5},{2,10},{6,14},... | collective-permute-start | bytes 1544 | tf_op jit(solution)/shard_map/ppermute | solution.py:43
  51.9 1.1 collective-permute-start
  53.1 1.1 collective-permute-start.2
  54.2 1.6 copy-start.11
  55.8 1.6 copy-start.12
  57.4 13.5 %copy-start.4 = (bf16[32,16,2048]{2,1,0:T(8,128)(2,1)S(1)}, bf16[32,16,2048]{2,1,0:T(8,128)(2,1)}, u32[]{:S(2)}) copy-start(bf16[32,16,2048]{2,1,0:T(8,128)(2,1)} %param.25) | copy-start | bytes 6291460
  57.4 13.5 %copy-start.10 = (bf16[32,16,256]{2,1,0:T(8,128)(2,1)S(1)}, bf16[32,16,256]{2,1,0:T(8,128)(2,1)}, u32[]{:S(2)}) copy-start(bf16[32,16,256]{2,1,0:T(8,128)(2,1)} %param.27) | copy-start | bytes 786436
  57.4 13.5 %copy-start.14 = (f32[128,2560]{1,0:T(8,128)S(1)}, f32[128,2560]{1,0:T(8,128)}, u32[]{:S(2)}) copy-start(f32[128,2560]{1,0:T(8,128)} %copy-done.13) | copy-start | bytes 3932164
  57.4 13.5 %copy-start.17 = (f32[128,1024]{1,0:T(8,128)S(1)}, f32[128,1024]{1,0:T(8,128)}, u32[]{:S(2)}) copy-start(f32[128,1024]{1,0:T(8,128)} %copy-done.16) | copy-start | bytes 1572868
  57.4 13.5 %copy-start.19 = (f32[128,1024]{1,0:T(8,128)S(1)}, f32[128,1024]{1,0:T(8,128)}, u32[]{:S(2)}) copy-start(f32[128,1024]{1,0:T(8,128)} %copy-done.18) | copy-start | bytes 1572868
  57.4 13.5 %copy-start.21 = (f32[128,512]{1,0:T(8,128)S(1)}, f32[128,512]{1,0:T(8,128)}, u32[]{:S(2)}) copy-start(f32[128,512]{1,0:T(8,128)} %copy-done.20) | copy-start | bytes 786436
  61.7 6.3 %collective-permute-start.8 = (f32[32,512]{1,0:T(8,128)S(1)}, f32[32,512]{1,0:T(8,128)S(1)}, u32[]{:S(2)}, u32[]{:S(2)}) collective-permute-start(f32[32,512]{1,0:T(8,128)S(1)} %shrink.1.refs_1_), channel_id=1, source_target_pairs={{0,1},{1,2},{2,3},{3,0},{4,5},{5,6},{6,7},{7,4},{8,9},{9,10},{10,1... | collective-permute-start | bytes 196616 | tf_op jit(solution)/shard_map/ppermute | solution.py:521
  63.3 7.4 %collective-permute-start.9 = (f32[32,512]{1,0:T(8,128)S(1)}, f32[32,512]{1,0:T(8,128)S(1)}, u32[]{:S(2)}, u32[]{:S(2)}) collective-permute-start(f32[32,512]{1,0:T(8,128)S(1)} %shrink.1.refs_1_), channel_id=1, source_target_pairs={{0,2},{1,3},{2,0},{3,1},{4,6},{5,7},{6,4},{7,5},{8,10},{9,11},{10,... | collective-permute-start | bytes 196616 | tf_op jit(solution)/shard_map/ppermute | solution.py:521
  65.9 5.0 %collective-permute-start.10 = (f32[32,512]{1,0:T(8,128)S(1)}, f32[32,512]{1,0:T(8,128)S(1)}, u32[]{:S(2)}, u32[]{:S(2)}) collective-permute-start(f32[32,512]{1,0:T(8,128)S(1)} %shrink.1.refs_1_), channel_id=1, source_target_pairs={{0,3},{1,0},{2,1},{3,2},{4,7},{5,4},{6,5},{7,6},{8,11},{9,8},{10,9... | collective-permute-start | bytes 196616 | tf_op jit(solution)/shard_map/ppermute | solution.py:521
  72.8 0.8 copy-start.22
  72.8 10.7 %copy-start.25 = (s32[128]{0:T(128)S(1)}, s32[128]{0:T(128)}, u32[]{:S(2)}) copy-start(s32[128]{0:T(128)} %param.22) | copy-start | bytes 1540
  73.6 3.4 %copy-start.1 = (bf16[2048,2048]{1,0:T(8,128)(2,1)S(1)}, bf16[2048,2048]{1,0:T(8,128)(2,1)}, u32[]{:S(2)}) copy-start(bf16[2048,2048]{1,0:T(8,128)(2,1)} %refs_7_.5) | copy-start | bytes 25165828
  82.8 1.3 collective-permute-start.16
  82.9 1.4 collective-permute-start.15
  83.4 1.3 collective-permute-start.14
  85.4 9.4 %collective-permute-start.17 = (bf16[48,2560]{1,0:T(8,128)(2,1)}, bf16[48,2560]{1,0:T(8,128)(2,1)}, u32[]{:S(2)}, u32[]{:S(2)}) collective-permute-start(bf16[48,2560]{1,0:T(8,128)(2,1)} %add_convert_fusion.1), channel_id=1, source_target_pairs={{0,8},{4,12},{8,0},{12,4},{1,9},{5,13},{9,1},{13,5},{2,10},{6,14},... | collective-permute-start | bytes 737288 | tf_op jit(solution)/shard_map/ppermute | solution.py:43
  92.2 0.9 copy-start.15
  93.2 2.3 %collective-permute-start.19 = (bf16[80,1024]{1,0:T(8,128)(2,1)}, bf16[80,1024]{1,0:T(8,128)(2,1)S(1)}, u32[]{:S(2)}, u32[]{:S(2)}) collective-permute-start(bf16[80,1024]{1,0:T(8,128)(2,1)} %get-tuple-element.69), channel_id=1, source_target_pairs={{0,4},{4,0},{8,12},{12,8},{1,5},{5,1},{9,13},{13,9},{2,6},{6,2},{1... | collective-permute-start | bytes 491528 | tf_op jit(solution)/shard_map/ppermute | solution.py:38
  93.2 2.3 %collective-permute-start.18 = (bf16[80,1024]{1,0:T(8,128)(2,1)}, bf16[80,1024]{1,0:T(8,128)(2,1)S(1)}, u32[]{:S(2)}, u32[]{:S(2)}) collective-permute-start(bf16[80,1024]{1,0:T(8,128)(2,1)} %get-tuple-element.68), channel_id=1, source_target_pairs={{0,4},{4,0},{8,12},{12,8},{1,5},{5,1},{9,13},{13,9},{2,6},{6,2},{1... | collective-permute-start | bytes 491528 | tf_op jit(solution)/shard_map/ppermute | solution.py:38
  94.1 1.3 collective-permute-start.20
  94.3 6.9 %collective-permute-start.11 = (bf16[128,2560]{1,0:T(8,128)(2,1)}, bf16[128,2560]{1,0:T(8,128)(2,1)S(1)}, u32[]{:S(2)}, u32[]{:S(2)}) collective-permute-start(bf16[128,2560]{1,0:T(8,128)(2,1)} %copy-done.22), channel_id=1, source_target_pairs={{0,4},{4,0},{8,12},{12,8},{1,5},{5,1},{9,13},{13,9},{2,6},{6,2},{1... | collective-permute-start | bytes 1966088 | tf_op jit(solution)/shard_map/ppermute | solution.py:38
  97.4 13.3 %collective-permute-start.21 = (bf16[80,2560]{1,0:T(8,128)(2,1)}, bf16[80,2560]{1,0:T(8,128)(2,1)S(1)}, u32[]{:S(2)}, u32[]{:S(2)}) collective-permute-start(bf16[80,2560]{1,0:T(8,128)(2,1)} %add_convert_fusion), channel_id=1, source_target_pairs={{0,8},{4,12},{8,0},{12,4},{1,9},{5,13},{9,1},{13,5},{2,10},{6,14},... | collective-permute-start | bytes 1228808 | tf_op jit(solution)/shard_map/ppermute | solution.py:43
  101.2 2.2 %copy-start.5 = (bf16[128,2,64,128]{3,2,1,0:T(8,128)(2,1)S(1)}, bf16[128,2,64,128]{3,2,1,0:T(8,128)(2,1)}, u32[]{:S(2)}) copy-start(bf16[128,2,64,128]{3,2,1,0:T(8,128)(2,1)} %refs_7_.7) | copy-start | bytes 12582916
  103.4 2.2 %copy-start.7 = (bf16[128,2,64,128]{3,2,1,0:T(8,128)(2,1)S(1)}, bf16[128,2,64,128]{3,2,1,0:T(8,128)(2,1)}, u32[]{:S(2)}) copy-start(bf16[128,2,64,128]{3,2,1,0:T(8,128)(2,1)} %refs_8_.7) | copy-start | bytes 12582916
  105.6 5.7 %copy-start.6 = (bf16[128,2,64,128]{3,2,1,0:T(8,128)(2,1)S(1)}, bf16[128,2,64,128]{3,2,1,0:T(8,128)(2,1)}, u32[]{:S(2)}) copy-start(bf16[128,2,64,128]{3,2,1,0:T(8,128)(2,1)} %refs_7_.7) | copy-start | bytes 12582916
  110.7 7.4 %collective-permute-start.23 = (bf16[48,2048]{1,0:T(8,128)(2,1)S(1)}, bf16[48,2048]{1,0:T(8,128)(2,1)S(1)}, u32[]{:S(2)}, u32[]{:S(2)}) collective-permute-start(bf16[48,2048]{1,0:T(8,128)(2,1)S(1)} %get-tuple-element.77.refs_1_), channel_id=1, source_target_pairs={{0,8},{4,12},{8,0},{12,4},{1,9},{5,13},{9,1},{13,5},{2,10},{6,14},... | collective-permute-start | bytes 589832 | tf_op jit(solution)/shard_map/ppermute | solution.py:43
  118.1 9.3 %collective-permute-start.28 = (bf16[80,2048]{1,0:T(8,128)(2,1)S(1)}, bf16[80,2048]{1,0:T(8,128)(2,1)S(1)}, u32[]{:S(2)}, u32[]{:S(2)}) collective-permute-start(bf16[80,2048]{1,0:T(8,128)(2,1)S(1)} %get-tuple-element.82.refs_1_), channel_id=1, source_target_pairs={{0,8},{4,12},{8,0},{12,4},{1,9},{5,13},{9,1},{13,5},{2,10},{6,14},... | collective-permute-start | bytes 983048 | tf_op jit(solution)/shard_map/ppermute | solution.py:43
  119.7 7.8 %collective-permute-start.22 = (bf16[48,2048]{1,0:T(8,128)(2,1)S(1)}, bf16[48,2048]{1,0:T(8,128)(2,1)S(1)}, u32[]{:S(2)}, u32[]{:S(2)}) collective-permute-start(bf16[48,2048]{1,0:T(8,128)(2,1)S(1)} %get-tuple-element.77.refs_1_), channel_id=1, source_target_pairs={{0,4},{4,0},{8,12},{12,8},{1,5},{5,1},{9,13},{13,9},{2,6},{6,2},{1... | collective-permute-start | bytes 589832 | tf_op jit(solution)/shard_map/ppermute | solution.py:38
  119.7 7.8 %collective-permute-start.24 = (bf16[48,2048]{1,0:T(8,128)(2,1)S(1)}, bf16[48,2048]{1,0:T(8,128)(2,1)S(1)}, u32[]{:S(2)}, u32[]{:S(2)}) collective-permute-start(bf16[48,2048]{1,0:T(8,128)(2,1)S(1)} %collective-permute-done.23.refs_3_), channel_id=1, source_target_pairs={{0,4},{4,0},{8,12},{12,8},{1,5},{5,1},{9,13},{13,9},{2,6},{6,2},{1... | collective-permute-start | bytes 589832 | tf_op jit(solution)/shard_map/ppermute | solution.py:38
  120.2 16.5 %collective-permute-start.27 = (bf16[80,2048]{1,0:T(8,128)(2,1)S(1)}, bf16[80,2048]{1,0:T(8,128)(2,1)S(1)}, u32[]{:S(2)}, u32[]{:S(2)}) collective-permute-start(bf16[80,2048]{1,0:T(8,128)(2,1)S(1)} %get-tuple-element.82.refs_1_), channel_id=1, source_target_pairs={{0,4},{4,0},{8,12},{12,8},{1,5},{5,1},{9,13},{13,9},{2,6},{6,2},{1... | collective-permute-start | bytes 983048 | tf_op jit(solution)/shard_map/ppermute | solution.py:38
  127.4 9.3 %collective-permute-start.29 = (bf16[80,2048]{1,0:T(8,128)(2,1)S(1)}, bf16[80,2048]{1,0:T(8,128)(2,1)S(1)}, u32[]{:S(2)}, u32[]{:S(2)}) collective-permute-start(bf16[80,2048]{1,0:T(8,128)(2,1)S(1)} %collective-permute-done.28.refs_3_), channel_id=1, source_target_pairs={{0,4},{4,0},{8,12},{12,8},{1,5},{5,1},{9,13},{13,9},{2,6},{6,2},{1... | collective-permute-start | bytes 983048 | tf_op jit(solution)/shard_map/ppermute | solution.py:38
  127.5 3.4 %copy-start.2 = (bf16[2048,2048]{1,0:T(8,128)(2,1)S(1)}, bf16[2048,2048]{1,0:T(8,128)(2,1)}, u32[]{:S(2)}) copy-start(bf16[2048,2048]{1,0:T(8,128)(2,1)} %refs_5_.5) | copy-start | bytes 25165828
  134.9 12.0 %collective-permute-start.25 = (bf16[96,2048]{1,0:T(8,128)(2,1)S(1)}, bf16[96,2048]{1,0:T(8,128)(2,1)S(1)}, u32[]{:S(2)}, u32[]{:S(2)}) collective-permute-start(bf16[96,2048]{1,0:T(8,128)(2,1)S(1)} %get-tuple-element.79), channel_id=1, source_target_pairs={{0,1},{1,0},{2,3},{3,2},{4,5},{5,4},{6,7},{7,6},{8,9},{9,8},{10,11... | collective-permute-start | bytes 1179656 | tf_op jit(solution)/shard_map/ppermute | solution.py:429
  136.7 3.4 %copy-start.3 = (bf16[2048,2048]{1,0:T(8,128)(2,1)S(1)}, bf16[2048,2048]{1,0:T(8,128)(2,1)}, u32[]{:S(2)}) copy-start(bf16[2048,2048]{1,0:T(8,128)(2,1)} %refs_5_.5) | copy-start | bytes 25165828
  145.2 21.1 %collective-permute-start.30 = (bf16[160,2048]{1,0:T(8,128)(2,1)S(1)}, bf16[160,2048]{1,0:T(8,128)(2,1)S(1)}, u32[]{:S(2)}, u32[]{:S(2)}) collective-permute-start(bf16[160,2048]{1,0:T(8,128)(2,1)S(1)} %get-tuple-element.84), channel_id=1, source_target_pairs={{0,1},{1,0},{2,3},{3,2},{4,5},{5,4},{6,7},{7,6},{8,9},{9,8},{10,11... | collective-permute-start | bytes 1966088 | tf_op jit(solution)/shard_map/ppermute | solution.py:429
  147.1 19.6 %collective-permute-start.26 = (bf16[48,2048]{1,0:T(8,128)(2,1)S(1)}, bf16[48,2048]{1,0:T(8,128)(2,1)S(1)}, u32[]{:S(2)}, u32[]{:S(2)}) collective-permute-start(bf16[48,2048]{1,0:T(8,128)(2,1)S(1)} %slice.41), channel_id=1, source_target_pairs={{0,2},{1,3},{2,0},{3,1},{4,6},{5,7},{6,4},{7,5},{8,10},{9,11},{10,... | collective-permute-start | bytes 589832 | tf_op jit(solution)/shard_map/ppermute | solution.py:429
  166.6 16.1 %collective-permute-start.31 = (bf16[80,2048]{1,0:T(8,128)(2,1)S(1)}, bf16[80,2048]{1,0:T(8,128)(2,1)S(1)}, u32[]{:S(2)}, u32[]{:S(2)}) collective-permute-start(bf16[80,2048]{1,0:T(8,128)(2,1)S(1)} %slice.40), channel_id=1, source_target_pairs={{0,2},{1,3},{2,0},{3,1},{4,6},{5,7},{6,4},{7,5},{8,10},{9,11},{10,... | collective-permute-start | bytes 983048 | tf_op jit(solution)/shard_map/ppermute | solution.py:429

commit v4 on v3

v4 whole, which is shorter than its diff:
```python
import functools
import math

import jax
import jax.numpy as jnp
from jax import lax
from jax.experimental import pallas as pl
from jax.experimental.pallas import tpu as pltpu
from jax.sharding import PartitionSpec as P

epsilon = 1e-05
adapter_scale = 0.5
rope_base = 500000.0
masked_score = -1e30


VMEM = pl.BlockSpec(memory_space=pltpu.VMEM)
HBM = pl.BlockSpec(memory_space=pltpu.HBM)
SMEM = pl.BlockSpec(memory_space=pltpu.SMEM)


def local_call(kernel, name, operands, outs, scratch, far=(), carried=()):
    near = [spec for _, spec in operands]
    counts = (len(operands), len(far), len(carried), len(outs), len(carried), len(scratch))

    def body(*refs):
        groups, at = [], 0
        for n in counts:
            groups.append(refs[at : at + n])
            at += n
        ins, far_refs, sources, out_refs, targets, scratch_refs = groups
        copies = [
            pltpu.make_async_copy(source, target, refs[-1].at[i])
            for i, (source, target) in enumerate(zip(sources, targets))
        ]
        kernel(ins, far_refs, out_refs, scratch_refs, [copy.start for copy in copies])
        for copy in copies:
            copy.wait()

    sems = [pltpu.SemaphoreType.DMA((len(carried),))] if carried else []
    return pl.pallas_call(
        body,
        in_specs=near + [HBM] * (len(far) + len(carried)),
        out_specs=[VMEM] * (len(outs) + len(carried)),
        out_shape=[*outs, *[pltpu.VMEM(x.shape, x.dtype) for x in carried]],
        scratch_shapes=[*scratch, *sems],
        compiler_params=pltpu.CompilerParams(vmem_limit_bytes=16 * 1024 * 1024),
        cost_estimate=pl.CostEstimate(flops=1000, bytes_accessed=1000, transcendentals=0),
        name=name,
    )(
        *[x for x, _ in operands],
        *[pltpu.with_memory_space_constraint(x, pltpu.HBM) for x in (*far, *carried)],
    )


def in_vmem(arrays):
    return [(x, VMEM) for x in arrays]


def shaped(shape, dtype=jnp.float32):
    return jax.ShapeDtypeStruct(shape, dtype)


def after(x, *earlier):
    return lax.optimization_barrier((x, *earlier))[0]


def core_swap(x, pool_count):
    return lax.ppermute(x, "pool", [(p, p ^ 1) for p in range(pool_count)])


def chip_move(x, pool_count, d, e=0):
    chips = pool_count // 2
    return lax.ppermute(
        x,
        "pool",
        [(p, (p // 2 + d) % chips * 2 + ((p % 2) ^ e)) for p in range(pool_count)],
    )


def shrink(ids, blocks, query_down, value_down, carried):
    slots, _ = query_down.shape
    rows = blocks[0].shape[0]
    adapters = slots // 16

    def kernel(ins, _, outs, scratch, starts):
        ids, *blocks, query_down, value_down = ins
        (out,) = outs
        for start in starts:
            start()
        for first in range(0, len(blocks), 2):
            x = jnp.concatenate([b[...] for b in blocks[first : first + 2]], axis=0)
            span = slice(first * rows, (first + 2) * rows)
            label = ids[:, span].reshape(1, 1, 2 * rows)
            chosen = lax.broadcasted_iota(jnp.int32, (adapters, 1, 2 * rows), 0) == label
            for at, table in enumerate((query_down, value_down)):
                terms = lax.dot_general(
                    table[...], x, (((1,), (1,)), ((), ())), preferred_element_type=jnp.float32
                ).reshape(adapters, 16, 2 * rows)
                out[at * 16 : (at + 1) * 16, span] = jnp.sum(
                    jnp.where(chosen, terms, 0.0), axis=0
                )

    return local_call(
        kernel,
        "shrink",
        in_vmem([ids, *blocks, query_down, value_down]),
        [shaped((32, rows * len(blocks)))],
        [],
        carried=carried,
    )


def spread_lows(low, ids, adapters):
    total = ids.shape[1]
    low = low.astype(jnp.bfloat16).astype(jnp.float32) * adapter_scale
    chosen = lax.broadcasted_iota(jnp.int32, (adapters, 1, total), 0) == ids.reshape(1, 1, total)
    return [
        jnp.where(chosen, low[at : at + 16][None], 0.0)
        .reshape(adapters * 16, total)
        .T.astype(jnp.bfloat16)
        for at in (0, 16)
    ]


def columns_at(start, width):
    return pl.ds(pl.multiple_of(start, width), width)


def project_own(blocks, wq, wk, wv, carried):
    rows, depth = blocks[0].shape
    wide, kv = wq.shape[1], wk.shape[1]
    tile = min(512, wide // 2)
    steps = wide // tile

    def kernel(ins, far, outs, scratch, starts):
        keep, send, *near = outs
        xs, sems = scratch

        def copies():
            for i in range(steps):
                yield far[0].at[:, columns_at(i * tile, tile)], near[0].at[
                    :, columns_at(i * tile, tile)
                ], sems.at[i]
            yield far[1], near[1], sems.at[steps]
            yield far[2], near[2], sems.at[steps + 1]

        for copy in copies():
            pltpu.make_async_copy(*copy).start()
        for start in starts:
            start()
        at = 0
        for block in ins:
            xs[at : at + block.shape[0], :] = block[...]
            at += block.shape[0]

        def write(w, columns):
            acc = jnp.dot(xs[...], w, preferred_element_type=jnp.float32)
            keep[:, columns] = acc[:rows]
            send[:, columns] = acc[rows:]

        @pl.loop(0, steps)
        def _(i):
            columns = columns_at(i * tile, tile)
            pltpu.make_async_copy(
                far[0].at[:, columns], near[0].at[:, columns], sems.at[i]
            ).wait()
            write(near[0][:, columns], columns)

        for j in range(2):
            pltpu.make_async_copy(far[1 + j], near[1 + j], sems.at[steps + j]).wait()
            write(near[1 + j][...], slice(wide + j * kv, wide + (j + 1) * kv))

    sums = shaped((rows, wide + 2 * kv))
    return local_call(
        kernel,
        "project_own",
        in_vmem(blocks),
        [sums, sums, *[pltpu.VMEM(w.shape, w.dtype) for w in (wq, wk, wv)]],
        [
            pltpu.VMEM((2 * rows, depth), jnp.bfloat16),
            pltpu.SemaphoreType.DMA((steps + 2,)),
        ],
        far=[wq, wk, wv],
        carried=carried,
    )


def project(name, window, spans, ids, lows, blocks, weights, carried):
    first, rows = window
    depth = blocks[0].shape[1]
    wide, kv, slots = weights[0].shape[1], weights[1].shape[1], weights[3].shape[0]
    tile = min(512, wide // 2)

    def kernel(ins, _, outs, scratch, starts):
        ids, *ins = ins
        low_refs, (b0, b1, wq, wk, wv, uq, uv) = ins[: len(lows)], ins[len(lows) :]
        keep, *sends = outs
        xs, spread_q, spread_v = scratch
        for start in starts:
            start()
        xs[:rows, :] = b0[first : first + rows, :]
        xs[rows:, :] = b1[first : first + rows, :]
        low = low_refs[0][...]
        for other in low_refs[1:]:
            low = low + other[...]
        low = jnp.concatenate([low[:, at : at + rows] for at in spans], axis=1)
        label = jnp.concatenate([ids[:, at : at + rows] for at in spans], axis=1)
        spread_q[...], spread_v[...] = spread_lows(low, label, slots // 16)

        def sums(w, spread=None, u=None):
            acc = jnp.dot(xs[...], w, preferred_element_type=jnp.float32)
            if u is not None:
                acc = acc + jnp.dot(spread[...], u, preferred_element_type=jnp.float32)
            return acc

        for half in range(2):

            @pl.loop(0, wide // 2 // tile)
            def _(j):
                columns = columns_at(half * (wide // 2) + j * tile, tile)
                acc = sums(wq[:, columns], spread_q, uq[:, columns])
                keep[:, columns] = acc[:rows]
                sends[half][:, columns_at(j * tile, tile)] = acc[rows:].astype(jnp.bfloat16)

        for j, acc in enumerate((sums(wk[...]), sums(wv[...], spread_v, uv[...]))):
            keep[:, wide + j * kv : wide + (j + 1) * kv] = acc[:rows]
            sends[2][:, j * kv : (j + 1) * kv] = acc[rows:].astype(jnp.bfloat16)

    spread = pltpu.VMEM((2 * rows, slots), jnp.bfloat16)
    results = local_call(
        kernel,
        name,
        in_vmem([ids, *lows, *blocks, *weights]),
        [
            shaped((rows, wide + 2 * kv)),
            *[shaped((rows, wide // 2), jnp.bfloat16)] * 2,
            shaped((rows, 2 * kv), jnp.bfloat16),
        ],
        [pltpu.VMEM((2 * rows, depth), jnp.bfloat16), spread, spread],
        carried=carried,
    )
    return results[0], results[1:4], results[4:]


def add_adapters(keep, send, ids, lows, uq, uv, carried):
    rows = keep.shape[0]
    wide, kv, slots = uq.shape[1], uv.shape[1], uq.shape[0]
    tile = min(512, wide)

    def kernel(ins, _, outs, scratch, starts):
        ids, *ins = ins
        low_refs, (keep0, send0, uq, uv) = ins[: len(lows)], ins[len(lows) :]
        keep, send = outs
        spread_q, spread_v = scratch
        for start in starts:
            start()
        low = low_refs[0][:, : 2 * rows]
        for other in low_refs[1:]:
            low = low + other[:, : 2 * rows]
        spread_q[...], spread_v[...] = spread_lows(low, ids[:, : 2 * rows], slots // 16)

        def write(extra, columns):
            keep[:, columns] = keep0[:, columns] + extra[:rows]
            send[:, columns] = (send0[:, columns] + extra[rows:]).astype(send.dtype)

        @pl.loop(0, wide // tile)
        def _(i):
            columns = columns_at(i * tile, tile)
            write(
                jnp.dot(spread_q[...], uq[:, columns], preferred_element_type=jnp.float32),
                columns,
            )

        keep[:, wide : wide + kv] = keep0[:, wide : wide + kv]
        send[:, wide : wide + kv] = send0[:, wide : wide + kv].astype(send.dtype)
        write(
            jnp.dot(spread_v[...], uv[...], preferred_element_type=jnp.float32),
            slice(wide + kv, wide + 2 * kv),
        )

    spread = pltpu.VMEM((2 * rows, slots), jnp.bfloat16)
    return local_call(
        kernel,
        "add_adapters",
        in_vmem([ids, *lows, keep, send, uq, uv]),
        [shaped(keep.shape), shaped(keep.shape, jnp.bfloat16)],
        [spread, spread],
        carried=carried,
    )


def attend_kernel(first_row, block, ins, outs):
    keep, swapped, *moved, scale, cosines, sines, lengths, keys, values = ins
    out, key_out, value_out = outs
    head = cosines.shape[1]
    rows = out.shape[0]
    _, kv_heads, cache, _ = keys.shape
    heads = out.shape[1] // head
    group = heads // kv_heads
    score_scale = 1.0 / math.sqrt(head)
    sub = 8
    column = lax.broadcasted_iota(jnp.int32, (sub, sub * cache), 1)
    start = lax.broadcasted_iota(jnp.int32, (sub, sub * cache), 0) * cache

    @pl.loop(0, rows // block)
    def _(i):
        attended, new_keys, new_values = [], [], []
        for half in range(block // sub):
            here = pl.ds(pl.multiple_of(i * block + half * sub, sub), sub)
            whole = pl.ds(pl.multiple_of(first_row + i * block + half * sub, sub), sub)
            x = keep[whole] + swapped[whole].astype(jnp.float32)
            for m in moved:
                x = x + m[here].astype(jnp.float32)
            x = x * scale[whole]
            cos, sin = cosines[whole], sines[whole]
            inside = (column >= start) & (column < start + lengths[whole])

            def piece(i):
                return x[:, i * head : (i + 1) * head]

            def turn(v):
                return v * cos + pltpu.roll(v, head // 2, 1) * sin

            for g in range(kv_heads):
                query = jnp.concatenate(
                    [turn(piece(g * group + h)) for h in range(group)], axis=0
                ).astype(jnp.bfloat16)
                new_key = turn(piece(heads + g)).astype(jnp.bfloat16).astype(jnp.float32)
                new_value = piece(heads + kv_heads + g).astype(jnp.bfloat16).astype(jnp.float32)
                k = keys[whole, g].reshape(sub * cache, head)
                v = values[whole, g].reshape(sub * cache, head)
                scores = (
                    lax.dot_general(
                        query, k, (((1,), (1,)), ((), ())), preferred_element_type=jnp.float32
                    )
                    * score_scale
                )
                own_key = jnp.concatenate([new_key] * group, axis=0)
                own = (
                    jnp.sum(query.astype(jnp.float32) * own_key, axis=1, keepdims=True)
                    * score_scale
                )
                scores = jnp.where(
                    inside[None], scores.reshape(group, sub, sub * cache), masked_score
                ).reshape(group * sub, sub * cache)
                peak = jnp.maximum(jnp.max(scores, axis=1, keepdims=True), own)
                weights = jnp.exp(scores - peak)
                own_weight = jnp.exp(own - peak)
                inverse = 1.0 / (jnp.sum(weights, axis=1, keepdims=True) + own_weight)
                mixed = jnp.dot(weights.astype(jnp.bfloat16), v, preferred_element_type=jnp.float32)
                own_value = jnp.concatenate([new_value] * group, axis=0)
                mixed = (mixed + own_weight * own_value) * inverse
                attended += [mixed[h * sub : (h + 1) * sub] for h in range(group)]
                new_keys.append(new_key)
                new_values.append(new_value)
        r = pl.ds(pl.multiple_of(i * block, block), block)

        def joined(pieces):
            n = len(pieces) * sub // block
            return jnp.concatenate(
                [jnp.concatenate(pieces[j::n], axis=0) for j in range(n)], axis=1
            ).astype(jnp.bfloat16)

        out[r] = joined(attended)
        key_out[r] = joined(new_keys)
        value_out[r] = joined(new_values)


def attend(name, window, keep, swapped, moved, rest, keys, values, carried):
    _, columns = keep.shape
    _, kv_heads, _, head = keys.shape
    kv_cols = kv_heads * head
    first, part = window

    def kernel(ins, _, outs, scratch, starts):
        for start in starts:
            start()
        attend_kernel(first, 16, ins, outs)

    widths = (columns - 2 * kv_cols, kv_cols, kv_cols)
    return local_call(
        kernel,
        name,
        in_vmem([keep, swapped, *moved, *rest, keys, values]),
        [shaped((part, w), jnp.bfloat16) for w in widths],
        [],
        carried=carried,
    )


def output_part(name, span, order, blocks, weights):
    rows = blocks[0].shape[0]
    first, columns = span
    depth = weights.shape[0]
    tile = math.gcd(512, columns)
    total = rows * len(blocks)

    def kernel(ins, _, outs, scratch, starts):
        order, *blocks, weights = ins
        keep, send = outs
        (xs,) = scratch
        for b, block in enumerate(blocks):
            xs[pl.ds(pl.multiple_of(order[b] * rows, rows), rows), :] = block[...]

        @pl.loop(0, columns // tile)
        def _(i):
            w = weights[:, columns_at(first + i * tile, tile)]
            acc = jnp.dot(xs[...], w, preferred_element_type=jnp.float32).astype(jnp.bfloat16)
            keep[:, columns_at(i * tile, tile)] = acc[: total // 2]
            send[:, columns_at(i * tile, tile)] = acc[total // 2 :]

    return local_call(
        kernel,
        name,
        [(order, SMEM), *in_vmem([*blocks, weights])],
        [shaped((total // 2, columns), jnp.bfloat16)] * 2,
        [pltpu.VMEM((total, depth), jnp.bfloat16)],
    )


def reversed_bits(x, count):
    out, bit = 0, 1
    while bit < count:
        out = out * 2 + (x // bit) % 2
        bit *= 2
    return out


def halving_steps(keep, send, count, earlier):
    step, totals = 1, []
    while True:
        got = lax.ppermute(send, "tp", [(z, z ^ step) for z in range(count)])
        step *= 2
        if step == count:
            return keep, got, totals
        if earlier:
            got = after(got, earlier[len(totals)])
        total = keep.astype(jnp.float32) + got.astype(jnp.float32)
        totals.append(total)
        half = total.shape[0] // 2
        keep, send = total[:half], total[half:].astype(jnp.bfloat16)


def shards(
    tokens,
    input_norm_gain,
    query_matrix,
    key_matrix,
    value_matrix,
    output_matrix,
    rotated_key_cache,
    cached_value_rows,
    cache_length_per_row,
    row_adapter_index,
    query_down_maps,
    query_up_maps,
    value_down_maps,
    value_up_maps,
):
    pool_count = lax.axis_size("pool")
    tp_count = lax.axis_size("tp")
    chips = pool_count // 2
    pool_at = lax.axis_index("pool")
    tp_at = lax.axis_index("tp")
    chip, core = pool_at // 2, pool_at % 2
    rows = tokens.shape[0]
    adapters, rank, piece = query_down_maps.shape
    base = query_matrix.shape[0]
    kv_heads = rotated_key_cache.shape[1]
    head = rotated_key_cache.shape[3]

    def scaled(start, width, tokens=tokens, gain=input_norm_gain, window=(0, rows)):
        x = lax.dynamic_slice(tokens, (window[0], start), (window[1], width)).astype(jnp.float32)
        factor = lax.dynamic_slice_in_dim(gain, start, width, 0).astype(jnp.float32)
        return (x * factor[None, :]).astype(jnp.bfloat16)

    ids = row_adapter_index.reshape(1, rows)
    ids = [ids] + [chip_move(ids, pool_count, d) for d in range(1, chips)]
    first = after(scaled(tp_at * piece, piece), *ids[1:])
    first, tokens_1, gain_1 = lax.optimization_barrier((first, tokens, input_norm_gain))
    same_core = [first] + [chip_move(first, pool_count, d) for d in range(1, chips)]
    ids = [b for x in ids for b in (x, core_swap(x, pool_count))]
    local_ids = jnp.concatenate(ids, axis=1) - pool_at * adapters

    cut = rows * 3 // 8
    chunks = [(0, cut), (cut, rows - cut)]
    own = scaled(pool_at * base, base, tokens_1, gain_1)
    partner_at = (pool_at // 2 * 2 + 1 - core) * base
    partner = [
        scaled(partner_at, base, tokens_1, gain_1, (at, rows // 2)) for at in (0, rows // 2)
    ]
    *partner, tokens_2, gain_2 = lax.optimization_barrier((*partner, tokens, input_norm_gain))
    partner = [core_swap(x, pool_count) for x in partner]
    away = {}
    for d in range(1, chips):
        for e in range(2):
            target = (chip + d) % chips * 2 + (core + e) % 2
            away[d, e] = scaled(target * base, base, tokens_2, gain_2)
    own = after(own, *away.values())
    flat_down = [x.reshape(adapters * rank, piece) for x in (query_down_maps, value_down_maps)]
    own_keep, own_send, *weights, down_q, down_v = project_own(
        [own, *partner], query_matrix, key_matrix, value_matrix, flat_down
    )
    remote = [[] for _ in range(chips)]
    for (d, e), x in away.items():
        remote[d].append(chip_move(after(x, *same_core[1:]), pool_count, d, e))

    same_core[1:] = [after(x, own_keep) for x in same_core[1:]]
    adapter_rows = [b for x in same_core for b in (x, core_swap(x, pool_count))]
    flat_up = [x.reshape(adapters * rank, x.shape[2]) for x in (query_up_maps, value_up_maps)]
    shrunk, up_q, up_v = shrink(local_ids, adapter_rows, down_q, down_v, flat_up)
    lows = [shrunk] + [
        lax.ppermute(shrunk, "tp", [(i, (i + d) % tp_count) for i in range(tp_count)])
        for d in range(1, tp_count)
    ]
    weights += [up_q, up_v]

    values = tokens.astype(jnp.float32)
    scale = lax.rsqrt(jnp.mean(values * values, axis=-1, keepdims=True) + epsilon)
    half_dim = head // 2
    frequency = jnp.power(
        jnp.float32(rope_base), jnp.arange(half_dim, dtype=jnp.float32) * (-2.0 / head)
    )
    angles = cache_length_per_row.astype(jnp.float32)[:, None] * frequency[None, :]
    cosines = jnp.concatenate([jnp.cos(angles)] * 2, axis=1)
    sines = jnp.concatenate([-jnp.sin(angles), jnp.sin(angles)], axis=1)
    lengths = cache_length_per_row.reshape(rows, 1)

    own_sums, own_send, keys = add_adapters(
        own_keep, own_send, local_ids, lows, up_q, up_v, [rotated_key_cache]
    )
    swapped = core_swap(own_send, pool_count)
    local_ids = after(local_ids, own_sums)
    moved = [[] for _ in chunks]
    both, to_carry, cached = None, [cached_value_rows], None
    for c, (at, part) in enumerate(chunks):
        for d in range(1, chips):
            spans = [(2 * d + e) * rows + at for e in range(2)]
            if both is not None:
                remote[d][0] = after(remote[d][0], both)
            keep, sends, carried = project(
                f"project_{c}_{d}",
                (at, part),
                spans,
                local_ids,
                lows,
                remote[d],
                weights,
                to_carry,
            )
            cached, to_carry = cached or carried, []
            swaps = [core_swap(x, pool_count) for x in sends]
            if c:
                keep = after(keep, moved[c - 1][-1])
            swaps = jnp.concatenate(swaps, axis=1)
            both = (keep + swaps.astype(jnp.float32)).astype(jnp.bfloat16)
            moved[c].append(chip_move(both, pool_count, -d))
    moved[0][0] = after(moved[0][0], both)

    share = pool_count // tp_count
    order = []
    for d in range(chips):
        for e in range(2):
            p = (chip - d) % chips * 2 + (core + e) % 2
            order.append(
                reversed_bits(jnp.bitwise_xor(p // share, tp_at), tp_count) * share + p % share
            )
    order = jnp.stack(order).astype(jnp.int32)

    attended, new_keys, new_values, out_weights = [], [], [], None
    for c, window in enumerate(chunks):
        out, new_key, new_value, *carried = attend(
            f"attend_{c}",
            window,
            own_sums,
            swapped,
            moved[c],
            (scale, cosines, sines, lengths),
            keys,
            cached[0],
            [] if c else [output_matrix],
        )
        out_weights = out_weights or carried
        if c + 1 < len(chunks):
            out, *moved[c + 1] = lax.optimization_barrier((out, *moved[c + 1]))
        if c:
            out = after(out, attended[-1][-1])
        attended.append([out] + [chip_move(out, pool_count, d) for d in range(1, chips)])
        new_keys.append(new_key)
        new_values.append(new_value)
    attended[0][0] = after(attended[0][0], *new_keys)

    pieces, totals, keep = [], [], None
    columns = output_matrix.shape[1]
    spans = [(0, columns * 3 // 4), (columns * 3 // 4, columns // 4)]
    for c in range(len(chunks)):
        if c:
            attended[c] = [after(x, keep) for x in attended[c]]
        gathered = [b for x in attended[c] for b in (x, core_swap(x, pool_count))]
        for j, span in enumerate(spans):
            if j:
                gathered[0] = after(gathered[0], keep)
            keep, send = output_part(f"output_{c}_{j}", span, order, gathered, out_weights[0])
            *halves, totals = halving_steps(keep, send, tp_count, totals)
            pieces.append(halves)
    outputs, row_count = [], len(spans)
    for c, (_, part) in enumerate(chunks):
        sums = []
        for mine, got in pieces[c * row_count : (c + 1) * row_count]:
            total = mine.astype(jnp.float32) + after(got, keep).astype(jnp.float32)
            keep = total.astype(jnp.bfloat16)
            sums.append(keep.reshape(-1, part, total.shape[1]))
        outputs.append(jnp.concatenate(sums, axis=2))
    attn_out = jnp.concatenate(outputs, axis=1)
    return (
        attn_out.reshape(-1, attn_out.shape[2]),
        jnp.concatenate(new_keys, axis=0),
        jnp.concatenate(new_values, axis=0),
    )


def solution(mesh):
    return jax.shard_map(
        shards,
        mesh=mesh,
        in_specs=(
            P(("groups", "pool"), None),
            P(),
            P("pool", "tp"),
            P("pool", "tp"),
            P("pool", "tp"),
            P("tp", "pool"),
            P(("groups", "pool"), "tp", None, None),
            P(("groups", "pool"), "tp", None, None),
            P(("groups", "pool")),
            P(("groups", "pool")),
            P("pool", None, "tp"),
            P("pool", None, "tp"),
            P("pool", None, "tp"),
            P("pool", None, "tp"),
        ),
        out_specs=(
            P(("groups", "tp"), "pool"),
            P(("groups", "pool"), "tp"),
            P(("groups", "pool"), "tp"),
        ),
        check_vma=False,
    )
```

time: 184 us -> 148 us (0.80)
  waiting for transfers between devices: 73.8 us -> 36.7 us
  starting transfers between devices: 21.9 us -> 31.2 us
  Pallas kernels: 46.4 us -> 40.2 us
  other arithmetic: 13.1 us -> 10.4 us
    ppermute x8, waiting for transfers between devices: 30.5 us -> 0.83 us  [chip_move(): lax.ppermute(x, 'pool', [(p, (p // 2 + d) % chips * 2 + (p % 2 ^ e)) for...]
    ppermute x4 -> x8, starting transfers between devices: 3.63 us -> 10.5 us  [halving_steps(): got = lax.ppermute(send, 'tp', [(z, z ^ step) for z in range(count)])]
    pallas_call x9 -> x11, Pallas kernels: 46.4 us -> 40.2 us  [local_call(): pl.pallas_call(body, in_specs=near + [HBM] * (len(far) + len(carried)), o...]
    ppermute x4 -> x8, waiting for transfers between devices: 33.9 us -> 29.4 us  [halving_steps(): got = lax.ppermute(send, 'tp', [(z, z ^ step) for z in range(count)])]
    ppermute x17, waiting for transfers between devices: 5.69 us -> 2.64 us  [core_swap(): return lax.ppermute(x, 'pool', [(p, p ^ 1) for p in range(pool_count)])]
    unnamed x54 -> x52, local copies, waits for them, and re-layouts: 26.2 us -> 27.5 us
    convert_element_type x6 -> x10, other arithmetic: 5.34 us -> 5.11 us  [the longest x4 3.62 us: scaled(): return (x * factor[None, :]).astype(jnp.bfloat16)]
  transfers between devices with their start and end apart: 32 -> 36, of which waited for: 15 -> 16; matrix products, arithmetic and copies ran while one was open for 6% -> 6% of each run, Pallas kernels for 22% -> 24%
where the time goes in v4:
time: 148 us; the launch traced here: 147 us
  Pallas kernels  40.2 us (27%)
  waiting for transfers between devices  36.7 us (25%)
  starting transfers between devices  31.2 us (21%)
  local copies, waits for them, and re-layouts  27.8 us (19%)
  other arithmetic  10.4 us (7%)
    pallas_call x11, Pallas kernels, local_call(): pl.pallas_call(body, in_specs=near + [HBM] * (len(far) + len(carried)), o...  40.2 us
    ppermute x8, waiting for transfers between devices, halving_steps(): got = lax.ppermute(send, 'tp', [(z, z ^ step) for z in range(count)])  29.4 us
    unnamed x52, local copies, waits for them, and re-layouts  27.5 us
    ppermute x8, starting transfers between devices, halving_steps(): got = lax.ppermute(send, 'tp', [(z, z ^ step) for z in range(count)])  10.5 us
    ppermute x8, starting transfers between devices, chip_move(): lax.ppermute(x, 'pool', [(p, (p // 2 + d) % chips * 2 + (p % 2 ^ e)) for...  10.5 us
    ppermute x3, starting transfers between devices, shards(): lax.ppermute(shrunk, 'tp', [(i, (i + d) % tp_count) for i in range(tp_cou...  5.55 us
    ppermute x17, starting transfers between devices, core_swap(): return lax.ppermute(x, 'pool', [(p, p ^ 1) for p in range(pool_count)])  4.56 us
    ppermute x3, waiting for transfers between devices, shards(): lax.ppermute(shrunk, 'tp', [(i, (i + d) % tp_count) for i in range(tp_cou...  3.8 us
  transfers between devices with their start and end apart: 36, of which 16 were waited for; matrix products, arithmetic and copies ran while one was open for 6% of the time, Pallas kernels for 24%

profile of v4, /device:TPU:0, one launch (start us, length us, event | category | flops | bytes accessed | tf_op | source)
XLA Modules:
  0.0 147.4 jit_solution(1945701639596860412)
XLA Ops:
  0.7 3.0 %collective-permute-start.1 = (s32[1,128]{1,0:T(1,128)}, s32[1,128]{1,0:T(1,128)S(1)}, u32[]{:S(2)}, u32[]{:S(2)}) collective-permute-start(s32[1,128]{1,0:T(1,128)} %bitcast.31), channel_id=1, source_target_pairs={{0,8},{4,12},{8,0},{12,4},{1,9},{5,13},{9,1},{13,5},{2,10},{6,14},... | collective-permute-start | bytes 1544 | tf_op jit(solution)/shard_map/ppermute | solution.py:74
  3.7 0.7 dynamic-slice_convert_fusion.4
  4.4 1.1 multiply_convert_fusion.3.refs_1_
  5.6 1.7 %collective-permute-start.4 = (bf16[128,2048]{1,0:T(8,128)(2,1)S(1)}, bf16[128,2048]{1,0:T(8,128)(2,1)}, u32[]{:S(2)}, u32[]{:S(2)}) collective-permute-start(bf16[128,2048]{1,0:T(8,128)(2,1)S(1)} %multiply_convert_fusion.3.refs_1_), channel_id=1, source_target_pairs={{0,8},{4,12},{8,0},{12,4},{1,9},{5,13},{9,1},{13,5},{2,10},{6,14},... | collective-permute-start | bytes 1572872 | tf_op jit(solution)/shard_map/ppermute | solution.py:74
  7.4 0.7 dynamic-slice_convert_fusion.2
  8.1 1.1 multiply_convert_fusion.4
  9.8 1.3 multiply_convert_fusion
  11.2 5.9 %project_own.1 = (f32[128,2560]{1,0:T(8,128)S(1)}, f32[128,2560]{1,0:T(8,128)S(1)}, bf16[2048,2048]{1,0:T(8,128)(2,1)S(1)}, bf16[2048,256]{1,0:T(8,128)(2,1)S(1)...) custom-call(bf16[128,2048]{1,0:T(8,128)(2,1)S(1)} %multiply_convert_fusion.2.refs_0_, ...), custom_call_target="tpu_custom_call" | custom-call | flops 1000 | bytes 1000 | tf_op jit(solution)/shard_map/project_own/pallas_call | solution.py:41
  17.1 3.3 %copy-done.2 = bf16[2048,2048]{1,0:T(8,128)(2,1)} copy-done((bf16[2048,2048]{1,0:T(8,128)(2,1)}, bf16[2048,2048]{1,0:T(8,128)(2,1)S(1)}, u32[]{:S(2)}) %copy-start.2) | copy-done | bytes 8388632
  20.4 1.3 copy-done.7
  21.8 1.4 copy-done.9
  23.2 1.1 copy-done.11
  24.3 1.1 copy-done.13
  25.9 1.3 collective-permute-start.13
  27.2 0.5 collective-permute-start
  27.7 0.8 collective-permute-done
  28.9 0.8 collective-permute-done.2
  29.7 1.6 %copy-done.8 = bf16[512,2048]{1,0:T(8,128)(2,1)S(1)} copy-done((bf16[512,2048]{1,0:T(8,128)(2,1)S(1)}, bf16[512,2048]{1,0:T(8,128)(2,1)}, u32[]{:S(2)}) %copy-start.8) | copy-done | bytes 2097176
  31.3 1.6 %copy-done.10 = bf16[512,2048]{1,0:T(8,128)(2,1)S(1)} copy-done((bf16[512,2048]{1,0:T(8,128)(2,1)S(1)}, bf16[512,2048]{1,0:T(8,128)(2,1)}, u32[]{:S(2)}) %copy-start.10) | copy-done | bytes 2097176
  32.9 3.7 %shrink.1 = (f32[32,512]{1,0:T(8,128)S(1)}, bf16[512,2048]{1,0:T(8,128)(2,1)S(1)}, bf16[512,256]{1,0:T(8,128)(2,1)S(1)}) custom-call(s32[1,512]{1,0:T(1,128)S(1)} %add_subtract_fusion.refs_0_, bf16[128,2048]{1,0:T(8,128)(2,1)S(1)} %multiply_convert_fusion.3.refs_1_, bf16[128,2048]{1,0:T(8,128)(2,1)S(1)} %collective-permute-done.3.refs_2_, ...), custom_call_target="tpu_custom_call" | custom-call | flops 1000 | bytes 1000 | tf_op jit(solution)/shard_map/shrink/pallas_call | solution.py:41
  36.6 1.6 %collective-permute-start.8 = (f32[32,512]{1,0:T(8,128)S(1)}, f32[32,512]{1,0:T(8,128)S(1)}, u32[]{:S(2)}, u32[]{:S(2)}) collective-permute-start(f32[32,512]{1,0:T(8,128)S(1)} %get-tuple-element.84.refs_1_), channel_id=1, source_target_pairs={{0,1},{1,2},{2,3},{3,0},{4,5},{5,6},{6,7},{7,4},{8,9},{9,10},{10,1... | collective-permute-start | bytes 196616 | tf_op jit(solution)/shard_map/ppermute | solution.py:514
  38.3 2.6 %collective-permute-start.9 = (f32[32,512]{1,0:T(8,128)S(1)}, f32[32,512]{1,0:T(8,128)S(1)}, u32[]{:S(2)}, u32[]{:S(2)}) collective-permute-start(f32[32,512]{1,0:T(8,128)S(1)} %get-tuple-element.84.refs_1_), channel_id=1, source_target_pairs={{0,2},{1,3},{2,0},{3,1},{4,6},{5,7},{6,4},{7,5},{8,10},{9,11},{10,... | collective-permute-start | bytes 196616 | tf_op jit(solution)/shard_map/ppermute | solution.py:514
  40.9 1.3 collective-permute-start.10
  42.2 0.8 collective-permute-done.8.refs_2_
  43.0 2.7 %collective-permute-done.9.refs_3_ = f32[32,512]{1,0:T(8,128)S(1)} collective-permute-done((f32[32,512]{1,0:T(8,128)S(1)}, f32[32,512]{1,0:T(8,128)S(1)}, u32[]{:S(2)}, u32[]{:S(2)}) %collective-permute-start.9) | collective-permute-done | bytes 65568 | tf_op jit(solution)/shard_map/ppermute | solution.py:514
  46.0 2.3 %add_adapters.1 = (f32[128,2560]{1,0:T(8,128)S(1)}, bf16[128,2560]{1,0:T(8,128)(2,1)S(1)}, bf16[128,2,64,128]{3,2,1,0:T(8,128)(2,1)S(1)}) custom-call(s32[1,512]{1,0:T(1,128)S(1)} %add_subtract_fusion.refs_0_, f32[32,512]{1,0:T(8,128)S(1)} %get-tuple-element.84.refs_1_, f32[32,512]{1,0:T(8,128)S(1)} %collective-permute-done.8.refs_2_, ...), custom_call_target="tpu_custom_call" | custom-call | flops 1000 | bytes 1000 | tf_op jit(solution)/shard_map/add_adapters/pallas_call | solution.py:41
  48.4 2.1 %copy-done.3 = bf16[128,2,64,128]{3,2,1,0:T(8,128)(2,1)} copy-done((bf16[128,2,64,128]{3,2,1,0:T(8,128)(2,1)}, bf16[128,2,64,128]{3,2,1,0:T(8,128)(2,1)S(1)}, u32[]{:S(2)}) %copy-start.3) | copy-done | bytes 4194328
  50.6 4.4 %project_0_1.1 = (f32[48,2560]{1,0:T(8,128)S(1)}, bf16[48,1024]{1,0:T(8,128)(2,1)S(1)}, bf16[48,1024]{1,0:T(8,128)(2,1)S(1)}, bf16[48,512]{1,0:T(8,128)(2,1)S(1)}, bf16[128,2,64,128]{3,2,1,0:T(8,128)(2,1)S(1)}) custom-call(s32[1,512]{1,0:T(1,128)S(1)} %add_subtract_fusion.refs_0_, f32[32,512]{1,0:T(8,128)S(1)} %get-tuple-element.84.refs_1_, ...), custom_call_target="tpu_custom_call" | custom-call | flops 1000 | bytes 1000 | tf_op jit(solution)/shard_map/project_0_1/pallas_call | solution.py:41
  55.0 2.0 %copy-done.5 = bf16[128,2,64,128]{3,2,1,0:T(8,128)(2,1)} copy-done((bf16[128,2,64,128]{3,2,1,0:T(8,128)(2,1)}, bf16[128,2,64,128]{3,2,1,0:T(8,128)(2,1)S(1)}, u32[]{:S(2)}) %copy-start.5) | copy-done | bytes 4194328
  58.0 0.9 collective-permute-done.16
  58.8 0.7 add_convert_fusion.1
  60.5 4.7 %project_1_1.1 = (f32[80,2560]{1,0:T(8,128)S(1)}, bf16[80,1024]{1,0:T(8,128)(2,1)}, bf16[80,1024]{1,0:T(8,128)(2,1)}, bf16[80,512]{1,0:T(8,128)(2,1)S(1)}) custom-call(s32[1,512]{1,0:T(1,128)S(1)} %add_subtract_fusion.refs_0_, f32[32,512]{1,0:T(8,128)S(1)} %get-tuple-element.84.refs_1_, f32[32,512]{1,0:T(8,128)S(1)} %collective-permute-done.8.refs_2_, ...), custom_call_target="tpu_custom_call" | custom-call | flops 1000 | bytes 1000 | tf_op jit(solution)/shard_map/project_1_1/pallas_call | solution.py:41
  65.1 0.9 copy-done.15
  66.9 0.5 collective-permute-start.11
  67.4 0.7 collective-permute-done.17.refs_2_
  68.2 1.2 add_convert_fusion
  69.4 1.7 %collective-permute-start.21 = (bf16[80,2560]{1,0:T(8,128)(2,1)S(1)}, bf16[80,2560]{1,0:T(8,128)(2,1)S(1)}, u32[]{:S(2)}, u32[]{:S(2)}) collective-permute-start(bf16[80,2560]{1,0:T(8,128)(2,1)S(1)} %add_convert_fusion), channel_id=1, source_target_pairs={{0,8},{4,12},{8,0},{12,4},{1,9},{5,13},{9,1},{13,5},{2,10},{6,14},... | collective-permute-start | bytes 1228808 | tf_op jit(solution)/shard_map/ppermute | solution.py:74
  71.6 2.2 %copy-done.4 = bf16[128,2,64,128]{3,2,1,0:T(8,128)(2,1)S(1)} copy-done((bf16[128,2,64,128]{3,2,1,0:T(8,128)(2,1)S(1)}, bf16[128,2,64,128]{3,2,1,0:T(8,128)(2,1)}, u32[]{:S(2)}) %copy-start.4) | copy-done | bytes 4194328
  73.8 2.2 %copy-done.6 = bf16[128,2,64,128]{3,2,1,0:T(8,128)(2,1)S(1)} copy-done((bf16[128,2,64,128]{3,2,1,0:T(8,128)(2,1)S(1)}, bf16[128,2,64,128]{3,2,1,0:T(8,128)(2,1)}, u32[]{:S(2)}) %copy-start.6) | copy-done | bytes 4194328
  75.9 4.7 %attend_0.1 = (bf16[48,2048]{1,0:T(8,128)(2,1)S(1)}, bf16[48,256]{1,0:T(8,128)(2,1)S(1)}, bf16[48,256]{1,0:T(8,128)(2,1)S(1)}, bf16[2048,2048]{1,0:T(8,128)(2,1)S(1)}) custom-call(f32[128,2560]{1,0:T(8,128)S(1)} %get-tuple-element.88.refs_0_, bf16[128,2560]{1,0:T(8,128)(2,1)S(1)} %collective-permute-done.11.refs_1_, ...), custom_call_target="tpu_custom_call" | custom-call | flops 1000 | bytes 1000 | tf_op jit(solution)/shard_map/attend_0/pallas_call | solution.py:41
  80.7 3.3 %copy-done = bf16[2048,2048]{1,0:T(8,128)(2,1)} copy-done((bf16[2048,2048]{1,0:T(8,128)(2,1)}, bf16[2048,2048]{1,0:T(8,128)(2,1)S(1)}, u32[]{:S(2)}) %copy-start) | copy-done | bytes 8388632
  84.4 6.3 %attend_1.1 = (bf16[80,2048]{1,0:T(8,128)(2,1)S(1)}, bf16[80,256]{1,0:T(8,128)(2,1)S(1)}, bf16[80,256]{1,0:T(8,128)(2,1)S(1)}) custom-call(f32[128,2560]{1,0:T(8,128)S(1)} %get-tuple-element.88.refs_0_, bf16[128,2560]{1,0:T(8,128)(2,1)S(1)} %collective-permute-done.11.refs_1_, bf16[80,2560]{1,0:T(8,128)(2,1)S(1)} %collective-permute-done.21.refs_2_, ...), custom_call_target="tpu_custom_call" | custom-call | flops 1000 | bytes 1000 | tf_op jit(solution)/shard_map/attend_1/pallas_call | solution.py:41
  91.3 1.7 %collective-permute-start.28 = (bf16[80,2048]{1,0:T(8,128)(2,1)S(1)}, bf16[80,2048]{1,0:T(8,128)(2,1)S(1)}, u32[]{:S(2)}, u32[]{:S(2)}) collective-permute-start(bf16[80,2048]{1,0:T(8,128)(2,1)S(1)} %get-tuple-element.125.refs_1_), channel_id=1, source_target_pairs={{0,8},{4,12},{8,0},{12,4},{1,9},{5,13},{9,1},{13,5},{2,10},{6,14},... | collective-permute-start | bytes 983048 | tf_op jit(solution)/shard_map/ppermute | solution.py:74
  93.0 3.4 %copy-done.1 = bf16[2048,2048]{1,0:T(8,128)(2,1)S(1)} copy-done((bf16[2048,2048]{1,0:T(8,128)(2,1)S(1)}, bf16[2048,2048]{1,0:T(8,128)(2,1)}, u32[]{:S(2)}) %copy-start.1) | copy-done | bytes 8388632
  96.4 2.4 %output_0_0.1 = (bf16[96,1536]{1,0:T(8,128)(2,1)S(1)}, bf16[96,1536]{1,0:T(8,128)(2,1)S(1)}) custom-call(s32[4]{0:T(128)S(1)} %pad_add_fusion.refs_0_, bf16[48,2048]{1,0:T(8,128)(2,1)S(1)} %get-tuple-element.120.refs_1_, bf16[48,2048]{1,0:T(8,128)(2,1)S(1)} %collective-permute-done.22.refs_2_, bf16[48,2048]{1,0:T(8,128)(2,1)S(1)} %collective-permute-done.23.refs_3_, ...), custom_call_target="tpu_custom_call" | custom-call | flops 1000 | bytes 1000 | tf_op jit(solution)/shard_map/output_0_0/pallas_call | solution.py:41
  98.8 1.6 %collective-permute-start.25 = (bf16[96,1536]{1,0:T(8,128)(2,1)S(1)}, bf16[96,1536]{1,0:T(8,128)(2,1)S(1)}, u32[]{:S(2)}, u32[]{:S(2)}) collective-permute-start(bf16[96,1536]{1,0:T(8,128)(2,1)S(1)} %get-tuple-element.117), channel_id=1, source_target_pairs={{0,1},{1,0},{2,3},{3,2},{4,5},{5,4},{6,7},{7,6},{8,9},{9,8},{10,11... | collective-permute-start | bytes 884744 | tf_op jit(solution)/shard_map/ppermute | solution.py:433
  100.4 0.6 pad_maximum_fusion.2
  101.1 0.6 pad_maximum_fusion.3
  101.7 1.2 output_0_1.1
  102.9 0.5 collective-permute-start.30
  103.6 5.0 %collective-permute-done.25 = bf16[96,1536]{1,0:T(8,128)(2,1)S(1)} collective-permute-done((bf16[96,1536]{1,0:T(8,128)(2,1)S(1)}, bf16[96,1536]{1,0:T(8,128)(2,1)S(1)}, u32[]{:S(2)}, u32[]{:S(2)}) %collective-permute-start.25) | collective-permute-done | bytes 294944 | tf_op jit(solution)/shard_map/ppermute | solution.py:433
  108.7 1.0 collective-permute-done.30
  109.7 2.6 %collective-permute-start.26 = (bf16[48,1536]{1,0:T(8,128)(2,1)S(1)}, bf16[48,1536]{1,0:T(8,128)(2,1)S(1)}, u32[]{:S(2)}, u32[]{:S(2)}) collective-permute-start(bf16[48,1536]{1,0:T(8,128)(2,1)S(1)} %slice.63), channel_id=1, source_target_pairs={{0,2},{1,3},{2,0},{3,1},{4,6},{5,7},{6,4},{7,5},{8,10},{9,11},{10,... | collective-permute-start | bytes 442376 | tf_op jit(solution)/shard_map/ppermute | solution.py:433
  112.3 3.2 %output_1_0.1 = (bf16[160,1536]{1,0:T(8,128)(2,1)S(1)}, bf16[160,1536]{1,0:T(8,128)(2,1)S(1)}) custom-call(s32[4]{0:T(128)S(1)} %pad_add_fusion.refs_0_, bf16[80,2048]{1,0:T(8,128)(2,1)S(1)} %get-tuple-element.125.refs_1_, bf16[80,2048]{1,0:T(8,128)(2,1)S(1)} %collective-permute-done.27.refs_2_, bf16[80,2048]{1,0:T(8,128)(2,1)S(1)} %collective-permute-done.28.refs_3_, ...), custom_call_target="tpu_custom_call" | custom-call | flops 1000 | bytes 1000 | tf_op jit(solution)/shard_map/output_1_0/pallas_call | solution.py:41
  115.5 1.6 %collective-permute-start.32 = (bf16[160,1536]{1,0:T(8,128)(2,1)S(1)}, bf16[160,1536]{1,0:T(8,128)(2,1)S(1)}, u32[]{:S(2)}, u32[]{:S(2)}) collective-permute-start(bf16[160,1536]{1,0:T(8,128)(2,1)S(1)} %get-tuple-element.131), channel_id=1, source_target_pairs={{0,1},{1,0},{2,3},{3,2},{4,5},{5,4},{6,7},{7,6},{8,9},{9,8},{10,11... | collective-permute-start | bytes 1474568 | tf_op jit(solution)/shard_map/ppermute | solution.py:433
  117.6 1.5 output_1_1.1
  119.6 9.7 %collective-permute-done.31 = bf16[48,512]{1,0:T(8,128)(2,1)S(1)} collective-permute-done((bf16[48,512]{1,0:T(8,128)(2,1)S(1)}, bf16[48,512]{1,0:T(8,128)(2,1)S(1)}, u32[]{:S(2)}, u32[]{:S(2)}) %collective-permute-start.31) | collective-permute-done | bytes 49184 | tf_op jit(solution)/shard_map/ppermute | solution.py:433
  129.3 1.5 %collective-permute-done.32 = bf16[160,1536]{1,0:T(8,128)(2,1)S(1)} collective-permute-done((bf16[160,1536]{1,0:T(8,128)(2,1)S(1)}, bf16[160,1536]{1,0:T(8,128)(2,1)S(1)}, u32[]{:S(2)}, u32[]{:S(2)}) %collective-permute-start.32) | collective-permute-done | bytes 491552 | tf_op jit(solution)/shard_map/ppermute | solution.py:433
  131.0 2.0 %collective-permute-start.33 = (bf16[80,1536]{1,0:T(8,128)(2,1)S(1)}, bf16[80,1536]{1,0:T(8,128)(2,1)S(1)}, u32[]{:S(2)}, u32[]{:S(2)}) collective-permute-start(bf16[80,1536]{1,0:T(8,128)(2,1)S(1)} %slice.62), channel_id=1, source_target_pairs={{0,2},{1,3},{2,0},{3,1},{4,6},{5,7},{6,4},{7,5},{8,10},{9,11},{10,... | collective-permute-start | bytes 737288 | tf_op jit(solution)/shard_map/ppermute | solution.py:433
  132.9 0.6 collective-permute-done.34
  133.6 1.3 collective-permute-start.35
  134.9 10.2 %collective-permute-done.33 = bf16[80,1536]{1,0:T(8,128)(2,1)S(1)} collective-permute-done((bf16[80,1536]{1,0:T(8,128)(2,1)S(1)}, bf16[80,1536]{1,0:T(8,128)(2,1)S(1)}, u32[]{:S(2)}, u32[]{:S(2)}) %collective-permute-start.33) | collective-permute-done | bytes 245792 | tf_op jit(solution)/shard_map/ppermute | solution.py:433
  145.2 1.4 collective-permute-done.35
  146.6 0.8 maximum_bitcast_fusion
  (107 shorter events, 7.8 us)
Async XLA Ops:
  0.6 9.2 %copy-start.19 = (bf16[8192]{0:T(1024)(128)(2,1)S(1)}, bf16[8192]{0:T(1024)(128)(2,1)}, u32[]{:S(2)}) copy-start(bf16[8192]{0:T(1024)(128)(2,1)} %param.15) | copy-start | bytes 49156
  0.6 9.1 %copy-start.17 = (bf16[128,8192]{1,0:T(8,128)(2,1)S(1)}, bf16[128,8192]{1,0:T(8,128)(2,1)}, u32[]{:S(2)}) copy-start(bf16[128,8192]{1,0:T(8,128)(2,1)} %param.14) | copy-start | bytes 6291460
  0.7 4.9 %collective-permute-start.1 = (s32[1,128]{1,0:T(1,128)}, s32[1,128]{1,0:T(1,128)S(1)}, u32[]{:S(2)}, u32[]{:S(2)}) collective-permute-start(s32[1,128]{1,0:T(1,128)} %bitcast.31), channel_id=1, source_target_pairs={{0,8},{4,12},{8,0},{12,4},{1,9},{5,13},{9,1},{13,5},{2,10},{6,14},... | collective-permute-start | bytes 1544 | tf_op jit(solution)/shard_map/ppermute | solution.py:74
  5.6 24.1 %collective-permute-start.3 = (bf16[128,2048]{1,0:T(8,128)(2,1)S(1)}, bf16[128,2048]{1,0:T(8,128)(2,1)S(1)}, u32[]{:S(2)}, u32[]{:S(2)}) collective-permute-start(bf16[128,2048]{1,0:T(8,128)(2,1)S(1)} %multiply_convert_fusion.3.refs_1_), channel_id=1, source_target_pairs={{0,4},{4,0},{8,12},{12,8},{1,5},{5,1},{9,13},{13,9},{2,6},{6,2},{1... | collective-permute-start | bytes 1572872 | tf_op jit(solution)/shard_map/ppermute | solution.py:69
  5.6 19.7 %collective-permute-start.4 = (bf16[128,2048]{1,0:T(8,128)(2,1)S(1)}, bf16[128,2048]{1,0:T(8,128)(2,1)}, u32[]{:S(2)}, u32[]{:S(2)}) collective-permute-start(bf16[128,2048]{1,0:T(8,128)(2,1)S(1)} %multiply_convert_fusion.3.refs_1_), channel_id=1, source_target_pairs={{0,8},{4,12},{8,0},{12,4},{1,9},{5,13},{9,1},{13,5},{2,10},{6,14},... | collective-permute-start | bytes 1572872 | tf_op jit(solution)/shard_map/ppermute | solution.py:74
  9.2 2.0 %collective-permute-start.5 = (bf16[64,2048]{1,0:T(8,128)(2,1)S(1)}, bf16[64,2048]{1,0:T(8,128)(2,1)S(1)}, u32[]{:S(2)}, u32[]{:S(2)}) collective-permute-start(bf16[64,2048]{1,0:T(8,128)(2,1)S(1)} %get-tuple-element.78), channel_id=1, source_target_pairs={{0,4},{4,0},{8,12},{12,8},{1,5},{5,1},{9,13},{13,9},{2,6},{6,2},{1... | collective-permute-start | bytes 786440 | tf_op jit(solution)/shard_map/ppermute | solution.py:69
  9.5 1.7 %collective-permute-start.6 = (bf16[64,2048]{1,0:T(8,128)(2,1)S(1)}, bf16[64,2048]{1,0:T(8,128)(2,1)S(1)}, u32[]{:S(2)}, u32[]{:S(2)}) collective-permute-start(bf16[64,2048]{1,0:T(8,128)(2,1)S(1)} %get-tuple-element.79), channel_id=1, source_target_pairs={{0,4},{4,0},{8,12},{12,8},{1,5},{5,1},{9,13},{13,9},{2,6},{6,2},{1... | collective-permute-start | bytes 786440 | tf_op jit(solution)/shard_map/ppermute | solution.py:69
  11.2 16.0 %copy-start.21 = (s32[128]{0:T(128)S(1)}, s32[128]{0:T(128)}, u32[]{:S(2)}) copy-start(s32[128]{0:T(128)} %param.23) | copy-start | bytes 1540
  17.1 3.3 %copy-start.2 = (bf16[2048,2048]{1,0:T(8,128)(2,1)}, bf16[2048,2048]{1,0:T(8,128)(2,1)S(1)}, u32[]{:S(2)}) copy-start(bf16[2048,2048]{1,0:T(8,128)(2,1)S(1)} %get-tuple-element.93.refs_7_) | copy-start | bytes 25165828
  20.4 1.3 copy-start.7
  21.8 1.4 copy-start.9
  23.2 1.1 copy-start.11
  24.3 1.1 copy-start.13
  25.4 4.3 %collective-permute-start.7 = (bf16[128,2048]{1,0:T(8,128)(2,1)}, bf16[128,2048]{1,0:T(8,128)(2,1)}, u32[]{:S(2)}, u32[]{:S(2)}) collective-permute-start(bf16[128,2048]{1,0:T(8,128)(2,1)} %collective-permute-done.4.refs_3_), channel_id=1, source_target_pairs={{0,4},{4,0},{8,12},{12,8},{1,5},{5,1},{9,13},{13,9},{2,6},{6,2},{1... | collective-permute-start | bytes 1572872 | tf_op jit(solution)/shard_map/ppermute | solution.py:69
  25.6 24.9 %collective-permute-start.12 = (bf16[128,2048]{1,0:T(8,128)(2,1)}, bf16[128,2048]{1,0:T(8,128)(2,1)}, u32[]{:S(2)}, u32[]{:S(2)}) collective-permute-start(bf16[128,2048]{1,0:T(8,128)(2,1)} %get-tuple-element.91), channel_id=1, source_target_pairs={{0,8},{4,12},{8,0},{12,4},{1,9},{5,13},{9,1},{13,5},{2,10},{6,14},... | collective-permute-start | bytes 1572872 | tf_op jit(solution)/shard_map/ppermute | solution.py:74
  25.9 24.7 %collective-permute-start.13 = (bf16[128,2048]{1,0:T(8,128)(2,1)}, bf16[128,2048]{1,0:T(8,128)(2,1)}, u32[]{:S(2)}, u32[]{:S(2)}) collective-permute-start(bf16[128,2048]{1,0:T(8,128)(2,1)} %get-tuple-element.92), channel_id=1, source_target_pairs={{0,12},{4,8},{8,4},{12,0},{1,13},{5,9},{9,5},{13,1},{2,14},{6,10},... | collective-permute-start | bytes 1572872 | tf_op jit(solution)/shard_map/ppermute | solution.py:74
  27.2 1.3 collective-permute-start
  28.6 1.1 collective-permute-start.2
  29.7 1.6 %copy-start.8 = (bf16[512,2048]{1,0:T(8,128)(2,1)S(1)}, bf16[512,2048]{1,0:T(8,128)(2,1)}, u32[]{:S(2)}) copy-start(bf16[512,2048]{1,0:T(8,128)(2,1)} %copy-done.7) | copy-start | bytes 6291460
  31.3 1.6 %copy-start.10 = (bf16[512,2048]{1,0:T(8,128)(2,1)S(1)}, bf16[512,2048]{1,0:T(8,128)(2,1)}, u32[]{:S(2)}) copy-start(bf16[512,2048]{1,0:T(8,128)(2,1)} %copy-done.9) | copy-start | bytes 6291460
  32.9 13.1 %copy-start.12 = (f32[128,2560]{1,0:T(8,128)S(1)}, f32[128,2560]{1,0:T(8,128)}, u32[]{:S(2)}) copy-start(f32[128,2560]{1,0:T(8,128)} %copy-done.11) | copy-start | bytes 3932164
  32.9 13.1 %copy-start.14 = (f32[128,2560]{1,0:T(8,128)S(1)}, f32[128,2560]{1,0:T(8,128)}, u32[]{:S(2)}) copy-start(f32[128,2560]{1,0:T(8,128)} %copy-done.13) | copy-start | bytes 3932164
  32.9 17.7 %slice-start.2 = ((s8[8388608]{0:T(1024)(128)(4,1)}), s8[4194304]{0:T(1024)(128)(4,1)S(1)}, s32[]{:S(2)}) async-start(s8[8388608]{0:T(1024)(128)(4,1)} %bitcast.21), calls=%async_computation.2 | async-start | bytes 8388608
  36.6 6.4 %collective-permute-start.8 = (f32[32,512]{1,0:T(8,128)S(1)}, f32[32,512]{1,0:T(8,128)S(1)}, u32[]{:S(2)}, u32[]{:S(2)}) collective-permute-start(f32[32,512]{1,0:T(8,128)S(1)} %get-tuple-element.84.refs_1_), channel_id=1, source_target_pairs={{0,1},{1,2},{2,3},{3,0},{4,5},{5,6},{6,7},{7,4},{8,9},{9,10},{10,1... | collective-permute-start | bytes 196616 | tf_op jit(solution)/shard_map/ppermute | solution.py:514
  38.3 7.5 %collective-permute-start.9 = (f32[32,512]{1,0:T(8,128)S(1)}, f32[32,512]{1,0:T(8,128)S(1)}, u32[]{:S(2)}, u32[]{:S(2)}) collective-permute-start(f32[32,512]{1,0:T(8,128)S(1)} %get-tuple-element.84.refs_1_), channel_id=1, source_target_pairs={{0,2},{1,3},{2,0},{3,1},{4,6},{5,7},{6,4},{7,5},{8,10},{9,11},{10,... | collective-permute-start | bytes 196616 | tf_op jit(solution)/shard_map/ppermute | solution.py:514
  40.9 5.1 %collective-permute-start.10 = (f32[32,512]{1,0:T(8,128)S(1)}, f32[32,512]{1,0:T(8,128)S(1)}, u32[]{:S(2)}, u32[]{:S(2)}) collective-permute-start(f32[32,512]{1,0:T(8,128)S(1)} %get-tuple-element.84.refs_1_), channel_id=1, source_target_pairs={{0,3},{1,0},{2,1},{3,2},{4,7},{5,4},{6,5},{7,6},{8,11},{9,8},{10,9... | collective-permute-start | bytes 196616 | tf_op jit(solution)/shard_map/ppermute | solution.py:514
  46.0 4.6 %slice-start.3 = ((s8[8388608]{0:T(1024)(128)(4,1)}), s8[4194304]{0:T(1024)(128)(4,1)S(1)}, s32[]{:S(2)}) async-start(s8[8388608]{0:T(1024)(128)(4,1)} %bitcast.21), calls=%async_computation.3 | async-start | bytes 8388608
  48.4 2.1 %copy-start.3 = (bf16[128,2,64,128]{3,2,1,0:T(8,128)(2,1)}, bf16[128,2,64,128]{3,2,1,0:T(8,128)(2,1)S(1)}, u32[]{:S(2)}) copy-start(bf16[128,2,64,128]{3,2,1,0:T(8,128)(2,1)S(1)} %get-tuple-element.107.refs_7_) | copy-start | bytes 12582916
  50.5 4.5 %copy-start.16 = (bf16[128,2560]{1,0:T(8,128)(2,1)}, bf16[128,2560]{1,0:T(8,128)(2,1)S(1)}, u32[]{:S(2)}) copy-start(bf16[128,2560]{1,0:T(8,128)(2,1)S(1)} %get-tuple-element.89) | copy-start | bytes 1966084
  50.6 9.4 %copy-start.18 = (bf16[128,8192]{1,0:T(8,128)(2,1)S(1)}, bf16[128,8192]{1,0:T(8,128)(2,1)}, u32[]{:S(2)}) copy-start(bf16[128,8192]{1,0:T(8,128)(2,1)} %param.14) | copy-start | bytes 6291460
  55.0 2.0 %copy-start.5 = (bf16[128,2,64,128]{3,2,1,0:T(8,128)(2,1)}, bf16[128,2,64,128]{3,2,1,0:T(8,128)(2,1)S(1)}, u32[]{:S(2)}) copy-start(bf16[128,2,64,128]{3,2,1,0:T(8,128)(2,1)S(1)} %get-tuple-element.108.refs_8_) | copy-start | bytes 12582916
  57.0 1.9 %collective-permute-start.15 = (bf16[48,1024]{1,0:T(8,128)(2,1)S(1)}, bf16[48,1024]{1,0:T(8,128)(2,1)S(1)}, u32[]{:S(2)}, u32[]{:S(2)}) collective-permute-start(bf16[48,1024]{1,0:T(8,128)(2,1)S(1)} %get-tuple-element.98), channel_id=1, source_target_pairs={{0,4},{4,0},{8,12},{12,8},{1,5},{5,1},{9,13},{13,9},{2,6},{6,2},{1... | collective-permute-start | bytes 294920 | tf_op jit(solution)/shard_map/ppermute | solution.py:69
  57.4 1.4 collective-permute-start.14
  57.5 1.4 collective-permute-start.16
  59.6 8.5 %collective-permute-start.17 = (bf16[48,2560]{1,0:T(8,128)(2,1)}, bf16[48,2560]{1,0:T(8,128)(2,1)}, u32[]{:S(2)}, u32[]{:S(2)}) collective-permute-start(bf16[48,2560]{1,0:T(8,128)(2,1)} %add_convert_fusion.1), channel_id=1, source_target_pairs={{0,8},{4,12},{8,0},{12,4},{1,9},{5,13},{9,1},{13,5},{2,10},{6,14},... | collective-permute-start | bytes 737288 | tf_op jit(solution)/shard_map/ppermute | solution.py:74
  60.4 6.3 %copy-start.20 = (s32[128]{0:T(128)S(1)}, s32[128]{0:T(128)}, u32[]{:S(2)}) copy-start(s32[128]{0:T(128)} %param.22) | copy-start | bytes 1540
  65.1 0.9 copy-start.15
  66.1 2.0 %collective-permute-start.20 = (bf16[80,512]{1,0:T(8,128)(2,1)S(1)}, bf16[80,512]{1,0:T(8,128)(2,1)S(1)}, u32[]{:S(2)}, u32[]{:S(2)}) collective-permute-start(bf16[80,512]{1,0:T(8,128)(2,1)S(1)} %get-tuple-element.105), channel_id=1, source_target_pairs={{0,4},{4,0},{8,12},{12,8},{1,5},{5,1},{9,13},{13,9},{2,6},{6,2},{1... | collective-permute-start | bytes 245768 | tf_op jit(solution)/shard_map/ppermute | solution.py:69
  66.1 2.0 %collective-permute-start.19 = (bf16[80,1024]{1,0:T(8,128)(2,1)}, bf16[80,1024]{1,0:T(8,128)(2,1)S(1)}, u32[]{:S(2)}, u32[]{:S(2)}) collective-permute-start(bf16[80,1024]{1,0:T(8,128)(2,1)} %get-tuple-element.104), channel_id=1, source_target_pairs={{0,4},{4,0},{8,12},{12,8},{1,5},{5,1},{9,13},{13,9},{2,6},{6,2},{1... | collective-permute-start | bytes 491528 | tf_op jit(solution)/shard_map/ppermute | solution.py:69
  66.6 1.6 %collective-permute-start.18 = (bf16[80,1024]{1,0:T(8,128)(2,1)}, bf16[80,1024]{1,0:T(8,128)(2,1)S(1)}, u32[]{:S(2)}, u32[]{:S(2)}) collective-permute-start(bf16[80,1024]{1,0:T(8,128)(2,1)} %get-tuple-element.103), channel_id=1, source_target_pairs={{0,4},{4,0},{8,12},{12,8},{1,5},{5,1},{9,13},{13,9},{2,6},{6,2},{1... | collective-permute-start | bytes 491528 | tf_op jit(solution)/shard_map/ppermute | solution.py:69
  66.9 4.7 %collective-permute-start.11 = (bf16[128,2560]{1,0:T(8,128)(2,1)}, bf16[128,2560]{1,0:T(8,128)(2,1)S(1)}, u32[]{:S(2)}, u32[]{:S(2)}) collective-permute-start(bf16[128,2560]{1,0:T(8,128)(2,1)} %copy-done.16), channel_id=1, source_target_pairs={{0,4},{4,0},{8,12},{12,8},{1,5},{5,1},{9,13},{13,9},{2,6},{6,2},{1... | collective-permute-start | bytes 1966088 | tf_op jit(solution)/shard_map/ppermute | solution.py:69
  69.4 14.6 %collective-permute-start.21 = (bf16[80,2560]{1,0:T(8,128)(2,1)S(1)}, bf16[80,2560]{1,0:T(8,128)(2,1)S(1)}, u32[]{:S(2)}, u32[]{:S(2)}) collective-permute-start(bf16[80,2560]{1,0:T(8,128)(2,1)S(1)} %add_convert_fusion), channel_id=1, source_target_pairs={{0,8},{4,12},{8,0},{12,4},{1,9},{5,13},{9,1},{13,5},{2,10},{6,14},... | collective-permute-start | bytes 1228808 | tf_op jit(solution)/shard_map/ppermute | solution.py:74
  71.6 2.2 %copy-start.4 = (bf16[128,2,64,128]{3,2,1,0:T(8,128)(2,1)S(1)}, bf16[128,2,64,128]{3,2,1,0:T(8,128)(2,1)}, u32[]{:S(2)}) copy-start(bf16[128,2,64,128]{3,2,1,0:T(8,128)(2,1)} %copy-done.3) | copy-start | bytes 12582916
  73.7 2.2 %copy-start.6 = (bf16[128,2,64,128]{3,2,1,0:T(8,128)(2,1)S(1)}, bf16[128,2,64,128]{3,2,1,0:T(8,128)(2,1)}, u32[]{:S(2)}) copy-start(bf16[128,2,64,128]{3,2,1,0:T(8,128)(2,1)} %copy-done.5) | copy-start | bytes 12582916
  80.7 3.3 %copy-start = (bf16[2048,2048]{1,0:T(8,128)(2,1)}, bf16[2048,2048]{1,0:T(8,128)(2,1)S(1)}, u32[]{:S(2)}) copy-start(bf16[2048,2048]{1,0:T(8,128)(2,1)S(1)} %get-tuple-element.115.refs_5_) | copy-start | bytes 25165828
  84.0 6.8 %collective-permute-start.23 = (bf16[48,2048]{1,0:T(8,128)(2,1)S(1)}, bf16[48,2048]{1,0:T(8,128)(2,1)S(1)}, u32[]{:S(2)}, u32[]{:S(2)}) collective-permute-start(bf16[48,2048]{1,0:T(8,128)(2,1)S(1)} %get-tuple-element.120.refs_1_), channel_id=1, source_target_pairs={{0,8},{4,12},{8,0},{12,4},{1,9},{5,13},{9,1},{13,5},{2,10},{6,14},... | collective-permute-start | bytes 589832 | tf_op jit(solution)/shard_map/ppermute | solution.py:74
  90.7 2.3 %collective-permute-start.22 = (bf16[48,2048]{1,0:T(8,128)(2,1)S(1)}, bf16[48,2048]{1,0:T(8,128)(2,1)S(1)}, u32[]{:S(2)}, u32[]{:S(2)}) collective-permute-start(bf16[48,2048]{1,0:T(8,128)(2,1)S(1)} %get-tuple-element.120.refs_1_), channel_id=1, source_target_pairs={{0,4},{4,0},{8,12},{12,8},{1,5},{5,1},{9,13},{13,9},{2,6},{6,2},{1... | collective-permute-start | bytes 589832 | tf_op jit(solution)/shard_map/ppermute | solution.py:69
  90.8 2.2 %collective-permute-start.24 = (bf16[48,2048]{1,0:T(8,128)(2,1)S(1)}, bf16[48,2048]{1,0:T(8,128)(2,1)S(1)}, u32[]{:S(2)}, u32[]{:S(2)}) collective-permute-start(bf16[48,2048]{1,0:T(8,128)(2,1)S(1)} %collective-permute-done.23.refs_3_), channel_id=1, source_target_pairs={{0,4},{4,0},{8,12},{12,8},{1,5},{5,1},{9,13},{13,9},{2,6},{6,2},{1... | collective-permute-start | bytes 589832 | tf_op jit(solution)/shard_map/ppermute | solution.py:69
  91.3 12.2 %collective-permute-start.28 = (bf16[80,2048]{1,0:T(8,128)(2,1)S(1)}, bf16[80,2048]{1,0:T(8,128)(2,1)S(1)}, u32[]{:S(2)}, u32[]{:S(2)}) collective-permute-start(bf16[80,2048]{1,0:T(8,128)(2,1)S(1)} %get-tuple-element.125.refs_1_), channel_id=1, source_target_pairs={{0,8},{4,12},{8,0},{12,4},{1,9},{5,13},{9,1},{13,5},{2,10},{6,14},... | collective-permute-start | bytes 983048 | tf_op jit(solution)/shard_map/ppermute | solution.py:74
  93.0 3.4 %copy-start.1 = (bf16[2048,2048]{1,0:T(8,128)(2,1)S(1)}, bf16[2048,2048]{1,0:T(8,128)(2,1)}, u32[]{:S(2)}) copy-start(bf16[2048,2048]{1,0:T(8,128)(2,1)} %copy-done) | copy-start | bytes 25165828
  96.4 15.9 %slice-start = ((s8[8388608]{0:T(1024)(128)(4,1)}), s8[4194304]{0:T(1024)(128)(4,1)S(1)}, s32[]{:S(2)}) async-start(s8[8388608]{0:T(1024)(128)(4,1)} %bitcast.19), calls=%async_computation | async-start | bytes 8388608
  98.8 9.8 %collective-permute-start.25 = (bf16[96,1536]{1,0:T(8,128)(2,1)S(1)}, bf16[96,1536]{1,0:T(8,128)(2,1)S(1)}, u32[]{:S(2)}, u32[]{:S(2)}) collective-permute-start(bf16[96,1536]{1,0:T(8,128)(2,1)S(1)} %get-tuple-element.117), channel_id=1, source_target_pairs={{0,1},{1,0},{2,3},{3,2},{4,5},{5,4},{6,7},{7,6},{8,9},{9,8},{10,11... | collective-permute-start | bytes 884744 | tf_op jit(solution)/shard_map/ppermute | solution.py:433
  101.7 10.6 %slice-start.1 = ((s8[8388608]{0:T(1024)(128)(4,1)}), s8[4194304]{0:T(1024)(128)(4,1)S(1)}, s32[]{:S(2)}) async-start(s8[8388608]{0:T(1024)(128)(4,1)} %bitcast.19), calls=%async_computation.1 | async-start | bytes 8388608
  102.9 9.4 %collective-permute-start.27 = (bf16[80,2048]{1,0:T(8,128)(2,1)S(1)}, bf16[80,2048]{1,0:T(8,128)(2,1)S(1)}, u32[]{:S(2)}, u32[]{:S(2)}) collective-permute-start(bf16[80,2048]{1,0:T(8,128)(2,1)S(1)} %get-tuple-element.125.refs_1_), channel_id=1, source_target_pairs={{0,4},{4,0},{8,12},{12,8},{1,5},{5,1},{9,13},{13,9},{2,6},{6,2},{1... | collective-permute-start | bytes 983048 | tf_op jit(solution)/shard_map/ppermute | solution.py:69
  102.9 6.7 %collective-permute-start.30 = (bf16[96,512]{1,0:T(8,128)(2,1)S(1)}, bf16[96,512]{1,0:T(8,128)(2,1)S(1)}, u32[]{:S(2)}, u32[]{:S(2)}) collective-permute-start(bf16[96,512]{1,0:T(8,128)(2,1)S(1)} %get-tuple-element.128), channel_id=1, source_target_pairs={{0,1},{1,0},{2,3},{3,2},{4,5},{5,4},{6,7},{7,6},{8,9},{9,8},{10,11... | collective-permute-start | bytes 294920 | tf_op jit(solution)/shard_map/ppermute | solution.py:433
  103.5 8.8 %collective-permute-start.29 = (bf16[80,2048]{1,0:T(8,128)(2,1)S(1)}, bf16[80,2048]{1,0:T(8,128)(2,1)S(1)}, u32[]{:S(2)}, u32[]{:S(2)}) collective-permute-start(bf16[80,2048]{1,0:T(8,128)(2,1)S(1)} %collective-permute-done.28.refs_3_), channel_id=1, source_target_pairs={{0,4},{4,0},{8,12},{12,8},{1,5},{5,1},{9,13},{13,9},{2,6},{6,2},{1... | collective-permute-start | bytes 983048 | tf_op jit(solution)/shard_map/ppermute | solution.py:69
  109.7 9.9 %collective-permute-start.26 = (bf16[48,1536]{1,0:T(8,128)(2,1)S(1)}, bf16[48,1536]{1,0:T(8,128)(2,1)S(1)}, u32[]{:S(2)}, u32[]{:S(2)}) collective-permute-start(bf16[48,1536]{1,0:T(8,128)(2,1)S(1)} %slice.63), channel_id=1, source_target_pairs={{0,2},{1,3},{2,0},{3,1},{4,6},{5,7},{6,4},{7,5},{8,10},{9,11},{10,... | collective-permute-start | bytes 442376 | tf_op jit(solution)/shard_map/ppermute | solution.py:433
  115.5 15.3 %collective-permute-start.32 = (bf16[160,1536]{1,0:T(8,128)(2,1)S(1)}, bf16[160,1536]{1,0:T(8,128)(2,1)S(1)}, u32[]{:S(2)}, u32[]{:S(2)}) collective-permute-start(bf16[160,1536]{1,0:T(8,128)(2,1)S(1)} %get-tuple-element.131), channel_id=1, source_target_pairs={{0,1},{1,0},{2,3},{3,2},{4,5},{5,4},{6,7},{7,6},{8,9},{9,8},{10,11... | collective-permute-start | bytes 1474568 | tf_op jit(solution)/shard_map/ppermute | solution.py:433
  117.2 12.1 %collective-permute-start.31 = (bf16[48,512]{1,0:T(8,128)(2,1)S(1)}, bf16[48,512]{1,0:T(8,128)(2,1)S(1)}, u32[]{:S(2)}, u32[]{:S(2)}) collective-permute-start(bf16[48,512]{1,0:T(8,128)(2,1)S(1)} %slice.65), channel_id=1, source_target_pairs={{0,2},{1,3},{2,0},{3,1},{4,6},{5,7},{6,4},{7,5},{8,10},{9,11},{10,... | collective-permute-start | bytes 147464 | tf_op jit(solution)/shard_map/ppermute | solution.py:433
  119.1 14.5 %collective-permute-start.34 = (bf16[160,512]{1,0:T(8,128)(2,1)S(1)}, bf16[160,512]{1,0:T(8,128)(2,1)S(1)}, u32[]{:S(2)}, u32[]{:S(2)}) collective-permute-start(bf16[160,512]{1,0:T(8,128)(2,1)S(1)} %get-tuple-element.134), channel_id=1, source_target_pairs={{0,1},{1,0},{2,3},{3,2},{4,5},{5,4},{6,7},{7,6},{8,9},{9,8},{10,11... | collective-permute-start | bytes 491528 | tf_op jit(solution)/shard_map/ppermute | solution.py:433
  131.0 14.2 %collective-permute-start.33 = (bf16[80,1536]{1,0:T(8,128)(2,1)S(1)}, bf16[80,1536]{1,0:T(8,128)(2,1)S(1)}, u32[]{:S(2)}, u32[]{:S(2)}) collective-permute-start(bf16[80,1536]{1,0:T(8,128)(2,1)S(1)} %slice.62), channel_id=1, source_target_pairs={{0,2},{1,3},{2,0},{3,1},{4,6},{5,7},{6,4},{7,5},{8,10},{9,11},{10,... | collective-permute-start | bytes 737288 | tf_op jit(solution)/shard_map/ppermute | solution.py:433
  133.6 12.9 %collective-permute-start.35 = (bf16[80,512]{1,0:T(8,128)(2,1)S(1)}, bf16[80,512]{1,0:T(8,128)(2,1)S(1)}, u32[]{:S(2)}, u32[]{:S(2)}) collective-permute-start(bf16[80,512]{1,0:T(8,128)(2,1)S(1)} %slice.64), channel_id=1, source_target_pairs={{0,2},{1,3},{2,0},{3,1},{4,6},{5,7},{6,4},{7,5},{8,10},{9,11},{10,... | collective-permute-start | bytes 245768 | tf_op jit(solution)/shard_map/ppermute | solution.py:433

commit v5 on v4

v5 whole, which is shorter than its diff:
```python
import functools
import math

import jax
import jax.numpy as jnp
from jax import lax
from jax.experimental import pallas as pl
from jax.experimental.pallas import tpu as pltpu
from jax.sharding import PartitionSpec as P

epsilon = 1e-05
adapter_scale = 0.5
rope_base = 500000.0
masked_score = -1e30


VMEM = pl.BlockSpec(memory_space=pltpu.VMEM)
HBM = pl.BlockSpec(memory_space=pltpu.HBM)
SMEM = pl.BlockSpec(memory_space=pltpu.SMEM)


def local_call(kernel, name, operands, outs, scratch, far=(), mib=16):
    counts = (len(operands), len(far), len(outs), len(scratch))

    def body(*refs):
        groups, at = [], 0
        for n in counts:
            groups.append(refs[at : at + n])
            at += n
        kernel(*groups)

    return pl.pallas_call(
        body,
        in_specs=[spec for _, spec in operands] + [HBM] * len(far),
        out_specs=[VMEM] * len(outs),
        out_shape=outs,
        scratch_shapes=scratch,
        compiler_params=pltpu.CompilerParams(vmem_limit_bytes=mib * 1024 * 1024),
        cost_estimate=pl.CostEstimate(flops=1000, bytes_accessed=1000, transcendentals=0),
        name=name,
    )(
        *[x for x, _ in operands],
        *[pltpu.with_memory_space_constraint(x, pltpu.HBM) for x in far],
    )


def held(x):
    return pltpu.VMEM(x.shape, x.dtype)


def in_vmem(arrays):
    return [(x, VMEM) for x in arrays]


def shaped(shape, dtype=jnp.float32):
    return jax.ShapeDtypeStruct(shape, dtype)


def after(x, *earlier):
    return lax.optimization_barrier((x, *earlier))[0]


def core_swap(x, pool_count):
    return lax.ppermute(x, "pool", [(p, p ^ 1) for p in range(pool_count)])


def chip_move(x, pool_count, d, e=0):
    chips = pool_count // 2
    return lax.ppermute(
        x,
        "pool",
        [(p, (p // 2 + d) % chips * 2 + ((p % 2) ^ e)) for p in range(pool_count)],
    )


def tp_swap(x, tp_count, step):
    return lax.ppermute(x, "tp", [(z, z ^ step) for z in range(tp_count)])


def shrink(ids, blocks, query_down, value_down):
    slots, _ = query_down.shape
    rows = blocks[0].shape[0]
    adapters = slots // 16

    def kernel(ins, far, outs, scratch):
        ids, *blocks = ins
        (out,) = outs
        *tables, sems = scratch
        copies = [
            pltpu.make_async_copy(source, table, sems.at[i])
            for i, (source, table) in enumerate(zip(far, tables))
        ]
        for copy in copies:
            copy.start()
        for at, table in enumerate(tables):
            copies[at].wait()
            for first in range(0, len(blocks), 2):
                x = jnp.concatenate([b[...] for b in blocks[first : first + 2]], axis=0)
                span = slice(first * rows, (first + 2) * rows)
                label = ids[:, span].reshape(1, 1, 2 * rows)
                chosen = lax.broadcasted_iota(jnp.int32, (adapters, 1, 2 * rows), 0) == label
                terms = lax.dot_general(
                    table[...], x, (((1,), (1,)), ((), ())), preferred_element_type=jnp.float32
                ).reshape(adapters, 16, 2 * rows)
                out[at * 16 : (at + 1) * 16, span] = jnp.sum(
                    jnp.where(chosen, terms, 0.0), axis=0
                )

    return local_call(
        kernel,
        "shrink",
        in_vmem([ids, *blocks]),
        [shaped((32, rows * len(blocks)))],
        [held(query_down), held(value_down), pltpu.SemaphoreType.DMA((2,))],
        far=[query_down, value_down],
    )[0]


def spread_lows(low, ids, adapters):
    total = ids.shape[1]
    low = low.astype(jnp.bfloat16).astype(jnp.float32) * adapter_scale
    chosen = lax.broadcasted_iota(jnp.int32, (adapters, 1, total), 0) == ids.reshape(1, 1, total)
    return [
        jnp.where(chosen, low[at : at + 16][None], 0.0)
        .reshape(adapters * 16, total)
        .T.astype(jnp.bfloat16)
        for at in (0, 16)
    ]


def columns_at(start, width):
    return pl.ds(pl.multiple_of(start, width), width)


def project(name, kinds, span, ids, lows, blocks, far):
    wq, wk, wv, uq, uv = far
    rows, depth = blocks[0].shape
    wide, kv, slots = wq.shape[1], wk.shape[1], uq.shape[0]
    tile = 2 * kv
    steps = wide // tile
    total = span[1]
    outs = []
    for _, count, dtype, split in kinds:
        outs += [shaped((count, tile), dtype)] * (steps + 1) if split else [
            shaped((count, wide + tile), dtype)
        ]

    def kernel(ins, far, outs, scratch):
        ids, *ins = ins
        low_refs, blocks = ins[: len(lows)], ins[len(lows) :]
        wq, wk, wv, uq, uv, xs, spread_q, spread_v, wide_sems, sems = scratch
        narrow = [
            pltpu.make_async_copy(far[i], near, sems.at[at])
            for at, (i, near) in enumerate(((1, wk), (2, wv), (4, uv)))
        ]

        def wide_copies(i):
            columns = columns_at(i * tile, tile)
            return [
                pltpu.make_async_copy(
                    far[which].at[:, columns], near.at[:, columns], wide_sems.at[at, i]
                )
                for at, (which, near) in enumerate(((0, wq), (3, uq)))
            ]

        for copy in narrow:
            copy.start()
        for i in range(steps):
            for copy in wide_copies(i):
                copy.start()

        at = 0
        for block in blocks:
            xs[at : at + block.shape[0], :] = block[...]
            at += block.shape[0]
        low = low_refs[0][:, span[0] : span[0] + total]
        for other in low_refs[1:]:
            low = low + other[:, span[0] : span[0] + total]
        spread_q[...], spread_v[...] = spread_lows(
            low, ids[:, span[0] : span[0] + total], slots // 16
        )

        def write(acc, i, start, width):
            at = 0
            for first, count, dtype, split in kinds:
                to = start if split else i * tile + start
                outs[at + i if split else at][:, to : to + width] = acc[
                    first : first + count
                ].astype(dtype)
                at += steps + 1 if split else 1

        def sums(w, spread=None, u=None):
            acc = jnp.dot(xs[...], w, preferred_element_type=jnp.float32)
            if u is not None:
                acc = acc + jnp.dot(spread[...], u, preferred_element_type=jnp.float32)
            return acc

        narrow[0].wait()
        write(sums(wk[...]), steps, 0, kv)
        narrow[1].wait()
        narrow[2].wait()
        write(sums(wv[...], spread_v, uv[...]), steps, kv, kv)
        for i in range(steps):
            for copy in wide_copies(i):
                copy.wait()
            columns = slice(i * tile, (i + 1) * tile)
            write(sums(wq[:, columns], spread_q, uq[:, columns]), i, 0, tile)

    spread = pltpu.VMEM((total, slots), jnp.bfloat16)
    return local_call(
        kernel,
        name,
        in_vmem([ids, *lows, *blocks]),
        outs,
        [
            *[held(x) for x in far],
            pltpu.VMEM((total, depth), jnp.bfloat16),
            spread,
            spread,
            pltpu.SemaphoreType.DMA((2, steps)),
            pltpu.SemaphoreType.DMA((3,)),
        ],
        far=far,
        mib=28,
    )


def attend_kernel(first_row, block, count, ins, far, outs, scratch):
    keep, *ins = ins
    swapped, (*moved, scale, cosines, sines, lengths) = ins[:count], ins[count:]
    keys, values, sems = scratch
    out, key_out, value_out = outs
    head = cosines.shape[1]
    rows = out.shape[0]
    _, kv_heads, cache, _ = keys.shape
    heads = out.shape[1] // head
    group = heads // kv_heads
    score_scale = 1.0 / math.sqrt(head)
    sub = 8

    def copies(i):
        to = pl.ds(pl.multiple_of(i * block, block), block)
        at = pl.ds(pl.multiple_of(first_row + i * block, block), block)
        return [
            pltpu.make_async_copy(source.at[at], near.at[to], sems.at[which, i])
            for which, (source, near) in enumerate(zip(far, (keys, values)))
        ]

    for i in range(rows // block):
        for copy in copies(i):
            copy.start()

    column = lax.broadcasted_iota(jnp.int32, (sub, sub * cache), 1)
    start = lax.broadcasted_iota(jnp.int32, (sub, sub * cache), 0) * cache

    @pl.loop(0, rows // block)
    def _(i):
        for copy in copies(i):
            copy.wait()
        attended, new_keys, new_values = [], [], []
        for half in range(block // sub):
            here = pl.ds(pl.multiple_of(i * block + half * sub, sub), sub)
            whole = pl.ds(pl.multiple_of(first_row + i * block + half * sub, sub), sub)
            x = jnp.concatenate([part[whole] for part in swapped], axis=1).astype(jnp.float32)
            x = x + keep[whole]
            for m in moved:
                x = x + m[here].astype(jnp.float32)
            x = x * scale[whole]
            cos, sin = cosines[whole], sines[whole]
            inside = (column >= start) & (column < start + lengths[whole])

            def piece(i):
                return x[:, i * head : (i + 1) * head]

            def turn(v):
                return v * cos + pltpu.roll(v, head // 2, 1) * sin

            for g in range(kv_heads):
                query = jnp.concatenate(
                    [turn(piece(g * group + h)) for h in range(group)], axis=0
                ).astype(jnp.bfloat16)
                new_key = turn(piece(heads + g)).astype(jnp.bfloat16).astype(jnp.float32)
                new_value = piece(heads + kv_heads + g).astype(jnp.bfloat16).astype(jnp.float32)
                k = keys[here, g].reshape(sub * cache, head)
                v = values[here, g].reshape(sub * cache, head)
                scores = (
                    lax.dot_general(
                        query, k, (((1,), (1,)), ((), ())), preferred_element_type=jnp.float32
                    )
                    * score_scale
                )
                own_key = jnp.concatenate([new_key] * group, axis=0)
                own = (
                    jnp.sum(query.astype(jnp.float32) * own_key, axis=1, keepdims=True)
                    * score_scale
                )
                scores = jnp.where(
                    inside[None], scores.reshape(group, sub, sub * cache), masked_score
                ).reshape(group * sub, sub * cache)
                peak = jnp.maximum(jnp.max(scores, axis=1, keepdims=True), own)
                weights = jnp.exp(scores - peak)
                own_weight = jnp.exp(own - peak)
                inverse = 1.0 / (jnp.sum(weights, axis=1, keepdims=True) + own_weight)
                mixed = jnp.dot(weights.astype(jnp.bfloat16), v, preferred_element_type=jnp.float32)
                own_value = jnp.concatenate([new_value] * group, axis=0)
                mixed = (mixed + own_weight * own_value) * inverse
                attended += [mixed[h * sub : (h + 1) * sub] for h in range(group)]
                new_keys.append(new_key)
                new_values.append(new_value)
        r = pl.ds(pl.multiple_of(i * block, block), block)

        def joined(pieces):
            n = len(pieces) * sub // block
            return jnp.concatenate(
                [jnp.concatenate(pieces[j::n], axis=0) for j in range(n)], axis=1
            ).astype(jnp.bfloat16)

        out[r] = joined(attended)
        key_out[r] = joined(new_keys)
        value_out[r] = joined(new_values)


def attend(name, window, keep, swapped, moved, rest, keys, values):
    _, columns = keep.shape
    _, kv_heads, cache, head = keys.shape
    kv_cols = kv_heads * head
    first, part = window
    block = 16
    widths = (columns - 2 * kv_cols, kv_cols, kv_cols)
    near = pltpu.VMEM((part, kv_heads, cache, head), keys.dtype)
    return local_call(
        functools.partial(attend_kernel, first, block, len(swapped)),
        name,
        in_vmem([keep, *swapped, *moved, *rest]),
        [shaped((part, w), jnp.bfloat16) for w in widths],
        [near, near, pltpu.SemaphoreType.DMA((2, part // block))],
        far=[keys, values],
    )


def output_part(name, span, order, blocks, weights):
    rows = blocks[0].shape[0]
    first, columns = span
    depth = weights.shape[0]
    tile = math.gcd(512, columns)
    total = rows * len(blocks)

    def kernel(ins, far, outs, scratch):
        order, *blocks = ins
        keep, send = outs
        held, xs, sems = scratch

        def copy(i):
            return pltpu.make_async_copy(
                far[0].at[:, columns_at(first + i * tile, tile)],
                held.at[:, columns_at(i * tile, tile)],
                sems.at[i],
            )

        for i in range(columns // tile):
            copy(i).start()
        for b, block in enumerate(blocks):
            xs[pl.ds(pl.multiple_of(order[b] * rows, rows), rows), :] = block[...]

        @pl.loop(0, columns // tile)
        def _(i):
            copy(i).wait()
            w = held[:, columns_at(i * tile, tile)]
            acc = jnp.dot(xs[...], w, preferred_element_type=jnp.float32).astype(jnp.bfloat16)
            keep[:, columns_at(i * tile, tile)] = acc[: total // 2]
            send[:, columns_at(i * tile, tile)] = acc[total // 2 :]

    return local_call(
        kernel,
        name,
        [(order, SMEM), *in_vmem(blocks)],
        [shaped((total // 2, columns), jnp.bfloat16)] * 2,
        [
            pltpu.VMEM((depth, columns), weights.dtype),
            pltpu.VMEM((total, depth), jnp.bfloat16),
            pltpu.SemaphoreType.DMA((columns // tile,)),
        ],
        far=[weights],
    )


def reversed_bits(x, count):
    out, bit = 0, 1
    while bit < count:
        out = out * 2 + (x // bit) % 2
        bit *= 2
    return out


def shards(
    tokens,
    input_norm_gain,
    query_matrix,
    key_matrix,
    value_matrix,
    output_matrix,
    rotated_key_cache,
    cached_value_rows,
    cache_length_per_row,
    row_adapter_index,
    query_down_maps,
    query_up_maps,
    value_down_maps,
    value_up_maps,
):
    pool_count = lax.axis_size("pool")
    tp_count = lax.axis_size("tp")
    chips = pool_count // 2
    pool_at = lax.axis_index("pool")
    tp_at = lax.axis_index("tp")
    chip, core = pool_at // 2, pool_at % 2
    rows = tokens.shape[0]
    adapters, rank, piece = query_down_maps.shape
    base = query_matrix.shape[0]
    kv_heads = rotated_key_cache.shape[1]
    head = rotated_key_cache.shape[3]

    def scaled(start, width, tokens=tokens, gain=input_norm_gain, window=(0, rows)):
        x = lax.dynamic_slice(tokens, (window[0], start), (window[1], width)).astype(jnp.float32)
        factor = lax.dynamic_slice_in_dim(gain, start, width, 0).astype(jnp.float32)
        return (x * factor[None, :]).astype(jnp.bfloat16)

    ids = row_adapter_index.reshape(1, rows)
    ids = [ids] + [chip_move(ids, pool_count, d) for d in range(1, chips)]
    first = after(scaled(tp_at * piece, piece), *ids[1:])
    first, tokens_1, gain_1 = lax.optimization_barrier((first, tokens, input_norm_gain))
    same_core = [first] + [chip_move(first, pool_count, d) for d in range(1, chips)]
    ids = [b for x in ids for b in (x, core_swap(x, pool_count))]
    local_ids = jnp.concatenate(ids, axis=1) - pool_at * adapters

    cut = rows // 2
    chunks = [(0, cut), (cut, rows - cut)]
    own = scaled(pool_at * base, base, tokens_1, gain_1)
    partner_at = (pool_at // 2 * 2 + 1 - core) * base
    partner = [
        scaled(partner_at, base, tokens_1, gain_1, (at, rows // 2)) for at in (0, rows // 2)
    ]
    *partner, tokens_2, gain_2 = lax.optimization_barrier((*partner, tokens, input_norm_gain))
    partner = [core_swap(x, pool_count) for x in partner]
    away = {}
    for d in range(1, chips):
        for e in range(2):
            target = (chip + d) % chips * 2 + (core + e) % 2
            away[d, e] = scaled(target * base, base, tokens_2, gain_2)
    remote = [[] for _ in range(chips)]
    for (d, e), x in away.items():
        remote[d].append(chip_move(after(x, *same_core[1:]), pool_count, d, e))
    same_core[1:] = [after(x, *away.values()) for x in same_core[1:]]

    adapter_rows = [b for x in same_core for b in (x, core_swap(x, pool_count))]
    flat_down = [x.reshape(adapters * rank, piece) for x in (query_down_maps, value_down_maps)]
    flat_up = [x.reshape(adapters * rank, x.shape[2]) for x in (query_up_maps, value_up_maps)]
    shrunk = shrink(local_ids, adapter_rows, *flat_down)
    lows = [shrunk] + [
        lax.ppermute(shrunk, "tp", [(i, (i + d) % tp_count) for i in range(tp_count)])
        for d in range(1, tp_count)
    ]
    weights = [query_matrix, key_matrix, value_matrix, *flat_up]

    values = tokens.astype(jnp.float32)
    scale = lax.rsqrt(jnp.mean(values * values, axis=-1, keepdims=True) + epsilon)
    half_dim = head // 2
    frequency = jnp.power(
        jnp.float32(rope_base), jnp.arange(half_dim, dtype=jnp.float32) * (-2.0 / head)
    )
    angles = cache_length_per_row.astype(jnp.float32)[:, None] * frequency[None, :]
    cosines = jnp.concatenate([jnp.cos(angles)] * 2, axis=1)
    sines = jnp.concatenate([-jnp.sin(angles), jnp.sin(angles)], axis=1)
    lengths = cache_length_per_row.reshape(rows, 1)

    own_sums, *own_sends = project(
        "project_own",
        [(0, rows, jnp.float32, False), (rows, rows, jnp.bfloat16, True)],
        (0, 2 * rows),
        local_ids,
        lows,
        [own, *partner],
        weights,
    )
    swapped = [core_swap(x, pool_count) for x in own_sends]
    local_ids = after(local_ids, own_sums)
    moved = [[] for _ in chunks]
    both = None
    for d in range(1, chips):
        if both is not None:
            remote[d][0] = after(remote[d][0], both)
        at = 2 * d * rows
        (keep,) = project(
            f"project_{d}_0",
            [(0, rows, jnp.float32, False)],
            (at, rows),
            local_ids,
            lows,
            remote[d][:1],
            weights,
        )
        sends = project(
            f"project_{d}_1",
            [(first, part, jnp.bfloat16, False) for first, part in chunks],
            (at + rows, rows),
            local_ids,
            lows,
            [after(remote[d][1], keep)],
            weights,
        )
        for c, (first, part) in enumerate(chunks):
            swap = core_swap(sends[c], pool_count)
            if c:
                swap = after(swap, both)
            both = keep[first : first + part] + swap.astype(jnp.float32)
            both = both.astype(jnp.bfloat16)
            moved[c].append(chip_move(both, pool_count, -d))
    share = pool_count // tp_count
    order = []
    for d in range(chips):
        for e in range(2):
            p = (chip - d) % chips * 2 + (core + e) % 2
            order.append(
                reversed_bits(jnp.bitwise_xor(p // share, tp_at), tp_count) * share + p % share
            )
    order = jnp.stack(order).astype(jnp.int32)

    attended, new_keys, new_values = [], [], []
    for c, window in enumerate(chunks):
        out, new_key, new_value = attend(
            f"attend_{c}",
            window,
            own_sums,
            swapped,
            moved[c],
            (scale, cosines, sines, lengths),
            rotated_key_cache,
            cached_value_rows,
        )
        if c + 1 < len(chunks):
            out, *moved[c + 1] = lax.optimization_barrier((out, *moved[c + 1]))
        if c:
            out = after(out, attended[-1][-1])
        attended.append([out] + [chip_move(out, pool_count, d) for d in range(1, chips)])
        new_keys.append(new_key)
        new_values.append(new_value)
    attended[0][0] = after(attended[0][0], *new_keys)

    columns = output_matrix.shape[1]
    layout = [(0, 0, 2), (0, 1, 2), (1, 0, 2), (1, 2, 4), (1, 3, 4)]
    gathered, keeps, sends, products = {}, [], [], []

    def multiply(total):
        c, at, count = layout[len(keeps)]
        if c not in gathered:
            parts = [after(x, total) for x in attended[c]] if c else attended[c]
            gathered[c] = [b for x in parts for b in (x, core_swap(x, pool_count))]
        else:
            gathered[c][0] = after(gathered[c][0], products[-1])
        width = columns // count
        keep, send = output_part(
            f"output_{c}_{at}_{count}", (at * width, width), order, gathered[c], output_matrix
        )
        keeps.append(keep)
        sends.append(send)
        products.append(keep)

    stages = reversed_bits(1, tp_count).bit_length()
    total, got = None, {}
    for slot in range(len(layout) + stages - 1):
        while len(keeps) < min(slot + 2, len(layout)):
            multiply(total)
        for stage in range(stages):
            i = slot - stage
            if not 0 <= i < len(layout):
                continue
            if stage == 0:
                got[i] = tp_swap(sends[i], tp_count, 1)
            earlier = [products[-1]] + ([] if total is None else [total])
            total = keeps[i].astype(jnp.float32) + after(got[i], *earlier).astype(jnp.float32)
            if stage + 1 < stages:
                half = total.shape[0] // 2
                keeps[i] = total[:half]
                got[i] = tp_swap(total[half:].astype(jnp.bfloat16), tp_count, 2 << stage)
            else:
                total = total.astype(jnp.bfloat16)
                keeps[i] = total
    outputs = []
    for c, (_, part) in enumerate(chunks):
        sums = [keeps[i] for i, piece in enumerate(layout) if piece[0] == c]
        outputs.append(
            jnp.concatenate([x.reshape(-1, part, x.shape[1]) for x in sums], axis=2)
        )
    attn_out = jnp.concatenate(outputs, axis=1)
    return (
        attn_out.reshape(-1, attn_out.shape[2]),
        jnp.concatenate(new_keys, axis=0),
        jnp.concatenate(new_values, axis=0),
    )


def solution(mesh):
    return jax.shard_map(
        shards,
        mesh=mesh,
        in_specs=(
            P(("groups", "pool"), None),
            P(),
            P("pool", "tp"),
            P("pool", "tp"),
            P("pool", "tp"),
            P("tp", "pool"),
            P(("groups", "pool"), "tp", None, None),
            P(("groups", "pool"), "tp", None, None),
            P(("groups", "pool")),
            P(("groups", "pool")),
            P("pool", None, "tp"),
            P("pool", None, "tp"),
            P("pool", None, "tp"),
            P("pool", None, "tp"),
        ),
        out_specs=(
            P(("groups", "tp"), "pool"),
            P(("groups", "pool"), "tp"),
            P(("groups", "pool"), "tp"),
        ),
        check_vma=False,
    )
```

time: 148 us -> 158 us (1.068)
  local copies, waits for them, and re-layouts: 27.8 us -> 0.94 us
  Pallas kernels: 40.2 us -> 62.1 us
  waiting for transfers between devices: 36.7 us -> 49.1 us
  other arithmetic: 10.4 us -> 12.6 us
    unnamed x52 -> x16, local copies, waits for them, and re-layouts: 27.5 us -> 0.64 us
    pallas_call x11, Pallas kernels: 40.2 us -> 62.1 us  [local_call(): pl.pallas_call(body, in_specs=[spec for _, spec in operands] + [HBM] * le...]
    ppermute x8, waiting for transfers between devices: 0.83 us -> 14.2 us  [chip_move(): lax.ppermute(x, 'pool', [(p, (p // 2 + d) % chips * 2 + (p % 2 ^ e)) for...]
    ppermute x8 -> x10, waiting for transfers between devices: 29.4 us -> 23.7 us  [tp_swap(): return lax.ppermute(x, 'tp', [(z, z ^ step) for z in range(tp_count)])]
    ppermute x17, waiting for transfers between devices: 2.64 us -> 5.19 us  [core_swap(): return lax.ppermute(x, 'pool', [(p, p ^ 1) for p in range(pool_count)])]
    ppermute x3, waiting for transfers between devices: 3.8 us -> 6.09 us  [shards(): lax.ppermute(shrunk, 'tp', [(i, (i + d) % tp_count) for i in range(tp_cou...]
    convert_element_type x4, other arithmetic: 3.62 us -> 5.32 us  [scaled(): return (x * factor[None, :]).astype(jnp.bfloat16)]
    ppermute x8 -> x10, starting transfers between devices: 10.5 us -> 12.1 us  [tp_swap(): return lax.ppermute(x, 'tp', [(z, z ^ step) for z in range(tp_count)])]
  transfers between devices with their start and end apart: 36 -> 38, of which waited for: 16 -> 15; matrix products, arithmetic and copies ran while one was open for 6% -> 8% of each run, Pallas kernels for 24% -> 32%
where the time goes in v5:
time: 158 us; the launch traced here: 157 us
  Pallas kernels  62.1 us (39%)
  waiting for transfers between devices  49.1 us (31%)
  starting transfers between devices  31.4 us (20%)
  other arithmetic  12.6 us (8%)
    pallas_call x11, Pallas kernels, local_call(): pl.pallas_call(body, in_specs=[spec for _, spec in operands] + [HBM] * le...  62.1 us
    ppermute x10, waiting for transfers between devices, tp_swap(): return lax.ppermute(x, 'tp', [(z, z ^ step) for z in range(tp_count)])  23.7 us
    ppermute x8, waiting for transfers between devices, chip_move(): lax.ppermute(x, 'pool', [(p, (p // 2 + d) % chips * 2 + (p % 2 ^ e)) for...  14.2 us
    ppermute x10, starting transfers between devices, tp_swap(): return lax.ppermute(x, 'tp', [(z, z ^ step) for z in range(tp_count)])  12.1 us
    ppermute x8, starting transfers between devices, chip_move(): lax.ppermute(x, 'pool', [(p, (p // 2 + d) % chips * 2 + (p % 2 ^ e)) for...  10.4 us
    ppermute x3, waiting for transfers between devices, shards(): lax.ppermute(shrunk, 'tp', [(i, (i + d) % tp_count) for i in range(tp_cou...  6.09 us
    convert_element_type x4, other arithmetic, scaled(): return (x * factor[None, :]).astype(jnp.bfloat16)  5.32 us
    ppermute x17, waiting for transfers between devices, core_swap(): return lax.ppermute(x, 'pool', [(p, p ^ 1) for p in range(pool_count)])  5.19 us
  transfers between devices with their start and end apart: 38, of which 15 were waited for; matrix products, arithmetic and copies ran while one was open for 8% of the time, Pallas kernels for 32%

profile of v5, /device:TPU:0, one launch (start us, length us, event | category | flops | bytes accessed | tf_op | source)
XLA Modules:
  0.0 157.2 jit_solution(2938087223643019550)
XLA Ops:
  0.6 3.0 %collective-permute-start.1 = (s32[1,128]{1,0:T(1,128)}, s32[1,128]{1,0:T(1,128)S(1)}, u32[]{:S(2)}, u32[]{:S(2)}) collective-permute-start(s32[1,128]{1,0:T(1,128)} %bitcast.33), channel_id=1, source_target_pairs={{0,8},{4,12},{8,0},{12,4},{1,9},{5,13},{9,1},{13,5},{2,10},{6,14},... | collective-permute-start | bytes 1544 | tf_op jit(solution)/shard_map/ppermute | solution.py:69
  3.7 0.7 dynamic-slice_convert_fusion.4
  4.4 1.2 multiply_convert_fusion.3.refs_1_
  5.6 1.8 %collective-permute-start.4 = (bf16[128,2048]{1,0:T(8,128)(2,1)S(1)}, bf16[128,2048]{1,0:T(8,128)(2,1)S(1)}, u32[]{:S(2)}, u32[]{:S(2)}) collective-permute-start(bf16[128,2048]{1,0:T(8,128)(2,1)S(1)} %multiply_convert_fusion.3.refs_1_), channel_id=1, source_target_pairs={{0,8},{4,12},{8,0},{12,4},{1,9},{5,13},{9,1},{13,5},{2,10},{6,14},... | collective-permute-start | bytes 1572872 | tf_op jit(solution)/shard_map/ppermute | solution.py:69
  7.4 0.7 dynamic-slice_convert_fusion
  8.1 1.8 %multiply_convert_fusion.4 = (bf16[64,2048]{1,0:T(8,128)(2,1)S(1)}, bf16[64,2048]{1,0:T(8,128)(2,1)}) fusion(bf16[128,8192]{1,0:T(8,128)(2,1)} %param.14, s32[]{:T(128)S(6)} %select_n.147, f32[2048]{0:T(1024)S(1)} %get-tuple-element.122), kind=kLoop, calls=%fused_computation.13 | loop fusion | flops 786432 | bytes 1056772 | tf_op jit(solution)/shard_map/convert_element_type | solution.py:426
  9.9 2.2 %multiply_convert_fusion.1 = (bf16[128,2048]{1,0:T(8,128)(2,1)S(1)}, bf16[128,2048]{1,0:T(8,128)(2,1)}) fusion(f32[2048]{0:T(1024)S(1)} %get-tuple-element.123, bf16[128,8192]{1,0:T(8,128)(2,1)} %param.14, s32[]{:T(128)S(6)} %select_n.150, f32[2048]{0:T(1024)S(1)} %get-tuple-element.124, s32[]{:T(128)S(6)} %select_n.149), kind=kLoop, calls=%fused_computation.2 | loop fusion | flops 1572864 | bytes 2113544 | tf_op jit(solution)/shard_map/convert_element_type | solution.py:426
  12.1 6.9 %collective-permute-done.4.refs_3_ = bf16[128,2048]{1,0:T(8,128)(2,1)S(1)} collective-permute-done((bf16[128,2048]{1,0:T(8,128)(2,1)S(1)}, bf16[128,2048]{1,0:T(8,128)(2,1)S(1)}, u32[]{:S(2)}, u32[]{:S(2)}) %collective-permute-start.4) | collective-permute-done | bytes 524320 | tf_op jit(solution)/shard_map/ppermute | solution.py:69
  19.0 0.5 collective-permute-start.9
  19.5 0.5 collective-permute-start
  20.0 1.6 %collective-permute-done = s32[1,128]{1,0:T(1,128)S(1)} collective-permute-done((s32[1,128]{1,0:T(1,128)S(1)}, s32[1,128]{1,0:T(1,128)S(1)}, u32[]{:S(2)}, u32[]{:S(2)}) %collective-permute-start) | collective-permute-done | bytes 544 | tf_op jit(solution)/shard_map/ppermute | solution.py:64
  21.8 1.0 collective-permute-done.2
  22.8 0.8 collective-permute-start.16
  23.6 0.7 collective-permute-start.17
  24.4 4.3 %shrink.1.refs_1_ = f32[32,512]{1,0:T(8,128)S(1)} custom-call(s32[1,512]{1,0:T(1,128)S(1)} %add_subtract_fusion.refs_0_, bf16[128,2048]{1,0:T(8,128)(2,1)S(1)} %multiply_convert_fusion.3.refs_1_, bf16[128,2048]{1,0:T(8,128)(2,1)S(1)} %collective-permute-done.3.refs_2_, bf16[128,2048]{1,0:T(8,128)(2,1)S(1)} %collective-permute-done.4.refs_3_, ...), custom_call_target="tpu_custom_call" | custom-call | flops 1000 | bytes 1000 | tf_op jit(solution)/shard_map/shrink/pallas_call | solution.py:32
  28.7 3.7 %collective-permute-start.8 = (f32[32,512]{1,0:T(8,128)S(1)}, f32[32,512]{1,0:T(8,128)S(1)}, u32[]{:S(2)}, u32[]{:S(2)}) collective-permute-start(f32[32,512]{1,0:T(8,128)S(1)} %shrink.1.refs_1_), channel_id=1, source_target_pairs={{0,3},{1,0},{2,1},{3,2},{4,7},{5,4},{6,5},{7,6},{8,11},{9,8},{10,9... | collective-permute-start | bytes 196616 | tf_op jit(solution)/shard_map/ppermute | solution.py:460
  32.4 1.0 collective-permute-start.6
  33.5 1.3 collective-permute-done.8.refs_4_
  34.8 4.8 %collective-permute-done.7.refs_3_ = f32[32,512]{1,0:T(8,128)S(1)} collective-permute-done((f32[32,512]{1,0:T(8,128)S(1)}, f32[32,512]{1,0:T(8,128)S(1)}, u32[]{:S(2)}, u32[]{:S(2)}) %collective-permute-start.7) | collective-permute-done | bytes 65568 | tf_op jit(solution)/shard_map/ppermute | solution.py:460
  39.6 11.5 %project_own.1 = (f32[128,2560]{1,0:T(8,128)S(1)}, bf16[128,512]{1,0:T(8,128)(2,1)S(1)}, bf16[128,512]{1,0:T(8,128)(2,1)S(1)}, bf16[128,512]{1,0:T(8,128)(2,1)S(...) custom-call(s32[1,512]{1,0:T(1,128)S(1)} %add_subtract_fusion.refs_0_, f32[32,512]{1,0:T(8,128)S(1)} %shrink.1.refs_1_, ...), custom_call_target="tpu_custom_call" | custom-call | flops 1000 | bytes 1000 | tf_op jit(solution)/shard_map/project_own/pallas_call | solution.py:32
  51.1 8.4 %project_1_0.1 = f32[128,2560]{1,0:T(8,128)S(1)} custom-call(s32[1,512]{1,0:T(1,128)S(1)} %add_subtract_fusion.refs_0_, f32[32,512]{1,0:T(8,128)S(1)} %shrink.1.refs_1_, f32[32,512]{1,0:T(8,128)S(1)} %collective-permute-done.6.refs_2_, f32[32,512]{1,0:T(8,128)S(1)} %collective-permute-done.7.refs_3_, f32[32,512]{1,0:T(8,128)S(1)} %collective-permute-done.8.refs_4_, ...), custom_call_target="tpu_custom_call" | custom-call | flops 1000 | bytes 1000 | tf_op jit(solution)/shard_map/project_1_0/pallas_call | solution.py:32
  59.6 8.5 %project_1_1.1 = (bf16[64,2560]{1,0:T(8,128)(2,1)S(1)}, bf16[64,2560]{1,0:T(8,128)(2,1)S(1)}) custom-call(s32[1,512]{1,0:T(1,128)S(1)} %add_subtract_fusion.refs_0_, f32[32,512]{1,0:T(8,128)S(1)} %shrink.1.refs_1_, f32[32,512]{1,0:T(8,128)S(1)} %collective-permute-done.6.refs_2_, f32[32,512]{1,0:T(8,128)S(1)} %collective-permute-done.7.refs_3_, ...), custom_call_target="tpu_custom_call" | custom-call | flops 1000 | bytes 1000 | tf_op jit(solution)/shard_map/project_1_1/pallas_call | solution.py:32
  68.1 1.0 fusion.8
  69.1 0.5 multiply_reduce_fusion
  69.6 0.5 collective-permute-start.11
  70.2 0.4 collective-permute-start.13
  70.7 0.4 collective-permute-start.20
  71.2 1.2 collective-permute-done.20
  72.4 0.3 collective-permute-start.15
  72.8 0.8 fusion
  73.6 0.8 collective-permute-start.19
  74.4 1.2 collective-permute-start.21
  75.8 1.0 pad_maximum_fusion
  76.9 7.2 %collective-permute-done.19.refs_6_ = bf16[64,2560]{1,0:T(8,128)(2,1)S(1)} collective-permute-done((bf16[64,2560]{1,0:T(8,128)(2,1)S(1)}, bf16[64,2560]{1,0:T(8,128)(2,1)S(1)}, u32[]{:S(2)}, u32[]{:S(2)}) %collective-permute-start.19) | collective-permute-done | bytes 327712 | tf_op jit(solution)/shard_map/ppermute | solution.py:69
  84.1 6.4 %attend_0.1 = (bf16[64,2048]{1,0:T(8,128)(2,1)S(1)}, bf16[64,256]{1,0:T(8,128)(2,1)S(1)}, bf16[64,256]{1,0:T(8,128)(2,1)S(1)}) custom-call(f32[128,2560]{1,0:T(8,128)S(1)} %get-tuple-element.69.refs_0_, bf16[128,512]{1,0:T(8,128)(2,1)S(1)} %collective-permute-done.11.refs_1_, bf16[128,512]{1,0:T(8,128)(2,1)S(1)} %collective-permute-done.12.refs_2_, ...), custom_call_target="tpu_custom_call" | custom-call | flops 1000 | bytes 1000 | tf_op jit(solution)/shard_map/attend_0/pallas_call | solution.py:32
  90.5 0.6 copy-done.2
  91.1 0.8 collective-permute-start.23
  91.9 6.4 %attend_1.1 = (bf16[64,2048]{1,0:T(8,128)(2,1)S(1)}, bf16[64,256]{1,0:T(8,128)(2,1)S(1)}, bf16[64,256]{1,0:T(8,128)(2,1)S(1)}) custom-call(f32[128,2560]{1,0:T(8,128)S(1)} %get-tuple-element.69.refs_0_, bf16[128,512]{1,0:T(8,128)(2,1)S(1)} %collective-permute-done.11.refs_1_, bf16[128,512]{1,0:T(8,128)(2,1)S(1)} %collective-permute-done.12.refs_2_, ...), custom_call_target="tpu_custom_call" | custom-call | flops 1000 | bytes 1000 | tf_op jit(solution)/shard_map/attend_1/pallas_call | solution.py:32
  98.4 0.5 collective-permute-start.24
  99.0 0.9 collective-permute-done.22.refs_2_
  99.9 0.4 collective-permute-done.24.refs_4_
  100.3 3.6 %output_0_0_2.1 = (bf16[128,1024]{1,0:T(8,128)(2,1)S(1)}, bf16[128,1024]{1,0:T(8,128)(2,1)S(1)}) custom-call(s32[4]{0:T(128)S(1)} %pad_add_fusion.refs_0_, bf16[64,2048]{1,0:T(8,128)(2,1)S(1)} %get-tuple-element.90.refs_1_, bf16[64,2048]{1,0:T(8,128)(2,1)S(1)} %collective-permute-done.22.refs_2_, bf16[64,2048]{1,0:T(8,128)(2,1)S(1)} %collective-permute-done.23.refs_3_, ...), custom_call_target="tpu_custom_call" | custom-call | flops 1000 | bytes 1000 | tf_op jit(solution)/shard_map/output_0_0_2/pallas_call | solution.py:32
  103.9 0.3 collective-permute-start.25
  104.2 1.2 collective-permute-start.28
  105.4 3.6 %output_0_1_2.1 = (bf16[128,1024]{1,0:T(8,128)(2,1)S(1)}, bf16[128,1024]{1,0:T(8,128)(2,1)S(1)}) custom-call(s32[4]{0:T(128)S(1)} %pad_add_fusion.refs_0_, bf16[64,2048]{1,0:T(8,128)(2,1)S(1)} %get-tuple-element.90.refs_1_, bf16[64,2048]{1,0:T(8,128)(2,1)S(1)} %collective-permute-done.22.refs_2_, bf16[64,2048]{1,0:T(8,128)(2,1)S(1)} %collective-permute-done.23.refs_3_, ...), custom_call_target="tpu_custom_call" | custom-call | flops 1000 | bytes 1000 | tf_op jit(solution)/shard_map/output_0_1_2/pallas_call | solution.py:32
  109.0 3.3 %collective-permute-done.25 = bf16[128,1024]{1,0:T(8,128)(2,1)S(1)} collective-permute-done((bf16[128,1024]{1,0:T(8,128)(2,1)S(1)}, bf16[128,1024]{1,0:T(8,128)(2,1)S(1)}, u32[]{:S(2)}, u32[]{:S(2)}) %collective-permute-start.25) | collective-permute-done | bytes 262176 | tf_op jit(solution)/shard_map/ppermute | solution.py:77
  112.5 0.5 collective-permute-start.29
  113.0 1.6 %collective-permute-start.30 = (bf16[128,1024]{1,0:T(8,128)(2,1)S(1)}, bf16[128,1024]{1,0:T(8,128)(2,1)S(1)}, u32[]{:S(2)}, u32[]{:S(2)}) collective-permute-start(bf16[128,1024]{1,0:T(8,128)(2,1)S(1)} %get-tuple-element.98), channel_id=1, source_target_pairs={{0,1},{1,0},{2,3},{3,2},{4,5},{5,4},{6,7},{7,6},{8,9},{9,8},{10,11... | collective-permute-start | bytes 786440 | tf_op jit(solution)/shard_map/ppermute | solution.py:77
  114.6 0.6 pad_maximum_fusion.2
  115.2 0.6 pad_maximum_fusion.3
  115.9 1.8 %collective-permute-start.26 = (bf16[64,1024]{1,0:T(8,128)(2,1)S(1)}, bf16[64,1024]{1,0:T(8,128)(2,1)S(1)}, u32[]{:S(2)}, u32[]{:S(2)}) collective-permute-start(bf16[64,1024]{1,0:T(8,128)(2,1)S(1)} %slice.95), channel_id=1, source_target_pairs={{0,2},{1,3},{2,0},{3,1},{4,6},{5,7},{6,4},{7,5},{8,10},{9,11},{10,... | collective-permute-start | bytes 393224 | tf_op jit(solution)/shard_map/ppermute | solution.py:77
  117.7 3.6 %output_1_0_2.1 = (bf16[128,1024]{1,0:T(8,128)(2,1)S(1)}, bf16[128,1024]{1,0:T(8,128)(2,1)S(1)}) custom-call(s32[4]{0:T(128)S(1)} %pad_add_fusion.refs_0_, bf16[64,2048]{1,0:T(8,128)(2,1)S(1)} %get-tuple-element.106.refs_1_, bf16[64,2048]{1,0:T(8,128)(2,1)S(1)} %collective-permute-done.27.refs_2_, bf16[64,2048]{1,0:T(8,128)(2,1)S(1)} %collective-permute-done.28.refs_3_, ...), custom_call_target="tpu_custom_call" | custom-call | flops 1000 | bytes 1000 | tf_op jit(solution)/shard_map/output_1_0_2/pallas_call | solution.py:32
  121.3 2.8 %collective-permute-done.30 = bf16[128,1024]{1,0:T(8,128)(2,1)S(1)} collective-permute-done((bf16[128,1024]{1,0:T(8,128)(2,1)S(1)}, bf16[128,1024]{1,0:T(8,128)(2,1)S(1)}, u32[]{:S(2)}, u32[]{:S(2)}) %collective-permute-start.30) | collective-permute-done | bytes 262176 | tf_op jit(solution)/shard_map/ppermute | solution.py:77
  124.2 3.3 %collective-permute-start.31 = (bf16[64,1024]{1,0:T(8,128)(2,1)S(1)}, bf16[64,1024]{1,0:T(8,128)(2,1)S(1)}, u32[]{:S(2)}, u32[]{:S(2)}) collective-permute-start(bf16[64,1024]{1,0:T(8,128)(2,1)S(1)} %slice.94), channel_id=1, source_target_pairs={{0,2},{1,3},{2,0},{3,1},{4,6},{5,7},{6,4},{7,5},{8,10},{9,11},{10,... | collective-permute-start | bytes 393224 | tf_op jit(solution)/shard_map/ppermute | solution.py:77
  127.5 2.9 %output_1_2_4.1 = (bf16[128,512]{1,0:T(8,128)(2,1)S(1)}, bf16[128,512]{1,0:T(8,128)(2,1)S(1)}) custom-call(s32[4]{0:T(128)S(1)} %pad_add_fusion.refs_0_, bf16[64,2048]{1,0:T(8,128)(2,1)S(1)} %get-tuple-element.106.refs_1_, bf16[64,2048]{1,0:T(8,128)(2,1)S(1)} %collective-permute-done.27.refs_2_, bf16[64,2048]{1,0:T(8,128)(2,1)S(1)} %collective-permute-done.28.refs_3_, ...), custom_call_target="tpu_custom_call" | custom-call | flops 1000 | bytes 1000 | tf_op jit(solution)/shard_map/output_1_2_4/pallas_call | solution.py:32
  130.4 2.9 %output_1_3_4.1 = (bf16[128,512]{1,0:T(8,128)(2,1)S(1)}, bf16[128,512]{1,0:T(8,128)(2,1)S(1)}) custom-call(s32[4]{0:T(128)S(1)} %pad_add_fusion.refs_0_, bf16[64,2048]{1,0:T(8,128)(2,1)S(1)} %get-tuple-element.106.refs_1_, bf16[64,2048]{1,0:T(8,128)(2,1)S(1)} %collective-permute-done.27.refs_2_, bf16[64,2048]{1,0:T(8,128)(2,1)S(1)} %collective-permute-done.28.refs_3_, ...), custom_call_target="tpu_custom_call" | custom-call | flops 1000 | bytes 1000 | tf_op jit(solution)/shard_map/output_1_3_4/pallas_call | solution.py:32
  133.4 2.0 %collective-permute-start.34 = (bf16[128,512]{1,0:T(8,128)(2,1)S(1)}, bf16[128,512]{1,0:T(8,128)(2,1)S(1)}, u32[]{:S(2)}, u32[]{:S(2)}) collective-permute-start(bf16[128,512]{1,0:T(8,128)(2,1)S(1)} %get-tuple-element.108), channel_id=1, source_target_pairs={{0,1},{1,0},{2,3},{3,2},{4,5},{5,4},{6,7},{7,6},{8,9},{9,8},{10,11... | collective-permute-start | bytes 393224 | tf_op jit(solution)/shard_map/ppermute | solution.py:77
  135.6 4.6 %collective-permute-done.34 = bf16[128,512]{1,0:T(8,128)(2,1)S(1)} collective-permute-done((bf16[128,512]{1,0:T(8,128)(2,1)S(1)}, bf16[128,512]{1,0:T(8,128)(2,1)S(1)}, u32[]{:S(2)}, u32[]{:S(2)}) %collective-permute-start.34) | collective-permute-done | bytes 131104 | tf_op jit(solution)/shard_map/ppermute | solution.py:77
  140.2 1.2 collective-permute-start.33
  141.4 1.8 %collective-permute-start.35 = (bf16[64,512]{1,0:T(8,128)(2,1)S(1)}, bf16[64,512]{1,0:T(8,128)(2,1)S(1)}, u32[]{:S(2)}, u32[]{:S(2)}) collective-permute-start(bf16[64,512]{1,0:T(8,128)(2,1)S(1)} %slice.97), channel_id=1, source_target_pairs={{0,2},{1,3},{2,0},{3,1},{4,6},{5,7},{6,4},{7,5},{8,10},{9,11},{10,... | collective-permute-start | bytes 196616 | tf_op jit(solution)/shard_map/ppermute | solution.py:77
  143.2 5.8 %collective-permute-done.33 = bf16[64,1024]{1,0:T(8,128)(2,1)S(1)} collective-permute-done((bf16[64,1024]{1,0:T(8,128)(2,1)S(1)}, bf16[64,1024]{1,0:T(8,128)(2,1)S(1)}, u32[]{:S(2)}, u32[]{:S(2)}) %collective-permute-start.33) | collective-permute-done | bytes 131104 | tf_op jit(solution)/shard_map/ppermute | solution.py:77
  149.2 0.6 collective-permute-done.35
  149.8 6.5 %collective-permute-done.37 = bf16[64,512]{1,0:T(8,128)(2,1)S(1)} collective-permute-done((bf16[64,512]{1,0:T(8,128)(2,1)S(1)}, bf16[64,512]{1,0:T(8,128)(2,1)S(1)}, u32[]{:S(2)}, u32[]{:S(2)}) %collective-permute-start.37) | collective-permute-done | bytes 65568 | tf_op jit(solution)/shard_map/ppermute | solution.py:77
  156.4 0.8 maximum_bitcast_fusion
  (76 shorter events, 1.7 us)
Async XLA Ops:
  0.6 9.3 %copy-start.5 = (bf16[8192]{0:T(1024)(128)(2,1)S(1)}, bf16[8192]{0:T(1024)(128)(2,1)}, u32[]{:S(2)}) copy-start(bf16[8192]{0:T(1024)(128)(2,1)} %param.15) | copy-start | bytes 49156
  0.6 4.9 %collective-permute-start.1 = (s32[1,128]{1,0:T(1,128)}, s32[1,128]{1,0:T(1,128)S(1)}, u32[]{:S(2)}, u32[]{:S(2)}) collective-permute-start(s32[1,128]{1,0:T(1,128)} %bitcast.33), channel_id=1, source_target_pairs={{0,8},{4,12},{8,0},{12,4},{1,9},{5,13},{9,1},{13,5},{2,10},{6,14},... | collective-permute-start | bytes 1544 | tf_op jit(solution)/shard_map/ppermute | solution.py:69
  4.4 15.2 %copy-start.7 = (s32[128]{0:T(128)S(1)}, s32[128]{0:T(128)}, u32[]{:S(2)}) copy-start(s32[128]{0:T(128)} %param.23) | copy-start | bytes 1540
  4.4 17.5 %copy-start.6 = (s32[128]{0:T(128)S(1)}, s32[128]{0:T(128)}, u32[]{:S(2)}) copy-start(s32[128]{0:T(128)} %param.22) | copy-start | bytes 1540
  5.6 13.4 %collective-permute-start.4 = (bf16[128,2048]{1,0:T(8,128)(2,1)S(1)}, bf16[128,2048]{1,0:T(8,128)(2,1)S(1)}, u32[]{:S(2)}, u32[]{:S(2)}) collective-permute-start(bf16[128,2048]{1,0:T(8,128)(2,1)S(1)} %multiply_convert_fusion.3.refs_1_), channel_id=1, source_target_pairs={{0,8},{4,12},{8,0},{12,4},{1,9},{5,13},{9,1},{13,5},{2,10},{6,14},... | collective-permute-start | bytes 1572872 | tf_op jit(solution)/shard_map/ppermute | solution.py:69
  7.3 16.3 %collective-permute-start.3 = (bf16[128,2048]{1,0:T(8,128)(2,1)S(1)}, bf16[128,2048]{1,0:T(8,128)(2,1)S(1)}, u32[]{:S(2)}, u32[]{:S(2)}) collective-permute-start(bf16[128,2048]{1,0:T(8,128)(2,1)S(1)} %multiply_convert_fusion.3.refs_1_), channel_id=1, source_target_pairs={{0,4},{4,0},{8,12},{12,8},{1,5},{5,1},{9,13},{13,9},{2,6},{6,2},{1... | collective-permute-start | bytes 1572872 | tf_op jit(solution)/shard_map/ppermute | solution.py:64
  19.0 5.4 %collective-permute-start.5 = (bf16[128,2048]{1,0:T(8,128)(2,1)S(1)}, bf16[128,2048]{1,0:T(8,128)(2,1)S(1)}, u32[]{:S(2)}, u32[]{:S(2)}) collective-permute-start(bf16[128,2048]{1,0:T(8,128)(2,1)S(1)} %collective-permute-done.4.refs_3_), channel_id=1, source_target_pairs={{0,4},{4,0},{8,12},{12,8},{1,5},{5,1},{9,13},{13,9},{2,6},{6,2},{1... | collective-permute-start | bytes 1572872 | tf_op jit(solution)/shard_map/ppermute | solution.py:64
  19.0 13.4 %collective-permute-start.9 = (bf16[64,2048]{1,0:T(8,128)(2,1)}, bf16[64,2048]{1,0:T(8,128)(2,1)S(1)}, u32[]{:S(2)}, u32[]{:S(2)}) collective-permute-start(bf16[64,2048]{1,0:T(8,128)(2,1)} %get-tuple-element.67), channel_id=1, source_target_pairs={{0,4},{4,0},{8,12},{12,8},{1,5},{5,1},{9,13},{13,9},{2,6},{6,2},{1... | collective-permute-start | bytes 786440 | tf_op jit(solution)/shard_map/ppermute | solution.py:64
  19.5 12.9 %collective-permute-start.10 = (bf16[64,2048]{1,0:T(8,128)(2,1)S(1)}, bf16[64,2048]{1,0:T(8,128)(2,1)S(1)}, u32[]{:S(2)}, u32[]{:S(2)}) collective-permute-start(bf16[64,2048]{1,0:T(8,128)(2,1)S(1)} %get-tuple-element.68), channel_id=1, source_target_pairs={{0,4},{4,0},{8,12},{12,8},{1,5},{5,1},{9,13},{13,9},{2,6},{6,2},{1... | collective-permute-start | bytes 786440 | tf_op jit(solution)/shard_map/ppermute | solution.py:64
  19.5 2.1 %collective-permute-start = (s32[1,128]{1,0:T(1,128)S(1)}, s32[1,128]{1,0:T(1,128)S(1)}, u32[]{:S(2)}, u32[]{:S(2)}) collective-permute-start(s32[1,128]{1,0:T(1,128)S(1)} %bitcast.34), channel_id=1, source_target_pairs={{0,4},{4,0},{8,12},{12,8},{1,5},{5,1},{9,13},{13,9},{2,6},{6,2},{1... | collective-permute-start | bytes 1544 | tf_op jit(solution)/shard_map/ppermute | solution.py:64
  21.7 1.1 collective-permute-start.2
  22.8 28.3 %collective-permute-start.16 = (bf16[128,2048]{1,0:T(8,128)(2,1)}, bf16[128,2048]{1,0:T(8,128)(2,1)S(1)}, u32[]{:S(2)}, u32[]{:S(2)}) collective-permute-start(bf16[128,2048]{1,0:T(8,128)(2,1)} %get-tuple-element.76), channel_id=1, source_target_pairs={{0,8},{4,12},{8,0},{12,4},{1,9},{5,13},{9,1},{13,5},{2,10},{6,14},... | collective-permute-start | bytes 1572872 | tf_op jit(solution)/shard_map/ppermute | solution.py:69
  23.6 35.9 %collective-permute-start.17 = (bf16[128,2048]{1,0:T(8,128)(2,1)S(1)}, bf16[128,2048]{1,0:T(8,128)(2,1)S(1)}, u32[]{:S(2)}, u32[]{:S(2)}) collective-permute-start(bf16[128,2048]{1,0:T(8,128)(2,1)S(1)} %get-tuple-element.77), channel_id=1, source_target_pairs={{0,12},{4,8},{8,4},{12,0},{1,13},{5,9},{9,5},{13,1},{2,14},{6,10},... | collective-permute-start | bytes 1572872 | tf_op jit(solution)/shard_map/ppermute | solution.py:69
  24.4 9.0 %copy-start.4 = (bf16[128,8192]{1,0:T(8,128)(2,1)S(1)}, bf16[128,8192]{1,0:T(8,128)(2,1)}, u32[]{:S(2)}) copy-start(bf16[128,8192]{1,0:T(8,128)(2,1)} %param.14) | copy-start | bytes 6291460
  28.7 6.1 %collective-permute-start.8 = (f32[32,512]{1,0:T(8,128)S(1)}, f32[32,512]{1,0:T(8,128)S(1)}, u32[]{:S(2)}, u32[]{:S(2)}) collective-permute-start(f32[32,512]{1,0:T(8,128)S(1)} %shrink.1.refs_1_), channel_id=1, source_target_pairs={{0,3},{1,0},{2,1},{3,2},{4,7},{5,4},{6,5},{7,6},{8,11},{9,8},{10,9... | collective-permute-start | bytes 196616 | tf_op jit(solution)/shard_map/ppermute | solution.py:460
  32.4 7.2 %collective-permute-start.7 = (f32[32,512]{1,0:T(8,128)S(1)}, f32[32,512]{1,0:T(8,128)S(1)}, u32[]{:S(2)}, u32[]{:S(2)}) collective-permute-start(f32[32,512]{1,0:T(8,128)S(1)} %shrink.1.refs_1_), channel_id=1, source_target_pairs={{0,2},{1,3},{2,0},{3,1},{4,6},{5,7},{6,4},{7,5},{8,10},{9,11},{10,... | collective-permute-start | bytes 196616 | tf_op jit(solution)/shard_map/ppermute | solution.py:460
  32.4 7.2 %collective-permute-start.6 = (f32[32,512]{1,0:T(8,128)S(1)}, f32[32,512]{1,0:T(8,128)S(1)}, u32[]{:S(2)}, u32[]{:S(2)}) collective-permute-start(f32[32,512]{1,0:T(8,128)S(1)} %shrink.1.refs_1_), channel_id=1, source_target_pairs={{0,1},{1,2},{2,3},{3,0},{4,5},{5,6},{6,7},{7,4},{8,9},{9,10},{10,1... | collective-permute-start | bytes 196616 | tf_op jit(solution)/shard_map/ppermute | solution.py:460
  68.0 2.7 %collective-permute-start.18 = (bf16[64,2560]{1,0:T(8,128)(2,1)S(1)}, bf16[64,2560]{1,0:T(8,128)(2,1)S(1)}, u32[]{:S(2)}, u32[]{:S(2)}) collective-permute-start(bf16[64,2560]{1,0:T(8,128)(2,1)S(1)} %get-tuple-element.79), channel_id=1, source_target_pairs={{0,4},{4,0},{8,12},{12,8},{1,5},{5,1},{9,13},{13,9},{2,6},{6,2},{1... | collective-permute-start | bytes 983048 | tf_op jit(solution)/shard_map/ppermute | solution.py:64
  69.6 4.0 %collective-permute-start.11 = (bf16[128,512]{1,0:T(8,128)(2,1)S(1)}, bf16[128,512]{1,0:T(8,128)(2,1)S(1)}, u32[]{:S(2)}, u32[]{:S(2)}) collective-permute-start(bf16[128,512]{1,0:T(8,128)(2,1)S(1)} %get-tuple-element.70), channel_id=1, source_target_pairs={{0,4},{4,0},{8,12},{12,8},{1,5},{5,1},{9,13},{13,9},{2,6},{6,2},{1... | collective-permute-start | bytes 393224 | tf_op jit(solution)/shard_map/ppermute | solution.py:64
  70.1 4.3 %collective-permute-start.12 = (bf16[128,512]{1,0:T(8,128)(2,1)S(1)}, bf16[128,512]{1,0:T(8,128)(2,1)S(1)}, u32[]{:S(2)}, u32[]{:S(2)}) collective-permute-start(bf16[128,512]{1,0:T(8,128)(2,1)S(1)} %get-tuple-element.71), channel_id=1, source_target_pairs={{0,4},{4,0},{8,12},{12,8},{1,5},{5,1},{9,13},{13,9},{2,6},{6,2},{1... | collective-permute-start | bytes 393224 | tf_op jit(solution)/shard_map/ppermute | solution.py:64
  70.2 6.7 %collective-permute-start.13 = (bf16[128,512]{1,0:T(8,128)(2,1)S(1)}, bf16[128,512]{1,0:T(8,128)(2,1)S(1)}, u32[]{:S(2)}, u32[]{:S(2)}) collective-permute-start(bf16[128,512]{1,0:T(8,128)(2,1)S(1)} %get-tuple-element.72), channel_id=1, source_target_pairs={{0,4},{4,0},{8,12},{12,8},{1,5},{5,1},{9,13},{13,9},{2,6},{6,2},{1... | collective-permute-start | bytes 393224 | tf_op jit(solution)/shard_map/ppermute | solution.py:64
  70.6 6.2 %collective-permute-start.14 = (bf16[128,512]{1,0:T(8,128)(2,1)S(1)}, bf16[128,512]{1,0:T(8,128)(2,1)S(1)}, u32[]{:S(2)}, u32[]{:S(2)}) collective-permute-start(bf16[128,512]{1,0:T(8,128)(2,1)S(1)} %get-tuple-element.73), channel_id=1, source_target_pairs={{0,4},{4,0},{8,12},{12,8},{1,5},{5,1},{9,13},{13,9},{2,6},{6,2},{1... | collective-permute-start | bytes 393224 | tf_op jit(solution)/shard_map/ppermute | solution.py:64
  70.7 1.7 %collective-permute-start.20 = (bf16[64,2560]{1,0:T(8,128)(2,1)S(1)}, bf16[64,2560]{1,0:T(8,128)(2,1)S(1)}, u32[]{:S(2)}, u32[]{:S(2)}) collective-permute-start(bf16[64,2560]{1,0:T(8,128)(2,1)S(1)} %get-tuple-element.81), channel_id=1, source_target_pairs={{0,4},{4,0},{8,12},{12,8},{1,5},{5,1},{9,13},{13,9},{2,6},{6,2},{1... | collective-permute-start | bytes 983048 | tf_op jit(solution)/shard_map/ppermute | solution.py:64
  72.4 4.4 %collective-permute-start.15 = (bf16[128,512]{1,0:T(8,128)(2,1)S(1)}, bf16[128,512]{1,0:T(8,128)(2,1)S(1)}, u32[]{:S(2)}, u32[]{:S(2)}) collective-permute-start(bf16[128,512]{1,0:T(8,128)(2,1)S(1)} %get-tuple-element.74), channel_id=1, source_target_pairs={{0,4},{4,0},{8,12},{12,8},{1,5},{5,1},{9,13},{13,9},{2,6},{6,2},{1... | collective-permute-start | bytes 393224 | tf_op jit(solution)/shard_map/ppermute | solution.py:64
  73.6 10.6 %collective-permute-start.19 = (bf16[64,2560]{1,0:T(8,128)(2,1)S(1)}, bf16[64,2560]{1,0:T(8,128)(2,1)S(1)}, u32[]{:S(2)}, u32[]{:S(2)}) collective-permute-start(bf16[64,2560]{1,0:T(8,128)(2,1)S(1)} %fusion.1), channel_id=1, source_target_pairs={{0,8},{4,12},{8,0},{12,4},{1,9},{5,13},{9,1},{13,5},{2,10},{6,14},... | collective-permute-start | bytes 983048 | tf_op jit(solution)/shard_map/ppermute | solution.py:69
  74.4 16.7 %collective-permute-start.21 = (bf16[64,2560]{1,0:T(8,128)(2,1)}, bf16[64,2560]{1,0:T(8,128)(2,1)S(1)}, u32[]{:S(2)}, u32[]{:S(2)}) collective-permute-start(bf16[64,2560]{1,0:T(8,128)(2,1)} %fusion), channel_id=1, source_target_pairs={{0,8},{4,12},{8,0},{12,4},{1,9},{5,13},{9,1},{13,5},{2,10},{6,14},... | collective-permute-start | bytes 983048 | tf_op jit(solution)/shard_map/ppermute | solution.py:69
  90.5 0.6 copy-start.2
  91.1 7.2 %copy-start = (bf16[64,256]{1,0:T(8,128)(2,1)}, bf16[64,256]{1,0:T(8,128)(2,1)S(1)}, u32[]{:S(2)}) copy-start(bf16[64,256]{1,0:T(8,128)(2,1)S(1)} %get-tuple-element.115) | copy-start | bytes 98308
  91.1 7.3 %collective-permute-start.23 = (bf16[64,2048]{1,0:T(8,128)(2,1)S(1)}, bf16[64,2048]{1,0:T(8,128)(2,1)S(1)}, u32[]{:S(2)}, u32[]{:S(2)}) collective-permute-start(bf16[64,2048]{1,0:T(8,128)(2,1)S(1)} %get-tuple-element.90.refs_1_), channel_id=1, source_target_pairs={{0,8},{4,12},{8,0},{12,4},{1,9},{5,13},{9,1},{13,5},{2,10},{6,14},... | collective-permute-start | bytes 786440 | tf_op jit(solution)/shard_map/ppermute | solution.py:69
  98.3 1.6 %collective-permute-start.22 = (bf16[64,2048]{1,0:T(8,128)(2,1)S(1)}, bf16[64,2048]{1,0:T(8,128)(2,1)S(1)}, u32[]{:S(2)}, u32[]{:S(2)}) collective-permute-start(bf16[64,2048]{1,0:T(8,128)(2,1)S(1)} %get-tuple-element.90.refs_1_), channel_id=1, source_target_pairs={{0,4},{4,0},{8,12},{12,8},{1,5},{5,1},{9,13},{13,9},{2,6},{6,2},{1... | collective-permute-start | bytes 786440 | tf_op jit(solution)/shard_map/ppermute | solution.py:64
  98.4 1.9 %collective-permute-start.24 = (bf16[64,2048]{1,0:T(8,128)(2,1)S(1)}, bf16[64,2048]{1,0:T(8,128)(2,1)S(1)}, u32[]{:S(2)}, u32[]{:S(2)}) collective-permute-start(bf16[64,2048]{1,0:T(8,128)(2,1)S(1)} %collective-permute-done.23.refs_3_), channel_id=1, source_target_pairs={{0,4},{4,0},{8,12},{12,8},{1,5},{5,1},{9,13},{13,9},{2,6},{6,2},{1... | collective-permute-start | bytes 786440 | tf_op jit(solution)/shard_map/ppermute | solution.py:64
  103.9 8.4 %collective-permute-start.25 = (bf16[128,1024]{1,0:T(8,128)(2,1)S(1)}, bf16[128,1024]{1,0:T(8,128)(2,1)S(1)}, u32[]{:S(2)}, u32[]{:S(2)}) collective-permute-start(bf16[128,1024]{1,0:T(8,128)(2,1)S(1)} %get-tuple-element.89), channel_id=1, source_target_pairs={{0,1},{1,0},{2,3},{3,2},{4,5},{5,4},{6,7},{7,6},{8,9},{9,8},{10,11... | collective-permute-start | bytes 786440 | tf_op jit(solution)/shard_map/ppermute | solution.py:77
  104.2 8.2 %collective-permute-start.28 = (bf16[64,2048]{1,0:T(8,128)(2,1)S(1)}, bf16[64,2048]{1,0:T(8,128)(2,1)S(1)}, u32[]{:S(2)}, u32[]{:S(2)}) collective-permute-start(bf16[64,2048]{1,0:T(8,128)(2,1)S(1)} %get-tuple-element.106.refs_1_), channel_id=1, source_target_pairs={{0,8},{4,12},{8,0},{12,4},{1,9},{5,13},{9,1},{13,5},{2,10},{6,14},... | collective-permute-start | bytes 786440 | tf_op jit(solution)/shard_map/ppermute | solution.py:69
  105.4 9.2 %copy-start.3 = (bf16[64,256]{1,0:T(8,128)(2,1)S(1)}, bf16[64,256]{1,0:T(8,128)(2,1)}, u32[]{:S(2)}) copy-start(bf16[64,256]{1,0:T(8,128)(2,1)} %copy-done.2) | copy-start | bytes 98308
  105.4 9.8 %copy-start.1 = (bf16[64,256]{1,0:T(8,128)(2,1)S(1)}, bf16[64,256]{1,0:T(8,128)(2,1)}, u32[]{:S(2)}) copy-start(bf16[64,256]{1,0:T(8,128)(2,1)} %copy-done) | copy-start | bytes 98308
  112.4 5.3 %collective-permute-start.27 = (bf16[64,2048]{1,0:T(8,128)(2,1)S(1)}, bf16[64,2048]{1,0:T(8,128)(2,1)S(1)}, u32[]{:S(2)}, u32[]{:S(2)}) collective-permute-start(bf16[64,2048]{1,0:T(8,128)(2,1)S(1)} %get-tuple-element.106.refs_1_), channel_id=1, source_target_pairs={{0,4},{4,0},{8,12},{12,8},{1,5},{5,1},{9,13},{13,9},{2,6},{6,2},{1... | collective-permute-start | bytes 786440 | tf_op jit(solution)/shard_map/ppermute | solution.py:64
  112.5 5.2 %collective-permute-start.29 = (bf16[64,2048]{1,0:T(8,128)(2,1)S(1)}, bf16[64,2048]{1,0:T(8,128)(2,1)S(1)}, u32[]{:S(2)}, u32[]{:S(2)}) collective-permute-start(bf16[64,2048]{1,0:T(8,128)(2,1)S(1)} %collective-permute-done.28.refs_3_), channel_id=1, source_target_pairs={{0,4},{4,0},{8,12},{12,8},{1,5},{5,1},{9,13},{13,9},{2,6},{6,2},{1... | collective-permute-start | bytes 786440 | tf_op jit(solution)/shard_map/ppermute | solution.py:64
  113.0 11.1 %collective-permute-start.30 = (bf16[128,1024]{1,0:T(8,128)(2,1)S(1)}, bf16[128,1024]{1,0:T(8,128)(2,1)S(1)}, u32[]{:S(2)}, u32[]{:S(2)}) collective-permute-start(bf16[128,1024]{1,0:T(8,128)(2,1)S(1)} %get-tuple-element.98), channel_id=1, source_target_pairs={{0,1},{1,0},{2,3},{3,2},{4,5},{5,4},{6,7},{7,6},{8,9},{9,8},{10,11... | collective-permute-start | bytes 786440 | tf_op jit(solution)/shard_map/ppermute | solution.py:77
  115.9 8.3 %collective-permute-start.26 = (bf16[64,1024]{1,0:T(8,128)(2,1)S(1)}, bf16[64,1024]{1,0:T(8,128)(2,1)S(1)}, u32[]{:S(2)}, u32[]{:S(2)}) collective-permute-start(bf16[64,1024]{1,0:T(8,128)(2,1)S(1)} %slice.95), channel_id=1, source_target_pairs={{0,2},{1,3},{2,0},{3,1},{4,6},{5,7},{6,4},{7,5},{8,10},{9,11},{10,... | collective-permute-start | bytes 393224 | tf_op jit(solution)/shard_map/ppermute | solution.py:77
  124.1 11.4 %collective-permute-start.32 = (bf16[128,1024]{1,0:T(8,128)(2,1)S(1)}, bf16[128,1024]{1,0:T(8,128)(2,1)S(1)}, u32[]{:S(2)}, u32[]{:S(2)}) collective-permute-start(bf16[128,1024]{1,0:T(8,128)(2,1)S(1)} %get-tuple-element.103), channel_id=1, source_target_pairs={{0,1},{1,0},{2,3},{3,2},{4,5},{5,4},{6,7},{7,6},{8,9},{9,8},{10,11... | collective-permute-start | bytes 786440 | tf_op jit(solution)/shard_map/ppermute | solution.py:77
  124.2 11.4 %collective-permute-start.31 = (bf16[64,1024]{1,0:T(8,128)(2,1)S(1)}, bf16[64,1024]{1,0:T(8,128)(2,1)S(1)}, u32[]{:S(2)}, u32[]{:S(2)}) collective-permute-start(bf16[64,1024]{1,0:T(8,128)(2,1)S(1)} %slice.94), channel_id=1, source_target_pairs={{0,2},{1,3},{2,0},{3,1},{4,6},{5,7},{6,4},{7,5},{8,10},{9,11},{10,... | collective-permute-start | bytes 393224 | tf_op jit(solution)/shard_map/ppermute | solution.py:77
  133.3 15.8 %collective-permute-start.36 = (bf16[128,512]{1,0:T(8,128)(2,1)S(1)}, bf16[128,512]{1,0:T(8,128)(2,1)S(1)}, u32[]{:S(2)}, u32[]{:S(2)}) collective-permute-start(bf16[128,512]{1,0:T(8,128)(2,1)S(1)} %get-tuple-element.111), channel_id=1, source_target_pairs={{0,1},{1,0},{2,3},{3,2},{4,5},{5,4},{6,7},{7,6},{8,9},{9,8},{10,11... | collective-permute-start | bytes 393224 | tf_op jit(solution)/shard_map/ppermute | solution.py:77
  133.4 6.8 %collective-permute-start.34 = (bf16[128,512]{1,0:T(8,128)(2,1)S(1)}, bf16[128,512]{1,0:T(8,128)(2,1)S(1)}, u32[]{:S(2)}, u32[]{:S(2)}) collective-permute-start(bf16[128,512]{1,0:T(8,128)(2,1)S(1)} %get-tuple-element.108), channel_id=1, source_target_pairs={{0,1},{1,0},{2,3},{3,2},{4,5},{5,4},{6,7},{7,6},{8,9},{9,8},{10,11... | collective-permute-start | bytes 393224 | tf_op jit(solution)/shard_map/ppermute | solution.py:77
  140.2 8.9 %collective-permute-start.33 = (bf16[64,1024]{1,0:T(8,128)(2,1)S(1)}, bf16[64,1024]{1,0:T(8,128)(2,1)S(1)}, u32[]{:S(2)}, u32[]{:S(2)}) collective-permute-start(bf16[64,1024]{1,0:T(8,128)(2,1)S(1)} %slice.93), channel_id=1, source_target_pairs={{0,2},{1,3},{2,0},{3,1},{4,6},{5,7},{6,4},{7,5},{8,10},{9,11},{10,... | collective-permute-start | bytes 393224 | tf_op jit(solution)/shard_map/ppermute | solution.py:77
  141.4 8.3 %collective-permute-start.35 = (bf16[64,512]{1,0:T(8,128)(2,1)S(1)}, bf16[64,512]{1,0:T(8,128)(2,1)S(1)}, u32[]{:S(2)}, u32[]{:S(2)}) collective-permute-start(bf16[64,512]{1,0:T(8,128)(2,1)S(1)} %slice.97), channel_id=1, source_target_pairs={{0,2},{1,3},{2,0},{3,1},{4,6},{5,7},{6,4},{7,5},{8,10},{9,11},{10,... | collective-permute-start | bytes 196616 | tf_op jit(solution)/shard_map/ppermute | solution.py:77
  149.8 6.6 %collective-permute-start.37 = (bf16[64,512]{1,0:T(8,128)(2,1)S(1)}, bf16[64,512]{1,0:T(8,128)(2,1)S(1)}, u32[]{:S(2)}, u32[]{:S(2)}) collective-permute-start(bf16[64,512]{1,0:T(8,128)(2,1)S(1)} %slice.96), channel_id=1, source_target_pairs={{0,2},{1,3},{2,0},{3,1},{4,6},{5,7},{6,4},{7,5},{8,10},{9,11},{10,... | collective-permute-start | bytes 196616 | tf_op jit(solution)/shard_map/ppermute | solution.py:77

commit v6 on v5

v6 whole, which is shorter than its diff:
```python
import functools
import math

import jax
import jax.numpy as jnp
from jax import lax
from jax.experimental import pallas as pl
from jax.experimental.pallas import tpu as pltpu
from jax.sharding import PartitionSpec as P

epsilon = 1e-05
adapter_scale = 0.5
rope_base = 500000.0
masked_score = -1e30


VMEM = pl.BlockSpec(memory_space=pltpu.VMEM)
HBM = pl.BlockSpec(memory_space=pltpu.HBM)
SMEM = pl.BlockSpec(memory_space=pltpu.SMEM)


def local_call(kernel, name, operands, outs, scratch=(), carried=(), mib=16):
    counts = (len(operands), len(carried), len(outs), len(carried), len(scratch))

    def body(*refs):
        groups, at = [], 0
        for n in counts:
            groups.append(refs[at : at + n])
            at += n
        ins, sources, out_refs, targets, scratch_refs = groups
        copies = [
            pltpu.make_async_copy(source, target, refs[-1].at[i])
            for i, (source, target) in enumerate(zip(sources, targets))
        ]
        for copy in copies:
            copy.start()
        kernel(ins, out_refs, scratch_refs)
        for copy in copies:
            copy.wait()

    sems = [pltpu.SemaphoreType.DMA((len(carried),))] if carried else []
    return pl.pallas_call(
        body,
        in_specs=[spec for _, spec in operands] + [HBM] * len(carried),
        out_specs=[VMEM] * (len(outs) + len(carried)),
        out_shape=[*outs, *[pltpu.VMEM(x.shape, x.dtype) for x in carried]],
        scratch_shapes=[*scratch, *sems],
        compiler_params=pltpu.CompilerParams(vmem_limit_bytes=mib * 1024 * 1024),
        cost_estimate=pl.CostEstimate(flops=1000, bytes_accessed=1000, transcendentals=0),
        name=name,
    )(
        *[x for x, _ in operands],
        *[pltpu.with_memory_space_constraint(x, pltpu.HBM) for x in carried],
    )


def in_vmem(arrays):
    return [(x, VMEM) for x in arrays]


def shaped(shape, dtype=jnp.float32):
    return jax.ShapeDtypeStruct(shape, dtype)


def after(x, *earlier):
    return lax.optimization_barrier((x, *earlier))[0]


def core_swap(x, pool_count):
    return lax.ppermute(x, "pool", [(p, p ^ 1) for p in range(pool_count)])


def chip_move(x, pool_count, d, e=0):
    chips = pool_count // 2
    return lax.ppermute(
        x,
        "pool",
        [(p, (p // 2 + d) % chips * 2 + ((p % 2) ^ e)) for p in range(pool_count)],
    )


def tp_swap(x, tp_count, step):
    return lax.ppermute(x, "tp", [(z, z ^ step) for z in range(tp_count)])


def shrink(first_id, ids, blocks, query_down, value_down):
    slots, _ = query_down.shape
    rows = blocks[0].shape[0]
    adapters = slots // 16
    count = len(blocks)

    def kernel(ins, outs, _):
        first_id, *ins = ins
        ids, blocks, tables = ins[:count], ins[count : 2 * count], ins[2 * count :]
        local_ids, out = outs
        for b in range(count):
            local_ids[:, b * rows : (b + 1) * rows] = ids[b][...] - first_id[0]
        for first in range(0, count, 2):
            x = jnp.concatenate([b[...] for b in blocks[first : first + 2]], axis=0)
            span = slice(first * rows, (first + 2) * rows)
            label = local_ids[:, span].reshape(1, 1, 2 * rows)
            chosen = lax.broadcasted_iota(jnp.int32, (adapters, 1, 2 * rows), 0) == label
            for at, table in enumerate(tables):
                terms = lax.dot_general(
                    table[...], x, (((1,), (1,)), ((), ())), preferred_element_type=jnp.float32
                ).reshape(adapters, 16, 2 * rows)
                out[at * 16 : (at + 1) * 16, span] = jnp.sum(
                    jnp.where(chosen, terms, 0.0), axis=0
                )

    return local_call(
        kernel,
        "shrink",
        [(first_id, SMEM), *in_vmem([*ids, *blocks, query_down, value_down])],
        [shaped((1, rows * count), jnp.int32), shaped((32, rows * count))],
    )


def tables(tokens, lengths, head):
    rows = tokens.shape[0]
    half = head // 2

    def kernel(ins, outs, _):
        tokens, lengths = ins
        scale, cosines, sines, column = outs
        values = tokens[...].astype(jnp.float32)
        mean_square = jnp.mean(values * values, axis=1, keepdims=True)
        scale[...] = lax.rsqrt(mean_square + epsilon)
        here = lax.broadcasted_iota(jnp.int32, (rows, rows), 0)
        there = lax.broadcasted_iota(jnp.int32, (rows, rows), 1)
        positions = jnp.sum(
            jnp.where(here == there, lengths[...].astype(jnp.float32), 0.0), axis=1, keepdims=True
        )
        column[...] = positions.astype(jnp.int32)
        lane = lax.broadcasted_iota(jnp.int32, (1, head), 1)
        exponent = (lane % half).astype(jnp.float32) * (-2.0 / head)
        angles = positions * jnp.exp(exponent * math.log(rope_base))
        cosines[...] = jnp.cos(angles)
        sines[...] = jnp.where(lane < half, -1.0, 1.0) * jnp.sin(angles)

    return local_call(
        kernel,
        "tables",
        in_vmem([tokens, lengths]),
        [
            shaped((rows, 1)),
            shaped((rows, head)),
            shaped((rows, head)),
            shaped((rows, 1), jnp.int32),
        ],
        mib=24,
    )


def load(arrays):
    def kernel(ins, outs, _):
        pass

    return local_call(kernel, "load", [], [], carried=arrays)


def spread_lows(low, ids, adapters):
    total = ids.shape[1]
    low = low.astype(jnp.bfloat16).astype(jnp.float32) * adapter_scale
    chosen = lax.broadcasted_iota(jnp.int32, (adapters, 1, total), 0) == ids.reshape(1, 1, total)
    return [
        jnp.where(chosen, low[at : at + 16][None], 0.0)
        .reshape(adapters * 16, total)
        .T.astype(jnp.bfloat16)
        for at in (0, 16)
    ]


def columns_at(start, width):
    return pl.ds(pl.multiple_of(start, width), width)


def project(name, kinds, span, ids, lows, blocks, weights, carried=()):
    wq, wk, wv, uq, uv = weights
    depth = blocks[0].shape[1]
    wide, kv, slots = wq.shape[1], wk.shape[1], uq.shape[0]
    tile = min(512, wide)
    start, total = span

    def kernel(ins, outs, scratch):
        ids, *ins = ins
        low_refs, blocks = ins[: len(lows)], ins[len(lows) : -5]
        wq, wk, wv, uq, uv = ins[-5:]
        xs, spread_q, spread_v = scratch
        at = 0
        for block in blocks:
            xs[at : at + block.shape[0], :] = block[...]
            at += block.shape[0]
        low = low_refs[0][:, start : start + total]
        for other in low_refs[1:]:
            low = low + other[:, start : start + total]
        spread_q[...], spread_v[...] = spread_lows(
            low, ids[:, start : start + total], slots // 16
        )

        def sums(w, spread=None, u=None):
            acc = jnp.dot(xs[...], w, preferred_element_type=jnp.float32)
            if u is not None:
                acc = acc + jnp.dot(spread[...], u, preferred_element_type=jnp.float32)
            return acc

        def write(acc, columns):
            for out, (first, count, dtype) in zip(outs, kinds):
                out[:, columns] = acc[first : first + count].astype(dtype)

        @pl.loop(0, wide // tile)
        def _(i):
            columns = columns_at(i * tile, tile)
            write(sums(wq[:, columns], spread_q, uq[:, columns]), columns)

        write(sums(wk[...]), slice(wide, wide + kv))
        write(sums(wv[...], spread_v, uv[...]), slice(wide + kv, wide + 2 * kv))

    spread = pltpu.VMEM((total, slots), jnp.bfloat16)
    return local_call(
        kernel,
        name,
        in_vmem([ids, *lows, *blocks, *weights]),
        [shaped((count, wide + 2 * kv), dtype) for _, count, dtype in kinds],
        [pltpu.VMEM((total, depth), jnp.bfloat16), spread, spread],
        carried=carried,
    )


def add_sums(name, window, keep, other):
    first, part = window

    def kernel(ins, outs, _):
        keep, other = ins
        outs[0][...] = (
            keep[first : first + part, :] + other[...].astype(jnp.float32)
        ).astype(jnp.bfloat16)

    return local_call(
        kernel, name, in_vmem([keep, other]), [shaped((part, keep.shape[1]), jnp.bfloat16)]
    )[0]


def attend_kernel(first_row, block, done, ins, outs, scratch):
    if done:
        for full, source in zip(outs[1:], ins[:2]):
            full[: source.shape[0], :] = source[...]
    keep, swapped, *moved, scale, cosines, sines, lengths, keys, values = ins[2:] if done else ins
    out, key_out, value_out = outs
    head = cosines.shape[1]
    rows = out.shape[0]
    _, kv_heads, cache, _ = keys.shape
    heads = out.shape[1] // head
    group = heads // kv_heads
    score_scale = 1.0 / math.sqrt(head)
    sub = 8

    column = lax.broadcasted_iota(jnp.int32, (sub, sub * cache), 1)
    start = lax.broadcasted_iota(jnp.int32, (sub, sub * cache), 0) * cache

    @pl.loop(0, rows // block)
    def _(i):
        attended, new_keys, new_values = [], [], []
        for half in range(block // sub):
            here = pl.ds(pl.multiple_of(i * block + half * sub, sub), sub)
            whole = pl.ds(pl.multiple_of(first_row + i * block + half * sub, sub), sub)
            x = keep[whole] + swapped[whole].astype(jnp.float32)
            for m in moved:
                x = x + m[here].astype(jnp.float32)
            x = x * scale[whole]
            cos, sin = cosines[whole], sines[whole]
            inside = (column >= start) & (column < start + lengths[whole])

            def piece(i):
                return x[:, i * head : (i + 1) * head]

            def turn(v):
                return v * cos + pltpu.roll(v, head // 2, 1) * sin

            for g in range(kv_heads):
                query = jnp.concatenate(
                    [turn(piece(g * group + h)) for h in range(group)], axis=0
                ).astype(jnp.bfloat16)
                new_key = turn(piece(heads + g)).astype(jnp.bfloat16).astype(jnp.float32)
                new_value = piece(heads + kv_heads + g).astype(jnp.bfloat16).astype(jnp.float32)
                k = keys[whole, g].reshape(sub * cache, head)
                v = values[whole, g].reshape(sub * cache, head)
                scores = (
                    lax.dot_general(
                        query, k, (((1,), (1,)), ((), ())), preferred_element_type=jnp.float32
                    )
                    * score_scale
                )
                own_key = jnp.concatenate([new_key] * group, axis=0)
                own = (
                    jnp.sum(query.astype(jnp.float32) * own_key, axis=1, keepdims=True)
                    * score_scale
                )
                scores = jnp.where(
                    inside[None], scores.reshape(group, sub, sub * cache), masked_score
                ).reshape(group * sub, sub * cache)
                peak = jnp.maximum(jnp.max(scores, axis=1, keepdims=True), own)
                weights = jnp.exp(scores - peak)
                own_weight = jnp.exp(own - peak)
                inverse = 1.0 / (jnp.sum(weights, axis=1, keepdims=True) + own_weight)
                mixed = jnp.dot(weights.astype(jnp.bfloat16), v, preferred_element_type=jnp.float32)
                own_value = jnp.concatenate([new_value] * group, axis=0)
                mixed = (mixed + own_weight * own_value) * inverse
                attended += [mixed[h * sub : (h + 1) * sub] for h in range(group)]
                new_keys.append(new_key)
                new_values.append(new_value)
        r = pl.ds(pl.multiple_of(i * block, block), block)

        def joined(pieces):
            n = len(pieces) * sub // block
            return jnp.concatenate(
                [jnp.concatenate(pieces[j::n], axis=0) for j in range(n)], axis=1
            ).astype(jnp.bfloat16)

        out[r] = joined(attended)
        r = pl.ds(pl.multiple_of((first_row if done else 0) + i * block, block), block)
        key_out[r] = joined(new_keys)
        value_out[r] = joined(new_values)


def attend(name, window, keep, swapped, moved, rest, keys, values, earlier, carried=()):
    _, columns = keep.shape
    _, kv_heads, _, head = keys.shape
    kv_cols = kv_heads * head
    first, part = window
    kv_rows = first + part if earlier else part
    return local_call(
        functools.partial(attend_kernel, first, 16, bool(earlier)),
        name,
        in_vmem([*earlier, keep, swapped, *moved, *rest, keys, values]),
        [
            shaped((part, columns - 2 * kv_cols), jnp.bfloat16),
            *[shaped((kv_rows, kv_cols), jnp.bfloat16)] * 2,
        ],
        carried=carried,
    )


def output_part(name, span, order, blocks, weights):
    rows = blocks[0].shape[0]
    first, columns = span
    depth = weights.shape[0]
    tile = math.gcd(512, columns)
    total = rows * len(blocks)

    def kernel(ins, outs, scratch):
        order, *blocks, weights = ins
        keep, send = outs
        (xs,) = scratch
        for b, block in enumerate(blocks):
            xs[pl.ds(pl.multiple_of(order[b] * rows, rows), rows), :] = block[...]

        @pl.loop(0, columns // tile)
        def _(i):
            w = weights[:, columns_at(first + i * tile, tile)]
            acc = jnp.dot(xs[...], w, preferred_element_type=jnp.float32).astype(jnp.bfloat16)
            keep[:, columns_at(i * tile, tile)] = acc[: total // 2]
            send[:, columns_at(i * tile, tile)] = acc[total // 2 :]

    return local_call(
        kernel,
        name,
        [(order, SMEM), *in_vmem([*blocks, weights])],
        [shaped((total // 2, columns), jnp.bfloat16)] * 2,
        [pltpu.VMEM((total, depth), jnp.bfloat16)],
    )


def add_halves(name, keep, got):
    half, columns = keep.shape[0] // 2, keep.shape[1]

    def kernel(ins, outs, _):
        keep, got = ins
        total = keep[...].astype(jnp.float32) + got[...].astype(jnp.float32)
        outs[0][...] = total[:half]
        outs[1][...] = total[half:].astype(jnp.bfloat16)

    return local_call(
        kernel,
        name,
        in_vmem([keep, got]),
        [shaped((half, columns)), shaped((half, columns), jnp.bfloat16)],
    )


def add_last(name, keep, got):
    def kernel(ins, outs, _):
        total = ins[0][...].astype(jnp.float32) + ins[1][...].astype(jnp.float32)
        outs[0][...] = total.astype(jnp.bfloat16)

    return local_call(kernel, name, in_vmem([keep, got]), [shaped(keep.shape, jnp.bfloat16)])[0]


def assemble(done, keep, got, places, rows, columns):
    def kernel(ins, outs, _):
        *done, keep, got = ins
        total = keep[...].astype(jnp.float32) + got[...].astype(jnp.float32)
        total = total.astype(jnp.bfloat16)
        for piece, spots in zip([*done, total], places):
            for at, to, count, column in spots:
                outs[0][to : to + count, column : column + piece.shape[1]] = piece[
                    at : at + count, :
                ]

    return local_call(
        kernel,
        "assemble",
        in_vmem([*done, keep, got]),
        [shaped((rows, columns), jnp.bfloat16)],
    )[0]


def reversed_bits(x, count):
    out, bit = 0, 1
    while bit < count:
        out = out * 2 + (x // bit) % 2
        bit *= 2
    return out


def shards(
    tokens,
    input_norm_gain,
    query_matrix,
    key_matrix,
    value_matrix,
    output_matrix,
    rotated_key_cache,
    cached_value_rows,
    cache_length_per_row,
    row_adapter_index,
    query_down_maps,
    query_up_maps,
    value_down_maps,
    value_up_maps,
):
    pool_count = lax.axis_size("pool")
    tp_count = lax.axis_size("tp")
    chips = pool_count // 2
    pool_at = lax.axis_index("pool")
    tp_at = lax.axis_index("tp")
    chip, core = pool_at // 2, pool_at % 2
    rows = tokens.shape[0]
    adapters, rank, piece = query_down_maps.shape
    base = query_matrix.shape[0]
    kv_heads = rotated_key_cache.shape[1]
    head = rotated_key_cache.shape[3]

    def scaled(start, width, tokens=tokens, gain=input_norm_gain, window=(0, rows)):
        x = lax.dynamic_slice(tokens, (window[0], start), (window[1], width)).astype(jnp.float32)
        factor = lax.dynamic_slice_in_dim(gain, start, width, 0).astype(jnp.float32)
        return (x * factor[None, :]).astype(jnp.bfloat16)

    own_ids = row_adapter_index.reshape(1, rows)
    ids = [
        own_ids if d == e == 0 else chip_move(own_ids, pool_count, d, e)
        for d in range(chips)
        for e in range(2)
    ]
    first = after(scaled(tp_at * piece, piece), *ids[1:])
    first, tokens_1, gain_1 = lax.optimization_barrier((first, tokens, input_norm_gain))
    same_core = [first] + [chip_move(first, pool_count, d) for d in range(1, chips)]

    cut = rows // 2
    chunks = [(0, cut), (cut, rows - cut)]
    own = scaled(pool_at * base, base, tokens_1, gain_1)
    partner_at = (pool_at // 2 * 2 + 1 - core) * base
    partner = [
        scaled(partner_at, base, tokens_1, gain_1, (at, rows // 2)) for at in (0, rows // 2)
    ]
    away = {}
    for d in range(1, chips):
        for e in range(2):
            target = (chip + d) % chips * 2 + (core + e) % 2
            away[d, e] = scaled(target * base, base, tokens_1, gain_1)
    first_id = (pool_at * adapters).reshape(1).astype(jnp.int32)
    lengths = cache_length_per_row.reshape(1, rows)
    share = pool_count // tp_count
    order = []
    for d in range(chips):
        for e in range(2):
            p = (chip - d) % chips * 2 + (core + e) % 2
            order.append(
                reversed_bits(jnp.bitwise_xor(p // share, tp_at), tp_count) * share + p % share
            )
    order = jnp.stack(order).astype(jnp.int32)

    flat_down = [x.reshape(adapters * rank, piece) for x in (query_down_maps, value_down_maps)]
    flat_up = [x.reshape(adapters * rank, x.shape[2]) for x in (query_up_maps, value_up_maps)]
    small = [own, *partner, *away.values(), first_id, lengths, order]
    query_matrix, *small = lax.optimization_barrier((query_matrix, *small))
    own, partner, small = small[0], small[1:3], small[3:]
    away = dict(zip(away, small))
    first_id, lengths, order = small[-3:]
    down_q, down_v, *weights = load(
        [*flat_down, query_matrix, key_matrix, value_matrix, *flat_up]
    )
    partner = [core_swap(x, pool_count) for x in partner]
    remote = [[] for _ in range(chips)]
    for (d, e), x in away.items():
        remote[d].append(chip_move(after(x, *same_core[1:]), pool_count, d, e))
    same_core[1:] = [after(x, down_q) for x in same_core[1:]]
    adapter_rows = [b for x in same_core for b in (x, core_swap(x, pool_count))]
    local_ids, shrunk = shrink(first_id, ids, adapter_rows, down_q, down_v)
    lows = [shrunk] + [
        lax.ppermute(shrunk, "tp", [(i, (i + d) % tp_count) for i in range(tp_count)])
        for d in range(1, tp_count)
    ]
    rest = tables(tokens, after(lengths, shrunk), head)
    own_sums, own_send, keys, values = project(
        "project_own",
        [(0, rows, jnp.float32), (rows, rows, jnp.bfloat16)],
        (0, 2 * rows),
        after(local_ids, rest[0]),
        lows,
        [own, *partner],
        weights,
        carried=[rotated_key_cache, cached_value_rows],
    )
    swapped = core_swap(own_send, pool_count)
    local_ids = after(local_ids, own_sums)
    moved = [[] for _ in chunks]
    both = None
    for d in range(1, chips):
        if both is not None:
            remote[d][0] = after(remote[d][0], both)
        at = 2 * d * rows
        (keep,) = project(
            f"project_{d}_0",
            [(0, rows, jnp.float32)],
            (at, rows),
            local_ids,
            lows,
            remote[d][:1],
            weights,
        )
        sends = project(
            f"project_{d}_1",
            [(first, part, jnp.bfloat16) for first, part in chunks],
            (at + rows, rows),
            local_ids,
            lows,
            [after(remote[d][1], keep)],
            weights,
        )
        for c, window in enumerate(chunks):
            swap = core_swap(sends[c], pool_count)
            if c:
                swap = after(swap, both)
            both = add_sums(f"add_{d}_{c}", window, keep, swap)
            moved[c].append(chip_move(both, pool_count, -d))
    moved[0][0] = after(moved[0][0], both)

    attended, earlier = [], []
    for c, window in enumerate(chunks):
        out, *earlier = attend(
            f"attend_{c}",
            window,
            own_sums,
            swapped,
            moved[c],
            rest,
            keys,
            values,
            earlier[:2],
            [] if c else [output_matrix],
        )
        if c == 0:
            out_weights = earlier[2]
        if c + 1 < len(chunks):
            out, *moved[c + 1] = lax.optimization_barrier((out, *moved[c + 1]))
        else:
            out = after(out, attended[-1][-1])
        attended.append([out] + [chip_move(out, pool_count, d) for d in range(1, chips)])
    new_key, new_value = earlier
    attended[0][0] = after(attended[0][0], new_key)

    columns = output_matrix.shape[1]
    layout = [(0, 0, 1), (1, 0, 2), (1, 2, 4), (1, 3, 4)]
    gathered, keeps, sends, products = {}, [], [], []

    def multiply():
        c, at, count = layout[len(keeps)]
        if c not in gathered:
            parts = [after(x, products[-1]) for x in attended[c]] if c else attended[c]
            gathered[c] = [b for x in parts for b in (x, core_swap(x, pool_count))]
        else:
            gathered[c][0] = after(gathered[c][0], products[-1])
        width = columns // count
        keep, send = output_part(
            f"output_{c}_{at}_{count}", (at * width, width), order, gathered[c], out_weights
        )
        keeps.append(keep)
        sends.append(send)
        products.append(keep)

    stages = reversed_bits(1, tp_count).bit_length()
    last = len(layout) - 1
    total, got, done, places = None, {}, [], []
    for i, (c, at, count) in enumerate(layout):
        start, part = chunks[c]
        column = at * columns // count
        places.append([(r * part, r * rows + start, part, column) for r in range(share)])
    for slot in range(last + stages):
        while len(keeps) < min(slot + 2, last + 1):
            multiply()
        for stage in range(stages):
            i = slot - stage
            if not 0 <= i <= last:
                continue
            if stage == 0:
                got[i] = tp_swap(sends[i], tp_count, 1)
            past = [products[-1]] + ([] if total is None else [total])
            came = after(got[i], *past)
            if stage + 1 < stages:
                keeps[i], total = add_halves(f"halves_{i}_{stage}", keeps[i], came)
                got[i] = tp_swap(total, tp_count, 2 << stage)
            elif i < last:
                total = add_last(f"last_{i}", keeps[i], came)
                done.append(total)
            else:
                attn_out = assemble(done, keeps[i], came, places, share * rows, columns)
    return attn_out, new_key, new_value


def solution(mesh):
    return jax.shard_map(
        shards,
        mesh=mesh,
        in_specs=(
            P(("groups", "pool"), None),
            P(),
            P("pool", "tp"),
            P("pool", "tp"),
            P("pool", "tp"),
            P("tp", "pool"),
            P(("groups", "pool"), "tp", None, None),
            P(("groups", "pool"), "tp", None, None),
            P(("groups", "pool")),
            P(("groups", "pool")),
            P("pool", None, "tp"),
            P("pool", None, "tp"),
            P("pool", None, "tp"),
            P("pool", None, "tp"),
        ),
        out_specs=(
            P(("groups", "tp"), "pool"),
            P(("groups", "pool"), "tp"),
            P(("groups", "pool"), "tp"),
        ),
        check_vma=False,
    )
```

time: 158 us -> 121 us (0.77)
  Pallas kernels: 62.1 us -> 39.1 us
  other arithmetic: 12.6 us -> 4.61 us
  waiting for transfers between devices: 49.1 us -> 43.4 us
    pallas_call x11 -> x22, Pallas kernels: 62.1 us -> 39.1 us  [local_call(): pl.pallas_call(body, in_specs=[spec for _, spec in operands] + [HBM] * le...]
    ppermute x10 -> x8, waiting for transfers between devices: 23.7 us -> 16.6 us  [tp_swap(): return lax.ppermute(x, 'tp', [(z, z ^ step) for z in range(tp_count)])]
    ppermute x8 -> x10, waiting for transfers between devices: 14.2 us -> 19.3 us  [chip_move(): lax.ppermute(x, 'pool', [(p, (p // 2 + d) % chips * 2 + (p % 2 ^ e)) for...]
    ppermute x17 -> x11, waiting for transfers between devices: 5.19 us -> 2.47 us  [core_swap(): return lax.ppermute(x, 'pool', [(p, p ^ 1) for p in range(pool_count)])]
    ppermute x10 -> x8, starting transfers between devices: 12.1 us -> 14.7 us  [tp_swap(): return lax.ppermute(x, 'tp', [(z, z ^ step) for z in range(tp_count)])]
    ppermute x17 -> x11, starting transfers between devices: 4.27 us -> 1.81 us  [core_swap(): return lax.ppermute(x, 'pool', [(p, p ^ 1) for p in range(pool_count)])]
    concatenate x3 -> x0, other arithmetic: 2.29 us -> none  [the longest x1 1.02 us: shards(): cosines = jnp.concatenate([jnp.cos(angles)] * 2, axis=1)]
    convert_element_type x4 -> x3, other arithmetic: 5.32 us -> 3.11 us  [scaled(): return (x * factor[None, :]).astype(jnp.bfloat16)]
  transfers between devices with their start and end apart: 38 -> 32, of which waited for: 15 -> 18; matrix products, arithmetic and copies ran while one was open for 8% -> 4% of each run, Pallas kernels for 32% -> 29%
where the time goes in v6:
time: 121 us
  waiting for transfers between devices  43.4 us (36%)
  Pallas kernels  39.1 us (32%)
  starting transfers between devices  32.6 us (27%)
  other arithmetic  4.61 us (4%)
    pallas_call x22, Pallas kernels, local_call(): pl.pallas_call(body, in_specs=[spec for _, spec in operands] + [HBM] * le...  39.1 us
    ppermute x10, waiting for transfers between devices, chip_move(): lax.ppermute(x, 'pool', [(p, (p // 2 + d) % chips * 2 + (p % 2 ^ e)) for...  19.3 us
    ppermute x8, waiting for transfers between devices, tp_swap(): return lax.ppermute(x, 'tp', [(z, z ^ step) for z in range(tp_count)])  16.6 us
    ppermute x8, starting transfers between devices, tp_swap(): return lax.ppermute(x, 'tp', [(z, z ^ step) for z in range(tp_count)])  14.7 us
    ppermute x10, starting transfers between devices, chip_move(): lax.ppermute(x, 'pool', [(p, (p // 2 + d) % chips * 2 + (p % 2 ^ e)) for...  11.5 us
    ppermute x3, waiting for transfers between devices, shards(): lax.ppermute(shrunk, 'tp', [(i, (i + d) % tp_count) for i in range(tp_cou...  5.12 us
    ppermute x3, starting transfers between devices, shards(): lax.ppermute(shrunk, 'tp', [(i, (i + d) % tp_count) for i in range(tp_cou...  4.67 us
    convert_element_type x3, other arithmetic, scaled(): return (x * factor[None, :]).astype(jnp.bfloat16)  3.11 us
  transfers between devices with their start and end apart: 32, of which 18 were waited for; matrix products, arithmetic and copies ran while one was open for 4% of the time, Pallas kernels for 29%

profile of v6, /device:TPU:0, one launch (start us, length us, event | category | flops | bytes accessed | tf_op | source)
XLA Modules:
  0.0 120.6 jit_solution(10268767380142402854)
XLA Ops:
  0.6 2.5 %collective-permute-start.2 = (s32[1,128]{1,0:T(1,128)}, s32[1,128]{1,0:T(1,128)S(1)}, u32[]{:S(2)}, u32[]{:S(2)}) collective-permute-start(s32[1,128]{1,0:T(1,128)} %bitcast.11), channel_id=1, source_target_pairs={{0,12},{4,8},{8,4},{12,0},{1,13},{5,9},{9,5},{13,1},{2,14},{6,10},... | collective-permute-start | bytes 1544 | tf_op jit(solution)/shard_map/ppermute | solution.py:75
  3.1 0.6 collective-permute-start.1
  3.8 0.7 dynamic-slice_convert_fusion.4
  4.5 1.3 %multiply_convert_fusion.3.refs_5_ = bf16[128,2048]{1,0:T(8,128)(2,1)S(1)} fusion(f32[2048]{0:T(1024)S(1)} %dynamic-slice_convert_fusion.4, bf16[128,8192]{1,0:T(8,128)(2,1)} %refs_0_.1, s32[]{:T(128)S(6)} %select_n.128), kind=kLoop, calls=%fused_computation.3 | loop fusion | flops 786432 | bytes 1056772 | tf_op jit(solution)/shard_map/convert_element_type | solution.py:457
  5.8 0.1 pad_add_fusion.refs_0_
  5.8 0.9 collective-permute-done.1.refs_3_
  6.8 0.9 collective-permute-start.4
  7.7 0.7 dynamic-slice_convert_fusion
  8.4 1.7 %multiply_convert_fusion = (bf16[128,2048]{1,0:T(8,128)(2,1)S(1)}, bf16[128,2048]{1,0:T(8,128)(2,1)S(1)}, bf16[128,2048]{1,0:T(8,128)(2,1)S(1)}) fusion(f32[2048]{0:T(1024)S(1)} %get-tuple-element.168, bf16[128,8192]{1,0:T(8,128)(2,1)} %refs_0_.1, s32[]{:T(128)S(6)} %select_n.137, f32[2048]{0:T(1024)S(1)} %get-tuple-element.169, s32[]{:T(128)S(6)} %select_n.135, ...), kind=kLoop, calls=%fused_computation | loop fusion | flops 2359296 | bytes 3170316 | tf_op jit(solution)/shard_map/convert_element_type | solution.py:457
  10.1 0.1 multiply_convert_fusion.4
  10.3 5.9 %load.1 = (bf16[512,2048]{1,0:T(8,128)(2,1)S(1)}, bf16[512,2048]{1,0:T(8,128)(2,1)S(1)}, bf16[2048,2048]{1,0:T(8,128)(2,1)S(1)}, bf16[2048,256]{1,0:T(8,128)(2,1...) custom-call(bf16[512,2048]{1,0:T(8,128)(2,1)} %bitcast.16, ...), custom_call_target="tpu_custom_call" | custom-call | flops 1000 | bytes 1000 | tf_op jit(solution)/shard_map/load/pallas_call | solution.py:42
  16.2 4.0 %collective-permute-done.4.refs_7_ = bf16[128,2048]{1,0:T(8,128)(2,1)S(1)} collective-permute-done((bf16[128,2048]{1,0:T(8,128)(2,1)S(1)}, bf16[128,2048]{1,0:T(8,128)(2,1)S(1)}, u32[]{:S(2)}, u32[]{:S(2)}) %collective-permute-start.4) | collective-permute-done | bytes 524320 | tf_op jit(solution)/shard_map/ppermute | solution.py:75
  20.2 1.4 %collective-permute-start.12 = (bf16[128,2048]{1,0:T(8,128)(2,1)S(1)}, bf16[128,2048]{1,0:T(8,128)(2,1)S(1)}, u32[]{:S(2)}, u32[]{:S(2)}) collective-permute-start(bf16[128,2048]{1,0:T(8,128)(2,1)S(1)} %get-tuple-element.111), channel_id=1, source_target_pairs={{0,8},{4,12},{8,0},{12,4},{1,9},{5,13},{9,1},{13,5},{2,10},{6,14},... | collective-permute-start | bytes 1572872 | tf_op jit(solution)/shard_map/ppermute | solution.py:75
  21.6 0.5 collective-permute-start.13
  22.1 0.3 collective-permute-start.9
  22.4 0.2 collective-permute-start.10
  22.6 2.4 %shrink.1 = (s32[1,512]{1,0:T(1,128)S(1)}, f32[32,512]{1,0:T(8,128)S(1)}) custom-call(s32[1]{0:T(128)} %bitcast.1.refs_0_, s32[1,128]{1,0:T(1,128)S(1)} %bitcast.14, s32[1,128]{1,0:T(1,128)S(1)} %collective-permute-done.refs_2_, s32[1,128]{1,0:T(1,128)S(1)} %collective-permute-done.1.refs_3_, s32[1,128]{1,0:T(1,128)S(1)} %collective-permute-done.2.refs_4_, ...), custom_call_target="tpu_custom_call" | custom-call | flops 1000 | bytes 1000 | tf_op jit(solution)/shard_map/shrink/pallas_call | solution.py:42
  25.0 3.7 %collective-permute-start.8 = (f32[32,512]{1,0:T(8,128)S(1)}, f32[32,512]{1,0:T(8,128)S(1)}, u32[]{:S(2)}, u32[]{:S(2)}) collective-permute-start(f32[32,512]{1,0:T(8,128)S(1)} %get-tuple-element.95.refs_1_), channel_id=1, source_target_pairs={{0,3},{1,0},{2,1},{3,2},{4,7},{5,4},{6,5},{7,6},{8,11},{9,8},{10,9... | collective-permute-start | bytes 196616 | tf_op jit(solution)/shard_map/ppermute | solution.py:511
  28.7 1.0 collective-permute-start.6
  29.7 0.8 tables.1
  30.4 0.7 collective-permute-done.8.refs_4_
  31.1 4.4 %collective-permute-done.7.refs_3_ = f32[32,512]{1,0:T(8,128)S(1)} collective-permute-done((f32[32,512]{1,0:T(8,128)S(1)}, f32[32,512]{1,0:T(8,128)S(1)}, u32[]{:S(2)}, u32[]{:S(2)}) %collective-permute-start.7) | collective-permute-done | bytes 65568 | tf_op jit(solution)/shard_map/ppermute | solution.py:511
  35.6 4.5 %project_own.1 = (f32[128,2560]{1,0:T(8,128)S(1)}, bf16[128,2560]{1,0:T(8,128)(2,1)S(1)}, bf16[128,2,64,128]{3,2,1,0:T(8,128)(2,1)S(1)}, bf16[128,2,64,128]{3,2,1,0:T(8,128)(2,1)S(1)}) custom-call(s32[1,512]{1,0:T(1,128)S(1)} %get-tuple-element.109.refs_0_, f32[32,512]{1,0:T(8,128)S(1)} %get-tuple-element.95.refs_1_, ...), custom_call_target="tpu_custom_call" | custom-call | flops 1000 | bytes 1000 | tf_op jit(solution)/shard_map/project_own/pallas_call | solution.py:42
  40.1 2.8 %project_1_0.1.refs_0_ = f32[128,2560]{1,0:T(8,128)S(1)} custom-call(s32[1,512]{1,0:T(1,128)S(1)} %get-tuple-element.109.refs_0_, f32[32,512]{1,0:T(8,128)S(1)} %get-tuple-element.95.refs_1_, f32[32,512]{1,0:T(8,128)S(1)} %collective-permute-done.6.refs_2_, f32[32,512]{1,0:T(8,128)S(1)} %collective-permute-done.7.refs_3_, ...), custom_call_target="tpu_custom_call" | custom-call | flops 1000 | bytes 1000 | tf_op jit(solution)/shard_map/project_1_0/pallas_call | solution.py:42
  42.9 2.5 %collective-permute-done.13.refs_5_ = bf16[128,2048]{1,0:T(8,128)(2,1)S(1)} collective-permute-done((bf16[128,2048]{1,0:T(8,128)(2,1)S(1)}, bf16[128,2048]{1,0:T(8,128)(2,1)S(1)}, u32[]{:S(2)}, u32[]{:S(2)}) %collective-permute-start.13) | collective-permute-done | bytes 524320 | tf_op jit(solution)/shard_map/ppermute | solution.py:75
  45.4 2.8 %project_1_1.1 = (bf16[64,2560]{1,0:T(8,128)(2,1)S(1)}, bf16[64,2560]{1,0:T(8,128)(2,1)S(1)}) custom-call(s32[1,512]{1,0:T(1,128)S(1)} %get-tuple-element.109.refs_0_, f32[32,512]{1,0:T(8,128)S(1)} %get-tuple-element.95.refs_1_, f32[32,512]{1,0:T(8,128)S(1)} %collective-permute-done.6.refs_2_, f32[32,512]{1,0:T(8,128)S(1)} %collective-permute-done.7.refs_3_, ...), custom_call_target="tpu_custom_call" | custom-call | flops 1000 | bytes 1000 | tf_op jit(solution)/shard_map/project_1_1/pallas_call | solution.py:42
  48.2 0.3 collective-permute-start.14
  48.5 0.3 collective-permute-start.11
  48.8 0.2 collective-permute-start.16
  49.0 0.9 collective-permute-done.14.refs_1_
  50.0 1.4 %collective-permute-start.15 = (bf16[64,2560]{1,0:T(8,128)(2,1)S(1)}, bf16[64,2560]{1,0:T(8,128)(2,1)S(1)}, u32[]{:S(2)}, u32[]{:S(2)}) collective-permute-start(bf16[64,2560]{1,0:T(8,128)(2,1)S(1)} %add_1_0.1), channel_id=1, source_target_pairs={{0,8},{4,12},{8,0},{12,4},{1,9},{5,13},{9,1},{13,5},{2,10},{6,14},... | collective-permute-start | bytes 983048 | tf_op jit(solution)/shard_map/ppermute | solution.py:75
  51.5 1.3 %collective-permute-start.17 = (bf16[64,2560]{1,0:T(8,128)(2,1)S(1)}, bf16[64,2560]{1,0:T(8,128)(2,1)S(1)}, u32[]{:S(2)}, u32[]{:S(2)}) collective-permute-start(bf16[64,2560]{1,0:T(8,128)(2,1)S(1)} %add_1_1.1), channel_id=1, source_target_pairs={{0,8},{4,12},{8,0},{12,4},{1,9},{5,13},{9,1},{13,5},{2,10},{6,14},... | collective-permute-start | bytes 983048 | tf_op jit(solution)/shard_map/ppermute | solution.py:75
  52.8 7.8 %collective-permute-done.15.refs_2_ = bf16[64,2560]{1,0:T(8,128)(2,1)S(1)} collective-permute-done((bf16[64,2560]{1,0:T(8,128)(2,1)S(1)}, bf16[64,2560]{1,0:T(8,128)(2,1)S(1)}, u32[]{:S(2)}, u32[]{:S(2)}) %collective-permute-start.15) | collective-permute-done | bytes 327712 | tf_op jit(solution)/shard_map/ppermute | solution.py:75
  60.6 5.1 %attend_0.1 = (bf16[64,2048]{1,0:T(8,128)(2,1)S(1)}, bf16[64,256]{1,0:T(8,128)(2,1)S(1)}, bf16[64,256]{1,0:T(8,128)(2,1)S(1)}, bf16[2048,2048]{1,0:T(8,128)(2,1)S(1)}) custom-call(f32[128,2560]{1,0:T(8,128)S(1)} %get-tuple-element.107.refs_0_.refs_2_, bf16[128,2560]{1,0:T(8,128)(2,1)S(1)} %collective-permute-done.11.refs_1_.refs_3_, ...), custom_call_target="tpu_custom_call" | custom-call | flops 1000 | bytes 1000 | tf_op jit(solution)/shard_map/attend_0/pallas_call | solution.py:42
  65.7 1.2 %collective-permute-done.17.refs_4_ = bf16[64,2560]{1,0:T(8,128)(2,1)S(1)} collective-permute-done((bf16[64,2560]{1,0:T(8,128)(2,1)S(1)}, bf16[64,2560]{1,0:T(8,128)(2,1)S(1)}, u32[]{:S(2)}, u32[]{:S(2)}) %collective-permute-start.17) | collective-permute-done | bytes 327712 | tf_op jit(solution)/shard_map/ppermute | solution.py:75
  66.9 1.4 %collective-permute-start.19 = (bf16[64,2048]{1,0:T(8,128)(2,1)S(1)}, bf16[64,2048]{1,0:T(8,128)(2,1)S(1)}, u32[]{:S(2)}, u32[]{:S(2)}) collective-permute-start(bf16[64,2048]{1,0:T(8,128)(2,1)S(1)} %get-tuple-element.130.refs_1_), channel_id=1, source_target_pairs={{0,8},{4,12},{8,0},{12,4},{1,9},{5,13},{9,1},{13,5},{2,10},{6,14},... | collective-permute-start | bytes 786440 | tf_op jit(solution)/shard_map/ppermute | solution.py:75
  68.3 5.5 %attend_1.1 = (bf16[64,2048]{1,0:T(8,128)(2,1)S(1)}, bf16[128,256]{1,0:T(8,128)(2,1)}, bf16[128,256]{1,0:T(8,128)(2,1)}) custom-call(bf16[64,256]{1,0:T(8,128)(2,1)S(1)} %get-tuple-element.126.refs_0_, bf16[64,256]{1,0:T(8,128)(2,1)S(1)} %get-tuple-element.127.refs_1_, f32[128,2560]{1,0:T(8,128)S(1)} %get-tuple-element.107.refs_0_.refs_2_, ...), custom_call_target="tpu_custom_call" | custom-call | flops 1000 | bytes 1000 | tf_op jit(solution)/shard_map/attend_1/pallas_call | solution.py:42
  73.8 0.7 collective-permute-done.19.refs_3_
  74.5 1.4 %collective-permute-start.23 = (bf16[64,2048]{1,0:T(8,128)(2,1)S(1)}, bf16[64,2048]{1,0:T(8,128)(2,1)S(1)}, u32[]{:S(2)}, u32[]{:S(2)}) collective-permute-start(bf16[64,2048]{1,0:T(8,128)(2,1)S(1)} %get-tuple-element.149.refs_1_), channel_id=1, source_target_pairs={{0,8},{4,12},{8,0},{12,4},{1,9},{5,13},{9,1},{13,5},{2,10},{6,14},... | collective-permute-start | bytes 786440 | tf_op jit(solution)/shard_map/ppermute | solution.py:75
  75.9 0.1 collective-permute-done.20.refs_4_
  76.0 3.5 %output_0_0_1.1 = (bf16[128,2048]{1,0:T(8,128)(2,1)S(1)}, bf16[128,2048]{1,0:T(8,128)(2,1)S(1)}) custom-call(s32[4]{0:T(128)S(1)} %pad_add_fusion.refs_0_, bf16[64,2048]{1,0:T(8,128)(2,1)S(1)} %get-tuple-element.130.refs_1_, bf16[64,2048]{1,0:T(8,128)(2,1)S(1)} %collective-permute-done.18.refs_2_, bf16[64,2048]{1,0:T(8,128)(2,1)S(1)} %collective-permute-done.19.refs_3_, ...), custom_call_target="tpu_custom_call" | custom-call | flops 1000 | bytes 1000 | tf_op jit(solution)/shard_map/output_0_0_1/pallas_call | solution.py:42
  79.5 1.6 %collective-permute-start.21 = (bf16[128,2048]{1,0:T(8,128)(2,1)S(1)}, bf16[128,2048]{1,0:T(8,128)(2,1)S(1)}, u32[]{:S(2)}, u32[]{:S(2)}) collective-permute-start(bf16[128,2048]{1,0:T(8,128)(2,1)S(1)} %get-tuple-element.133), channel_id=1, source_target_pairs={{0,1},{1,0},{2,3},{3,2},{4,5},{5,4},{6,7},{7,6},{8,9},{9,8},{10,11... | collective-permute-start | bytes 1572872 | tf_op jit(solution)/shard_map/ppermute | solution.py:83
  81.1 2.1 %collective-permute-done.23.refs_3_ = bf16[64,2048]{1,0:T(8,128)(2,1)S(1)} collective-permute-done((bf16[64,2048]{1,0:T(8,128)(2,1)S(1)}, bf16[64,2048]{1,0:T(8,128)(2,1)S(1)}, u32[]{:S(2)}, u32[]{:S(2)}) %collective-permute-start.23) | collective-permute-done | bytes 262176 | tf_op jit(solution)/shard_map/ppermute | solution.py:75
  83.2 0.5 collective-permute-start.24
  83.7 1.0 collective-permute-done.22.refs_2_
  84.7 0.4 collective-permute-done.24.refs_4_
  85.1 2.0 %output_1_0_2.1 = (bf16[128,1024]{1,0:T(8,128)(2,1)S(1)}, bf16[128,1024]{1,0:T(8,128)(2,1)S(1)}) custom-call(s32[4]{0:T(128)S(1)} %pad_add_fusion.refs_0_, bf16[64,2048]{1,0:T(8,128)(2,1)S(1)} %get-tuple-element.149.refs_1_, bf16[64,2048]{1,0:T(8,128)(2,1)S(1)} %collective-permute-done.22.refs_2_, bf16[64,2048]{1,0:T(8,128)(2,1)S(1)} %collective-permute-done.23.refs_3_, ...), custom_call_target="tpu_custom_call" | custom-call | flops 1000 | bytes 1000 | tf_op jit(solution)/shard_map/output_1_0_2/pallas_call | solution.py:42
  87.2 1.6 %collective-permute-start.26 = (bf16[128,1024]{1,0:T(8,128)(2,1)S(1)}, bf16[128,1024]{1,0:T(8,128)(2,1)S(1)}, u32[]{:S(2)}, u32[]{:S(2)}) collective-permute-start(bf16[128,1024]{1,0:T(8,128)(2,1)S(1)} %get-tuple-element.144), channel_id=1, source_target_pairs={{0,1},{1,0},{2,3},{3,2},{4,5},{5,4},{6,7},{7,6},{8,9},{9,8},{10,11... | collective-permute-start | bytes 786440 | tf_op jit(solution)/shard_map/ppermute | solution.py:83
  88.8 5.5 %collective-permute-done.21.refs_1_ = bf16[128,2048]{1,0:T(8,128)(2,1)S(1)} collective-permute-done((bf16[128,2048]{1,0:T(8,128)(2,1)S(1)}, bf16[128,2048]{1,0:T(8,128)(2,1)S(1)}, u32[]{:S(2)}, u32[]{:S(2)}) %collective-permute-start.21) | collective-permute-done | bytes 524320 | tf_op jit(solution)/shard_map/ppermute | solution.py:83
  94.3 0.1 halves_0_0.1
  94.4 2.7 %collective-permute-start.25 = (bf16[64,2048]{1,0:T(8,128)(2,1)S(1)}, bf16[64,2048]{1,0:T(8,128)(2,1)S(1)}, u32[]{:S(2)}, u32[]{:S(2)}) collective-permute-start(bf16[64,2048]{1,0:T(8,128)(2,1)S(1)} %get-tuple-element.141), channel_id=1, source_target_pairs={{0,2},{1,3},{2,0},{3,1},{4,6},{5,7},{6,4},{7,5},{8,10},{9,11},{10,... | collective-permute-start | bytes 786440 | tf_op jit(solution)/shard_map/ppermute | solution.py:83
  97.1 1.3 %output_1_2_4.1 = (bf16[128,512]{1,0:T(8,128)(2,1)S(1)}, bf16[128,512]{1,0:T(8,128)(2,1)S(1)}) custom-call(s32[4]{0:T(128)S(1)} %pad_add_fusion.refs_0_, bf16[64,2048]{1,0:T(8,128)(2,1)S(1)} %get-tuple-element.149.refs_1_, bf16[64,2048]{1,0:T(8,128)(2,1)S(1)} %collective-permute-done.22.refs_2_, bf16[64,2048]{1,0:T(8,128)(2,1)S(1)} %collective-permute-done.23.refs_3_, ...), custom_call_target="tpu_custom_call" | custom-call | flops 1000 | bytes 1000 | tf_op jit(solution)/shard_map/output_1_2_4/pallas_call | solution.py:42
  98.4 1.6 %collective-permute-start.28 = (bf16[128,512]{1,0:T(8,128)(2,1)S(1)}, bf16[128,512]{1,0:T(8,128)(2,1)S(1)}, u32[]{:S(2)}, u32[]{:S(2)}) collective-permute-start(bf16[128,512]{1,0:T(8,128)(2,1)S(1)} %get-tuple-element.151), channel_id=1, source_target_pairs={{0,1},{1,0},{2,3},{3,2},{4,5},{5,4},{6,7},{7,6},{8,9},{9,8},{10,11... | collective-permute-start | bytes 393224 | tf_op jit(solution)/shard_map/ppermute | solution.py:83
  100.1 4.6 %collective-permute-done.26.refs_1_ = bf16[128,1024]{1,0:T(8,128)(2,1)S(1)} collective-permute-done((bf16[128,1024]{1,0:T(8,128)(2,1)S(1)}, bf16[128,1024]{1,0:T(8,128)(2,1)S(1)}, u32[]{:S(2)}, u32[]{:S(2)}) %collective-permute-start.26) | collective-permute-done | bytes 262176 | tf_op jit(solution)/shard_map/ppermute | solution.py:83
  104.7 0.1 halves_1_0.1
  104.7 0.1 collective-permute-start.27
  104.8 1.3 %output_1_3_4.1 = (bf16[128,512]{1,0:T(8,128)(2,1)S(1)}, bf16[128,512]{1,0:T(8,128)(2,1)S(1)}) custom-call(s32[4]{0:T(128)S(1)} %pad_add_fusion.refs_0_, bf16[64,2048]{1,0:T(8,128)(2,1)S(1)} %get-tuple-element.149.refs_1_, bf16[64,2048]{1,0:T(8,128)(2,1)S(1)} %collective-permute-done.22.refs_2_, bf16[64,2048]{1,0:T(8,128)(2,1)S(1)} %collective-permute-done.23.refs_3_, ...), custom_call_target="tpu_custom_call" | custom-call | flops 1000 | bytes 1000 | tf_op jit(solution)/shard_map/output_1_3_4/pallas_call | solution.py:42
  106.1 1.9 %collective-permute-start.30 = (bf16[128,512]{1,0:T(8,128)(2,1)S(1)}, bf16[128,512]{1,0:T(8,128)(2,1)S(1)}, u32[]{:S(2)}, u32[]{:S(2)}) collective-permute-start(bf16[128,512]{1,0:T(8,128)(2,1)S(1)} %get-tuple-element.156), channel_id=1, source_target_pairs={{0,1},{1,0},{2,3},{3,2},{4,5},{5,4},{6,7},{7,6},{8,9},{9,8},{10,11... | collective-permute-start | bytes 393224 | tf_op jit(solution)/shard_map/ppermute | solution.py:83
  108.1 0.3 collective-permute-done.25.refs_1_
  108.5 2.6 %collective-permute-start.29 = (bf16[64,512]{1,0:T(8,128)(2,1)S(1)}, bf16[64,512]{1,0:T(8,128)(2,1)S(1)}, u32[]{:S(2)}, u32[]{:S(2)}) collective-permute-start(bf16[64,512]{1,0:T(8,128)(2,1)S(1)} %get-tuple-element.153), channel_id=1, source_target_pairs={{0,2},{1,3},{2,0},{3,1},{4,6},{5,7},{6,4},{7,5},{8,10},{9,11},{10,... | collective-permute-start | bytes 196616 | tf_op jit(solution)/shard_map/ppermute | solution.py:83
  111.1 3.0 %collective-permute-done.27.refs_1_ = bf16[64,1024]{1,0:T(8,128)(2,1)S(1)} collective-permute-done((bf16[64,1024]{1,0:T(8,128)(2,1)S(1)}, bf16[64,1024]{1,0:T(8,128)(2,1)S(1)}, u32[]{:S(2)}, u32[]{:S(2)}) %collective-permute-start.27) | collective-permute-done | bytes 131104 | tf_op jit(solution)/shard_map/ppermute | solution.py:83
  114.2 2.5 %collective-permute-start.31 = (bf16[64,512]{1,0:T(8,128)(2,1)S(1)}, bf16[64,512]{1,0:T(8,128)(2,1)S(1)}, u32[]{:S(2)}, u32[]{:S(2)}) collective-permute-start(bf16[64,512]{1,0:T(8,128)(2,1)S(1)} %get-tuple-element.158), channel_id=1, source_target_pairs={{0,2},{1,3},{2,0},{3,1},{4,6},{5,7},{6,4},{7,5},{8,10},{9,11},{10,... | collective-permute-start | bytes 196616 | tf_op jit(solution)/shard_map/ppermute | solution.py:83
  116.7 3.1 %collective-permute-done.31.refs_4_ = bf16[64,512]{1,0:T(8,128)(2,1)S(1)} collective-permute-done((bf16[64,512]{1,0:T(8,128)(2,1)S(1)}, bf16[64,512]{1,0:T(8,128)(2,1)S(1)}, u32[]{:S(2)}, u32[]{:S(2)}) %collective-permute-start.31) | collective-permute-done | bytes 65568 | tf_op jit(solution)/shard_map/ppermute | solution.py:83
  119.8 0.8 assemble.1
  (34 shorter events, 0.4 us)
Async XLA Ops:
  0.6 5.2 %collective-permute-start.2 = (s32[1,128]{1,0:T(1,128)}, s32[1,128]{1,0:T(1,128)S(1)}, u32[]{:S(2)}, u32[]{:S(2)}) collective-permute-start(s32[1,128]{1,0:T(1,128)} %bitcast.11), channel_id=1, source_target_pairs={{0,12},{4,8},{8,4},{12,0},{1,13},{5,9},{9,5},{13,1},{2,14},{6,10},... | collective-permute-start | bytes 1544 | tf_op jit(solution)/shard_map/ppermute | solution.py:75
  3.1 3.7 %collective-permute-start.1 = (s32[1,128]{1,0:T(1,128)}, s32[1,128]{1,0:T(1,128)S(1)}, u32[]{:S(2)}, u32[]{:S(2)}) collective-permute-start(s32[1,128]{1,0:T(1,128)} %bitcast.12), channel_id=1, source_target_pairs={{0,8},{4,12},{8,0},{12,4},{1,9},{5,13},{9,1},{13,5},{2,10},{6,14},... | collective-permute-start | bytes 1544 | tf_op jit(solution)/shard_map/ppermute | solution.py:75
  3.7 3.0 %collective-permute-start = (s32[1,128]{1,0:T(1,128)}, s32[1,128]{1,0:T(1,128)S(1)}, u32[]{:S(2)}, u32[]{:S(2)}) collective-permute-start(s32[1,128]{1,0:T(1,128)} %bitcast.13), channel_id=1, source_target_pairs={{0,4},{4,0},{8,12},{12,8},{1,5},{5,1},{9,13},{13,9},{2,6},{6,2},{1... | collective-permute-start | bytes 1544 | tf_op jit(solution)/shard_map/ppermute | solution.py:75
  4.5 5.7 %copy-start = (bf16[128,8192]{1,0:T(8,128)(2,1)S(1)}, bf16[128,8192]{1,0:T(8,128)(2,1)}, u32[]{:S(2)}) copy-start(bf16[128,8192]{1,0:T(8,128)(2,1)} %refs_0_.1) | copy-start | bytes 6291460
  6.8 13.4 %collective-permute-start.4 = (bf16[128,2048]{1,0:T(8,128)(2,1)S(1)}, bf16[128,2048]{1,0:T(8,128)(2,1)S(1)}, u32[]{:S(2)}, u32[]{:S(2)}) collective-permute-start(bf16[128,2048]{1,0:T(8,128)(2,1)S(1)} %multiply_convert_fusion.3.refs_5_), channel_id=1, source_target_pairs={{0,8},{4,12},{8,0},{12,4},{1,9},{5,13},{9,1},{13,5},{2,10},{6,14},... | collective-permute-start | bytes 1572872 | tf_op jit(solution)/shard_map/ppermute | solution.py:75
  7.7 14.7 %collective-permute-start.3 = (bf16[128,2048]{1,0:T(8,128)(2,1)S(1)}, bf16[128,2048]{1,0:T(8,128)(2,1)S(1)}, u32[]{:S(2)}, u32[]{:S(2)}) collective-permute-start(bf16[128,2048]{1,0:T(8,128)(2,1)S(1)} %multiply_convert_fusion.3.refs_5_), channel_id=1, source_target_pairs={{0,4},{4,0},{8,12},{12,8},{1,5},{5,1},{9,13},{13,9},{2,6},{6,2},{1... | collective-permute-start | bytes 1572872 | tf_op jit(solution)/shard_map/ppermute | solution.py:70
  10.3 12.4 %copy-start.1 = (s32[128]{0:T(128)S(1)}, s32[128]{0:T(128)}, u32[]{:S(2)}) copy-start(s32[128]{0:T(128)} %param.23) | copy-start | bytes 1540
  20.2 2.4 %collective-permute-start.5 = (bf16[128,2048]{1,0:T(8,128)(2,1)S(1)}, bf16[128,2048]{1,0:T(8,128)(2,1)S(1)}, u32[]{:S(2)}, u32[]{:S(2)}) collective-permute-start(bf16[128,2048]{1,0:T(8,128)(2,1)S(1)} %collective-permute-done.4.refs_7_), channel_id=1, source_target_pairs={{0,4},{4,0},{8,12},{12,8},{1,5},{5,1},{9,13},{13,9},{2,6},{6,2},{1... | collective-permute-start | bytes 1572872 | tf_op jit(solution)/shard_map/ppermute | solution.py:70
  20.2 19.8 %collective-permute-start.12 = (bf16[128,2048]{1,0:T(8,128)(2,1)S(1)}, bf16[128,2048]{1,0:T(8,128)(2,1)S(1)}, u32[]{:S(2)}, u32[]{:S(2)}) collective-permute-start(bf16[128,2048]{1,0:T(8,128)(2,1)S(1)} %get-tuple-element.111), channel_id=1, source_target_pairs={{0,8},{4,12},{8,0},{12,4},{1,9},{5,13},{9,1},{13,5},{2,10},{6,14},... | collective-permute-start | bytes 1572872 | tf_op jit(solution)/shard_map/ppermute | solution.py:75
  21.6 23.8 %collective-permute-start.13 = (bf16[128,2048]{1,0:T(8,128)(2,1)S(1)}, bf16[128,2048]{1,0:T(8,128)(2,1)S(1)}, u32[]{:S(2)}, u32[]{:S(2)}) collective-permute-start(bf16[128,2048]{1,0:T(8,128)(2,1)S(1)} %get-tuple-element.113), channel_id=1, source_target_pairs={{0,12},{4,8},{8,4},{12,0},{1,13},{5,9},{9,5},{13,1},{2,14},{6,10},... | collective-permute-start | bytes 1572872 | tf_op jit(solution)/shard_map/ppermute | solution.py:75
  22.1 6.6 %collective-permute-start.9 = (bf16[64,2048]{1,0:T(8,128)(2,1)S(1)}, bf16[64,2048]{1,0:T(8,128)(2,1)S(1)}, u32[]{:S(2)}, u32[]{:S(2)}) collective-permute-start(bf16[64,2048]{1,0:T(8,128)(2,1)S(1)} %get-tuple-element.100), channel_id=1, source_target_pairs={{0,4},{4,0},{8,12},{12,8},{1,5},{5,1},{9,13},{13,9},{2,6},{6,2},{1... | collective-permute-start | bytes 786440 | tf_op jit(solution)/shard_map/ppermute | solution.py:70
  22.4 6.3 %collective-permute-start.10 = (bf16[64,2048]{1,0:T(8,128)(2,1)S(1)}, bf16[64,2048]{1,0:T(8,128)(2,1)S(1)}, u32[]{:S(2)}, u32[]{:S(2)}) collective-permute-start(bf16[64,2048]{1,0:T(8,128)(2,1)S(1)} %get-tuple-element.101), channel_id=1, source_target_pairs={{0,4},{4,0},{8,12},{12,8},{1,5},{5,1},{9,13},{13,9},{2,6},{6,2},{1... | collective-permute-start | bytes 786440 | tf_op jit(solution)/shard_map/ppermute | solution.py:70
  22.6 7.1 %copy-start.2 = (s32[128]{0:T(128)S(1)}, s32[128]{0:T(128)}, u32[]{:S(2)}) copy-start(s32[128]{0:T(128)} %param.22) | copy-start | bytes 1540
  25.0 6.1 %collective-permute-start.8 = (f32[32,512]{1,0:T(8,128)S(1)}, f32[32,512]{1,0:T(8,128)S(1)}, u32[]{:S(2)}, u32[]{:S(2)}) collective-permute-start(f32[32,512]{1,0:T(8,128)S(1)} %get-tuple-element.95.refs_1_), channel_id=1, source_target_pairs={{0,3},{1,0},{2,1},{3,2},{4,7},{5,4},{6,5},{7,6},{8,11},{9,8},{10,9... | collective-permute-start | bytes 196616 | tf_op jit(solution)/shard_map/ppermute | solution.py:511
  28.6 6.9 %collective-permute-start.7 = (f32[32,512]{1,0:T(8,128)S(1)}, f32[32,512]{1,0:T(8,128)S(1)}, u32[]{:S(2)}, u32[]{:S(2)}) collective-permute-start(f32[32,512]{1,0:T(8,128)S(1)} %get-tuple-element.95.refs_1_), channel_id=1, source_target_pairs={{0,2},{1,3},{2,0},{3,1},{4,6},{5,7},{6,4},{7,5},{8,10},{9,11},{10,... | collective-permute-start | bytes 196616 | tf_op jit(solution)/shard_map/ppermute | solution.py:511
  28.7 6.9 %collective-permute-start.6 = (f32[32,512]{1,0:T(8,128)S(1)}, f32[32,512]{1,0:T(8,128)S(1)}, u32[]{:S(2)}, u32[]{:S(2)}) collective-permute-start(f32[32,512]{1,0:T(8,128)S(1)} %get-tuple-element.95.refs_1_), channel_id=1, source_target_pairs={{0,1},{1,2},{2,3},{3,0},{4,5},{5,6},{6,7},{7,4},{8,9},{9,10},{10,1... | collective-permute-start | bytes 196616 | tf_op jit(solution)/shard_map/ppermute | solution.py:511
  48.2 1.7 %collective-permute-start.14 = (bf16[64,2560]{1,0:T(8,128)(2,1)S(1)}, bf16[64,2560]{1,0:T(8,128)(2,1)S(1)}, u32[]{:S(2)}, u32[]{:S(2)}) collective-permute-start(bf16[64,2560]{1,0:T(8,128)(2,1)S(1)} %get-tuple-element.115), channel_id=1, source_target_pairs={{0,4},{4,0},{8,12},{12,8},{1,5},{5,1},{9,13},{13,9},{2,6},{6,2},{1... | collective-permute-start | bytes 983048 | tf_op jit(solution)/shard_map/ppermute | solution.py:70
  48.5 12.1 %collective-permute-start.11 = (bf16[128,2560]{1,0:T(8,128)(2,1)S(1)}, bf16[128,2560]{1,0:T(8,128)(2,1)S(1)}, u32[]{:S(2)}, u32[]{:S(2)}) collective-permute-start(bf16[128,2560]{1,0:T(8,128)(2,1)S(1)} %get-tuple-element.108), channel_id=1, source_target_pairs={{0,4},{4,0},{8,12},{12,8},{1,5},{5,1},{9,13},{13,9},{2,6},{6,2},{1... | collective-permute-start | bytes 1966088 | tf_op jit(solution)/shard_map/ppermute | solution.py:70
  48.8 2.6 %collective-permute-start.16 = (bf16[64,2560]{1,0:T(8,128)(2,1)S(1)}, bf16[64,2560]{1,0:T(8,128)(2,1)S(1)}, u32[]{:S(2)}, u32[]{:S(2)}) collective-permute-start(bf16[64,2560]{1,0:T(8,128)(2,1)S(1)} %get-tuple-element.116), channel_id=1, source_target_pairs={{0,4},{4,0},{8,12},{12,8},{1,5},{5,1},{9,13},{13,9},{2,6},{6,2},{1... | collective-permute-start | bytes 983048 | tf_op jit(solution)/shard_map/ppermute | solution.py:70
  50.0 10.6 %collective-permute-start.15 = (bf16[64,2560]{1,0:T(8,128)(2,1)S(1)}, bf16[64,2560]{1,0:T(8,128)(2,1)S(1)}, u32[]{:S(2)}, u32[]{:S(2)}) collective-permute-start(bf16[64,2560]{1,0:T(8,128)(2,1)S(1)} %add_1_0.1), channel_id=1, source_target_pairs={{0,8},{4,12},{8,0},{12,4},{1,9},{5,13},{9,1},{13,5},{2,10},{6,14},... | collective-permute-start | bytes 983048 | tf_op jit(solution)/shard_map/ppermute | solution.py:75
  51.5 15.4 %collective-permute-start.17 = (bf16[64,2560]{1,0:T(8,128)(2,1)S(1)}, bf16[64,2560]{1,0:T(8,128)(2,1)S(1)}, u32[]{:S(2)}, u32[]{:S(2)}) collective-permute-start(bf16[64,2560]{1,0:T(8,128)(2,1)S(1)} %add_1_1.1), channel_id=1, source_target_pairs={{0,8},{4,12},{8,0},{12,4},{1,9},{5,13},{9,1},{13,5},{2,10},{6,14},... | collective-permute-start | bytes 983048 | tf_op jit(solution)/shard_map/ppermute | solution.py:75
  66.9 7.6 %collective-permute-start.19 = (bf16[64,2048]{1,0:T(8,128)(2,1)S(1)}, bf16[64,2048]{1,0:T(8,128)(2,1)S(1)}, u32[]{:S(2)}, u32[]{:S(2)}) collective-permute-start(bf16[64,2048]{1,0:T(8,128)(2,1)S(1)} %get-tuple-element.130.refs_1_), channel_id=1, source_target_pairs={{0,8},{4,12},{8,0},{12,4},{1,9},{5,13},{9,1},{13,5},{2,10},{6,14},... | collective-permute-start | bytes 786440 | tf_op jit(solution)/shard_map/ppermute | solution.py:75
  73.8 2.1 %collective-permute-start.18 = (bf16[64,2048]{1,0:T(8,128)(2,1)S(1)}, bf16[64,2048]{1,0:T(8,128)(2,1)S(1)}, u32[]{:S(2)}, u32[]{:S(2)}) collective-permute-start(bf16[64,2048]{1,0:T(8,128)(2,1)S(1)} %get-tuple-element.130.refs_1_), channel_id=1, source_target_pairs={{0,4},{4,0},{8,12},{12,8},{1,5},{5,1},{9,13},{13,9},{2,6},{6,2},{1... | collective-permute-start | bytes 786440 | tf_op jit(solution)/shard_map/ppermute | solution.py:70
  74.5 1.5 %collective-permute-start.20 = (bf16[64,2048]{1,0:T(8,128)(2,1)S(1)}, bf16[64,2048]{1,0:T(8,128)(2,1)S(1)}, u32[]{:S(2)}, u32[]{:S(2)}) collective-permute-start(bf16[64,2048]{1,0:T(8,128)(2,1)S(1)} %collective-permute-done.19.refs_3_), channel_id=1, source_target_pairs={{0,4},{4,0},{8,12},{12,8},{1,5},{5,1},{9,13},{13,9},{2,6},{6,2},{1... | collective-permute-start | bytes 786440 | tf_op jit(solution)/shard_map/ppermute | solution.py:70
  74.5 8.7 %collective-permute-start.23 = (bf16[64,2048]{1,0:T(8,128)(2,1)S(1)}, bf16[64,2048]{1,0:T(8,128)(2,1)S(1)}, u32[]{:S(2)}, u32[]{:S(2)}) collective-permute-start(bf16[64,2048]{1,0:T(8,128)(2,1)S(1)} %get-tuple-element.149.refs_1_), channel_id=1, source_target_pairs={{0,8},{4,12},{8,0},{12,4},{1,9},{5,13},{9,1},{13,5},{2,10},{6,14},... | collective-permute-start | bytes 786440 | tf_op jit(solution)/shard_map/ppermute | solution.py:75
  79.5 14.8 %collective-permute-start.21 = (bf16[128,2048]{1,0:T(8,128)(2,1)S(1)}, bf16[128,2048]{1,0:T(8,128)(2,1)S(1)}, u32[]{:S(2)}, u32[]{:S(2)}) collective-permute-start(bf16[128,2048]{1,0:T(8,128)(2,1)S(1)} %get-tuple-element.133), channel_id=1, source_target_pairs={{0,1},{1,0},{2,3},{3,2},{4,5},{5,4},{6,7},{7,6},{8,9},{9,8},{10,11... | collective-permute-start | bytes 1572872 | tf_op jit(solution)/shard_map/ppermute | solution.py:83
  83.2 1.5 %collective-permute-start.22 = (bf16[64,2048]{1,0:T(8,128)(2,1)S(1)}, bf16[64,2048]{1,0:T(8,128)(2,1)S(1)}, u32[]{:S(2)}, u32[]{:S(2)}) collective-permute-start(bf16[64,2048]{1,0:T(8,128)(2,1)S(1)} %get-tuple-element.149.refs_1_), channel_id=1, source_target_pairs={{0,4},{4,0},{8,12},{12,8},{1,5},{5,1},{9,13},{13,9},{2,6},{6,2},{1... | collective-permute-start | bytes 786440 | tf_op jit(solution)/shard_map/ppermute | solution.py:70
  83.2 1.9 %collective-permute-start.24 = (bf16[64,2048]{1,0:T(8,128)(2,1)S(1)}, bf16[64,2048]{1,0:T(8,128)(2,1)S(1)}, u32[]{:S(2)}, u32[]{:S(2)}) collective-permute-start(bf16[64,2048]{1,0:T(8,128)(2,1)S(1)} %collective-permute-done.23.refs_3_), channel_id=1, source_target_pairs={{0,4},{4,0},{8,12},{12,8},{1,5},{5,1},{9,13},{13,9},{2,6},{6,2},{1... | collective-permute-start | bytes 786440 | tf_op jit(solution)/shard_map/ppermute | solution.py:70
  87.2 17.5 %collective-permute-start.26 = (bf16[128,1024]{1,0:T(8,128)(2,1)S(1)}, bf16[128,1024]{1,0:T(8,128)(2,1)S(1)}, u32[]{:S(2)}, u32[]{:S(2)}) collective-permute-start(bf16[128,1024]{1,0:T(8,128)(2,1)S(1)} %get-tuple-element.144), channel_id=1, source_target_pairs={{0,1},{1,0},{2,3},{3,2},{4,5},{5,4},{6,7},{7,6},{8,9},{9,8},{10,11... | collective-permute-start | bytes 786440 | tf_op jit(solution)/shard_map/ppermute | solution.py:83
  94.4 13.9 %collective-permute-start.25 = (bf16[64,2048]{1,0:T(8,128)(2,1)S(1)}, bf16[64,2048]{1,0:T(8,128)(2,1)S(1)}, u32[]{:S(2)}, u32[]{:S(2)}) collective-permute-start(bf16[64,2048]{1,0:T(8,128)(2,1)S(1)} %get-tuple-element.141), channel_id=1, source_target_pairs={{0,2},{1,3},{2,0},{3,1},{4,6},{5,7},{6,4},{7,5},{8,10},{9,11},{10,... | collective-permute-start | bytes 786440 | tf_op jit(solution)/shard_map/ppermute | solution.py:83
  98.4 10.0 %collective-permute-start.28 = (bf16[128,512]{1,0:T(8,128)(2,1)S(1)}, bf16[128,512]{1,0:T(8,128)(2,1)S(1)}, u32[]{:S(2)}, u32[]{:S(2)}) collective-permute-start(bf16[128,512]{1,0:T(8,128)(2,1)S(1)} %get-tuple-element.151), channel_id=1, source_target_pairs={{0,1},{1,0},{2,3},{3,2},{4,5},{5,4},{6,7},{7,6},{8,9},{9,8},{10,11... | collective-permute-start | bytes 393224 | tf_op jit(solution)/shard_map/ppermute | solution.py:83
  104.7 9.4 %collective-permute-start.27 = (bf16[64,1024]{1,0:T(8,128)(2,1)S(1)}, bf16[64,1024]{1,0:T(8,128)(2,1)S(1)}, u32[]{:S(2)}, u32[]{:S(2)}) collective-permute-start(bf16[64,1024]{1,0:T(8,128)(2,1)S(1)} %get-tuple-element.146), channel_id=1, source_target_pairs={{0,2},{1,3},{2,0},{3,1},{4,6},{5,7},{6,4},{7,5},{8,10},{9,11},{10,... | collective-permute-start | bytes 393224 | tf_op jit(solution)/shard_map/ppermute | solution.py:83
  106.1 8.1 %collective-permute-start.30 = (bf16[128,512]{1,0:T(8,128)(2,1)S(1)}, bf16[128,512]{1,0:T(8,128)(2,1)S(1)}, u32[]{:S(2)}, u32[]{:S(2)}) collective-permute-start(bf16[128,512]{1,0:T(8,128)(2,1)S(1)} %get-tuple-element.156), channel_id=1, source_target_pairs={{0,1},{1,0},{2,3},{3,2},{4,5},{5,4},{6,7},{7,6},{8,9},{9,8},{10,11... | collective-permute-start | bytes 393224 | tf_op jit(solution)/shard_map/ppermute | solution.py:83
  108.5 8.2 %collective-permute-start.29 = (bf16[64,512]{1,0:T(8,128)(2,1)S(1)}, bf16[64,512]{1,0:T(8,128)(2,1)S(1)}, u32[]{:S(2)}, u32[]{:S(2)}) collective-permute-start(bf16[64,512]{1,0:T(8,128)(2,1)S(1)} %get-tuple-element.153), channel_id=1, source_target_pairs={{0,2},{1,3},{2,0},{3,1},{4,6},{5,7},{6,4},{7,5},{8,10},{9,11},{10,... | collective-permute-start | bytes 196616 | tf_op jit(solution)/shard_map/ppermute | solution.py:83
  114.2 5.5 %collective-permute-start.31 = (bf16[64,512]{1,0:T(8,128)(2,1)S(1)}, bf16[64,512]{1,0:T(8,128)(2,1)S(1)}, u32[]{:S(2)}, u32[]{:S(2)}) collective-permute-start(bf16[64,512]{1,0:T(8,128)(2,1)S(1)} %get-tuple-element.158), channel_id=1, source_target_pairs={{0,2},{1,3},{2,0},{3,1},{4,6},{5,7},{6,4},{7,5},{8,10},{9,11},{10,... | collective-permute-start | bytes 196616 | tf_op jit(solution)/shard_map/ppermute | solution.py:83

commit v7 on v6

--- a/solution.py
+++ b/solution.py
@@ -466,8 +466,8 @@
     first, tokens_1, gain_1 = lax.optimization_barrier((first, tokens, input_norm_gain))
     same_core = [first] + [chip_move(first, pool_count, d) for d in range(1, chips)]
 
-    cut = rows // 2
-    chunks = [(0, cut), (cut, rows - cut)]
+    cuts = [0, rows // 4, rows // 2, rows]
+    chunks = [(start, stop - start) for start, stop in zip(cuts, cuts[1:])]
     own = scaled(pool_at * base, base, tokens_1, gain_1)
     partner_at = (pool_at // 2 * 2 + 1 - core) * base
     partner = [
@@ -524,11 +524,10 @@
     )
     swapped = core_swap(own_send, pool_count)
     local_ids = after(local_ids, own_sums)
-    moved = [[] for _ in chunks]
-    both = None
+    partial, send = [], None
     for d in range(1, chips):
-        if both is not None:
-            remote[d][0] = after(remote[d][0], both)
+        if partial:
+            remote[d][0] = after(remote[d][0], sends[0])
         at = 2 * d * rows
         (keep,) = project(
             f"project_{d}_0",
@@ -548,16 +547,46 @@
             [after(remote[d][1], keep)],
             weights,
         )
-        for c, window in enumerate(chunks):
-            swap = core_swap(sends[c], pool_count)
-            if c:
-                swap = after(swap, both)
-            both = add_sums(f"add_{d}_{c}", window, keep, swap)
-            moved[c].append(chip_move(both, pool_count, -d))
+        partial.append((d, keep, sends))
+
+    def reduced(c, *earlier):
+        arrived = []
+        for d, keep, sends in partial:
+            swap = after(core_swap(sends[c], pool_count), *earlier)
+            both = add_sums(f"add_{d}_{c}", chunks[c], keep, swap)
+            arrived.append(chip_move(both, pool_count, -d))
+            earlier = [both]
+        return arrived, both
+
+    moved = [None] * len(chunks)
+    moved[0], both = reduced(0)
+    moved[1], both = reduced(1, both)
     moved[0][0] = after(moved[0][0], both)
 
-    attended, earlier = [], []
+    columns = output_matrix.shape[1]
+    layout = [(0, 0, 1), (1, 0, 1), (2, 0, 2), (2, 2, 4), (2, 3, 4)]
+    attended, gathered, keeps, sends, products = [], {}, [], [], []
+
+    def multiply(*earlier):
+        c, at, count = layout[len(keeps)]
+        if c not in gathered:
+            parts = [after(x, *earlier) for x in attended[c]]
+            gathered[c] = [b for x in parts for b in (x, core_swap(x, pool_count))]
+        else:
+            gathered[c][0] = after(gathered[c][0], products[-1])
+        width = columns // count
+        keep, send = output_part(
+            f"output_{c}_{at}_{count}", (at * width, width), order, gathered[c], out_weights
+        )
+        keeps.append(keep)
+        sends.append(send)
+        products.append(keep)
+
+    earlier = []
     for c, window in enumerate(chunks):
+        if c == 2:
+            multiply(earlier[0], both)
+            moved[c][0] = after(moved[c][0], products[-1])
         out, *earlier = attend(
             f"attend_{c}",
             window,
@@ -572,32 +601,13 @@
         )
         if c == 0:
             out_weights = earlier[2]
-        if c + 1 < len(chunks):
-            out, *moved[c + 1] = lax.optimization_barrier((out, *moved[c + 1]))
+            out, *moved[1] = lax.optimization_barrier((out, *moved[1]))
         else:
             out = after(out, attended[-1][-1])
         attended.append([out] + [chip_move(out, pool_count, d) for d in range(1, chips)])
+        if c + 2 < len(chunks):
+            moved[c + 2], both = reduced(c + 2, attended[c][-1])
     new_key, new_value = earlier
-    attended[0][0] = after(attended[0][0], new_key)
-
-    columns = output_matrix.shape[1]
-    layout = [(0, 0, 1), (1, 0, 2), (1, 2, 4), (1, 3, 4)]
-    gathered, keeps, sends, products = {}, [], [], []
-
-    def multiply():
-        c, at, count = layout[len(keeps)]
-        if c not in gathered:
-            parts = [after(x, products[-1]) for x in attended[c]] if c else attended[c]
-            gathered[c] = [b for x in parts for b in (x, core_swap(x, pool_count))]
-        else:
-            gathered[c][0] = after(gathered[c][0], products[-1])
-        width = columns // count
-        keep, send = output_part(
-            f"output_{c}_{at}_{count}", (at * width, width), order, gathered[c], out_weights
-        )
-        keeps.append(keep)
-        sends.append(send)
-        products.append(keep)
 
     stages = reversed_bits(1, tp_count).bit_length()
     last = len(layout) - 1
@@ -607,9 +617,9 @@
         column = at * columns // count
         places.append([(r * part, r * rows + start, part, column) for r in range(share)])
     for slot in range(last + stages):
-        while len(keeps) < min(slot + 2, last + 1):
-            multiply()
-        for stage in range(stages):
+        while len(keeps) < min(slot + 1 if slot < 2 else slot + 2, last + 1):
+            multiply(products[-1], total, new_key)
+        for stage in reversed(range(stages)) if slot < 3 else range(stages):
             i = slot - stage
             if not 0 <= i <= last:
                 continue

time: 121 us -> 132 us (1.091)
  starting transfers between devices: 32.6 us -> 42.3 us
  Pallas kernels: 39.1 us -> 41.4 us
    ppermute x8 -> x10, starting transfers between devices: 14.7 us -> 21.2 us  [tp_swap(): return lax.ppermute(x, 'tp', [(z, z ^ step) for z in range(tp_count)])]
    pallas_call x22 -> x27, Pallas kernels: 39.1 us -> 41.4 us  [local_call(): pl.pallas_call(body, in_specs=[spec for _, spec in operands] + [HBM] * le...]
    ppermute x10 -> x12, starting transfers between devices: 11.5 us -> 13.3 us  [chip_move(): lax.ppermute(x, 'pool', [(p, (p // 2 + d) % chips * 2 + (p % 2 ^ e)) for...]
    ppermute x10 -> x12, waiting for transfers between devices: 19.3 us -> 17.9 us  [chip_move(): lax.ppermute(x, 'pool', [(p, (p // 2 + d) % chips * 2 + (p % 2 ^ e)) for...]
    ppermute x11 -> x14, starting transfers between devices: 1.81 us -> 3.07 us  [core_swap(): return lax.ppermute(x, 'pool', [(p, p ^ 1) for p in range(pool_count)])]
    ppermute x11 -> x14, waiting for transfers between devices: 2.47 us -> 3.12 us  [core_swap(): return lax.ppermute(x, 'pool', [(p, p ^ 1) for p in range(pool_count)])]
    ppermute x8 -> x10, waiting for transfers between devices: 16.6 us -> 16 us  [tp_swap(): return lax.ppermute(x, 'tp', [(z, z ^ step) for z in range(tp_count)])]
  transfers between devices with their start and end apart: 32 -> 39, of which waited for: 18 -> 18; matrix products, arithmetic and copies ran while one was open for 4% -> 4% of each run, Pallas kernels for 29% -> 27%
where the time goes in v7:
time: 132 us; the launch traced here: 131 us
  starting transfers between devices  42.3 us (32%)
  waiting for transfers between devices  42.1 us (32%)
  Pallas kernels  41.4 us (31%)
  other arithmetic  4.72 us (4%)
    pallas_call x27, Pallas kernels, local_call(): pl.pallas_call(body, in_specs=[spec for _, spec in operands] + [HBM] * le...  41.4 us
    ppermute x10, starting transfers between devices, tp_swap(): return lax.ppermute(x, 'tp', [(z, z ^ step) for z in range(tp_count)])  21.2 us
    ppermute x12, waiting for transfers between devices, chip_move(): lax.ppermute(x, 'pool', [(p, (p // 2 + d) % chips * 2 + (p % 2 ^ e)) for...  17.9 us
    ppermute x10, waiting for transfers between devices, tp_swap(): return lax.ppermute(x, 'tp', [(z, z ^ step) for z in range(tp_count)])  16 us
    ppermute x12, starting transfers between devices, chip_move(): lax.ppermute(x, 'pool', [(p, (p // 2 + d) % chips * 2 + (p % 2 ^ e)) for...  13.3 us
    ppermute x3, waiting for transfers between devices, shards(): lax.ppermute(shrunk, 'tp', [(i, (i + d) % tp_count) for i in range(tp_cou...  5.12 us
    ppermute x3, starting transfers between devices, shards(): lax.ppermute(shrunk, 'tp', [(i, (i + d) % tp_count) for i in range(tp_cou...  4.67 us
    convert_element_type x3, other arithmetic, scaled(): return (x * factor[None, :]).astype(jnp.bfloat16)  3.22 us
  transfers between devices with their start and end apart: 39, of which 18 were waited for; matrix products, arithmetic and copies ran while one was open for 4% of the time, Pallas kernels for 27%

profile of v7, /device:TPU:0, one launch (start us, length us, event | category | flops | bytes accessed | tf_op | source)
XLA Modules:
  0.0 131.4 jit_solution(1508477177431547255)
XLA Ops:
  0.6 2.5 %collective-permute-start.2 = (s32[1,128]{1,0:T(1,128)}, s32[1,128]{1,0:T(1,128)S(1)}, u32[]{:S(2)}, u32[]{:S(2)}) collective-permute-start(s32[1,128]{1,0:T(1,128)} %bitcast.11), channel_id=1, source_target_pairs={{0,12},{4,8},{8,4},{12,0},{1,13},{5,9},{9,5},{13,1},{2,14},{6,10},... | collective-permute-start | bytes 1544 | tf_op jit(solution)/shard_map/ppermute | solution.py:75
  3.1 0.6 collective-permute-start.1
  3.8 0.7 dynamic-slice_convert_fusion.4
  4.5 1.3 multiply_convert_fusion.3.refs_5_
  5.8 0.9 collective-permute-done.1.refs_3_
  6.8 0.9 collective-permute-start.4
  7.7 0.7 dynamic-slice_convert_fusion
  8.4 1.8 %multiply_convert_fusion = (bf16[128,2048]{1,0:T(8,128)(2,1)S(1)}, bf16[128,2048]{1,0:T(8,128)(2,1)S(1)}, bf16[128,2048]{1,0:T(8,128)(2,1)S(1)}) fusion(f32[2048]{0:T(1024)S(1)} %get-tuple-element.200, bf16[128,8192]{1,0:T(8,128)(2,1)} %refs_0_.1, s32[]{:T(128)S(6)} %select_n.137, f32[2048]{0:T(1024)S(1)} %get-tuple-element.201, s32[]{:T(128)S(6)} %select_n.135, ...), kind=kLoop, calls=%fused_computation | loop fusion | flops 2359296 | bytes 3170316 | tf_op jit(solution)/shard_map/convert_element_type | solution.py:457
  10.4 5.9 %load.1 = (bf16[512,2048]{1,0:T(8,128)(2,1)S(1)}, bf16[512,2048]{1,0:T(8,128)(2,1)S(1)}, bf16[2048,2048]{1,0:T(8,128)(2,1)S(1)}, bf16[2048,256]{1,0:T(8,128)(2,1...) custom-call(bf16[512,2048]{1,0:T(8,128)(2,1)} %bitcast.16, ...), custom_call_target="tpu_custom_call" | custom-call | flops 1000 | bytes 1000 | tf_op jit(solution)/shard_map/load/pallas_call | solution.py:42
  16.3 3.9 %collective-permute-done.4.refs_7_ = bf16[128,2048]{1,0:T(8,128)(2,1)S(1)} collective-permute-done((bf16[128,2048]{1,0:T(8,128)(2,1)S(1)}, bf16[128,2048]{1,0:T(8,128)(2,1)S(1)}, u32[]{:S(2)}, u32[]{:S(2)}) %collective-permute-start.4) | collective-permute-done | bytes 524320 | tf_op jit(solution)/shard_map/ppermute | solution.py:75
  20.2 0.5 collective-permute-start.9
  20.7 1.4 %collective-permute-start.12 = (bf16[128,2048]{1,0:T(8,128)(2,1)S(1)}, bf16[128,2048]{1,0:T(8,128)(2,1)S(1)}, u32[]{:S(2)}, u32[]{:S(2)}) collective-permute-start(bf16[128,2048]{1,0:T(8,128)(2,1)S(1)} %get-tuple-element.127), channel_id=1, source_target_pairs={{0,8},{4,12},{8,0},{12,4},{1,9},{5,13},{9,1},{13,5},{2,10},{6,14},... | collective-permute-start | bytes 1572872 | tf_op jit(solution)/shard_map/ppermute | solution.py:75
  22.1 0.5 collective-permute-start.13
  22.6 2.4 %shrink.1 = (s32[1,512]{1,0:T(1,128)S(1)}, f32[32,512]{1,0:T(8,128)S(1)}) custom-call(s32[1]{0:T(128)} %bitcast.1.refs_0_, s32[1,128]{1,0:T(1,128)S(1)} %bitcast.14, s32[1,128]{1,0:T(1,128)S(1)} %collective-permute-done.refs_2_, s32[1,128]{1,0:T(1,128)S(1)} %collective-permute-done.1.refs_3_, s32[1,128]{1,0:T(1,128)S(1)} %collective-permute-done.2.refs_4_, ...), custom_call_target="tpu_custom_call" | custom-call | flops 1000 | bytes 1000 | tf_op jit(solution)/shard_map/shrink/pallas_call | solution.py:42
  25.0 3.7 %collective-permute-start.8 = (f32[32,512]{1,0:T(8,128)S(1)}, f32[32,512]{1,0:T(8,128)S(1)}, u32[]{:S(2)}, u32[]{:S(2)}) collective-permute-start(f32[32,512]{1,0:T(8,128)S(1)} %get-tuple-element.111.refs_1_), channel_id=1, source_target_pairs={{0,3},{1,0},{2,1},{3,2},{4,7},{5,4},{6,5},{7,6},{8,11},{9,8},{10,9... | collective-permute-start | bytes 196616 | tf_op jit(solution)/shard_map/ppermute | solution.py:511
  28.7 1.0 collective-permute-start.6
  29.7 0.8 tables.1
  30.4 0.7 collective-permute-done.8.refs_4_
  31.1 4.4 %collective-permute-done.7.refs_3_ = f32[32,512]{1,0:T(8,128)S(1)} collective-permute-done((f32[32,512]{1,0:T(8,128)S(1)}, f32[32,512]{1,0:T(8,128)S(1)}, u32[]{:S(2)}, u32[]{:S(2)}) %collective-permute-start.7) | collective-permute-done | bytes 65568 | tf_op jit(solution)/shard_map/ppermute | solution.py:511
  35.6 4.5 %project_own.1 = (f32[128,2560]{1,0:T(8,128)S(1)}, bf16[128,2560]{1,0:T(8,128)(2,1)S(1)}, bf16[128,2,64,128]{3,2,1,0:T(8,128)(2,1)S(1)}, bf16[128,2,64,128]{3,2,1,0:T(8,128)(2,1)S(1)}) custom-call(s32[1,512]{1,0:T(1,128)S(1)} %get-tuple-element.125.refs_0_, f32[32,512]{1,0:T(8,128)S(1)} %get-tuple-element.111.refs_1_, ...), custom_call_target="tpu_custom_call" | custom-call | flops 1000 | bytes 1000 | tf_op jit(solution)/shard_map/project_own/pallas_call | solution.py:42
  40.1 2.8 %project_1_0.1.refs_0_ = f32[128,2560]{1,0:T(8,128)S(1)} custom-call(s32[1,512]{1,0:T(1,128)S(1)} %get-tuple-element.125.refs_0_, f32[32,512]{1,0:T(8,128)S(1)} %get-tuple-element.111.refs_1_, f32[32,512]{1,0:T(8,128)S(1)} %collective-permute-done.6.refs_2_, f32[32,512]{1,0:T(8,128)S(1)} %collective-permute-done.7.refs_3_, ...), custom_call_target="tpu_custom_call" | custom-call | flops 1000 | bytes 1000 | tf_op jit(solution)/shard_map/project_1_0/pallas_call | solution.py:42
  42.9 3.0 %collective-permute-done.13.refs_5_ = bf16[128,2048]{1,0:T(8,128)(2,1)S(1)} collective-permute-done((bf16[128,2048]{1,0:T(8,128)(2,1)S(1)}, bf16[128,2048]{1,0:T(8,128)(2,1)S(1)}, u32[]{:S(2)}, u32[]{:S(2)}) %collective-permute-start.13) | collective-permute-done | bytes 524320 | tf_op jit(solution)/shard_map/ppermute | solution.py:75
  45.9 2.8 %project_1_1.1 = (bf16[32,2560]{1,0:T(8,128)(2,1)S(1)}, bf16[32,2560]{1,0:T(8,128)(2,1)S(1)}, bf16[64,2560]{1,0:T(8,128)(2,1)S(1)}) custom-call(s32[1,512]{1,0:T(1,128)S(1)} %get-tuple-element.125.refs_0_, f32[32,512]{1,0:T(8,128)S(1)} %get-tuple-element.111.refs_1_, f32[32,512]{1,0:T(8,128)S(1)} %collective-permute-done.6.refs_2_, ...), custom_call_target="tpu_custom_call" | custom-call | flops 1000 | bytes 1000 | tf_op jit(solution)/shard_map/project_1_1/pallas_call | solution.py:42
  49.0 0.3 collective-permute-start.16
  49.5 0.7 collective-permute-done.14.refs_1_
  50.2 1.4 %collective-permute-start.15 = (bf16[32,2560]{1,0:T(8,128)(2,1)S(1)}, bf16[32,2560]{1,0:T(8,128)(2,1)S(1)}, u32[]{:S(2)}, u32[]{:S(2)}) collective-permute-start(bf16[32,2560]{1,0:T(8,128)(2,1)S(1)} %add_1_0.1), channel_id=1, source_target_pairs={{0,8},{4,12},{8,0},{12,4},{1,9},{5,13},{9,1},{13,5},{2,10},{6,14},... | collective-permute-start | bytes 491528 | tf_op jit(solution)/shard_map/ppermute | solution.py:75
  51.7 0.7 collective-permute-start.17
  52.4 4.9 %collective-permute-done.15.refs_2_ = bf16[32,2560]{1,0:T(8,128)(2,1)S(1)} collective-permute-done((bf16[32,2560]{1,0:T(8,128)(2,1)S(1)}, bf16[32,2560]{1,0:T(8,128)(2,1)S(1)}, u32[]{:S(2)}, u32[]{:S(2)}) %collective-permute-start.15) | collective-permute-done | bytes 163872 | tf_op jit(solution)/shard_map/ppermute | solution.py:75
  57.3 3.4 %attend_0.1 = (bf16[32,2048]{1,0:T(8,128)(2,1)S(1)}, bf16[32,256]{1,0:T(8,128)(2,1)S(1)}, bf16[32,256]{1,0:T(8,128)(2,1)S(1)}, bf16[2048,2048]{1,0:T(8,128)(2,1)S(1)}) custom-call(f32[128,2560]{1,0:T(8,128)S(1)} %get-tuple-element.123.refs_0_.refs_2_, bf16[128,2560]{1,0:T(8,128)(2,1)S(1)} %collective-permute-done.11.refs_1_.refs_3_, ...), custom_call_target="tpu_custom_call" | custom-call | flops 1000 | bytes 1000 | tf_op jit(solution)/shard_map/attend_0/pallas_call | solution.py:42
  60.8 1.4 %collective-permute-start.19 = (bf16[32,2048]{1,0:T(8,128)(2,1)S(1)}, bf16[32,2048]{1,0:T(8,128)(2,1)S(1)}, u32[]{:S(2)}, u32[]{:S(2)}) collective-permute-start(bf16[32,2048]{1,0:T(8,128)(2,1)S(1)} %get-tuple-element.148.refs_1_), channel_id=1, source_target_pairs={{0,8},{4,12},{8,0},{12,4},{1,9},{5,13},{9,1},{13,5},{2,10},{6,14},... | collective-permute-start | bytes 393224 | tf_op jit(solution)/shard_map/ppermute | solution.py:75
  62.2 2.5 %attend_1.1 = (bf16[32,2048]{1,0:T(8,128)(2,1)S(1)}, bf16[64,256]{1,0:T(8,128)(2,1)S(1)}, bf16[64,256]{1,0:T(8,128)(2,1)S(1)}) custom-call(bf16[32,256]{1,0:T(8,128)(2,1)S(1)} %get-tuple-element.142.refs_0_, bf16[32,256]{1,0:T(8,128)(2,1)S(1)} %get-tuple-element.143.refs_1_, f32[128,2560]{1,0:T(8,128)S(1)} %get-tuple-element.123.refs_0_.refs_2_, ...), custom_call_target="tpu_custom_call" | custom-call | flops 1000 | bytes 1000 | tf_op jit(solution)/shard_map/attend_1/pallas_call | solution.py:42
  64.7 1.0 collective-permute-done.19.refs_3_
  66.0 0.5 collective-permute-start.21
  66.4 1.4 %collective-permute-start.24 = (bf16[64,2560]{1,0:T(8,128)(2,1)S(1)}, bf16[64,2560]{1,0:T(8,128)(2,1)S(1)}, u32[]{:S(2)}, u32[]{:S(2)}) collective-permute-start(bf16[64,2560]{1,0:T(8,128)(2,1)S(1)} %add_1_2.1), channel_id=1, source_target_pairs={{0,8},{4,12},{8,0},{12,4},{1,9},{5,13},{9,1},{13,5},{2,10},{6,14},... | collective-permute-start | bytes 983048 | tf_op jit(solution)/shard_map/ppermute | solution.py:75
  67.8 2.4 %output_0_0_1.1 = (bf16[64,2048]{1,0:T(8,128)(2,1)S(1)}, bf16[64,2048]{1,0:T(8,128)(2,1)S(1)}) custom-call(s32[4]{0:T(128)S(1)} %pad_add_fusion.refs_0_, bf16[32,2048]{1,0:T(8,128)(2,1)S(1)} %get-tuple-element.148.refs_1_, bf16[32,2048]{1,0:T(8,128)(2,1)S(1)} %collective-permute-done.20.refs_2_, bf16[32,2048]{1,0:T(8,128)(2,1)S(1)} %collective-permute-done.19.refs_3_, ...), custom_call_target="tpu_custom_call" | custom-call | flops 1000 | bytes 1000 | tf_op jit(solution)/shard_map/output_0_0_1/pallas_call | solution.py:42
  70.3 1.6 %collective-permute-start.22 = (bf16[64,2048]{1,0:T(8,128)(2,1)S(1)}, bf16[64,2048]{1,0:T(8,128)(2,1)S(1)}, u32[]{:S(2)}, u32[]{:S(2)}) collective-permute-start(bf16[64,2048]{1,0:T(8,128)(2,1)S(1)} %get-tuple-element.152), channel_id=1, source_target_pairs={{0,1},{1,0},{2,3},{3,2},{4,5},{5,4},{6,7},{7,6},{8,9},{9,8},{10,11... | collective-permute-start | bytes 786440 | tf_op jit(solution)/shard_map/ppermute | solution.py:83
  71.9 1.0 collective-permute-start.26
  72.9 4.1 %collective-permute-done.24.refs_4_ = bf16[64,2560]{1,0:T(8,128)(2,1)S(1)} collective-permute-done((bf16[64,2560]{1,0:T(8,128)(2,1)S(1)}, bf16[64,2560]{1,0:T(8,128)(2,1)S(1)}, u32[]{:S(2)}, u32[]{:S(2)}) %collective-permute-start.24) | collective-permute-done | bytes 327712 | tf_op jit(solution)/shard_map/ppermute | solution.py:75
  77.0 5.5 %attend_2.1 = (bf16[64,2048]{1,0:T(8,128)(2,1)S(1)}, bf16[128,256]{1,0:T(8,128)(2,1)}, bf16[128,256]{1,0:T(8,128)(2,1)}) custom-call(bf16[64,256]{1,0:T(8,128)(2,1)S(1)} %get-tuple-element.145.refs_0_, bf16[64,256]{1,0:T(8,128)(2,1)S(1)} %get-tuple-element.158.refs_1_, f32[128,2560]{1,0:T(8,128)S(1)} %get-tuple-element.123.refs_0_.refs_2_, ...), custom_call_target="tpu_custom_call" | custom-call | flops 1000 | bytes 1000 | tf_op jit(solution)/shard_map/attend_2/pallas_call | solution.py:42
  82.7 0.5 collective-permute-start.27
  83.2 0.8 collective-permute-done.25.refs_2_
  84.2 2.4 %output_1_0_1.1 = (bf16[64,2048]{1,0:T(8,128)(2,1)S(1)}, bf16[64,2048]{1,0:T(8,128)(2,1)S(1)}) custom-call(s32[4]{0:T(128)S(1)} %pad_add_fusion.refs_0_, bf16[32,2048]{1,0:T(8,128)(2,1)S(1)} %get-tuple-element.161.refs_1_, bf16[32,2048]{1,0:T(8,128)(2,1)S(1)} %collective-permute-done.25.refs_2_, bf16[32,2048]{1,0:T(8,128)(2,1)S(1)} %collective-permute-done.26.refs_3_, ...), custom_call_target="tpu_custom_call" | custom-call | flops 1000 | bytes 1000 | tf_op jit(solution)/shard_map/output_1_0_1/pallas_call | solution.py:42
  86.6 1.6 %collective-permute-start.28 = (bf16[64,2048]{1,0:T(8,128)(2,1)S(1)}, bf16[64,2048]{1,0:T(8,128)(2,1)S(1)}, u32[]{:S(2)}, u32[]{:S(2)}) collective-permute-start(bf16[64,2048]{1,0:T(8,128)(2,1)S(1)} %get-tuple-element.165), channel_id=1, source_target_pairs={{0,1},{1,0},{2,3},{3,2},{4,5},{5,4},{6,7},{7,6},{8,9},{9,8},{10,11... | collective-permute-start | bytes 786440 | tf_op jit(solution)/shard_map/ppermute | solution.py:83
  88.2 1.4 %collective-permute-start.31 = (bf16[64,2048]{1,0:T(8,128)(2,1)S(1)}, bf16[64,2048]{1,0:T(8,128)(2,1)S(1)}, u32[]{:S(2)}, u32[]{:S(2)}) collective-permute-start(bf16[64,2048]{1,0:T(8,128)(2,1)S(1)} %get-tuple-element.181.refs_1_), channel_id=1, source_target_pairs={{0,8},{4,12},{8,0},{12,4},{1,9},{5,13},{9,1},{13,5},{2,10},{6,14},... | collective-permute-start | bytes 786440 | tf_op jit(solution)/shard_map/ppermute | solution.py:75
  89.6 2.6 %collective-permute-start.23 = (bf16[32,2048]{1,0:T(8,128)(2,1)S(1)}, bf16[32,2048]{1,0:T(8,128)(2,1)S(1)}, u32[]{:S(2)}, u32[]{:S(2)}) collective-permute-start(bf16[32,2048]{1,0:T(8,128)(2,1)S(1)} %get-tuple-element.155), channel_id=1, source_target_pairs={{0,2},{1,3},{2,0},{3,1},{4,6},{5,7},{6,4},{7,5},{8,10},{9,11},{10,... | collective-permute-start | bytes 393224 | tf_op jit(solution)/shard_map/ppermute | solution.py:83
  92.2 4.9 %collective-permute-done.23.refs_1_ = bf16[32,2048]{1,0:T(8,128)(2,1)S(1)} collective-permute-done((bf16[32,2048]{1,0:T(8,128)(2,1)S(1)}, bf16[32,2048]{1,0:T(8,128)(2,1)S(1)}, u32[]{:S(2)}, u32[]{:S(2)}) %collective-permute-start.23) | collective-permute-done | bytes 131104 | tf_op jit(solution)/shard_map/ppermute | solution.py:83
  97.1 0.9 collective-permute-done.28.refs_1_
  98.2 0.5 collective-permute-start.32
  98.7 1.0 collective-permute-done.30.refs_2_
  99.7 0.4 collective-permute-done.32.refs_4_
  100.1 2.0 %output_2_0_2.1 = (bf16[128,1024]{1,0:T(8,128)(2,1)S(1)}, bf16[128,1024]{1,0:T(8,128)(2,1)S(1)}) custom-call(s32[4]{0:T(128)S(1)} %pad_add_fusion.refs_0_, bf16[64,2048]{1,0:T(8,128)(2,1)S(1)} %get-tuple-element.181.refs_1_, bf16[64,2048]{1,0:T(8,128)(2,1)S(1)} %collective-permute-done.30.refs_2_, bf16[64,2048]{1,0:T(8,128)(2,1)S(1)} %collective-permute-done.31.refs_3_, ...), custom_call_target="tpu_custom_call" | custom-call | flops 1000 | bytes 1000 | tf_op jit(solution)/shard_map/output_2_0_2/pallas_call | solution.py:42
  102.1 2.7 %collective-permute-start.33 = (bf16[128,1024]{1,0:T(8,128)(2,1)S(1)}, bf16[128,1024]{1,0:T(8,128)(2,1)S(1)}, u32[]{:S(2)}, u32[]{:S(2)}) collective-permute-start(bf16[128,1024]{1,0:T(8,128)(2,1)S(1)} %get-tuple-element.177), channel_id=1, source_target_pairs={{0,1},{1,0},{2,3},{3,2},{4,5},{5,4},{6,7},{7,6},{8,9},{9,8},{10,11... | collective-permute-start | bytes 786440 | tf_op jit(solution)/shard_map/ppermute | solution.py:83
  104.8 1.5 %collective-permute-start.29 = (bf16[32,2048]{1,0:T(8,128)(2,1)S(1)}, bf16[32,2048]{1,0:T(8,128)(2,1)S(1)}, u32[]{:S(2)}, u32[]{:S(2)}) collective-permute-start(bf16[32,2048]{1,0:T(8,128)(2,1)S(1)} %get-tuple-element.168), channel_id=1, source_target_pairs={{0,2},{1,3},{2,0},{3,1},{4,6},{5,7},{6,4},{7,5},{8,10},{9,11},{10,... | collective-permute-start | bytes 393224 | tf_op jit(solution)/shard_map/ppermute | solution.py:83
  106.3 1.3 output_2_2_4.1
  107.6 5.8 %collective-permute-done.29.refs_1_ = bf16[32,2048]{1,0:T(8,128)(2,1)S(1)} collective-permute-done((bf16[32,2048]{1,0:T(8,128)(2,1)S(1)}, bf16[32,2048]{1,0:T(8,128)(2,1)S(1)}, u32[]{:S(2)}, u32[]{:S(2)}) %collective-permute-start.29) | collective-permute-done | bytes 131104 | tf_op jit(solution)/shard_map/ppermute | solution.py:83
  113.5 2.4 %collective-permute-start.35 = (bf16[128,512]{1,0:T(8,128)(2,1)S(1)}, bf16[128,512]{1,0:T(8,128)(2,1)S(1)}, u32[]{:S(2)}, u32[]{:S(2)}) collective-permute-start(bf16[128,512]{1,0:T(8,128)(2,1)S(1)} %get-tuple-element.183), channel_id=1, source_target_pairs={{0,1},{1,0},{2,3},{3,2},{4,5},{5,4},{6,7},{7,6},{8,9},{9,8},{10,11... | collective-permute-start | bytes 393224 | tf_op jit(solution)/shard_map/ppermute | solution.py:83
  116.0 1.1 collective-permute-start.34
  117.0 1.3 output_2_3_4.1
  118.3 2.1 %collective-permute-start.37 = (bf16[128,512]{1,0:T(8,128)(2,1)S(1)}, bf16[128,512]{1,0:T(8,128)(2,1)S(1)}, u32[]{:S(2)}, u32[]{:S(2)}) collective-permute-start(bf16[128,512]{1,0:T(8,128)(2,1)S(1)} %get-tuple-element.188), channel_id=1, source_target_pairs={{0,1},{1,0},{2,3},{3,2},{4,5},{5,4},{6,7},{7,6},{8,9},{9,8},{10,11... | collective-permute-start | bytes 393224 | tf_op jit(solution)/shard_map/ppermute | solution.py:83
  120.5 2.9 %collective-permute-start.36 = (bf16[64,512]{1,0:T(8,128)(2,1)S(1)}, bf16[64,512]{1,0:T(8,128)(2,1)S(1)}, u32[]{:S(2)}, u32[]{:S(2)}) collective-permute-start(bf16[64,512]{1,0:T(8,128)(2,1)S(1)} %get-tuple-element.185), channel_id=1, source_target_pairs={{0,2},{1,3},{2,0},{3,1},{4,6},{5,7},{6,4},{7,5},{8,10},{9,11},{10,... | collective-permute-start | bytes 196616 | tf_op jit(solution)/shard_map/ppermute | solution.py:83
  123.4 1.8 %collective-permute-done.37.refs_1_ = bf16[128,512]{1,0:T(8,128)(2,1)S(1)} collective-permute-done((bf16[128,512]{1,0:T(8,128)(2,1)S(1)}, bf16[128,512]{1,0:T(8,128)(2,1)S(1)}, u32[]{:S(2)}, u32[]{:S(2)}) %collective-permute-start.37) | collective-permute-done | bytes 131104 | tf_op jit(solution)/shard_map/ppermute | solution.py:83
  125.3 2.7 %collective-permute-start.38 = (bf16[64,512]{1,0:T(8,128)(2,1)S(1)}, bf16[64,512]{1,0:T(8,128)(2,1)S(1)}, u32[]{:S(2)}, u32[]{:S(2)}) collective-permute-start(bf16[64,512]{1,0:T(8,128)(2,1)S(1)} %get-tuple-element.190), channel_id=1, source_target_pairs={{0,2},{1,3},{2,0},{3,1},{4,6},{5,7},{6,4},{7,5},{8,10},{9,11},{10,... | collective-permute-start | bytes 196616 | tf_op jit(solution)/shard_map/ppermute | solution.py:83
  128.0 2.5 %collective-permute-done.38.refs_5_ = bf16[64,512]{1,0:T(8,128)(2,1)S(1)} collective-permute-done((bf16[64,512]{1,0:T(8,128)(2,1)S(1)}, bf16[64,512]{1,0:T(8,128)(2,1)S(1)}, u32[]{:S(2)}, u32[]{:S(2)}) %collective-permute-start.38) | collective-permute-done | bytes 65568 | tf_op jit(solution)/shard_map/ppermute | solution.py:83
  130.5 0.8 assemble.1
  (53 shorter events, 1.8 us)
Async XLA Ops:
  0.6 5.2 %collective-permute-start.2 = (s32[1,128]{1,0:T(1,128)}, s32[1,128]{1,0:T(1,128)S(1)}, u32[]{:S(2)}, u32[]{:S(2)}) collective-permute-start(s32[1,128]{1,0:T(1,128)} %bitcast.11), channel_id=1, source_target_pairs={{0,12},{4,8},{8,4},{12,0},{1,13},{5,9},{9,5},{13,1},{2,14},{6,10},... | collective-permute-start | bytes 1544 | tf_op jit(solution)/shard_map/ppermute | solution.py:75
  3.1 3.7 %collective-permute-start.1 = (s32[1,128]{1,0:T(1,128)}, s32[1,128]{1,0:T(1,128)S(1)}, u32[]{:S(2)}, u32[]{:S(2)}) collective-permute-start(s32[1,128]{1,0:T(1,128)} %bitcast.12), channel_id=1, source_target_pairs={{0,8},{4,12},{8,0},{12,4},{1,9},{5,13},{9,1},{13,5},{2,10},{6,14},... | collective-permute-start | bytes 1544 | tf_op jit(solution)/shard_map/ppermute | solution.py:75
  3.7 3.0 %collective-permute-start = (s32[1,128]{1,0:T(1,128)}, s32[1,128]{1,0:T(1,128)S(1)}, u32[]{:S(2)}, u32[]{:S(2)}) collective-permute-start(s32[1,128]{1,0:T(1,128)} %bitcast.13), channel_id=1, source_target_pairs={{0,4},{4,0},{8,12},{12,8},{1,5},{5,1},{9,13},{13,9},{2,6},{6,2},{1... | collective-permute-start | bytes 1544 | tf_op jit(solution)/shard_map/ppermute | solution.py:75
  4.5 5.8 %copy-start = (bf16[128,8192]{1,0:T(8,128)(2,1)S(1)}, bf16[128,8192]{1,0:T(8,128)(2,1)}, u32[]{:S(2)}) copy-start(bf16[128,8192]{1,0:T(8,128)(2,1)} %refs_0_.1) | copy-start | bytes 6291460
  6.8 13.4 %collective-permute-start.4 = (bf16[128,2048]{1,0:T(8,128)(2,1)S(1)}, bf16[128,2048]{1,0:T(8,128)(2,1)S(1)}, u32[]{:S(2)}, u32[]{:S(2)}) collective-permute-start(bf16[128,2048]{1,0:T(8,128)(2,1)S(1)} %multiply_convert_fusion.3.refs_5_), channel_id=1, source_target_pairs={{0,8},{4,12},{8,0},{12,4},{1,9},{5,13},{9,1},{13,5},{2,10},{6,14},... | collective-permute-start | bytes 1572872 | tf_op jit(solution)/shard_map/ppermute | solution.py:75
  7.7 14.5 %collective-permute-start.3 = (bf16[128,2048]{1,0:T(8,128)(2,1)S(1)}, bf16[128,2048]{1,0:T(8,128)(2,1)S(1)}, u32[]{:S(2)}, u32[]{:S(2)}) collective-permute-start(bf16[128,2048]{1,0:T(8,128)(2,1)S(1)} %multiply_convert_fusion.3.refs_5_), channel_id=1, source_target_pairs={{0,4},{4,0},{8,12},{12,8},{1,5},{5,1},{9,13},{13,9},{2,6},{6,2},{1... | collective-permute-start | bytes 1572872 | tf_op jit(solution)/shard_map/ppermute | solution.py:70
  10.4 12.2 %copy-start.1 = (s32[128]{0:T(128)S(1)}, s32[128]{0:T(128)}, u32[]{:S(2)}) copy-start(s32[128]{0:T(128)} %param.23) | copy-start | bytes 1540
  20.2 2.4 %collective-permute-start.5 = (bf16[128,2048]{1,0:T(8,128)(2,1)S(1)}, bf16[128,2048]{1,0:T(8,128)(2,1)S(1)}, u32[]{:S(2)}, u32[]{:S(2)}) collective-permute-start(bf16[128,2048]{1,0:T(8,128)(2,1)S(1)} %collective-permute-done.4.refs_7_), channel_id=1, source_target_pairs={{0,4},{4,0},{8,12},{12,8},{1,5},{5,1},{9,13},{13,9},{2,6},{6,2},{1... | collective-permute-start | bytes 1572872 | tf_op jit(solution)/shard_map/ppermute | solution.py:70
  20.2 8.4 %collective-permute-start.9 = (bf16[64,2048]{1,0:T(8,128)(2,1)S(1)}, bf16[64,2048]{1,0:T(8,128)(2,1)S(1)}, u32[]{:S(2)}, u32[]{:S(2)}) collective-permute-start(bf16[64,2048]{1,0:T(8,128)(2,1)S(1)} %get-tuple-element.116), channel_id=1, source_target_pairs={{0,4},{4,0},{8,12},{12,8},{1,5},{5,1},{9,13},{13,9},{2,6},{6,2},{1... | collective-permute-start | bytes 786440 | tf_op jit(solution)/shard_map/ppermute | solution.py:70
  20.7 7.9 %collective-permute-start.10 = (bf16[64,2048]{1,0:T(8,128)(2,1)S(1)}, bf16[64,2048]{1,0:T(8,128)(2,1)S(1)}, u32[]{:S(2)}, u32[]{:S(2)}) collective-permute-start(bf16[64,2048]{1,0:T(8,128)(2,1)S(1)} %get-tuple-element.117), channel_id=1, source_target_pairs={{0,4},{4,0},{8,12},{12,8},{1,5},{5,1},{9,13},{13,9},{2,6},{6,2},{1... | collective-permute-start | bytes 786440 | tf_op jit(solution)/shard_map/ppermute | solution.py:70
  20.7 19.4 %collective-permute-start.12 = (bf16[128,2048]{1,0:T(8,128)(2,1)S(1)}, bf16[128,2048]{1,0:T(8,128)(2,1)S(1)}, u32[]{:S(2)}, u32[]{:S(2)}) collective-permute-start(bf16[128,2048]{1,0:T(8,128)(2,1)S(1)} %get-tuple-element.127), channel_id=1, source_target_pairs={{0,8},{4,12},{8,0},{12,4},{1,9},{5,13},{9,1},{13,5},{2,10},{6,14},... | collective-permute-start | bytes 1572872 | tf_op jit(solution)/shard_map/ppermute | solution.py:75
  22.1 23.8 %collective-permute-start.13 = (bf16[128,2048]{1,0:T(8,128)(2,1)S(1)}, bf16[128,2048]{1,0:T(8,128)(2,1)S(1)}, u32[]{:S(2)}, u32[]{:S(2)}) collective-permute-start(bf16[128,2048]{1,0:T(8,128)(2,1)S(1)} %get-tuple-element.129), channel_id=1, source_target_pairs={{0,12},{4,8},{8,4},{12,0},{1,13},{5,9},{9,5},{13,1},{2,14},{6,10},... | collective-permute-start | bytes 1572872 | tf_op jit(solution)/shard_map/ppermute | solution.py:75
  22.6 7.1 %copy-start.2 = (s32[128]{0:T(128)S(1)}, s32[128]{0:T(128)}, u32[]{:S(2)}) copy-start(s32[128]{0:T(128)} %param.22) | copy-start | bytes 1540
  25.0 6.1 %collective-permute-start.8 = (f32[32,512]{1,0:T(8,128)S(1)}, f32[32,512]{1,0:T(8,128)S(1)}, u32[]{:S(2)}, u32[]{:S(2)}) collective-permute-start(f32[32,512]{1,0:T(8,128)S(1)} %get-tuple-element.111.refs_1_), channel_id=1, source_target_pairs={{0,3},{1,0},{2,1},{3,2},{4,7},{5,4},{6,5},{7,6},{8,11},{9,8},{10,9... | collective-permute-start | bytes 196616 | tf_op jit(solution)/shard_map/ppermute | solution.py:511
  28.6 6.9 %collective-permute-start.7 = (f32[32,512]{1,0:T(8,128)S(1)}, f32[32,512]{1,0:T(8,128)S(1)}, u32[]{:S(2)}, u32[]{:S(2)}) collective-permute-start(f32[32,512]{1,0:T(8,128)S(1)} %get-tuple-element.111.refs_1_), channel_id=1, source_target_pairs={{0,2},{1,3},{2,0},{3,1},{4,6},{5,7},{6,4},{7,5},{8,10},{9,11},{10,... | collective-permute-start | bytes 196616 | tf_op jit(solution)/shard_map/ppermute | solution.py:511
  28.7 6.9 %collective-permute-start.6 = (f32[32,512]{1,0:T(8,128)S(1)}, f32[32,512]{1,0:T(8,128)S(1)}, u32[]{:S(2)}, u32[]{:S(2)}) collective-permute-start(f32[32,512]{1,0:T(8,128)S(1)} %get-tuple-element.111.refs_1_), channel_id=1, source_target_pairs={{0,1},{1,2},{2,3},{3,0},{4,5},{5,6},{6,7},{7,4},{8,9},{9,10},{10,1... | collective-permute-start | bytes 196616 | tf_op jit(solution)/shard_map/ppermute | solution.py:511
  40.0 17.3 %collective-permute-start.11 = (bf16[128,2560]{1,0:T(8,128)(2,1)S(1)}, bf16[128,2560]{1,0:T(8,128)(2,1)S(1)}, u32[]{:S(2)}, u32[]{:S(2)}) collective-permute-start(bf16[128,2560]{1,0:T(8,128)(2,1)S(1)} %get-tuple-element.124), channel_id=1, source_target_pairs={{0,4},{4,0},{8,12},{12,8},{1,5},{5,1},{9,13},{13,9},{2,6},{6,2},{1... | collective-permute-start | bytes 1966088 | tf_op jit(solution)/shard_map/ppermute | solution.py:70
  48.7 1.5 %collective-permute-start.14 = (bf16[32,2560]{1,0:T(8,128)(2,1)S(1)}, bf16[32,2560]{1,0:T(8,128)(2,1)S(1)}, u32[]{:S(2)}, u32[]{:S(2)}) collective-permute-start(bf16[32,2560]{1,0:T(8,128)(2,1)S(1)} %get-tuple-element.131), channel_id=1, source_target_pairs={{0,4},{4,0},{8,12},{12,8},{1,5},{5,1},{9,13},{13,9},{2,6},{6,2},{1... | collective-permute-start | bytes 491528 | tf_op jit(solution)/shard_map/ppermute | solution.py:70
  49.0 2.7 %collective-permute-start.16 = (bf16[32,2560]{1,0:T(8,128)(2,1)S(1)}, bf16[32,2560]{1,0:T(8,128)(2,1)S(1)}, u32[]{:S(2)}, u32[]{:S(2)}) collective-permute-start(bf16[32,2560]{1,0:T(8,128)(2,1)S(1)} %get-tuple-element.132), channel_id=1, source_target_pairs={{0,4},{4,0},{8,12},{12,8},{1,5},{5,1},{9,13},{13,9},{2,6},{6,2},{1... | collective-permute-start | bytes 491528 | tf_op jit(solution)/shard_map/ppermute | solution.py:70
  49.3 15.4 %collective-permute-start.18 = (bf16[64,2560]{1,0:T(8,128)(2,1)S(1)}, bf16[64,2560]{1,0:T(8,128)(2,1)S(1)}, u32[]{:S(2)}, u32[]{:S(2)}) collective-permute-start(bf16[64,2560]{1,0:T(8,128)(2,1)S(1)} %get-tuple-element.146), channel_id=1, source_target_pairs={{0,4},{4,0},{8,12},{12,8},{1,5},{5,1},{9,13},{13,9},{2,6},{6,2},{1... | collective-permute-start | bytes 983048 | tf_op jit(solution)/shard_map/ppermute | solution.py:70
  50.2 7.1 %collective-permute-start.15 = (bf16[32,2560]{1,0:T(8,128)(2,1)S(1)}, bf16[32,2560]{1,0:T(8,128)(2,1)S(1)}, u32[]{:S(2)}, u32[]{:S(2)}) collective-permute-start(bf16[32,2560]{1,0:T(8,128)(2,1)S(1)} %add_1_0.1), channel_id=1, source_target_pairs={{0,8},{4,12},{8,0},{12,4},{1,9},{5,13},{9,1},{13,5},{2,10},{6,14},... | collective-permute-start | bytes 491528 | tf_op jit(solution)/shard_map/ppermute | solution.py:75
  51.7 9.0 %collective-permute-start.17 = (bf16[32,2560]{1,0:T(8,128)(2,1)S(1)}, bf16[32,2560]{1,0:T(8,128)(2,1)S(1)}, u32[]{:S(2)}, u32[]{:S(2)}) collective-permute-start(bf16[32,2560]{1,0:T(8,128)(2,1)S(1)} %add_1_1.1), channel_id=1, source_target_pairs={{0,8},{4,12},{8,0},{12,4},{1,9},{5,13},{9,1},{13,5},{2,10},{6,14},... | collective-permute-start | bytes 491528 | tf_op jit(solution)/shard_map/ppermute | solution.py:75
  60.8 5.0 %collective-permute-start.19 = (bf16[32,2048]{1,0:T(8,128)(2,1)S(1)}, bf16[32,2048]{1,0:T(8,128)(2,1)S(1)}, u32[]{:S(2)}, u32[]{:S(2)}) collective-permute-start(bf16[32,2048]{1,0:T(8,128)(2,1)S(1)} %get-tuple-element.148.refs_1_), channel_id=1, source_target_pairs={{0,8},{4,12},{8,0},{12,4},{1,9},{5,13},{9,1},{13,5},{2,10},{6,14},... | collective-permute-start | bytes 393224 | tf_op jit(solution)/shard_map/ppermute | solution.py:75
  65.9 2.0 %collective-permute-start.20 = (bf16[32,2048]{1,0:T(8,128)(2,1)S(1)}, bf16[32,2048]{1,0:T(8,128)(2,1)S(1)}, u32[]{:S(2)}, u32[]{:S(2)}) collective-permute-start(bf16[32,2048]{1,0:T(8,128)(2,1)S(1)} %get-tuple-element.148.refs_1_), channel_id=1, source_target_pairs={{0,4},{4,0},{8,12},{12,8},{1,5},{5,1},{9,13},{13,9},{2,6},{6,2},{1... | collective-permute-start | bytes 393224 | tf_op jit(solution)/shard_map/ppermute | solution.py:70
  66.0 1.9 %collective-permute-start.21 = (bf16[32,2048]{1,0:T(8,128)(2,1)S(1)}, bf16[32,2048]{1,0:T(8,128)(2,1)S(1)}, u32[]{:S(2)}, u32[]{:S(2)}) collective-permute-start(bf16[32,2048]{1,0:T(8,128)(2,1)S(1)} %collective-permute-done.19.refs_3_), channel_id=1, source_target_pairs={{0,4},{4,0},{8,12},{12,8},{1,5},{5,1},{9,13},{13,9},{2,6},{6,2},{1... | collective-permute-start | bytes 393224 | tf_op jit(solution)/shard_map/ppermute | solution.py:70
  66.4 10.6 %collective-permute-start.24 = (bf16[64,2560]{1,0:T(8,128)(2,1)S(1)}, bf16[64,2560]{1,0:T(8,128)(2,1)S(1)}, u32[]{:S(2)}, u32[]{:S(2)}) collective-permute-start(bf16[64,2560]{1,0:T(8,128)(2,1)S(1)} %add_1_2.1), channel_id=1, source_target_pairs={{0,8},{4,12},{8,0},{12,4},{1,9},{5,13},{9,1},{13,5},{2,10},{6,14},... | collective-permute-start | bytes 983048 | tf_op jit(solution)/shard_map/ppermute | solution.py:75
  70.3 12.2 %collective-permute-start.22 = (bf16[64,2048]{1,0:T(8,128)(2,1)S(1)}, bf16[64,2048]{1,0:T(8,128)(2,1)S(1)}, u32[]{:S(2)}, u32[]{:S(2)}) collective-permute-start(bf16[64,2048]{1,0:T(8,128)(2,1)S(1)} %get-tuple-element.152), channel_id=1, source_target_pairs={{0,1},{1,0},{2,3},{3,2},{4,5},{5,4},{6,7},{7,6},{8,9},{9,8},{10,11... | collective-permute-start | bytes 786440 | tf_op jit(solution)/shard_map/ppermute | solution.py:83
  71.9 10.7 %collective-permute-start.26 = (bf16[32,2048]{1,0:T(8,128)(2,1)S(1)}, bf16[32,2048]{1,0:T(8,128)(2,1)S(1)}, u32[]{:S(2)}, u32[]{:S(2)}) collective-permute-start(bf16[32,2048]{1,0:T(8,128)(2,1)S(1)} %get-tuple-element.161.refs_1_), channel_id=1, source_target_pairs={{0,8},{4,12},{8,0},{12,4},{1,9},{5,13},{9,1},{13,5},{2,10},{6,14},... | collective-permute-start | bytes 393224 | tf_op jit(solution)/shard_map/ppermute | solution.py:75
  82.6 1.4 %collective-permute-start.25 = (bf16[32,2048]{1,0:T(8,128)(2,1)S(1)}, bf16[32,2048]{1,0:T(8,128)(2,1)S(1)}, u32[]{:S(2)}, u32[]{:S(2)}) collective-permute-start(bf16[32,2048]{1,0:T(8,128)(2,1)S(1)} %get-tuple-element.161.refs_1_), channel_id=1, source_target_pairs={{0,4},{4,0},{8,12},{12,8},{1,5},{5,1},{9,13},{13,9},{2,6},{6,2},{1... | collective-permute-start | bytes 393224 | tf_op jit(solution)/shard_map/ppermute | solution.py:70
  82.7 1.5 %collective-permute-start.27 = (bf16[32,2048]{1,0:T(8,128)(2,1)S(1)}, bf16[32,2048]{1,0:T(8,128)(2,1)S(1)}, u32[]{:S(2)}, u32[]{:S(2)}) collective-permute-start(bf16[32,2048]{1,0:T(8,128)(2,1)S(1)} %collective-permute-done.26.refs_3_), channel_id=1, source_target_pairs={{0,4},{4,0},{8,12},{12,8},{1,5},{5,1},{9,13},{13,9},{2,6},{6,2},{1... | collective-permute-start | bytes 393224 | tf_op jit(solution)/shard_map/ppermute | solution.py:70
  86.6 11.4 %collective-permute-start.28 = (bf16[64,2048]{1,0:T(8,128)(2,1)S(1)}, bf16[64,2048]{1,0:T(8,128)(2,1)S(1)}, u32[]{:S(2)}, u32[]{:S(2)}) collective-permute-start(bf16[64,2048]{1,0:T(8,128)(2,1)S(1)} %get-tuple-element.165), channel_id=1, source_target_pairs={{0,1},{1,0},{2,3},{3,2},{4,5},{5,4},{6,7},{7,6},{8,9},{9,8},{10,11... | collective-permute-start | bytes 786440 | tf_op jit(solution)/shard_map/ppermute | solution.py:83
  88.2 9.9 %collective-permute-start.31 = (bf16[64,2048]{1,0:T(8,128)(2,1)S(1)}, bf16[64,2048]{1,0:T(8,128)(2,1)S(1)}, u32[]{:S(2)}, u32[]{:S(2)}) collective-permute-start(bf16[64,2048]{1,0:T(8,128)(2,1)S(1)} %get-tuple-element.181.refs_1_), channel_id=1, source_target_pairs={{0,8},{4,12},{8,0},{12,4},{1,9},{5,13},{9,1},{13,5},{2,10},{6,14},... | collective-permute-start | bytes 786440 | tf_op jit(solution)/shard_map/ppermute | solution.py:75
  89.6 7.5 %collective-permute-start.23 = (bf16[32,2048]{1,0:T(8,128)(2,1)S(1)}, bf16[32,2048]{1,0:T(8,128)(2,1)S(1)}, u32[]{:S(2)}, u32[]{:S(2)}) collective-permute-start(bf16[32,2048]{1,0:T(8,128)(2,1)S(1)} %get-tuple-element.155), channel_id=1, source_target_pairs={{0,2},{1,3},{2,0},{3,1},{4,6},{5,7},{6,4},{7,5},{8,10},{9,11},{10,... | collective-permute-start | bytes 393224 | tf_op jit(solution)/shard_map/ppermute | solution.py:83
  98.1 1.6 %collective-permute-start.30 = (bf16[64,2048]{1,0:T(8,128)(2,1)S(1)}, bf16[64,2048]{1,0:T(8,128)(2,1)S(1)}, u32[]{:S(2)}, u32[]{:S(2)}) collective-permute-start(bf16[64,2048]{1,0:T(8,128)(2,1)S(1)} %get-tuple-element.181.refs_1_), channel_id=1, source_target_pairs={{0,4},{4,0},{8,12},{12,8},{1,5},{5,1},{9,13},{13,9},{2,6},{6,2},{1... | collective-permute-start | bytes 786440 | tf_op jit(solution)/shard_map/ppermute | solution.py:70
  98.2 1.9 %collective-permute-start.32 = (bf16[64,2048]{1,0:T(8,128)(2,1)S(1)}, bf16[64,2048]{1,0:T(8,128)(2,1)S(1)}, u32[]{:S(2)}, u32[]{:S(2)}) collective-permute-start(bf16[64,2048]{1,0:T(8,128)(2,1)S(1)} %collective-permute-done.31.refs_3_), channel_id=1, source_target_pairs={{0,4},{4,0},{8,12},{12,8},{1,5},{5,1},{9,13},{13,9},{2,6},{6,2},{1... | collective-permute-start | bytes 786440 | tf_op jit(solution)/shard_map/ppermute | solution.py:70
  102.1 13.8 %collective-permute-start.33 = (bf16[128,1024]{1,0:T(8,128)(2,1)S(1)}, bf16[128,1024]{1,0:T(8,128)(2,1)S(1)}, u32[]{:S(2)}, u32[]{:S(2)}) collective-permute-start(bf16[128,1024]{1,0:T(8,128)(2,1)S(1)} %get-tuple-element.177), channel_id=1, source_target_pairs={{0,1},{1,0},{2,3},{3,2},{4,5},{5,4},{6,7},{7,6},{8,9},{9,8},{10,11... | collective-permute-start | bytes 786440 | tf_op jit(solution)/shard_map/ppermute | solution.py:83
  104.8 8.7 %collective-permute-start.29 = (bf16[32,2048]{1,0:T(8,128)(2,1)S(1)}, bf16[32,2048]{1,0:T(8,128)(2,1)S(1)}, u32[]{:S(2)}, u32[]{:S(2)}) collective-permute-start(bf16[32,2048]{1,0:T(8,128)(2,1)S(1)} %get-tuple-element.168), channel_id=1, source_target_pairs={{0,2},{1,3},{2,0},{3,1},{4,6},{5,7},{6,4},{7,5},{8,10},{9,11},{10,... | collective-permute-start | bytes 393224 | tf_op jit(solution)/shard_map/ppermute | solution.py:83
  113.5 7.0 %collective-permute-start.35 = (bf16[128,512]{1,0:T(8,128)(2,1)S(1)}, bf16[128,512]{1,0:T(8,128)(2,1)S(1)}, u32[]{:S(2)}, u32[]{:S(2)}) collective-permute-start(bf16[128,512]{1,0:T(8,128)(2,1)S(1)} %get-tuple-element.183), channel_id=1, source_target_pairs={{0,1},{1,0},{2,3},{3,2},{4,5},{5,4},{6,7},{7,6},{8,9},{9,8},{10,11... | collective-permute-start | bytes 393224 | tf_op jit(solution)/shard_map/ppermute | solution.py:83
  116.0 7.4 %collective-permute-start.34 = (bf16[64,1024]{1,0:T(8,128)(2,1)S(1)}, bf16[64,1024]{1,0:T(8,128)(2,1)S(1)}, u32[]{:S(2)}, u32[]{:S(2)}) collective-permute-start(bf16[64,1024]{1,0:T(8,128)(2,1)S(1)} %get-tuple-element.180), channel_id=1, source_target_pairs={{0,2},{1,3},{2,0},{3,1},{4,6},{5,7},{6,4},{7,5},{8,10},{9,11},{10,... | collective-permute-start | bytes 393224 | tf_op jit(solution)/shard_map/ppermute | solution.py:83
  118.3 6.9 %collective-permute-start.37 = (bf16[128,512]{1,0:T(8,128)(2,1)S(1)}, bf16[128,512]{1,0:T(8,128)(2,1)S(1)}, u32[]{:S(2)}, u32[]{:S(2)}) collective-permute-start(bf16[128,512]{1,0:T(8,128)(2,1)S(1)} %get-tuple-element.188), channel_id=1, source_target_pairs={{0,1},{1,0},{2,3},{3,2},{4,5},{5,4},{6,7},{7,6},{8,9},{9,8},{10,11... | collective-permute-start | bytes 393224 | tf_op jit(solution)/shard_map/ppermute | solution.py:83
  120.5 7.5 %collective-permute-start.36 = (bf16[64,512]{1,0:T(8,128)(2,1)S(1)}, bf16[64,512]{1,0:T(8,128)(2,1)S(1)}, u32[]{:S(2)}, u32[]{:S(2)}) collective-permute-start(bf16[64,512]{1,0:T(8,128)(2,1)S(1)} %get-tuple-element.185), channel_id=1, source_target_pairs={{0,2},{1,3},{2,0},{3,1},{4,6},{5,7},{6,4},{7,5},{8,10},{9,11},{10,... | collective-permute-start | bytes 196616 | tf_op jit(solution)/shard_map/ppermute | solution.py:83
  125.3 5.2 %collective-permute-start.38 = (bf16[64,512]{1,0:T(8,128)(2,1)S(1)}, bf16[64,512]{1,0:T(8,128)(2,1)S(1)}, u32[]{:S(2)}, u32[]{:S(2)}) collective-permute-start(bf16[64,512]{1,0:T(8,128)(2,1)S(1)} %get-tuple-element.190), channel_id=1, source_target_pairs={{0,2},{1,3},{2,0},{3,1},{4,6},{5,7},{6,4},{7,5},{8,10},{9,11},{10,... | collective-permute-start | bytes 196616 | tf_op jit(solution)/shard_map/ppermute | solution.py:83

commit v8 on v7

--- a/solution.py
+++ b/solution.py
@@ -606,7 +606,7 @@
             out = after(out, attended[-1][-1])
         attended.append([out] + [chip_move(out, pool_count, d) for d in range(1, chips)])
         if c + 2 < len(chunks):
-            moved[c + 2], both = reduced(c + 2, attended[c][-1])
+            moved[c + 2], both = reduced(c + 2, attended[c][0])
     new_key, new_value = earlier
 
     stages = reversed_bits(1, tp_count).bit_length()
@@ -617,9 +617,9 @@
         column = at * columns // count
         places.append([(r * part, r * rows + start, part, column) for r in range(share)])
     for slot in range(last + stages):
-        while len(keeps) < min(slot + 1 if slot < 2 else slot + 2, last + 1):
-            multiply(products[-1], total, new_key)
-        for stage in reversed(range(stages)) if slot < 3 else range(stages):
+        while len(keeps) < min(slot + 2 if slot > 1 else slot + 1, last + 1):
+            multiply(products[-1], new_key, total)
+        for stage in reversed(range(stages)) if slot == 1 else range(stages):
             i = slot - stage
             if not 0 <= i <= last:
                 continue

time: 132 us -> 131 us (level)
  starting transfers between devices: 42.3 us -> 35.3 us
  waiting for transfers between devices: 42.1 us -> 48.4 us
    ppermute x10, starting transfers between devices: 21.2 us -> 14.5 us  [tp_swap(): return lax.ppermute(x, 'tp', [(z, z ^ step) for z in range(tp_count)])]
    ppermute x10, waiting for transfers between devices: 16 us -> 22.8 us  [tp_swap(): return lax.ppermute(x, 'tp', [(z, z ^ step) for z in range(tp_count)])]
  transfers between devices with their start and end apart: 39 -> 39, of which waited for: 18 -> 20; matrix products, arithmetic and copies ran while one was open for 4% -> 4% of each run, Pallas kernels for 27% -> 28%
where the time goes in v8:
time: 131 us
  waiting for transfers between devices  48.4 us (37%)
  Pallas kernels  41.3 us (32%)
  starting transfers between devices  35.3 us (27%)
  other arithmetic  4.72 us (4%)
    pallas_call x27, Pallas kernels, local_call(): pl.pallas_call(body, in_specs=[spec for _, spec in operands] + [HBM] * le...  41.3 us
    ppermute x10, waiting for transfers between devices, tp_swap(): return lax.ppermute(x, 'tp', [(z, z ^ step) for z in range(tp_count)])  22.8 us
    ppermute x12, waiting for transfers between devices, chip_move(): lax.ppermute(x, 'pool', [(p, (p // 2 + d) % chips * 2 + (p % 2 ^ e)) for...  17.4 us
    ppermute x10, starting transfers between devices, tp_swap(): return lax.ppermute(x, 'tp', [(z, z ^ step) for z in range(tp_count)])  14.5 us
    ppermute x12, starting transfers between devices, chip_move(): lax.ppermute(x, 'pool', [(p, (p // 2 + d) % chips * 2 + (p % 2 ^ e)) for...  13.6 us
    ppermute x3, waiting for transfers between devices, shards(): lax.ppermute(shrunk, 'tp', [(i, (i + d) % tp_count) for i in range(tp_cou...  5.12 us
    ppermute x3, starting transfers between devices, shards(): lax.ppermute(shrunk, 'tp', [(i, (i + d) % tp_count) for i in range(tp_cou...  4.67 us
    convert_element_type x3, other arithmetic, scaled(): return (x * factor[None, :]).astype(jnp.bfloat16)  3.22 us
  transfers between devices with their start and end apart: 39, of which 20 were waited for; matrix products, arithmetic and copies ran while one was open for 4% of the time, Pallas kernels for 28%

profile of v8, /device:TPU:0, one launch (start us, length us, event | category | flops | bytes accessed | tf_op | source)
XLA Modules:
  0.0 130.7 jit_solution(3975808198018853252)
XLA Ops:
  0.6 2.5 %collective-permute-start.2 = (s32[1,128]{1,0:T(1,128)}, s32[1,128]{1,0:T(1,128)S(1)}, u32[]{:S(2)}, u32[]{:S(2)}) collective-permute-start(s32[1,128]{1,0:T(1,128)} %bitcast.11), channel_id=1, source_target_pairs={{0,12},{4,8},{8,4},{12,0},{1,13},{5,9},{9,5},{13,1},{2,14},{6,10},... | collective-permute-start | bytes 1544 | tf_op jit(solution)/shard_map/ppermute | solution.py:75
  3.1 0.6 collective-permute-start.1
  3.8 0.7 dynamic-slice_convert_fusion.4
  4.5 1.3 multiply_convert_fusion.3.refs_5_
  5.8 0.9 collective-permute-done.1.refs_3_
  6.8 0.9 collective-permute-start.4
  7.7 0.7 dynamic-slice_convert_fusion
  8.4 1.8 %multiply_convert_fusion = (bf16[128,2048]{1,0:T(8,128)(2,1)S(1)}, bf16[128,2048]{1,0:T(8,128)(2,1)S(1)}, bf16[128,2048]{1,0:T(8,128)(2,1)S(1)}) fusion(f32[2048]{0:T(1024)S(1)} %get-tuple-element.200, bf16[128,8192]{1,0:T(8,128)(2,1)} %refs_0_.1, s32[]{:T(128)S(6)} %select_n.137, f32[2048]{0:T(1024)S(1)} %get-tuple-element.201, s32[]{:T(128)S(6)} %select_n.135, ...), kind=kLoop, calls=%fused_computation | loop fusion | flops 2359296 | bytes 3170316 | tf_op jit(solution)/shard_map/convert_element_type | solution.py:457
  10.4 5.9 %load.1 = (bf16[512,2048]{1,0:T(8,128)(2,1)S(1)}, bf16[512,2048]{1,0:T(8,128)(2,1)S(1)}, bf16[2048,2048]{1,0:T(8,128)(2,1)S(1)}, bf16[2048,256]{1,0:T(8,128)(2,1...) custom-call(bf16[512,2048]{1,0:T(8,128)(2,1)} %bitcast.16, ...), custom_call_target="tpu_custom_call" | custom-call | flops 1000 | bytes 1000 | tf_op jit(solution)/shard_map/load/pallas_call | solution.py:42
  16.3 3.9 %collective-permute-done.4.refs_7_ = bf16[128,2048]{1,0:T(8,128)(2,1)S(1)} collective-permute-done((bf16[128,2048]{1,0:T(8,128)(2,1)S(1)}, bf16[128,2048]{1,0:T(8,128)(2,1)S(1)}, u32[]{:S(2)}, u32[]{:S(2)}) %collective-permute-start.4) | collective-permute-done | bytes 524320 | tf_op jit(solution)/shard_map/ppermute | solution.py:75
  20.2 0.5 collective-permute-start.9
  20.7 1.4 %collective-permute-start.12 = (bf16[128,2048]{1,0:T(8,128)(2,1)S(1)}, bf16[128,2048]{1,0:T(8,128)(2,1)S(1)}, u32[]{:S(2)}, u32[]{:S(2)}) collective-permute-start(bf16[128,2048]{1,0:T(8,128)(2,1)S(1)} %get-tuple-element.127), channel_id=1, source_target_pairs={{0,8},{4,12},{8,0},{12,4},{1,9},{5,13},{9,1},{13,5},{2,10},{6,14},... | collective-permute-start | bytes 1572872 | tf_op jit(solution)/shard_map/ppermute | solution.py:75
  22.1 0.5 collective-permute-start.13
  22.6 2.4 %shrink.1 = (s32[1,512]{1,0:T(1,128)S(1)}, f32[32,512]{1,0:T(8,128)S(1)}) custom-call(s32[1]{0:T(128)} %bitcast.1.refs_0_, s32[1,128]{1,0:T(1,128)S(1)} %bitcast.14, s32[1,128]{1,0:T(1,128)S(1)} %collective-permute-done.refs_2_, s32[1,128]{1,0:T(1,128)S(1)} %collective-permute-done.1.refs_3_, s32[1,128]{1,0:T(1,128)S(1)} %collective-permute-done.2.refs_4_, ...), custom_call_target="tpu_custom_call" | custom-call | flops 1000 | bytes 1000 | tf_op jit(solution)/shard_map/shrink/pallas_call | solution.py:42
  25.0 3.7 %collective-permute-start.8 = (f32[32,512]{1,0:T(8,128)S(1)}, f32[32,512]{1,0:T(8,128)S(1)}, u32[]{:S(2)}, u32[]{:S(2)}) collective-permute-start(f32[32,512]{1,0:T(8,128)S(1)} %get-tuple-element.111.refs_1_), channel_id=1, source_target_pairs={{0,3},{1,0},{2,1},{3,2},{4,7},{5,4},{6,5},{7,6},{8,11},{9,8},{10,9... | collective-permute-start | bytes 196616 | tf_op jit(solution)/shard_map/ppermute | solution.py:511
  28.7 1.0 collective-permute-start.6
  29.7 0.8 tables.1
  30.4 0.7 collective-permute-done.8.refs_4_
  31.1 4.4 %collective-permute-done.7.refs_3_ = f32[32,512]{1,0:T(8,128)S(1)} collective-permute-done((f32[32,512]{1,0:T(8,128)S(1)}, f32[32,512]{1,0:T(8,128)S(1)}, u32[]{:S(2)}, u32[]{:S(2)}) %collective-permute-start.7) | collective-permute-done | bytes 65568 | tf_op jit(solution)/shard_map/ppermute | solution.py:511
  35.6 4.5 %project_own.1 = (f32[128,2560]{1,0:T(8,128)S(1)}, bf16[128,2560]{1,0:T(8,128)(2,1)S(1)}, bf16[128,2,64,128]{3,2,1,0:T(8,128)(2,1)S(1)}, bf16[128,2,64,128]{3,2,1,0:T(8,128)(2,1)S(1)}) custom-call(s32[1,512]{1,0:T(1,128)S(1)} %get-tuple-element.125.refs_0_, f32[32,512]{1,0:T(8,128)S(1)} %get-tuple-element.111.refs_1_, ...), custom_call_target="tpu_custom_call" | custom-call | flops 1000 | bytes 1000 | tf_op jit(solution)/shard_map/project_own/pallas_call | solution.py:42
  40.1 2.8 %project_1_0.1.refs_0_ = f32[128,2560]{1,0:T(8,128)S(1)} custom-call(s32[1,512]{1,0:T(1,128)S(1)} %get-tuple-element.125.refs_0_, f32[32,512]{1,0:T(8,128)S(1)} %get-tuple-element.111.refs_1_, f32[32,512]{1,0:T(8,128)S(1)} %collective-permute-done.6.refs_2_, f32[32,512]{1,0:T(8,128)S(1)} %collective-permute-done.7.refs_3_, ...), custom_call_target="tpu_custom_call" | custom-call | flops 1000 | bytes 1000 | tf_op jit(solution)/shard_map/project_1_0/pallas_call | solution.py:42
  42.9 3.0 %collective-permute-done.13.refs_5_ = bf16[128,2048]{1,0:T(8,128)(2,1)S(1)} collective-permute-done((bf16[128,2048]{1,0:T(8,128)(2,1)S(1)}, bf16[128,2048]{1,0:T(8,128)(2,1)S(1)}, u32[]{:S(2)}, u32[]{:S(2)}) %collective-permute-start.13) | collective-permute-done | bytes 524320 | tf_op jit(solution)/shard_map/ppermute | solution.py:75
  45.9 2.8 %project_1_1.1 = (bf16[32,2560]{1,0:T(8,128)(2,1)S(1)}, bf16[32,2560]{1,0:T(8,128)(2,1)S(1)}, bf16[64,2560]{1,0:T(8,128)(2,1)S(1)}) custom-call(s32[1,512]{1,0:T(1,128)S(1)} %get-tuple-element.125.refs_0_, f32[32,512]{1,0:T(8,128)S(1)} %get-tuple-element.111.refs_1_, f32[32,512]{1,0:T(8,128)S(1)} %collective-permute-done.6.refs_2_, ...), custom_call_target="tpu_custom_call" | custom-call | flops 1000 | bytes 1000 | tf_op jit(solution)/shard_map/project_1_1/pallas_call | solution.py:42
  48.7 0.3 collective-permute-start.14
  49.0 0.3 collective-permute-start.16
  49.5 0.7 collective-permute-done.14.refs_1_
  50.2 1.4 %collective-permute-start.15 = (bf16[32,2560]{1,0:T(8,128)(2,1)S(1)}, bf16[32,2560]{1,0:T(8,128)(2,1)S(1)}, u32[]{:S(2)}, u32[]{:S(2)}) collective-permute-start(bf16[32,2560]{1,0:T(8,128)(2,1)S(1)} %add_1_0.1), channel_id=1, source_target_pairs={{0,8},{4,12},{8,0},{12,4},{1,9},{5,13},{9,1},{13,5},{2,10},{6,14},... | collective-permute-start | bytes 491528 | tf_op jit(solution)/shard_map/ppermute | solution.py:75
  51.7 0.7 collective-permute-start.17
  52.4 4.9 %collective-permute-done.15.refs_2_ = bf16[32,2560]{1,0:T(8,128)(2,1)S(1)} collective-permute-done((bf16[32,2560]{1,0:T(8,128)(2,1)S(1)}, bf16[32,2560]{1,0:T(8,128)(2,1)S(1)}, u32[]{:S(2)}, u32[]{:S(2)}) %collective-permute-start.15) | collective-permute-done | bytes 163872 | tf_op jit(solution)/shard_map/ppermute | solution.py:75
  57.3 3.4 %attend_0.1 = (bf16[32,2048]{1,0:T(8,128)(2,1)S(1)}, bf16[32,256]{1,0:T(8,128)(2,1)S(1)}, bf16[32,256]{1,0:T(8,128)(2,1)S(1)}, bf16[2048,2048]{1,0:T(8,128)(2,1)S(1)}) custom-call(f32[128,2560]{1,0:T(8,128)S(1)} %get-tuple-element.123.refs_0_.refs_2_, bf16[128,2560]{1,0:T(8,128)(2,1)S(1)} %collective-permute-done.11.refs_1_.refs_3_, ...), custom_call_target="tpu_custom_call" | custom-call | flops 1000 | bytes 1000 | tf_op jit(solution)/shard_map/attend_0/pallas_call | solution.py:42
  60.8 1.4 %collective-permute-start.20 = (bf16[32,2048]{1,0:T(8,128)(2,1)S(1)}, bf16[32,2048]{1,0:T(8,128)(2,1)S(1)}, u32[]{:S(2)}, u32[]{:S(2)}) collective-permute-start(bf16[32,2048]{1,0:T(8,128)(2,1)S(1)} %get-tuple-element.148.refs_1_), channel_id=1, source_target_pairs={{0,8},{4,12},{8,0},{12,4},{1,9},{5,13},{9,1},{13,5},{2,10},{6,14},... | collective-permute-start | bytes 393224 | tf_op jit(solution)/shard_map/ppermute | solution.py:75
  62.3 2.5 %attend_1.1 = (bf16[32,2048]{1,0:T(8,128)(2,1)S(1)}, bf16[64,256]{1,0:T(8,128)(2,1)S(1)}, bf16[64,256]{1,0:T(8,128)(2,1)S(1)}) custom-call(bf16[32,256]{1,0:T(8,128)(2,1)S(1)} %get-tuple-element.142.refs_0_, bf16[32,256]{1,0:T(8,128)(2,1)S(1)} %get-tuple-element.143.refs_1_, f32[128,2560]{1,0:T(8,128)S(1)} %get-tuple-element.123.refs_0_.refs_2_, ...), custom_call_target="tpu_custom_call" | custom-call | flops 1000 | bytes 1000 | tf_op jit(solution)/shard_map/attend_1/pallas_call | solution.py:42
  64.9 0.9 collective-permute-done.20.refs_3_
  65.8 1.4 %collective-permute-start.24 = (bf16[64,2560]{1,0:T(8,128)(2,1)S(1)}, bf16[64,2560]{1,0:T(8,128)(2,1)S(1)}, u32[]{:S(2)}, u32[]{:S(2)}) collective-permute-start(bf16[64,2560]{1,0:T(8,128)(2,1)S(1)} %add_1_2.1), channel_id=1, source_target_pairs={{0,8},{4,12},{8,0},{12,4},{1,9},{5,13},{9,1},{13,5},{2,10},{6,14},... | collective-permute-start | bytes 983048 | tf_op jit(solution)/shard_map/ppermute | solution.py:75
  67.2 2.4 %output_0_0_1.1 = (bf16[64,2048]{1,0:T(8,128)(2,1)S(1)}, bf16[64,2048]{1,0:T(8,128)(2,1)S(1)}) custom-call(s32[4]{0:T(128)S(1)} %pad_add_fusion.refs_0_, bf16[32,2048]{1,0:T(8,128)(2,1)S(1)} %get-tuple-element.148.refs_1_, bf16[32,2048]{1,0:T(8,128)(2,1)S(1)} %collective-permute-done.19.refs_2_, bf16[32,2048]{1,0:T(8,128)(2,1)S(1)} %collective-permute-done.20.refs_3_, ...), custom_call_target="tpu_custom_call" | custom-call | flops 1000 | bytes 1000 | tf_op jit(solution)/shard_map/output_0_0_1/pallas_call | solution.py:42
  69.6 1.6 %collective-permute-start.22 = (bf16[64,2048]{1,0:T(8,128)(2,1)S(1)}, bf16[64,2048]{1,0:T(8,128)(2,1)S(1)}, u32[]{:S(2)}, u32[]{:S(2)}) collective-permute-start(bf16[64,2048]{1,0:T(8,128)(2,1)S(1)} %get-tuple-element.152), channel_id=1, source_target_pairs={{0,1},{1,0},{2,3},{3,2},{4,5},{5,4},{6,7},{7,6},{8,9},{9,8},{10,11... | collective-permute-start | bytes 786440 | tf_op jit(solution)/shard_map/ppermute | solution.py:83
  71.2 1.3 %collective-permute-start.26 = (bf16[32,2048]{1,0:T(8,128)(2,1)S(1)}, bf16[32,2048]{1,0:T(8,128)(2,1)S(1)}, u32[]{:S(2)}, u32[]{:S(2)}) collective-permute-start(bf16[32,2048]{1,0:T(8,128)(2,1)S(1)} %get-tuple-element.161.refs_1_), channel_id=1, source_target_pairs={{0,8},{4,12},{8,0},{12,4},{1,9},{5,13},{9,1},{13,5},{2,10},{6,14},... | collective-permute-start | bytes 393224 | tf_op jit(solution)/shard_map/ppermute | solution.py:75
  72.6 3.7 %collective-permute-done.24.refs_4_ = bf16[64,2560]{1,0:T(8,128)(2,1)S(1)} collective-permute-done((bf16[64,2560]{1,0:T(8,128)(2,1)S(1)}, bf16[64,2560]{1,0:T(8,128)(2,1)S(1)}, u32[]{:S(2)}, u32[]{:S(2)}) %collective-permute-start.24) | collective-permute-done | bytes 327712 | tf_op jit(solution)/shard_map/ppermute | solution.py:75
  76.3 5.5 %attend_2.1 = (bf16[64,2048]{1,0:T(8,128)(2,1)S(1)}, bf16[128,256]{1,0:T(8,128)(2,1)}, bf16[128,256]{1,0:T(8,128)(2,1)}) custom-call(bf16[64,256]{1,0:T(8,128)(2,1)S(1)} %get-tuple-element.145.refs_0_, bf16[64,256]{1,0:T(8,128)(2,1)S(1)} %get-tuple-element.158.refs_1_, f32[128,2560]{1,0:T(8,128)S(1)} %get-tuple-element.123.refs_0_.refs_2_, ...), custom_call_target="tpu_custom_call" | custom-call | flops 1000 | bytes 1000 | tf_op jit(solution)/shard_map/attend_2/pallas_call | solution.py:42
  81.9 0.5 collective-permute-start.27
  82.4 0.8 collective-permute-done.25.refs_2_
  83.5 2.4 %output_1_0_1.1 = (bf16[64,2048]{1,0:T(8,128)(2,1)S(1)}, bf16[64,2048]{1,0:T(8,128)(2,1)S(1)}) custom-call(s32[4]{0:T(128)S(1)} %pad_add_fusion.refs_0_, bf16[32,2048]{1,0:T(8,128)(2,1)S(1)} %get-tuple-element.161.refs_1_, bf16[32,2048]{1,0:T(8,128)(2,1)S(1)} %collective-permute-done.25.refs_2_, bf16[32,2048]{1,0:T(8,128)(2,1)S(1)} %collective-permute-done.26.refs_3_, ...), custom_call_target="tpu_custom_call" | custom-call | flops 1000 | bytes 1000 | tf_op jit(solution)/shard_map/output_1_0_1/pallas_call | solution.py:42
  85.9 1.6 %collective-permute-start.28 = (bf16[64,2048]{1,0:T(8,128)(2,1)S(1)}, bf16[64,2048]{1,0:T(8,128)(2,1)S(1)}, u32[]{:S(2)}, u32[]{:S(2)}) collective-permute-start(bf16[64,2048]{1,0:T(8,128)(2,1)S(1)} %get-tuple-element.165), channel_id=1, source_target_pairs={{0,1},{1,0},{2,3},{3,2},{4,5},{5,4},{6,7},{7,6},{8,9},{9,8},{10,11... | collective-permute-start | bytes 786440 | tf_op jit(solution)/shard_map/ppermute | solution.py:83
  87.5 1.4 %collective-permute-start.31 = (bf16[64,2048]{1,0:T(8,128)(2,1)S(1)}, bf16[64,2048]{1,0:T(8,128)(2,1)S(1)}, u32[]{:S(2)}, u32[]{:S(2)}) collective-permute-start(bf16[64,2048]{1,0:T(8,128)(2,1)S(1)} %get-tuple-element.181.refs_1_), channel_id=1, source_target_pairs={{0,8},{4,12},{8,0},{12,4},{1,9},{5,13},{9,1},{13,5},{2,10},{6,14},... | collective-permute-start | bytes 786440 | tf_op jit(solution)/shard_map/ppermute | solution.py:75
  88.9 2.6 %collective-permute-start.23 = (bf16[32,2048]{1,0:T(8,128)(2,1)S(1)}, bf16[32,2048]{1,0:T(8,128)(2,1)S(1)}, u32[]{:S(2)}, u32[]{:S(2)}) collective-permute-start(bf16[32,2048]{1,0:T(8,128)(2,1)S(1)} %get-tuple-element.155), channel_id=1, source_target_pairs={{0,2},{1,3},{2,0},{3,1},{4,6},{5,7},{6,4},{7,5},{8,10},{9,11},{10,... | collective-permute-start | bytes 393224 | tf_op jit(solution)/shard_map/ppermute | solution.py:83
  91.5 4.9 %collective-permute-done.23.refs_1_ = bf16[32,2048]{1,0:T(8,128)(2,1)S(1)} collective-permute-done((bf16[32,2048]{1,0:T(8,128)(2,1)S(1)}, bf16[32,2048]{1,0:T(8,128)(2,1)S(1)}, u32[]{:S(2)}, u32[]{:S(2)}) %collective-permute-start.23) | collective-permute-done | bytes 131104 | tf_op jit(solution)/shard_map/ppermute | solution.py:83
  96.4 0.9 collective-permute-done.28.refs_1_
  97.5 0.5 collective-permute-start.32
  98.0 1.0 collective-permute-done.30.refs_2_
  99.0 0.4 collective-permute-done.32.refs_4_
  99.3 2.0 %output_2_0_2.1 = (bf16[128,1024]{1,0:T(8,128)(2,1)S(1)}, bf16[128,1024]{1,0:T(8,128)(2,1)S(1)}) custom-call(s32[4]{0:T(128)S(1)} %pad_add_fusion.refs_0_, bf16[64,2048]{1,0:T(8,128)(2,1)S(1)} %get-tuple-element.181.refs_1_, bf16[64,2048]{1,0:T(8,128)(2,1)S(1)} %collective-permute-done.30.refs_2_, bf16[64,2048]{1,0:T(8,128)(2,1)S(1)} %collective-permute-done.31.refs_3_, ...), custom_call_target="tpu_custom_call" | custom-call | flops 1000 | bytes 1000 | tf_op jit(solution)/shard_map/output_2_0_2/pallas_call | solution.py:42
  101.4 2.7 %collective-permute-start.33 = (bf16[128,1024]{1,0:T(8,128)(2,1)S(1)}, bf16[128,1024]{1,0:T(8,128)(2,1)S(1)}, u32[]{:S(2)}, u32[]{:S(2)}) collective-permute-start(bf16[128,1024]{1,0:T(8,128)(2,1)S(1)} %get-tuple-element.176), channel_id=1, source_target_pairs={{0,1},{1,0},{2,3},{3,2},{4,5},{5,4},{6,7},{7,6},{8,9},{9,8},{10,11... | collective-permute-start | bytes 786440 | tf_op jit(solution)/shard_map/ppermute | solution.py:83
  104.1 1.5 %collective-permute-start.29 = (bf16[32,2048]{1,0:T(8,128)(2,1)S(1)}, bf16[32,2048]{1,0:T(8,128)(2,1)S(1)}, u32[]{:S(2)}, u32[]{:S(2)}) collective-permute-start(bf16[32,2048]{1,0:T(8,128)(2,1)S(1)} %get-tuple-element.168), channel_id=1, source_target_pairs={{0,2},{1,3},{2,0},{3,1},{4,6},{5,7},{6,4},{7,5},{8,10},{9,11},{10,... | collective-permute-start | bytes 393224 | tf_op jit(solution)/shard_map/ppermute | solution.py:83
  105.6 1.3 output_2_2_4.1
  106.9 0.4 collective-permute-start.35
  107.4 6.6 %collective-permute-done.33.refs_1_ = bf16[128,1024]{1,0:T(8,128)(2,1)S(1)} collective-permute-done((bf16[128,1024]{1,0:T(8,128)(2,1)S(1)}, bf16[128,1024]{1,0:T(8,128)(2,1)S(1)}, u32[]{:S(2)}, u32[]{:S(2)}) %collective-permute-start.33) | collective-permute-done | bytes 262176 | tf_op jit(solution)/shard_map/ppermute | solution.py:83
  114.0 1.2 collective-permute-start.34
  115.2 1.3 output_2_3_4.1
  116.5 2.5 %collective-permute-start.37 = (bf16[128,512]{1,0:T(8,128)(2,1)S(1)}, bf16[128,512]{1,0:T(8,128)(2,1)S(1)}, u32[]{:S(2)}, u32[]{:S(2)}) collective-permute-start(bf16[128,512]{1,0:T(8,128)(2,1)S(1)} %get-tuple-element.188), channel_id=1, source_target_pairs={{0,1},{1,0},{2,3},{3,2},{4,5},{5,4},{6,7},{7,6},{8,9},{9,8},{10,11... | collective-permute-start | bytes 393224 | tf_op jit(solution)/shard_map/ppermute | solution.py:83
  119.2 4.5 %collective-permute-done.34.refs_1_ = bf16[64,1024]{1,0:T(8,128)(2,1)S(1)} collective-permute-done((bf16[64,1024]{1,0:T(8,128)(2,1)S(1)}, bf16[64,1024]{1,0:T(8,128)(2,1)S(1)}, u32[]{:S(2)}, u32[]{:S(2)}) %collective-permute-start.34) | collective-permute-done | bytes 131104 | tf_op jit(solution)/shard_map/ppermute | solution.py:83
  123.8 0.5 collective-permute-done.37.refs_1_
  124.4 0.7 collective-permute-done.36.refs_1_
  125.1 4.7 %collective-permute-done.38.refs_5_ = bf16[64,512]{1,0:T(8,128)(2,1)S(1)} collective-permute-done((bf16[64,512]{1,0:T(8,128)(2,1)S(1)}, bf16[64,512]{1,0:T(8,128)(2,1)S(1)}, u32[]{:S(2)}, u32[]{:S(2)}) %collective-permute-start.38) | collective-permute-done | bytes 65568 | tf_op jit(solution)/shard_map/ppermute | solution.py:83
  129.8 0.8 assemble.1
  (53 shorter events, 1.7 us)
Async XLA Ops:
  0.6 5.2 %collective-permute-start.2 = (s32[1,128]{1,0:T(1,128)}, s32[1,128]{1,0:T(1,128)S(1)}, u32[]{:S(2)}, u32[]{:S(2)}) collective-permute-start(s32[1,128]{1,0:T(1,128)} %bitcast.11), channel_id=1, source_target_pairs={{0,12},{4,8},{8,4},{12,0},{1,13},{5,9},{9,5},{13,1},{2,14},{6,10},... | collective-permute-start | bytes 1544 | tf_op jit(solution)/shard_map/ppermute | solution.py:75
  3.1 3.7 %collective-permute-start.1 = (s32[1,128]{1,0:T(1,128)}, s32[1,128]{1,0:T(1,128)S(1)}, u32[]{:S(2)}, u32[]{:S(2)}) collective-permute-start(s32[1,128]{1,0:T(1,128)} %bitcast.12), channel_id=1, source_target_pairs={{0,8},{4,12},{8,0},{12,4},{1,9},{5,13},{9,1},{13,5},{2,10},{6,14},... | collective-permute-start | bytes 1544 | tf_op jit(solution)/shard_map/ppermute | solution.py:75
  3.7 3.0 %collective-permute-start = (s32[1,128]{1,0:T(1,128)}, s32[1,128]{1,0:T(1,128)S(1)}, u32[]{:S(2)}, u32[]{:S(2)}) collective-permute-start(s32[1,128]{1,0:T(1,128)} %bitcast.13), channel_id=1, source_target_pairs={{0,4},{4,0},{8,12},{12,8},{1,5},{5,1},{9,13},{13,9},{2,6},{6,2},{1... | collective-permute-start | bytes 1544 | tf_op jit(solution)/shard_map/ppermute | solution.py:75
  4.5 5.8 %copy-start = (bf16[128,8192]{1,0:T(8,128)(2,1)S(1)}, bf16[128,8192]{1,0:T(8,128)(2,1)}, u32[]{:S(2)}) copy-start(bf16[128,8192]{1,0:T(8,128)(2,1)} %refs_0_.1) | copy-start | bytes 6291460
  6.8 13.4 %collective-permute-start.4 = (bf16[128,2048]{1,0:T(8,128)(2,1)S(1)}, bf16[128,2048]{1,0:T(8,128)(2,1)S(1)}, u32[]{:S(2)}, u32[]{:S(2)}) collective-permute-start(bf16[128,2048]{1,0:T(8,128)(2,1)S(1)} %multiply_convert_fusion.3.refs_5_), channel_id=1, source_target_pairs={{0,8},{4,12},{8,0},{12,4},{1,9},{5,13},{9,1},{13,5},{2,10},{6,14},... | collective-permute-start | bytes 1572872 | tf_op jit(solution)/shard_map/ppermute | solution.py:75
  7.7 14.5 %collective-permute-start.3 = (bf16[128,2048]{1,0:T(8,128)(2,1)S(1)}, bf16[128,2048]{1,0:T(8,128)(2,1)S(1)}, u32[]{:S(2)}, u32[]{:S(2)}) collective-permute-start(bf16[128,2048]{1,0:T(8,128)(2,1)S(1)} %multiply_convert_fusion.3.refs_5_), channel_id=1, source_target_pairs={{0,4},{4,0},{8,12},{12,8},{1,5},{5,1},{9,13},{13,9},{2,6},{6,2},{1... | collective-permute-start | bytes 1572872 | tf_op jit(solution)/shard_map/ppermute | solution.py:70
  10.4 12.2 %copy-start.1 = (s32[128]{0:T(128)S(1)}, s32[128]{0:T(128)}, u32[]{:S(2)}) copy-start(s32[128]{0:T(128)} %param.23) | copy-start | bytes 1540
  20.2 2.4 %collective-permute-start.5 = (bf16[128,2048]{1,0:T(8,128)(2,1)S(1)}, bf16[128,2048]{1,0:T(8,128)(2,1)S(1)}, u32[]{:S(2)}, u32[]{:S(2)}) collective-permute-start(bf16[128,2048]{1,0:T(8,128)(2,1)S(1)} %collective-permute-done.4.refs_7_), channel_id=1, source_target_pairs={{0,4},{4,0},{8,12},{12,8},{1,5},{5,1},{9,13},{13,9},{2,6},{6,2},{1... | collective-permute-start | bytes 1572872 | tf_op jit(solution)/shard_map/ppermute | solution.py:70
  20.2 8.4 %collective-permute-start.9 = (bf16[64,2048]{1,0:T(8,128)(2,1)S(1)}, bf16[64,2048]{1,0:T(8,128)(2,1)S(1)}, u32[]{:S(2)}, u32[]{:S(2)}) collective-permute-start(bf16[64,2048]{1,0:T(8,128)(2,1)S(1)} %get-tuple-element.116), channel_id=1, source_target_pairs={{0,4},{4,0},{8,12},{12,8},{1,5},{5,1},{9,13},{13,9},{2,6},{6,2},{1... | collective-permute-start | bytes 786440 | tf_op jit(solution)/shard_map/ppermute | solution.py:70
  20.7 7.9 %collective-permute-start.10 = (bf16[64,2048]{1,0:T(8,128)(2,1)S(1)}, bf16[64,2048]{1,0:T(8,128)(2,1)S(1)}, u32[]{:S(2)}, u32[]{:S(2)}) collective-permute-start(bf16[64,2048]{1,0:T(8,128)(2,1)S(1)} %get-tuple-element.117), channel_id=1, source_target_pairs={{0,4},{4,0},{8,12},{12,8},{1,5},{5,1},{9,13},{13,9},{2,6},{6,2},{1... | collective-permute-start | bytes 786440 | tf_op jit(solution)/shard_map/ppermute | solution.py:70
  20.7 19.4 %collective-permute-start.12 = (bf16[128,2048]{1,0:T(8,128)(2,1)S(1)}, bf16[128,2048]{1,0:T(8,128)(2,1)S(1)}, u32[]{:S(2)}, u32[]{:S(2)}) collective-permute-start(bf16[128,2048]{1,0:T(8,128)(2,1)S(1)} %get-tuple-element.127), channel_id=1, source_target_pairs={{0,8},{4,12},{8,0},{12,4},{1,9},{5,13},{9,1},{13,5},{2,10},{6,14},... | collective-permute-start | bytes 1572872 | tf_op jit(solution)/shard_map/ppermute | solution.py:75
  22.1 23.8 %collective-permute-start.13 = (bf16[128,2048]{1,0:T(8,128)(2,1)S(1)}, bf16[128,2048]{1,0:T(8,128)(2,1)S(1)}, u32[]{:S(2)}, u32[]{:S(2)}) collective-permute-start(bf16[128,2048]{1,0:T(8,128)(2,1)S(1)} %get-tuple-element.129), channel_id=1, source_target_pairs={{0,12},{4,8},{8,4},{12,0},{1,13},{5,9},{9,5},{13,1},{2,14},{6,10},... | collective-permute-start | bytes 1572872 | tf_op jit(solution)/shard_map/ppermute | solution.py:75
  22.6 7.1 %copy-start.2 = (s32[128]{0:T(128)S(1)}, s32[128]{0:T(128)}, u32[]{:S(2)}) copy-start(s32[128]{0:T(128)} %param.22) | copy-start | bytes 1540
  25.0 6.1 %collective-permute-start.8 = (f32[32,512]{1,0:T(8,128)S(1)}, f32[32,512]{1,0:T(8,128)S(1)}, u32[]{:S(2)}, u32[]{:S(2)}) collective-permute-start(f32[32,512]{1,0:T(8,128)S(1)} %get-tuple-element.111.refs_1_), channel_id=1, source_target_pairs={{0,3},{1,0},{2,1},{3,2},{4,7},{5,4},{6,5},{7,6},{8,11},{9,8},{10,9... | collective-permute-start | bytes 196616 | tf_op jit(solution)/shard_map/ppermute | solution.py:511
  28.6 6.9 %collective-permute-start.7 = (f32[32,512]{1,0:T(8,128)S(1)}, f32[32,512]{1,0:T(8,128)S(1)}, u32[]{:S(2)}, u32[]{:S(2)}) collective-permute-start(f32[32,512]{1,0:T(8,128)S(1)} %get-tuple-element.111.refs_1_), channel_id=1, source_target_pairs={{0,2},{1,3},{2,0},{3,1},{4,6},{5,7},{6,4},{7,5},{8,10},{9,11},{10,... | collective-permute-start | bytes 196616 | tf_op jit(solution)/shard_map/ppermute | solution.py:511
  28.7 6.9 %collective-permute-start.6 = (f32[32,512]{1,0:T(8,128)S(1)}, f32[32,512]{1,0:T(8,128)S(1)}, u32[]{:S(2)}, u32[]{:S(2)}) collective-permute-start(f32[32,512]{1,0:T(8,128)S(1)} %get-tuple-element.111.refs_1_), channel_id=1, source_target_pairs={{0,1},{1,2},{2,3},{3,0},{4,5},{5,6},{6,7},{7,4},{8,9},{9,10},{10,1... | collective-permute-start | bytes 196616 | tf_op jit(solution)/shard_map/ppermute | solution.py:511
  40.0 17.3 %collective-permute-start.11 = (bf16[128,2560]{1,0:T(8,128)(2,1)S(1)}, bf16[128,2560]{1,0:T(8,128)(2,1)S(1)}, u32[]{:S(2)}, u32[]{:S(2)}) collective-permute-start(bf16[128,2560]{1,0:T(8,128)(2,1)S(1)} %get-tuple-element.124), channel_id=1, source_target_pairs={{0,4},{4,0},{8,12},{12,8},{1,5},{5,1},{9,13},{13,9},{2,6},{6,2},{1... | collective-permute-start | bytes 1966088 | tf_op jit(solution)/shard_map/ppermute | solution.py:70
  48.7 1.5 %collective-permute-start.14 = (bf16[32,2560]{1,0:T(8,128)(2,1)S(1)}, bf16[32,2560]{1,0:T(8,128)(2,1)S(1)}, u32[]{:S(2)}, u32[]{:S(2)}) collective-permute-start(bf16[32,2560]{1,0:T(8,128)(2,1)S(1)} %get-tuple-element.131), channel_id=1, source_target_pairs={{0,4},{4,0},{8,12},{12,8},{1,5},{5,1},{9,13},{13,9},{2,6},{6,2},{1... | collective-permute-start | bytes 491528 | tf_op jit(solution)/shard_map/ppermute | solution.py:70
  49.0 2.7 %collective-permute-start.16 = (bf16[32,2560]{1,0:T(8,128)(2,1)S(1)}, bf16[32,2560]{1,0:T(8,128)(2,1)S(1)}, u32[]{:S(2)}, u32[]{:S(2)}) collective-permute-start(bf16[32,2560]{1,0:T(8,128)(2,1)S(1)} %get-tuple-element.132), channel_id=1, source_target_pairs={{0,4},{4,0},{8,12},{12,8},{1,5},{5,1},{9,13},{13,9},{2,6},{6,2},{1... | collective-permute-start | bytes 491528 | tf_op jit(solution)/shard_map/ppermute | solution.py:70
  49.3 12.9 %collective-permute-start.18 = (bf16[64,2560]{1,0:T(8,128)(2,1)S(1)}, bf16[64,2560]{1,0:T(8,128)(2,1)S(1)}, u32[]{:S(2)}, u32[]{:S(2)}) collective-permute-start(bf16[64,2560]{1,0:T(8,128)(2,1)S(1)} %get-tuple-element.146), channel_id=1, source_target_pairs={{0,4},{4,0},{8,12},{12,8},{1,5},{5,1},{9,13},{13,9},{2,6},{6,2},{1... | collective-permute-start | bytes 983048 | tf_op jit(solution)/shard_map/ppermute | solution.py:70
  50.2 7.1 %collective-permute-start.15 = (bf16[32,2560]{1,0:T(8,128)(2,1)S(1)}, bf16[32,2560]{1,0:T(8,128)(2,1)S(1)}, u32[]{:S(2)}, u32[]{:S(2)}) collective-permute-start(bf16[32,2560]{1,0:T(8,128)(2,1)S(1)} %add_1_0.1), channel_id=1, source_target_pairs={{0,8},{4,12},{8,0},{12,4},{1,9},{5,13},{9,1},{13,5},{2,10},{6,14},... | collective-permute-start | bytes 491528 | tf_op jit(solution)/shard_map/ppermute | solution.py:75
  51.7 9.0 %collective-permute-start.17 = (bf16[32,2560]{1,0:T(8,128)(2,1)S(1)}, bf16[32,2560]{1,0:T(8,128)(2,1)S(1)}, u32[]{:S(2)}, u32[]{:S(2)}) collective-permute-start(bf16[32,2560]{1,0:T(8,128)(2,1)S(1)} %add_1_1.1), channel_id=1, source_target_pairs={{0,8},{4,12},{8,0},{12,4},{1,9},{5,13},{9,1},{13,5},{2,10},{6,14},... | collective-permute-start | bytes 491528 | tf_op jit(solution)/shard_map/ppermute | solution.py:75
  60.8 5.0 %collective-permute-start.20 = (bf16[32,2048]{1,0:T(8,128)(2,1)S(1)}, bf16[32,2048]{1,0:T(8,128)(2,1)S(1)}, u32[]{:S(2)}, u32[]{:S(2)}) collective-permute-start(bf16[32,2048]{1,0:T(8,128)(2,1)S(1)} %get-tuple-element.148.refs_1_), channel_id=1, source_target_pairs={{0,8},{4,12},{8,0},{12,4},{1,9},{5,13},{9,1},{13,5},{2,10},{6,14},... | collective-permute-start | bytes 393224 | tf_op jit(solution)/shard_map/ppermute | solution.py:75
  64.8 2.4 %collective-permute-start.19 = (bf16[32,2048]{1,0:T(8,128)(2,1)S(1)}, bf16[32,2048]{1,0:T(8,128)(2,1)S(1)}, u32[]{:S(2)}, u32[]{:S(2)}) collective-permute-start(bf16[32,2048]{1,0:T(8,128)(2,1)S(1)} %get-tuple-element.148.refs_1_), channel_id=1, source_target_pairs={{0,4},{4,0},{8,12},{12,8},{1,5},{5,1},{9,13},{13,9},{2,6},{6,2},{1... | collective-permute-start | bytes 393224 | tf_op jit(solution)/shard_map/ppermute | solution.py:70
  65.8 1.4 %collective-permute-start.21 = (bf16[32,2048]{1,0:T(8,128)(2,1)S(1)}, bf16[32,2048]{1,0:T(8,128)(2,1)S(1)}, u32[]{:S(2)}, u32[]{:S(2)}) collective-permute-start(bf16[32,2048]{1,0:T(8,128)(2,1)S(1)} %collective-permute-done.20.refs_3_), channel_id=1, source_target_pairs={{0,4},{4,0},{8,12},{12,8},{1,5},{5,1},{9,13},{13,9},{2,6},{6,2},{1... | collective-permute-start | bytes 393224 | tf_op jit(solution)/shard_map/ppermute | solution.py:70
  65.8 10.5 %collective-permute-start.24 = (bf16[64,2560]{1,0:T(8,128)(2,1)S(1)}, bf16[64,2560]{1,0:T(8,128)(2,1)S(1)}, u32[]{:S(2)}, u32[]{:S(2)}) collective-permute-start(bf16[64,2560]{1,0:T(8,128)(2,1)S(1)} %add_1_2.1), channel_id=1, source_target_pairs={{0,8},{4,12},{8,0},{12,4},{1,9},{5,13},{9,1},{13,5},{2,10},{6,14},... | collective-permute-start | bytes 983048 | tf_op jit(solution)/shard_map/ppermute | solution.py:75
  69.6 12.2 %collective-permute-start.22 = (bf16[64,2048]{1,0:T(8,128)(2,1)S(1)}, bf16[64,2048]{1,0:T(8,128)(2,1)S(1)}, u32[]{:S(2)}, u32[]{:S(2)}) collective-permute-start(bf16[64,2048]{1,0:T(8,128)(2,1)S(1)} %get-tuple-element.152), channel_id=1, source_target_pairs={{0,1},{1,0},{2,3},{3,2},{4,5},{5,4},{6,7},{7,6},{8,9},{9,8},{10,11... | collective-permute-start | bytes 786440 | tf_op jit(solution)/shard_map/ppermute | solution.py:83
  71.2 10.6 %collective-permute-start.26 = (bf16[32,2048]{1,0:T(8,128)(2,1)S(1)}, bf16[32,2048]{1,0:T(8,128)(2,1)S(1)}, u32[]{:S(2)}, u32[]{:S(2)}) collective-permute-start(bf16[32,2048]{1,0:T(8,128)(2,1)S(1)} %get-tuple-element.161.refs_1_), channel_id=1, source_target_pairs={{0,8},{4,12},{8,0},{12,4},{1,9},{5,13},{9,1},{13,5},{2,10},{6,14},... | collective-permute-start | bytes 393224 | tf_op jit(solution)/shard_map/ppermute | solution.py:75
  81.9 1.4 %collective-permute-start.25 = (bf16[32,2048]{1,0:T(8,128)(2,1)S(1)}, bf16[32,2048]{1,0:T(8,128)(2,1)S(1)}, u32[]{:S(2)}, u32[]{:S(2)}) collective-permute-start(bf16[32,2048]{1,0:T(8,128)(2,1)S(1)} %get-tuple-element.161.refs_1_), channel_id=1, source_target_pairs={{0,4},{4,0},{8,12},{12,8},{1,5},{5,1},{9,13},{13,9},{2,6},{6,2},{1... | collective-permute-start | bytes 393224 | tf_op jit(solution)/shard_map/ppermute | solution.py:70
  81.9 1.5 %collective-permute-start.27 = (bf16[32,2048]{1,0:T(8,128)(2,1)S(1)}, bf16[32,2048]{1,0:T(8,128)(2,1)S(1)}, u32[]{:S(2)}, u32[]{:S(2)}) collective-permute-start(bf16[32,2048]{1,0:T(8,128)(2,1)S(1)} %collective-permute-done.26.refs_3_), channel_id=1, source_target_pairs={{0,4},{4,0},{8,12},{12,8},{1,5},{5,1},{9,13},{13,9},{2,6},{6,2},{1... | collective-permute-start | bytes 393224 | tf_op jit(solution)/shard_map/ppermute | solution.py:70
  85.9 11.4 %collective-permute-start.28 = (bf16[64,2048]{1,0:T(8,128)(2,1)S(1)}, bf16[64,2048]{1,0:T(8,128)(2,1)S(1)}, u32[]{:S(2)}, u32[]{:S(2)}) collective-permute-start(bf16[64,2048]{1,0:T(8,128)(2,1)S(1)} %get-tuple-element.165), channel_id=1, source_target_pairs={{0,1},{1,0},{2,3},{3,2},{4,5},{5,4},{6,7},{7,6},{8,9},{9,8},{10,11... | collective-permute-start | bytes 786440 | tf_op jit(solution)/shard_map/ppermute | solution.py:83
  87.5 9.9 %collective-permute-start.31 = (bf16[64,2048]{1,0:T(8,128)(2,1)S(1)}, bf16[64,2048]{1,0:T(8,128)(2,1)S(1)}, u32[]{:S(2)}, u32[]{:S(2)}) collective-permute-start(bf16[64,2048]{1,0:T(8,128)(2,1)S(1)} %get-tuple-element.181.refs_1_), channel_id=1, source_target_pairs={{0,8},{4,12},{8,0},{12,4},{1,9},{5,13},{9,1},{13,5},{2,10},{6,14},... | collective-permute-start | bytes 786440 | tf_op jit(solution)/shard_map/ppermute | solution.py:75
  88.9 7.5 %collective-permute-start.23 = (bf16[32,2048]{1,0:T(8,128)(2,1)S(1)}, bf16[32,2048]{1,0:T(8,128)(2,1)S(1)}, u32[]{:S(2)}, u32[]{:S(2)}) collective-permute-start(bf16[32,2048]{1,0:T(8,128)(2,1)S(1)} %get-tuple-element.155), channel_id=1, source_target_pairs={{0,2},{1,3},{2,0},{3,1},{4,6},{5,7},{6,4},{7,5},{8,10},{9,11},{10,... | collective-permute-start | bytes 393224 | tf_op jit(solution)/shard_map/ppermute | solution.py:83
  97.4 1.6 %collective-permute-start.30 = (bf16[64,2048]{1,0:T(8,128)(2,1)S(1)}, bf16[64,2048]{1,0:T(8,128)(2,1)S(1)}, u32[]{:S(2)}, u32[]{:S(2)}) collective-permute-start(bf16[64,2048]{1,0:T(8,128)(2,1)S(1)} %get-tuple-element.181.refs_1_), channel_id=1, source_target_pairs={{0,4},{4,0},{8,12},{12,8},{1,5},{5,1},{9,13},{13,9},{2,6},{6,2},{1... | collective-permute-start | bytes 786440 | tf_op jit(solution)/shard_map/ppermute | solution.py:70
  97.5 1.9 %collective-permute-start.32 = (bf16[64,2048]{1,0:T(8,128)(2,1)S(1)}, bf16[64,2048]{1,0:T(8,128)(2,1)S(1)}, u32[]{:S(2)}, u32[]{:S(2)}) collective-permute-start(bf16[64,2048]{1,0:T(8,128)(2,1)S(1)} %collective-permute-done.31.refs_3_), channel_id=1, source_target_pairs={{0,4},{4,0},{8,12},{12,8},{1,5},{5,1},{9,13},{13,9},{2,6},{6,2},{1... | collective-permute-start | bytes 786440 | tf_op jit(solution)/shard_map/ppermute | solution.py:70
  101.4 12.6 %collective-permute-start.33 = (bf16[128,1024]{1,0:T(8,128)(2,1)S(1)}, bf16[128,1024]{1,0:T(8,128)(2,1)S(1)}, u32[]{:S(2)}, u32[]{:S(2)}) collective-permute-start(bf16[128,1024]{1,0:T(8,128)(2,1)S(1)} %get-tuple-element.176), channel_id=1, source_target_pairs={{0,1},{1,0},{2,3},{3,2},{4,5},{5,4},{6,7},{7,6},{8,9},{9,8},{10,11... | collective-permute-start | bytes 786440 | tf_op jit(solution)/shard_map/ppermute | solution.py:83
  104.1 15.0 %collective-permute-start.29 = (bf16[32,2048]{1,0:T(8,128)(2,1)S(1)}, bf16[32,2048]{1,0:T(8,128)(2,1)S(1)}, u32[]{:S(2)}, u32[]{:S(2)}) collective-permute-start(bf16[32,2048]{1,0:T(8,128)(2,1)S(1)} %get-tuple-element.168), channel_id=1, source_target_pairs={{0,2},{1,3},{2,0},{3,1},{4,6},{5,7},{6,4},{7,5},{8,10},{9,11},{10,... | collective-permute-start | bytes 393224 | tf_op jit(solution)/shard_map/ppermute | solution.py:83
  106.9 12.2 %collective-permute-start.35 = (bf16[128,512]{1,0:T(8,128)(2,1)S(1)}, bf16[128,512]{1,0:T(8,128)(2,1)S(1)}, u32[]{:S(2)}, u32[]{:S(2)}) collective-permute-start(bf16[128,512]{1,0:T(8,128)(2,1)S(1)} %get-tuple-element.183), channel_id=1, source_target_pairs={{0,1},{1,0},{2,3},{3,2},{4,5},{5,4},{6,7},{7,6},{8,9},{9,8},{10,11... | collective-permute-start | bytes 393224 | tf_op jit(solution)/shard_map/ppermute | solution.py:83
  114.0 9.7 %collective-permute-start.34 = (bf16[64,1024]{1,0:T(8,128)(2,1)S(1)}, bf16[64,1024]{1,0:T(8,128)(2,1)S(1)}, u32[]{:S(2)}, u32[]{:S(2)}) collective-permute-start(bf16[64,1024]{1,0:T(8,128)(2,1)S(1)} %get-tuple-element.178), channel_id=1, source_target_pairs={{0,2},{1,3},{2,0},{3,1},{4,6},{5,7},{6,4},{7,5},{8,10},{9,11},{10,... | collective-permute-start | bytes 393224 | tf_op jit(solution)/shard_map/ppermute | solution.py:83
  116.5 7.7 %collective-permute-start.37 = (bf16[128,512]{1,0:T(8,128)(2,1)S(1)}, bf16[128,512]{1,0:T(8,128)(2,1)S(1)}, u32[]{:S(2)}, u32[]{:S(2)}) collective-permute-start(bf16[128,512]{1,0:T(8,128)(2,1)S(1)} %get-tuple-element.188), channel_id=1, source_target_pairs={{0,1},{1,0},{2,3},{3,2},{4,5},{5,4},{6,7},{7,6},{8,9},{9,8},{10,11... | collective-permute-start | bytes 393224 | tf_op jit(solution)/shard_map/ppermute | solution.py:83
  119.2 5.9 %collective-permute-start.36 = (bf16[64,512]{1,0:T(8,128)(2,1)S(1)}, bf16[64,512]{1,0:T(8,128)(2,1)S(1)}, u32[]{:S(2)}, u32[]{:S(2)}) collective-permute-start(bf16[64,512]{1,0:T(8,128)(2,1)S(1)} %get-tuple-element.185), channel_id=1, source_target_pairs={{0,2},{1,3},{2,0},{3,1},{4,6},{5,7},{6,4},{7,5},{8,10},{9,11},{10,... | collective-permute-start | bytes 196616 | tf_op jit(solution)/shard_map/ppermute | solution.py:83
  124.3 5.5 %collective-permute-start.38 = (bf16[64,512]{1,0:T(8,128)(2,1)S(1)}, bf16[64,512]{1,0:T(8,128)(2,1)S(1)}, u32[]{:S(2)}, u32[]{:S(2)}) collective-permute-start(bf16[64,512]{1,0:T(8,128)(2,1)S(1)} %get-tuple-element.190), channel_id=1, source_target_pairs={{0,2},{1,3},{2,0},{3,1},{4,6},{5,7},{6,4},{7,5},{8,10},{9,11},{10,... | collective-permute-start | bytes 196616 | tf_op jit(solution)/shard_map/ppermute | solution.py:83

commit v9 on v6

--- a/solution.py
+++ b/solution.py
@@ -83,16 +83,55 @@
     return lax.ppermute(x, "tp", [(z, z ^ step) for z in range(tp_count)])
 
 
-def shrink(first_id, ids, blocks, query_down, value_down):
+def scaled_slices(name, starts, tokens, gain, width, wanted):
+    rows = tokens.shape[0]
+    count = starts.shape[0]
+
+    def kernel(ins, outs, scratch):
+        starts, gain, tokens = ins
+        held, sems = scratch
+
+        def copy(i):
+            columns = pl.ds(pl.multiple_of(starts[i], 128), width)
+            return pltpu.make_async_copy(tokens.at[:, columns], held.at[i], sems.at[i])
+
+        for i in range(count):
+            copy(i).start()
+        for i in range(count):
+            copy(i).wait()
+            columns = pl.ds(pl.multiple_of(starts[i], 128), width)
+            factor = gain[:, columns].astype(jnp.float32)
+            for out, (which, first, part) in zip(outs, wanted):
+                if which == i:
+                    values = held[i, first : first + part].astype(jnp.float32)
+                    out[...] = (values * factor).astype(jnp.bfloat16)
+
+    tokens = pltpu.with_memory_space_constraint(tokens, pltpu.HBM)
+    return local_call(
+        kernel,
+        name,
+        [(starts, SMEM), (gain, VMEM), (tokens, HBM)],
+        [shaped((part, width), jnp.bfloat16) for _, _, part in wanted],
+        [
+            pltpu.VMEM((count, rows, width), jnp.bfloat16),
+            pltpu.SemaphoreType.DMA((count,)),
+        ],
+    )
+
+
+def shrink(first_id, at, ids, blocks, query_down, value_down, width, tail):
     slots, _ = query_down.shape
     rows = blocks[0].shape[0]
     adapters = slots // 16
     count = len(blocks)
 
     def kernel(ins, outs, _):
-        first_id, *ins = ins
+        first_id, at, *ins = ins
         ids, blocks, tables = ins[:count], ins[count : 2 * count], ins[2 * count :]
-        local_ids, out = outs
+        local_ids, out, *tails = outs
+        for b, tail_out in enumerate(tails):
+            columns = pl.ds(pl.multiple_of(at[0], 128), width)
+            tail_out[...] = blocks[2 * b + 3][rows - tail :, columns]
         for b in range(count):
             local_ids[:, b * rows : (b + 1) * rows] = ids[b][...] - first_id[0]
         for first in range(0, count, 2):
@@ -111,8 +150,12 @@
     return local_call(
         kernel,
         "shrink",
-        [(first_id, SMEM), *in_vmem([*ids, *blocks, query_down, value_down])],
-        [shaped((1, rows * count), jnp.int32), shaped((32, rows * count))],
+        [(first_id, SMEM), (at, SMEM), *in_vmem([*ids, *blocks, query_down, value_down])],
+        [
+            shaped((1, rows * count), jnp.int32),
+            shaped((32, rows * count)),
+            *[shaped((tail, width), jnp.bfloat16)] * (count // 2 - 1),
+        ],
     )
 
 
@@ -175,7 +218,7 @@
     return pl.ds(pl.multiple_of(start, width), width)
 
 
-def project(name, kinds, span, ids, lows, blocks, weights, carried=()):
+def project(name, kinds, span, ids, lows, blocks, weights, which=None, options=()):
     wq, wk, wv, uq, uv = weights
     depth = blocks[0].shape[1]
     wide, kv, slots = wq.shape[1], wk.shape[1], uq.shape[0]
@@ -183,14 +226,23 @@
     start, total = span
 
     def kernel(ins, outs, scratch):
+        if options:
+            which, *ins = ins
         ids, *ins = ins
-        low_refs, blocks = ins[: len(lows)], ins[len(lows) : -5]
         wq, wk, wv, uq, uv = ins[-5:]
+        low_refs, ins = ins[: len(lows)], ins[len(lows) : -5]
+        blocks, choices = ins[: len(ins) - len(options)], ins[len(ins) - len(options) :]
         xs, spread_q, spread_v = scratch
         at = 0
         for block in blocks:
             xs[at : at + block.shape[0], :] = block[...]
             at += block.shape[0]
+        for j, choice in enumerate(choices):
+
+            @pl.when(which[0] == j)
+            def _():
+                xs[at:, :] = choice[...]
+
         low = low_refs[0][:, start : start + total]
         for other in low_refs[1:]:
             low = low + other[:, start : start + total]
@@ -220,10 +272,90 @@
     return local_call(
         kernel,
         name,
-        in_vmem([ids, *lows, *blocks, *weights]),
+        [(which, SMEM)] * bool(options)
+        + in_vmem([ids, *lows, *blocks, *options, *weights]),
         [shaped((count, wide + 2 * kv), dtype) for _, count, dtype in kinds],
         [pltpu.VMEM((total, depth), jnp.bfloat16), spread, spread],
+    )
+
+
+def project_base(blocks, weights, carried):
+    rows, depth = blocks[0].shape
+    wide, kv = weights[0].shape[1], weights[1].shape[1]
+    tile = min(512, wide)
+
+    def kernel(ins, outs, scratch):
+        *blocks, wq, wk, wv = ins
+        (xs,) = scratch
+        at = 0
+        for block in blocks:
+            xs[at : at + block.shape[0], :] = block[...]
+            at += block.shape[0]
+
+        def write(w, columns):
+            acc = jnp.dot(xs[...], w, preferred_element_type=jnp.float32)
+            outs[0][:, columns] = acc[:rows]
+            outs[1][:, columns] = acc[rows:]
+
+        @pl.loop(0, wide // tile)
+        def _(i):
+            columns = columns_at(i * tile, tile)
+            write(wq[:, columns], columns)
+
+        write(wk[...], slice(wide, wide + kv))
+        write(wv[...], slice(wide + kv, wide + 2 * kv))
+
+    return local_call(
+        kernel,
+        "project_base",
+        in_vmem([*blocks, *weights]),
+        [shaped((rows, wide + 2 * kv))] * 2,
+        [pltpu.VMEM((2 * rows, depth), jnp.bfloat16)],
         carried=carried,
+    )
+
+
+def add_adapters(keep, send, ids, lows, uq, uv):
+    rows = keep.shape[0]
+    wide, kv, slots = uq.shape[1], uv.shape[1], uq.shape[0]
+    tile = min(512, wide)
+
+    def kernel(ins, outs, scratch):
+        ids, *ins = ins
+        low_refs, (keep0, send0, uq, uv) = ins[: len(lows)], ins[len(lows) :]
+        keep, send = outs
+        spread_q, spread_v = scratch
+        low = low_refs[0][:, : 2 * rows]
+        for other in low_refs[1:]:
+            low = low + other[:, : 2 * rows]
+        spread_q[...], spread_v[...] = spread_lows(low, ids[:, : 2 * rows], slots // 16)
+
+        def write(extra, columns):
+            keep[:, columns] = keep0[:, columns] + extra[:rows]
+            send[:, columns] = (send0[:, columns] + extra[rows:]).astype(send.dtype)
+
+        @pl.loop(0, wide // tile)
+        def _(i):
+            columns = columns_at(i * tile, tile)
+            write(
+                jnp.dot(spread_q[...], uq[:, columns], preferred_element_type=jnp.float32),
+                columns,
+            )
+
+        keep[:, wide : wide + kv] = keep0[:, wide : wide + kv]
+        send[:, wide : wide + kv] = send0[:, wide : wide + kv].astype(send.dtype)
+        write(
+            jnp.dot(spread_v[...], uv[...], preferred_element_type=jnp.float32),
+            slice(wide + kv, wide + 2 * kv),
+        )
+
+    spread = pltpu.VMEM((2 * rows, slots), jnp.bfloat16)
+    return local_call(
+        kernel,
+        "add_adapters",
+        in_vmem([ids, *lows, keep, send, uq, uv]),
+        [shaped(keep.shape), shaped(keep.shape, jnp.bfloat16)],
+        [spread, spread],
     )
 
 
@@ -451,34 +583,36 @@
     kv_heads = rotated_key_cache.shape[1]
     head = rotated_key_cache.shape[3]
 
-    def scaled(start, width, tokens=tokens, gain=input_norm_gain, window=(0, rows)):
-        x = lax.dynamic_slice(tokens, (window[0], start), (window[1], width)).astype(jnp.float32)
-        factor = lax.dynamic_slice_in_dim(gain, start, width, 0).astype(jnp.float32)
-        return (x * factor[None, :]).astype(jnp.bfloat16)
-
     own_ids = row_adapter_index.reshape(1, rows)
     ids = [
         own_ids if d == e == 0 else chip_move(own_ids, pool_count, d, e)
         for d in range(chips)
         for e in range(2)
     ]
-    first = after(scaled(tp_at * piece, piece), *ids[1:])
-    first, tokens_1, gain_1 = lax.optimization_barrier((first, tokens, input_norm_gain))
+    gain = input_norm_gain.reshape(1, -1)
+    (first,) = scaled_slices(
+        "slice_tp", (tp_at * piece).reshape(1), tokens, gain, piece, [(0, 0, rows)]
+    )
+    first = after(first, *ids[1:])
+    first, gain_1 = lax.optimization_barrier((first, gain))
     same_core = [first] + [chip_move(first, pool_count, d) for d in range(1, chips)]
 
     cut = rows // 2
     chunks = [(0, cut), (cut, rows - cut)]
-    own = scaled(pool_at * base, base, tokens_1, gain_1)
-    partner_at = (pool_at // 2 * 2 + 1 - core) * base
-    partner = [
-        scaled(partner_at, base, tokens_1, gain_1, (at, rows // 2)) for at in (0, rows // 2)
-    ]
-    away = {}
-    for d in range(1, chips):
-        for e in range(2):
-            target = (chip + d) % chips * 2 + (core + e) % 2
-            away[d, e] = scaled(target * base, base, tokens_1, gain_1)
+    tail = rows * 3 // 8
+    starts = [pool_at * base, (pool_at // 2 * 2 + 1 - core) * base]
+    wanted = [(0, 0, rows), (1, 0, rows // 2), (1, rows // 2, rows // 2)]
+    places = [(d, e) for d in range(1, chips) for e in range(2)]
+    for i, (d, e) in enumerate(places):
+        starts.append(((chip + d) % chips * 2 + (core + e) % 2) * base)
+        wanted.append((2 + i, 0, rows - tail if e else rows))
+    own, *slices = scaled_slices(
+        "slice_pool", jnp.stack(starts).astype(jnp.int32), tokens, gain_1, base, wanted
+    )
+    partner, away = slices[:2], dict(zip(places, slices[2:]))
     first_id = (pool_at * adapters).reshape(1).astype(jnp.int32)
+    at_piece = (pool_at * base % piece).reshape(1).astype(jnp.int32)
+    which = ((tp_at - pool_at * base // piece) % tp_count).reshape(1).astype(jnp.int32)
     lengths = cache_length_per_row.reshape(1, rows)
     share = pool_count // tp_count
     order = []
@@ -492,35 +626,41 @@
 
     flat_down = [x.reshape(adapters * rank, piece) for x in (query_down_maps, value_down_maps)]
     flat_up = [x.reshape(adapters * rank, x.shape[2]) for x in (query_up_maps, value_up_maps)]
-    small = [own, *partner, *away.values(), first_id, lengths, order]
+    small = [own, first_id, at_piece, which, lengths, order]
     query_matrix, *small = lax.optimization_barrier((query_matrix, *small))
-    own, partner, small = small[0], small[1:3], small[3:]
-    away = dict(zip(away, small))
-    first_id, lengths, order = small[-3:]
+    own, first_id, at_piece, which, lengths, order = small
     down_q, down_v, *weights = load(
         [*flat_down, query_matrix, key_matrix, value_matrix, *flat_up]
     )
     partner = [core_swap(x, pool_count) for x in partner]
+    own_keep, own_send, keys, values = project_base(
+        [own, *partner], weights[:3], [rotated_key_cache, cached_value_rows]
+    )
     remote = [[] for _ in range(chips)]
     for (d, e), x in away.items():
         remote[d].append(chip_move(after(x, *same_core[1:]), pool_count, d, e))
-    same_core[1:] = [after(x, down_q) for x in same_core[1:]]
+    same_core[1:] = [after(x, own_keep) for x in same_core[1:]]
     adapter_rows = [b for x in same_core for b in (x, core_swap(x, pool_count))]
-    local_ids, shrunk = shrink(first_id, ids, adapter_rows, down_q, down_v)
+    local_ids, shrunk, *tails = shrink(
+        first_id, at_piece, ids, adapter_rows, down_q, down_v, base, tail
+    )
     lows = [shrunk] + [
         lax.ppermute(shrunk, "tp", [(i, (i + d) % tp_count) for i in range(tp_count)])
         for d in range(1, tp_count)
     ]
     rest = tables(tokens, after(lengths, shrunk), head)
-    own_sums, own_send, keys, values = project(
-        "project_own",
-        [(0, rows, jnp.float32), (rows, rows, jnp.bfloat16)],
-        (0, 2 * rows),
-        after(local_ids, rest[0]),
-        lows,
-        [own, *partner],
-        weights,
-        carried=[rotated_key_cache, cached_value_rows],
+
+    def along_tp(x, k):
+        pairs = []
+        for p in range(pool_count):
+            z = p * base // piece
+            pairs.append((p * tp_count + z, p * tp_count + (z + k) % tp_count))
+        return lax.ppermute(x, ("pool", "tp"), pairs)
+
+    tails = [after(x, rest[0]) for x in tails]
+    tails = [[x] + [along_tp(x, k) for k in range(1, tp_count)] for x in tails]
+    own_sums, own_send = add_adapters(
+        own_keep, own_send, after(local_ids, rest[0]), lows, *weights[3:]
     )
     swapped = core_swap(own_send, pool_count)
     local_ids = after(local_ids, own_sums)
@@ -547,6 +687,8 @@
             lows,
             [after(remote[d][1], keep)],
             weights,
+            which,
+            tails[d - 1],
         )
         for c, window in enumerate(chunks):
             swap = core_swap(sends[c], pool_count)

time: 121 us -> 121 us (level)
  other arithmetic: 4.61 us -> 0.15 us
  Pallas kernels: 39.1 us -> 43.3 us
    ppermute x0 -> x3, starting transfers between devices: none -> 9.79 us  [along_tp(): return lax.ppermute(x, ('pool', 'tp'), pairs)]
    ppermute x8, starting transfers between devices: 14.7 us -> 8.25 us  [tp_swap(): return lax.ppermute(x, 'tp', [(z, z ^ step) for z in range(tp_count)])]
    ppermute x8, waiting for transfers between devices: 16.6 us -> 21.9 us  [tp_swap(): return lax.ppermute(x, 'tp', [(z, z ^ step) for z in range(tp_count)])]
    convert_element_type x5 -> x0, other arithmetic: 4.53 us -> none  [the longest x3 3.11 us: scaled(): return (x * factor[None, :]).astype(jnp.bfloat16)]
    ppermute x3, waiting for transfers between devices: 5.12 us -> 0.65 us  [shards(): lax.ppermute(shrunk, 'tp', [(i, (i + d) % tp_count) for i in range(tp_cou...]
    pallas_call x22 -> x25, Pallas kernels: 39.1 us -> 43.3 us  [local_call(): pl.pallas_call(body, in_specs=[spec for _, spec in operands] + [HBM] * le...]
    ppermute x10, starting transfers between devices: 11.5 us -> 7.5 us  [chip_move(): lax.ppermute(x, 'pool', [(p, (p // 2 + d) % chips * 2 + (p % 2 ^ e)) for...]
    ppermute x10, waiting for transfers between devices: 19.3 us -> 16.1 us  [chip_move(): lax.ppermute(x, 'pool', [(p, (p // 2 + d) % chips * 2 + (p % 2 ^ e)) for...]
  transfers between devices with their start and end apart: 32 -> 35, of which waited for: 18 -> 18; matrix products, arithmetic and copies ran while one was open for 4% -> 1% of each run, Pallas kernels for 29% -> 33%
where the time goes in v9:
time: 121 us
  waiting for transfers between devices  43.4 us (36%)
  Pallas kernels  43.3 us (36%)
  starting transfers between devices  32 us (26%)
    pallas_call x25, Pallas kernels, local_call(): pl.pallas_call(body, in_specs=[spec for _, spec in operands] + [HBM] * le...  43.3 us
    ppermute x8, waiting for transfers between devices, tp_swap(): return lax.ppermute(x, 'tp', [(z, z ^ step) for z in range(tp_count)])  21.9 us
    ppermute x10, waiting for transfers between devices, chip_move(): lax.ppermute(x, 'pool', [(p, (p // 2 + d) % chips * 2 + (p % 2 ^ e)) for...  16.1 us
    ppermute x3, starting transfers between devices, along_tp(): return lax.ppermute(x, ('pool', 'tp'), pairs)  9.79 us
    ppermute x8, starting transfers between devices, tp_swap(): return lax.ppermute(x, 'tp', [(z, z ^ step) for z in range(tp_count)])  8.25 us
    ppermute x10, starting transfers between devices, chip_move(): lax.ppermute(x, 'pool', [(p, (p // 2 + d) % chips * 2 + (p % 2 ^ e)) for...  7.5 us
    ppermute x11, waiting for transfers between devices, core_swap(): return lax.ppermute(x, 'pool', [(p, p ^ 1) for p in range(pool_count)])  4.69 us
    ppermute x3, starting transfers between devices, shards(): lax.ppermute(shrunk, 'tp', [(i, (i + d) % tp_count) for i in range(tp_cou...  4.67 us
  transfers between devices with their start and end apart: 35, of which 18 were waited for; matrix products, arithmetic and copies ran while one was open for 1% of the time, Pallas kernels for 33%

profile of v9, /device:TPU:0, one launch (start us, length us, event | category | flops | bytes accessed | tf_op | source)
XLA Modules:
  0.0 120.6 jit_solution(5816915079418561954)
XLA Ops:
  0.6 0.5 collective-permute-start
  1.1 2.6 %collective-permute-start.1 = (s32[1,128]{1,0:T(1,128)}, s32[1,128]{1,0:T(1,128)S(1)}, u32[]{:S(2)}, u32[]{:S(2)}) collective-permute-start(s32[1,128]{1,0:T(1,128)} %bitcast.19), channel_id=1, source_target_pairs={{0,8},{4,12},{8,0},{12,4},{1,9},{5,13},{9,1},{13,5},{2,10},{6,14},... | collective-permute-start | bytes 1544 | tf_op jit(solution)/shard_map/ppermute | solution.py:75
  3.8 0.7 reshape.40.refs_1_
  4.6 1.1 slice_tp.1.refs_6_
  5.7 1.1 collective-permute-done.2.refs_5_
  6.8 0.7 collective-permute-start.4
  7.5 0.1 pad_add_fusion.refs_0_
  7.6 2.2 %slice_pool.1 = (bf16[128,2048]{1,0:T(8,128)(2,1)S(1)}, bf16[64,2048]{1,0:T(8,128)(2,1)S(1)}, bf16[64,2048]{1,0:T(8,128)(2,1)S(1)}, bf16[128,2048]{1,0:T(8,128)(2,1)S(1)}, bf16[80,2048]{1,0:T(8,128)(2,1)S(1)}) custom-call(s32[4]{0:T(128)S(1)} %pad_add_fusion.refs_0_, bf16[1,8192]{1,0:T(2,128)(2,1)S(1)} %reshape.40.refs_1_, bf16[128,8192]{1,0:T(8,128)(2,1)} %refs_0_.1), custom_call_target="tpu_custom_call" | custom-call | flops 1000 | bytes 1000 | tf_op jit(solution)/shard_map/slice_pool/pallas_call | solution.py:42
  9.8 0.1 collective-permute-start.5
  9.9 0.4 collective-permute-start.6
  10.4 0.1 pad_add_fusion.1.refs_0_
  10.4 0.1 collective-permute-start.3
  10.5 5.9 %load.1 = (bf16[512,2048]{1,0:T(8,128)(2,1)S(1)}, bf16[512,2048]{1,0:T(8,128)(2,1)S(1)}, bf16[2048,2048]{1,0:T(8,128)(2,1)S(1)}, bf16[2048,256]{1,0:T(8,128)(2,1...) custom-call(bf16[512,2048]{1,0:T(8,128)(2,1)} %bitcast.23, ...), custom_call_target="tpu_custom_call" | custom-call | flops 1000 | bytes 1000 | tf_op jit(solution)/shard_map/load/pallas_call | solution.py:42
  16.5 3.7 %project_base.1 = (f32[128,2560]{1,0:T(8,128)S(1)}, f32[128,2560]{1,0:T(8,128)S(1)}, bf16[128,2,64,128]{3,2,1,0:T(8,128)(2,1)S(1)}, bf16[128,2,64,128]{3,2,1,0:T(8,128)(2,1)S(1)}) custom-call(bf16[128,2048]{1,0:T(8,128)(2,1)S(1)} %get-tuple-element.96.refs_0_, bf16[64,2048]{1,0:T(8,128)(2,1)S(1)} %collective-permute-done.5.refs_1_, ...), custom_call_target="tpu_custom_call" | custom-call | flops 1000 | bytes 1000 | tf_op jit(solution)/shard_map/project_base/pallas_call | solution.py:42
  20.1 0.7 collective-permute-done.4.refs_8_
  20.8 1.1 collective-permute-start.12
  22.0 0.7 collective-permute-start.13
  22.8 2.4 %shrink.1 = (s32[1,512]{1,0:T(1,128)S(1)}, f32[32,512]{1,0:T(8,128)S(1)}, bf16[48,2048]{1,0:T(8,128)(2,1)S(1)}) custom-call(s32[1]{0:T(128)} %bitcast.6.refs_0_, s32[1]{0:T(128)} %bitcast.7.refs_1_, s32[1,128]{1,0:T(1,128)S(1)} %bitcast.21, s32[1,128]{1,0:T(1,128)S(1)} %collective-permute-done.refs_3_, s32[1,128]{1,0:T(1,128)S(1)} %collective-permute-done.1.refs_4_, ...), custom_call_target="tpu_custom_call" | custom-call | flops 1000 | bytes 1000 | tf_op jit(solution)/shard_map/shrink/pallas_call | solution.py:42
  25.1 3.7 %collective-permute-start.10 = (f32[32,512]{1,0:T(8,128)S(1)}, f32[32,512]{1,0:T(8,128)S(1)}, u32[]{:S(2)}, u32[]{:S(2)}) collective-permute-start(f32[32,512]{1,0:T(8,128)S(1)} %get-tuple-element.109.refs_1_.refs_2_), channel_id=1, source_target_pairs={{0,3},{1,0},{2,1},{3,2},{4,7},{5,4},{6,5},{7,6},{8,11},{9,8},{10,9... | collective-permute-start | bytes 196616 | tf_op jit(solution)/shard_map/ppermute | solution.py:648
  28.8 1.0 collective-permute-start.9
  29.8 0.8 tables.1
  30.6 0.6 collective-permute-done.10.refs_4_.refs_5_
  31.2 4.7 %collective-permute-start.14 = (bf16[48,2048]{1,0:T(8,128)(2,1)S(1)}, bf16[48,2048]{1,0:T(8,128)(2,1)S(1)}, u32[]{:S(2)}, u32[]{:S(2)}) collective-permute-start(bf16[48,2048]{1,0:T(8,128)(2,1)S(1)} %get-tuple-element.126.refs_7_), channel_id=1, source_target_pairs={{0,1},{5,6},{10,11},{15,12},{16,17},{21,22},{26,27},{31,28}} | collective-permute-start | bytes 589832 | tf_op jit(solution)/shard_map/ppermute | solution.py:658
  35.9 1.3 %collective-permute-start.15 = (bf16[48,2048]{1,0:T(8,128)(2,1)S(1)}, bf16[48,2048]{1,0:T(8,128)(2,1)S(1)}, u32[]{:S(2)}, u32[]{:S(2)}) collective-permute-start(bf16[48,2048]{1,0:T(8,128)(2,1)S(1)} %get-tuple-element.126.refs_7_), channel_id=1, source_target_pairs={{0,2},{5,7},{10,8},{15,13},{16,18},{21,23},{26,24},{31,29}} | collective-permute-start | bytes 589832 | tf_op jit(solution)/shard_map/ppermute | solution.py:658
  37.2 3.8 %collective-permute-start.16 = (bf16[48,2048]{1,0:T(8,128)(2,1)S(1)}, bf16[48,2048]{1,0:T(8,128)(2,1)S(1)}, u32[]{:S(2)}, u32[]{:S(2)}) collective-permute-start(bf16[48,2048]{1,0:T(8,128)(2,1)S(1)} %get-tuple-element.126.refs_7_), channel_id=1, source_target_pairs={{0,3},{5,4},{10,9},{15,14},{16,19},{21,20},{26,25},{31,30}} | collective-permute-start | bytes 589832 | tf_op jit(solution)/shard_map/ppermute | solution.py:658
  41.1 1.7 %add_adapters.1 = (f32[128,2560]{1,0:T(8,128)S(1)}, bf16[128,2560]{1,0:T(8,128)(2,1)S(1)}) custom-call(s32[1,512]{1,0:T(1,128)S(1)} %get-tuple-element.118.refs_0_.refs_1_, f32[32,512]{1,0:T(8,128)S(1)} %get-tuple-element.109.refs_1_.refs_2_, f32[32,512]{1,0:T(8,128)S(1)} %collective-permute-done.8.refs_2_.refs_3_, ...), custom_call_target="tpu_custom_call" | custom-call | flops 1000 | bytes 1000 | tf_op jit(solution)/shard_map/add_adapters/pallas_call | solution.py:42
  42.7 2.7 %project_1_0.1.refs_0_ = f32[128,2560]{1,0:T(8,128)S(1)} custom-call(s32[1,512]{1,0:T(1,128)S(1)} %get-tuple-element.118.refs_0_.refs_1_, f32[32,512]{1,0:T(8,128)S(1)} %get-tuple-element.109.refs_1_.refs_2_, f32[32,512]{1,0:T(8,128)S(1)} %collective-permute-done.8.refs_2_.refs_3_, f32[32,512]{1,0:T(8,128)S(1)} %collective-permute-done.9.refs_3_.refs_4_, ...), custom_call_target="tpu_custom_call" | custom-call | flops 1000 | bytes 1000 | tf_op jit(solution)/shard_map/project_1_0/pallas_call | solution.py:42
  45.5 3.0 %project_1_1.1 = (bf16[64,2560]{1,0:T(8,128)(2,1)S(1)}, bf16[64,2560]{1,0:T(8,128)(2,1)S(1)}) custom-call(s32[1]{0:T(128)} %bitcast.8.refs_0_, s32[1,512]{1,0:T(1,128)S(1)} %get-tuple-element.118.refs_0_.refs_1_, f32[32,512]{1,0:T(8,128)S(1)} %get-tuple-element.109.refs_1_.refs_2_, f32[32,512]{1,0:T(8,128)S(1)} %collective-permute-done.8.refs_2_.refs_3_, ...), custom_call_target="tpu_custom_call" | custom-call | flops 1000 | bytes 1000 | tf_op jit(solution)/shard_map/project_1_1/pallas_call | solution.py:42
  48.5 0.1 collective-permute-start.17
  48.6 0.5 collective-permute-start.11
  49.1 0.1 collective-permute-start.19
  49.2 1.0 collective-permute-done.17.refs_1_
  50.4 1.3 %collective-permute-done.19.refs_1_ = bf16[64,2560]{1,0:T(8,128)(2,1)S(1)} collective-permute-done((bf16[64,2560]{1,0:T(8,128)(2,1)S(1)}, bf16[64,2560]{1,0:T(8,128)(2,1)S(1)}, u32[]{:S(2)}, u32[]{:S(2)}) %collective-permute-start.19) | collective-permute-done | bytes 327712 | tf_op jit(solution)/shard_map/ppermute | solution.py:70
  51.7 0.8 collective-permute-start.20
  52.5 8.4 %collective-permute-done.18.refs_2_ = bf16[64,2560]{1,0:T(8,128)(2,1)S(1)} collective-permute-done((bf16[64,2560]{1,0:T(8,128)(2,1)S(1)}, bf16[64,2560]{1,0:T(8,128)(2,1)S(1)}, u32[]{:S(2)}, u32[]{:S(2)}) %collective-permute-start.18) | collective-permute-done | bytes 327712 | tf_op jit(solution)/shard_map/ppermute | solution.py:75
  60.9 5.1 %attend_0.1 = (bf16[64,2048]{1,0:T(8,128)(2,1)S(1)}, bf16[64,256]{1,0:T(8,128)(2,1)S(1)}, bf16[64,256]{1,0:T(8,128)(2,1)S(1)}, bf16[2048,2048]{1,0:T(8,128)(2,1)S(1)}) custom-call(f32[128,2560]{1,0:T(8,128)S(1)} %get-tuple-element.116.refs_0_.refs_2_, bf16[128,2560]{1,0:T(8,128)(2,1)S(1)} %collective-permute-done.11.refs_1_.refs_3_, ...), custom_call_target="tpu_custom_call" | custom-call | flops 1000 | bytes 1000 | tf_op jit(solution)/shard_map/attend_0/pallas_call | solution.py:42
  66.0 1.1 collective-permute-done.20.refs_4_
  67.1 0.3 collective-permute-start.22
  67.4 5.5 %attend_1.1 = (bf16[64,2048]{1,0:T(8,128)(2,1)S(1)}, bf16[128,256]{1,0:T(8,128)(2,1)}, bf16[128,256]{1,0:T(8,128)(2,1)}) custom-call(bf16[64,256]{1,0:T(8,128)(2,1)S(1)} %get-tuple-element.138.refs_0_, bf16[64,256]{1,0:T(8,128)(2,1)S(1)} %get-tuple-element.139.refs_1_, f32[128,2560]{1,0:T(8,128)S(1)} %get-tuple-element.116.refs_0_.refs_2_, ...), custom_call_target="tpu_custom_call" | custom-call | flops 1000 | bytes 1000 | tf_op jit(solution)/shard_map/attend_1/pallas_call | solution.py:42
  72.9 1.7 %collective-permute-done.22.refs_3_ = bf16[64,2048]{1,0:T(8,128)(2,1)S(1)} collective-permute-done((bf16[64,2048]{1,0:T(8,128)(2,1)S(1)}, bf16[64,2048]{1,0:T(8,128)(2,1)S(1)}, u32[]{:S(2)}, u32[]{:S(2)}) %collective-permute-start.22) | collective-permute-done | bytes 262176 | tf_op jit(solution)/shard_map/ppermute | solution.py:75
  74.7 0.6 collective-permute-start.26
  75.3 0.9 collective-permute-done.23.refs_4_
  76.2 3.5 %output_0_0_1.1 = (bf16[128,2048]{1,0:T(8,128)(2,1)S(1)}, bf16[128,2048]{1,0:T(8,128)(2,1)S(1)}) custom-call(s32[4]{0:T(128)S(1)} %pad_add_fusion.1.refs_0_, bf16[64,2048]{1,0:T(8,128)(2,1)S(1)} %get-tuple-element.142.refs_1_, bf16[64,2048]{1,0:T(8,128)(2,1)S(1)} %collective-permute-done.21.refs_2_, bf16[64,2048]{1,0:T(8,128)(2,1)S(1)} %collective-permute-done.22.refs_3_, ...), custom_call_target="tpu_custom_call" | custom-call | flops 1000 | bytes 1000 | tf_op jit(solution)/shard_map/output_0_0_1/pallas_call | solution.py:42
  79.7 0.7 collective-permute-start.24
  80.4 3.0 %collective-permute-done.26.refs_3_ = bf16[64,2048]{1,0:T(8,128)(2,1)S(1)} collective-permute-done((bf16[64,2048]{1,0:T(8,128)(2,1)S(1)}, bf16[64,2048]{1,0:T(8,128)(2,1)S(1)}, u32[]{:S(2)}, u32[]{:S(2)}) %collective-permute-start.26) | collective-permute-done | bytes 262176 | tf_op jit(solution)/shard_map/ppermute | solution.py:75
  83.4 0.5 collective-permute-start.25
  83.9 1.0 collective-permute-done.27.refs_4_
  84.9 0.4 collective-permute-done.25.refs_2_
  85.3 2.0 %output_1_0_2.1 = (bf16[128,1024]{1,0:T(8,128)(2,1)S(1)}, bf16[128,1024]{1,0:T(8,128)(2,1)S(1)}) custom-call(s32[4]{0:T(128)S(1)} %pad_add_fusion.1.refs_0_, bf16[64,2048]{1,0:T(8,128)(2,1)S(1)} %get-tuple-element.161.refs_1_, bf16[64,2048]{1,0:T(8,128)(2,1)S(1)} %collective-permute-done.25.refs_2_, bf16[64,2048]{1,0:T(8,128)(2,1)S(1)} %collective-permute-done.26.refs_3_, ...), custom_call_target="tpu_custom_call" | custom-call | flops 1000 | bytes 1000 | tf_op jit(solution)/shard_map/output_1_0_2/pallas_call | solution.py:42
  87.3 0.7 collective-permute-start.29
  88.0 6.5 %collective-permute-done.24.refs_1_ = bf16[128,2048]{1,0:T(8,128)(2,1)S(1)} collective-permute-done((bf16[128,2048]{1,0:T(8,128)(2,1)S(1)}, bf16[128,2048]{1,0:T(8,128)(2,1)S(1)}, u32[]{:S(2)}, u32[]{:S(2)}) %collective-permute-start.24) | collective-permute-done | bytes 524320 | tf_op jit(solution)/shard_map/ppermute | solution.py:83
  94.5 0.1 halves_0_0.1
  94.6 1.5 %collective-permute-start.28 = (bf16[64,2048]{1,0:T(8,128)(2,1)S(1)}, bf16[64,2048]{1,0:T(8,128)(2,1)S(1)}, u32[]{:S(2)}, u32[]{:S(2)}) collective-permute-start(bf16[64,2048]{1,0:T(8,128)(2,1)S(1)} %get-tuple-element.153), channel_id=1, source_target_pairs={{0,2},{1,3},{2,0},{3,1},{4,6},{5,7},{6,4},{7,5},{8,10},{9,11},{10,... | collective-permute-start | bytes 786440 | tf_op jit(solution)/shard_map/ppermute | solution.py:83
  96.1 1.3 %output_1_2_4.1 = (bf16[128,512]{1,0:T(8,128)(2,1)S(1)}, bf16[128,512]{1,0:T(8,128)(2,1)S(1)}) custom-call(s32[4]{0:T(128)S(1)} %pad_add_fusion.1.refs_0_, bf16[64,2048]{1,0:T(8,128)(2,1)S(1)} %get-tuple-element.161.refs_1_, bf16[64,2048]{1,0:T(8,128)(2,1)S(1)} %collective-permute-done.25.refs_2_, bf16[64,2048]{1,0:T(8,128)(2,1)S(1)} %collective-permute-done.26.refs_3_, ...), custom_call_target="tpu_custom_call" | custom-call | flops 1000 | bytes 1000 | tf_op jit(solution)/shard_map/output_1_2_4/pallas_call | solution.py:42
  97.4 2.1 %collective-permute-start.31 = (bf16[128,512]{1,0:T(8,128)(2,1)S(1)}, bf16[128,512]{1,0:T(8,128)(2,1)S(1)}, u32[]{:S(2)}, u32[]{:S(2)}) collective-permute-start(bf16[128,512]{1,0:T(8,128)(2,1)S(1)} %get-tuple-element.163), channel_id=1, source_target_pairs={{0,1},{1,0},{2,3},{3,2},{4,5},{5,4},{6,7},{7,6},{8,9},{9,8},{10,11... | collective-permute-start | bytes 393224 | tf_op jit(solution)/shard_map/ppermute | solution.py:83
  99.5 4.5 %collective-permute-done.29.refs_1_ = bf16[128,1024]{1,0:T(8,128)(2,1)S(1)} collective-permute-done((bf16[128,1024]{1,0:T(8,128)(2,1)S(1)}, bf16[128,1024]{1,0:T(8,128)(2,1)S(1)}, u32[]{:S(2)}, u32[]{:S(2)}) %collective-permute-start.29) | collective-permute-done | bytes 262176 | tf_op jit(solution)/shard_map/ppermute | solution.py:83
  104.2 1.3 %output_1_3_4.1 = (bf16[128,512]{1,0:T(8,128)(2,1)S(1)}, bf16[128,512]{1,0:T(8,128)(2,1)S(1)}) custom-call(s32[4]{0:T(128)S(1)} %pad_add_fusion.1.refs_0_, bf16[64,2048]{1,0:T(8,128)(2,1)S(1)} %get-tuple-element.161.refs_1_, bf16[64,2048]{1,0:T(8,128)(2,1)S(1)} %collective-permute-done.25.refs_2_, bf16[64,2048]{1,0:T(8,128)(2,1)S(1)} %collective-permute-done.26.refs_3_, ...), custom_call_target="tpu_custom_call" | custom-call | flops 1000 | bytes 1000 | tf_op jit(solution)/shard_map/output_1_3_4/pallas_call | solution.py:42
  105.5 1.9 %collective-permute-start.33 = (bf16[128,512]{1,0:T(8,128)(2,1)S(1)}, bf16[128,512]{1,0:T(8,128)(2,1)S(1)}, u32[]{:S(2)}, u32[]{:S(2)}) collective-permute-start(bf16[128,512]{1,0:T(8,128)(2,1)S(1)} %get-tuple-element.168), channel_id=1, source_target_pairs={{0,1},{1,0},{2,3},{3,2},{4,5},{5,4},{6,7},{7,6},{8,9},{9,8},{10,11... | collective-permute-start | bytes 393224 | tf_op jit(solution)/shard_map/ppermute | solution.py:83
  107.3 4.9 %collective-permute-done.28.refs_1_ = bf16[64,2048]{1,0:T(8,128)(2,1)S(1)} collective-permute-done((bf16[64,2048]{1,0:T(8,128)(2,1)S(1)}, bf16[64,2048]{1,0:T(8,128)(2,1)S(1)}, u32[]{:S(2)}, u32[]{:S(2)}) %collective-permute-start.28) | collective-permute-done | bytes 262176 | tf_op jit(solution)/shard_map/ppermute | solution.py:83
  112.4 2.0 %collective-permute-done.30.refs_1_ = bf16[64,1024]{1,0:T(8,128)(2,1)S(1)} collective-permute-done((bf16[64,1024]{1,0:T(8,128)(2,1)S(1)}, bf16[64,1024]{1,0:T(8,128)(2,1)S(1)}, u32[]{:S(2)}, u32[]{:S(2)}) %collective-permute-start.30) | collective-permute-done | bytes 131104 | tf_op jit(solution)/shard_map/ppermute | solution.py:83
  114.5 1.2 %collective-permute-start.34 = (bf16[64,512]{1,0:T(8,128)(2,1)S(1)}, bf16[64,512]{1,0:T(8,128)(2,1)S(1)}, u32[]{:S(2)}, u32[]{:S(2)}) collective-permute-start(bf16[64,512]{1,0:T(8,128)(2,1)S(1)} %get-tuple-element.170), channel_id=1, source_target_pairs={{0,2},{1,3},{2,0},{3,1},{4,6},{5,7},{6,4},{7,5},{8,10},{9,11},{10,... | collective-permute-start | bytes 196616 | tf_op jit(solution)/shard_map/ppermute | solution.py:83
  115.8 2.1 %collective-permute-done.32.refs_1_ = bf16[64,512]{1,0:T(8,128)(2,1)S(1)} collective-permute-done((bf16[64,512]{1,0:T(8,128)(2,1)S(1)}, bf16[64,512]{1,0:T(8,128)(2,1)S(1)}, u32[]{:S(2)}, u32[]{:S(2)}) %collective-permute-start.32) | collective-permute-done | bytes 65568 | tf_op jit(solution)/shard_map/ppermute | solution.py:83
  117.9 1.9 %collective-permute-done.34.refs_4_ = bf16[64,512]{1,0:T(8,128)(2,1)S(1)} collective-permute-done((bf16[64,512]{1,0:T(8,128)(2,1)S(1)}, bf16[64,512]{1,0:T(8,128)(2,1)S(1)}, u32[]{:S(2)}, u32[]{:S(2)}) %collective-permute-start.34) | collective-permute-done | bytes 65568 | tf_op jit(solution)/shard_map/ppermute | solution.py:83
  119.8 0.8 assemble.1
  (40 shorter events, 0.7 us)
Async XLA Ops:
  0.6 5.1 %collective-permute-start = (s32[1,128]{1,0:T(1,128)}, s32[1,128]{1,0:T(1,128)S(1)}, u32[]{:S(2)}, u32[]{:S(2)}) collective-permute-start(s32[1,128]{1,0:T(1,128)} %bitcast.18), channel_id=1, source_target_pairs={{0,4},{4,0},{8,12},{12,8},{1,5},{5,1},{9,13},{13,9},{2,6},{6,2},{1... | collective-permute-start | bytes 1544 | tf_op jit(solution)/shard_map/ppermute | solution.py:75
  1.1 4.6 %collective-permute-start.1 = (s32[1,128]{1,0:T(1,128)}, s32[1,128]{1,0:T(1,128)S(1)}, u32[]{:S(2)}, u32[]{:S(2)}) collective-permute-start(s32[1,128]{1,0:T(1,128)} %bitcast.19), channel_id=1, source_target_pairs={{0,8},{4,12},{8,0},{12,4},{1,9},{5,13},{9,1},{13,5},{2,10},{6,14},... | collective-permute-start | bytes 1544 | tf_op jit(solution)/shard_map/ppermute | solution.py:75
  3.7 3.1 %collective-permute-start.2 = (s32[1,128]{1,0:T(1,128)}, s32[1,128]{1,0:T(1,128)S(1)}, u32[]{:S(2)}, u32[]{:S(2)}) collective-permute-start(s32[1,128]{1,0:T(1,128)} %bitcast.20), channel_id=1, source_target_pairs={{0,12},{4,8},{8,4},{12,0},{1,13},{5,9},{9,5},{13,1},{2,14},{6,10},... | collective-permute-start | bytes 1544 | tf_op jit(solution)/shard_map/ppermute | solution.py:75
  6.8 14.0 %collective-permute-start.4 = (bf16[128,2048]{1,0:T(8,128)(2,1)S(1)}, bf16[128,2048]{1,0:T(8,128)(2,1)S(1)}, u32[]{:S(2)}, u32[]{:S(2)}) collective-permute-start(bf16[128,2048]{1,0:T(8,128)(2,1)S(1)} %slice_tp.1.refs_6_), channel_id=1, source_target_pairs={{0,8},{4,12},{8,0},{12,4},{1,9},{5,13},{9,1},{13,5},{2,10},{6,14},... | collective-permute-start | bytes 1572872 | tf_op jit(solution)/shard_map/ppermute | solution.py:75
  9.8 6.6 %collective-permute-start.5 = (bf16[64,2048]{1,0:T(8,128)(2,1)S(1)}, bf16[64,2048]{1,0:T(8,128)(2,1)S(1)}, u32[]{:S(2)}, u32[]{:S(2)}) collective-permute-start(bf16[64,2048]{1,0:T(8,128)(2,1)S(1)} %get-tuple-element.97), channel_id=1, source_target_pairs={{0,4},{4,0},{8,12},{12,8},{1,5},{5,1},{9,13},{13,9},{2,6},{6,2},{1... | collective-permute-start | bytes 786440 | tf_op jit(solution)/shard_map/ppermute | solution.py:70
  9.9 6.5 %collective-permute-start.6 = (bf16[64,2048]{1,0:T(8,128)(2,1)S(1)}, bf16[64,2048]{1,0:T(8,128)(2,1)S(1)}, u32[]{:S(2)}, u32[]{:S(2)}) collective-permute-start(bf16[64,2048]{1,0:T(8,128)(2,1)S(1)} %get-tuple-element.98), channel_id=1, source_target_pairs={{0,4},{4,0},{8,12},{12,8},{1,5},{5,1},{9,13},{13,9},{2,6},{6,2},{1... | collective-permute-start | bytes 786440 | tf_op jit(solution)/shard_map/ppermute | solution.py:70
  10.4 12.3 %collective-permute-start.3 = (bf16[128,2048]{1,0:T(8,128)(2,1)S(1)}, bf16[128,2048]{1,0:T(8,128)(2,1)S(1)}, u32[]{:S(2)}, u32[]{:S(2)}) collective-permute-start(bf16[128,2048]{1,0:T(8,128)(2,1)S(1)} %slice_tp.1.refs_6_), channel_id=1, source_target_pairs={{0,4},{4,0},{8,12},{12,8},{1,5},{5,1},{9,13},{13,9},{2,6},{6,2},{1... | collective-permute-start | bytes 1572872 | tf_op jit(solution)/shard_map/ppermute | solution.py:70
  16.4 6.3 %copy-start.1 = (s32[128]{0:T(128)S(1)}, s32[128]{0:T(128)}, u32[]{:S(2)}) copy-start(s32[128]{0:T(128)} %param.23) | copy-start | bytes 1540
  20.8 1.9 %collective-permute-start.7 = (bf16[128,2048]{1,0:T(8,128)(2,1)S(1)}, bf16[128,2048]{1,0:T(8,128)(2,1)S(1)}, u32[]{:S(2)}, u32[]{:S(2)}) collective-permute-start(bf16[128,2048]{1,0:T(8,128)(2,1)S(1)} %collective-permute-done.4.refs_8_), channel_id=1, source_target_pairs={{0,4},{4,0},{8,12},{12,8},{1,5},{5,1},{9,13},{13,9},{2,6},{6,2},{1... | collective-permute-start | bytes 1572872 | tf_op jit(solution)/shard_map/ppermute | solution.py:70
  20.8 21.9 %collective-permute-start.12 = (bf16[128,2048]{1,0:T(8,128)(2,1)S(1)}, bf16[128,2048]{1,0:T(8,128)(2,1)S(1)}, u32[]{:S(2)}, u32[]{:S(2)}) collective-permute-start(bf16[128,2048]{1,0:T(8,128)(2,1)S(1)} %get-tuple-element.120), channel_id=1, source_target_pairs={{0,8},{4,12},{8,0},{12,4},{1,9},{5,13},{9,1},{13,5},{2,10},{6,14},... | collective-permute-start | bytes 1572872 | tf_op jit(solution)/shard_map/ppermute | solution.py:75
  22.0 23.5 %collective-permute-start.13 = (bf16[80,2048]{1,0:T(8,128)(2,1)S(1)}, bf16[80,2048]{1,0:T(8,128)(2,1)S(1)}, u32[]{:S(2)}, u32[]{:S(2)}) collective-permute-start(bf16[80,2048]{1,0:T(8,128)(2,1)S(1)} %get-tuple-element.123), channel_id=1, source_target_pairs={{0,12},{4,8},{8,4},{12,0},{1,13},{5,9},{9,5},{13,1},{2,14},{6,10},... | collective-permute-start | bytes 983048 | tf_op jit(solution)/shard_map/ppermute | solution.py:75
  22.8 7.0 %copy-start = (bf16[128,8192]{1,0:T(8,128)(2,1)S(1)}, bf16[128,8192]{1,0:T(8,128)(2,1)}, u32[]{:S(2)}) copy-start(bf16[128,8192]{1,0:T(8,128)(2,1)} %refs_0_.1) | copy-start | bytes 6291460
  22.8 7.0 %copy-start.2 = (s32[128]{0:T(128)S(1)}, s32[128]{0:T(128)}, u32[]{:S(2)}) copy-start(s32[128]{0:T(128)} %param.22) | copy-start | bytes 1540
  25.1 6.1 %collective-permute-start.10 = (f32[32,512]{1,0:T(8,128)S(1)}, f32[32,512]{1,0:T(8,128)S(1)}, u32[]{:S(2)}, u32[]{:S(2)}) collective-permute-start(f32[32,512]{1,0:T(8,128)S(1)} %get-tuple-element.109.refs_1_.refs_2_), channel_id=1, source_target_pairs={{0,3},{1,0},{2,1},{3,2},{4,7},{5,4},{6,5},{7,6},{8,11},{9,8},{10,9... | collective-permute-start | bytes 196616 | tf_op jit(solution)/shard_map/ppermute | solution.py:648
  28.8 7.1 %collective-permute-start.8 = (f32[32,512]{1,0:T(8,128)S(1)}, f32[32,512]{1,0:T(8,128)S(1)}, u32[]{:S(2)}, u32[]{:S(2)}) collective-permute-start(f32[32,512]{1,0:T(8,128)S(1)} %get-tuple-element.109.refs_1_.refs_2_), channel_id=1, source_target_pairs={{0,1},{1,2},{2,3},{3,0},{4,5},{5,6},{6,7},{7,4},{8,9},{9,10},{10,1... | collective-permute-start | bytes 196616 | tf_op jit(solution)/shard_map/ppermute | solution.py:648
  28.8 8.4 %collective-permute-start.9 = (f32[32,512]{1,0:T(8,128)S(1)}, f32[32,512]{1,0:T(8,128)S(1)}, u32[]{:S(2)}, u32[]{:S(2)}) collective-permute-start(f32[32,512]{1,0:T(8,128)S(1)} %get-tuple-element.109.refs_1_.refs_2_), channel_id=1, source_target_pairs={{0,2},{1,3},{2,0},{3,1},{4,6},{5,7},{6,4},{7,5},{8,10},{9,11},{10,... | collective-permute-start | bytes 196616 | tf_op jit(solution)/shard_map/ppermute | solution.py:648
  31.2 14.3 %collective-permute-start.14 = (bf16[48,2048]{1,0:T(8,128)(2,1)S(1)}, bf16[48,2048]{1,0:T(8,128)(2,1)S(1)}, u32[]{:S(2)}, u32[]{:S(2)}) collective-permute-start(bf16[48,2048]{1,0:T(8,128)(2,1)S(1)} %get-tuple-element.126.refs_7_), channel_id=1, source_target_pairs={{0,1},{5,6},{10,11},{15,12},{16,17},{21,22},{26,27},{31,28}} | collective-permute-start | bytes 589832 | tf_op jit(solution)/shard_map/ppermute | solution.py:658
  35.9 9.6 %collective-permute-start.15 = (bf16[48,2048]{1,0:T(8,128)(2,1)S(1)}, bf16[48,2048]{1,0:T(8,128)(2,1)S(1)}, u32[]{:S(2)}, u32[]{:S(2)}) collective-permute-start(bf16[48,2048]{1,0:T(8,128)(2,1)S(1)} %get-tuple-element.126.refs_7_), channel_id=1, source_target_pairs={{0,2},{5,7},{10,8},{15,13},{16,18},{21,23},{26,24},{31,29}} | collective-permute-start | bytes 589832 | tf_op jit(solution)/shard_map/ppermute | solution.py:658
  37.2 8.3 %collective-permute-start.16 = (bf16[48,2048]{1,0:T(8,128)(2,1)S(1)}, bf16[48,2048]{1,0:T(8,128)(2,1)S(1)}, u32[]{:S(2)}, u32[]{:S(2)}) collective-permute-start(bf16[48,2048]{1,0:T(8,128)(2,1)S(1)} %get-tuple-element.126.refs_7_), channel_id=1, source_target_pairs={{0,3},{5,4},{10,9},{15,14},{16,19},{21,20},{26,25},{31,30}} | collective-permute-start | bytes 589832 | tf_op jit(solution)/shard_map/ppermute | solution.py:658
  48.5 1.7 %collective-permute-start.17 = (bf16[64,2560]{1,0:T(8,128)(2,1)S(1)}, bf16[64,2560]{1,0:T(8,128)(2,1)S(1)}, u32[]{:S(2)}, u32[]{:S(2)}) collective-permute-start(bf16[64,2560]{1,0:T(8,128)(2,1)S(1)} %get-tuple-element.127), channel_id=1, source_target_pairs={{0,4},{4,0},{8,12},{12,8},{1,5},{5,1},{9,13},{13,9},{2,6},{6,2},{1... | collective-permute-start | bytes 983048 | tf_op jit(solution)/shard_map/ppermute | solution.py:70
  48.6 12.3 %collective-permute-start.11 = (bf16[128,2560]{1,0:T(8,128)(2,1)S(1)}, bf16[128,2560]{1,0:T(8,128)(2,1)S(1)}, u32[]{:S(2)}, u32[]{:S(2)}) collective-permute-start(bf16[128,2560]{1,0:T(8,128)(2,1)S(1)} %get-tuple-element.117), channel_id=1, source_target_pairs={{0,4},{4,0},{8,12},{12,8},{1,5},{5,1},{9,13},{13,9},{2,6},{6,2},{1... | collective-permute-start | bytes 1966088 | tf_op jit(solution)/shard_map/ppermute | solution.py:70
  49.1 2.5 %collective-permute-start.19 = (bf16[64,2560]{1,0:T(8,128)(2,1)S(1)}, bf16[64,2560]{1,0:T(8,128)(2,1)S(1)}, u32[]{:S(2)}, u32[]{:S(2)}) collective-permute-start(bf16[64,2560]{1,0:T(8,128)(2,1)S(1)} %get-tuple-element.128), channel_id=1, source_target_pairs={{0,4},{4,0},{8,12},{12,8},{1,5},{5,1},{9,13},{13,9},{2,6},{6,2},{1... | collective-permute-start | bytes 983048 | tf_op jit(solution)/shard_map/ppermute | solution.py:70
  50.3 10.6 %collective-permute-start.18 = (bf16[64,2560]{1,0:T(8,128)(2,1)S(1)}, bf16[64,2560]{1,0:T(8,128)(2,1)S(1)}, u32[]{:S(2)}, u32[]{:S(2)}) collective-permute-start(bf16[64,2560]{1,0:T(8,128)(2,1)S(1)} %add_1_0.1), channel_id=1, source_target_pairs={{0,8},{4,12},{8,0},{12,4},{1,9},{5,13},{9,1},{13,5},{2,10},{6,14},... | collective-permute-start | bytes 983048 | tf_op jit(solution)/shard_map/ppermute | solution.py:75
  51.7 15.4 %collective-permute-start.20 = (bf16[64,2560]{1,0:T(8,128)(2,1)S(1)}, bf16[64,2560]{1,0:T(8,128)(2,1)S(1)}, u32[]{:S(2)}, u32[]{:S(2)}) collective-permute-start(bf16[64,2560]{1,0:T(8,128)(2,1)S(1)} %add_1_1.1), channel_id=1, source_target_pairs={{0,8},{4,12},{8,0},{12,4},{1,9},{5,13},{9,1},{13,5},{2,10},{6,14},... | collective-permute-start | bytes 983048 | tf_op jit(solution)/shard_map/ppermute | solution.py:75
  67.1 7.5 %collective-permute-start.22 = (bf16[64,2048]{1,0:T(8,128)(2,1)S(1)}, bf16[64,2048]{1,0:T(8,128)(2,1)S(1)}, u32[]{:S(2)}, u32[]{:S(2)}) collective-permute-start(bf16[64,2048]{1,0:T(8,128)(2,1)S(1)} %get-tuple-element.142.refs_1_), channel_id=1, source_target_pairs={{0,8},{4,12},{8,0},{12,4},{1,9},{5,13},{9,1},{13,5},{2,10},{6,14},... | collective-permute-start | bytes 786440 | tf_op jit(solution)/shard_map/ppermute | solution.py:75
  72.9 2.4 %collective-permute-start.21 = (bf16[64,2048]{1,0:T(8,128)(2,1)S(1)}, bf16[64,2048]{1,0:T(8,128)(2,1)S(1)}, u32[]{:S(2)}, u32[]{:S(2)}) collective-permute-start(bf16[64,2048]{1,0:T(8,128)(2,1)S(1)} %get-tuple-element.142.refs_1_), channel_id=1, source_target_pairs={{0,4},{4,0},{8,12},{12,8},{1,5},{5,1},{9,13},{13,9},{2,6},{6,2},{1... | collective-permute-start | bytes 786440 | tf_op jit(solution)/shard_map/ppermute | solution.py:70
  74.6 1.5 %collective-permute-start.23 = (bf16[64,2048]{1,0:T(8,128)(2,1)S(1)}, bf16[64,2048]{1,0:T(8,128)(2,1)S(1)}, u32[]{:S(2)}, u32[]{:S(2)}) collective-permute-start(bf16[64,2048]{1,0:T(8,128)(2,1)S(1)} %collective-permute-done.22.refs_3_), channel_id=1, source_target_pairs={{0,4},{4,0},{8,12},{12,8},{1,5},{5,1},{9,13},{13,9},{2,6},{6,2},{1... | collective-permute-start | bytes 786440 | tf_op jit(solution)/shard_map/ppermute | solution.py:70
  74.7 8.7 %collective-permute-start.26 = (bf16[64,2048]{1,0:T(8,128)(2,1)S(1)}, bf16[64,2048]{1,0:T(8,128)(2,1)S(1)}, u32[]{:S(2)}, u32[]{:S(2)}) collective-permute-start(bf16[64,2048]{1,0:T(8,128)(2,1)S(1)} %get-tuple-element.161.refs_1_), channel_id=1, source_target_pairs={{0,8},{4,12},{8,0},{12,4},{1,9},{5,13},{9,1},{13,5},{2,10},{6,14},... | collective-permute-start | bytes 786440 | tf_op jit(solution)/shard_map/ppermute | solution.py:75
  79.7 14.8 %collective-permute-start.24 = (bf16[128,2048]{1,0:T(8,128)(2,1)S(1)}, bf16[128,2048]{1,0:T(8,128)(2,1)S(1)}, u32[]{:S(2)}, u32[]{:S(2)}) collective-permute-start(bf16[128,2048]{1,0:T(8,128)(2,1)S(1)} %get-tuple-element.145), channel_id=1, source_target_pairs={{0,1},{1,0},{2,3},{3,2},{4,5},{5,4},{6,7},{7,6},{8,9},{9,8},{10,11... | collective-permute-start | bytes 1572872 | tf_op jit(solution)/shard_map/ppermute | solution.py:83
  83.4 1.5 %collective-permute-start.27 = (bf16[64,2048]{1,0:T(8,128)(2,1)S(1)}, bf16[64,2048]{1,0:T(8,128)(2,1)S(1)}, u32[]{:S(2)}, u32[]{:S(2)}) collective-permute-start(bf16[64,2048]{1,0:T(8,128)(2,1)S(1)} %collective-permute-done.26.refs_3_), channel_id=1, source_target_pairs={{0,4},{4,0},{8,12},{12,8},{1,5},{5,1},{9,13},{13,9},{2,6},{6,2},{1... | collective-permute-start | bytes 786440 | tf_op jit(solution)/shard_map/ppermute | solution.py:70
  83.4 1.9 %collective-permute-start.25 = (bf16[64,2048]{1,0:T(8,128)(2,1)S(1)}, bf16[64,2048]{1,0:T(8,128)(2,1)S(1)}, u32[]{:S(2)}, u32[]{:S(2)}) collective-permute-start(bf16[64,2048]{1,0:T(8,128)(2,1)S(1)} %get-tuple-element.161.refs_1_), channel_id=1, source_target_pairs={{0,4},{4,0},{8,12},{12,8},{1,5},{5,1},{9,13},{13,9},{2,6},{6,2},{1... | collective-permute-start | bytes 786440 | tf_op jit(solution)/shard_map/ppermute | solution.py:70
  87.3 16.7 %collective-permute-start.29 = (bf16[128,1024]{1,0:T(8,128)(2,1)S(1)}, bf16[128,1024]{1,0:T(8,128)(2,1)S(1)}, u32[]{:S(2)}, u32[]{:S(2)}) collective-permute-start(bf16[128,1024]{1,0:T(8,128)(2,1)S(1)} %get-tuple-element.156), channel_id=1, source_target_pairs={{0,1},{1,0},{2,3},{3,2},{4,5},{5,4},{6,7},{7,6},{8,9},{9,8},{10,11... | collective-permute-start | bytes 786440 | tf_op jit(solution)/shard_map/ppermute | solution.py:83
  94.6 17.6 %collective-permute-start.28 = (bf16[64,2048]{1,0:T(8,128)(2,1)S(1)}, bf16[64,2048]{1,0:T(8,128)(2,1)S(1)}, u32[]{:S(2)}, u32[]{:S(2)}) collective-permute-start(bf16[64,2048]{1,0:T(8,128)(2,1)S(1)} %get-tuple-element.153), channel_id=1, source_target_pairs={{0,2},{1,3},{2,0},{3,1},{4,6},{5,7},{6,4},{7,5},{8,10},{9,11},{10,... | collective-permute-start | bytes 786440 | tf_op jit(solution)/shard_map/ppermute | solution.py:83
  97.4 14.9 %collective-permute-start.31 = (bf16[128,512]{1,0:T(8,128)(2,1)S(1)}, bf16[128,512]{1,0:T(8,128)(2,1)S(1)}, u32[]{:S(2)}, u32[]{:S(2)}) collective-permute-start(bf16[128,512]{1,0:T(8,128)(2,1)S(1)} %get-tuple-element.163), channel_id=1, source_target_pairs={{0,1},{1,0},{2,3},{3,2},{4,5},{5,4},{6,7},{7,6},{8,9},{9,8},{10,11... | collective-permute-start | bytes 393224 | tf_op jit(solution)/shard_map/ppermute | solution.py:83
  104.1 10.4 %collective-permute-start.30 = (bf16[64,1024]{1,0:T(8,128)(2,1)S(1)}, bf16[64,1024]{1,0:T(8,128)(2,1)S(1)}, u32[]{:S(2)}, u32[]{:S(2)}) collective-permute-start(bf16[64,1024]{1,0:T(8,128)(2,1)S(1)} %get-tuple-element.158), channel_id=1, source_target_pairs={{0,2},{1,3},{2,0},{3,1},{4,6},{5,7},{6,4},{7,5},{8,10},{9,11},{10,... | collective-permute-start | bytes 393224 | tf_op jit(solution)/shard_map/ppermute | solution.py:83
  105.5 9.0 %collective-permute-start.33 = (bf16[128,512]{1,0:T(8,128)(2,1)S(1)}, bf16[128,512]{1,0:T(8,128)(2,1)S(1)}, u32[]{:S(2)}, u32[]{:S(2)}) collective-permute-start(bf16[128,512]{1,0:T(8,128)(2,1)S(1)} %get-tuple-element.168), channel_id=1, source_target_pairs={{0,1},{1,0},{2,3},{3,2},{4,5},{5,4},{6,7},{7,6},{8,9},{9,8},{10,11... | collective-permute-start | bytes 393224 | tf_op jit(solution)/shard_map/ppermute | solution.py:83
  112.3 5.5 %collective-permute-start.32 = (bf16[64,512]{1,0:T(8,128)(2,1)S(1)}, bf16[64,512]{1,0:T(8,128)(2,1)S(1)}, u32[]{:S(2)}, u32[]{:S(2)}) collective-permute-start(bf16[64,512]{1,0:T(8,128)(2,1)S(1)} %get-tuple-element.165), channel_id=1, source_target_pairs={{0,2},{1,3},{2,0},{3,1},{4,6},{5,7},{6,4},{7,5},{8,10},{9,11},{10,... | collective-permute-start | bytes 196616 | tf_op jit(solution)/shard_map/ppermute | solution.py:83
  114.5 5.2 %collective-permute-start.34 = (bf16[64,512]{1,0:T(8,128)(2,1)S(1)}, bf16[64,512]{1,0:T(8,128)(2,1)S(1)}, u32[]{:S(2)}, u32[]{:S(2)}) collective-permute-start(bf16[64,512]{1,0:T(8,128)(2,1)S(1)} %get-tuple-element.170), channel_id=1, source_target_pairs={{0,2},{1,3},{2,0},{3,1},{4,6},{5,7},{6,4},{7,5},{8,10},{9,11},{10,... | collective-permute-start | bytes 196616 | tf_op jit(solution)/shard_map/ppermute | solution.py:83

commit v10 on v9

--- a/solution.py
+++ b/solution.py
@@ -599,7 +599,7 @@
 
     cut = rows // 2
     chunks = [(0, cut), (cut, rows - cut)]
-    tail = rows * 3 // 8
+    tail = rows // 4
     starts = [pool_at * base, (pool_at // 2 * 2 + 1 - core) * base]
     wanted = [(0, 0, rows), (1, 0, rows // 2), (1, rows // 2, rows // 2)]
     places = [(d, e) for d in range(1, chips) for e in range(2)]
@@ -714,9 +714,7 @@
         )
         if c == 0:
             out_weights = earlier[2]
-        if c + 1 < len(chunks):
-            out, *moved[c + 1] = lax.optimization_barrier((out, *moved[c + 1]))
-        else:
+        if c:
             out = after(out, attended[-1][-1])
         attended.append([out] + [chip_move(out, pool_count, d) for d in range(1, chips)])
     new_key, new_value = earlier

time: 121 us -> 120 us (level)
  starting transfers between devices: 32 us -> 30.7 us
    ppermute x8, waiting for transfers between devices: 21.9 us -> 24.5 us  [tp_swap(): return lax.ppermute(x, 'tp', [(z, z ^ step) for z in range(tp_count)])]
    ppermute x8, starting transfers between devices: 8.25 us -> 6.47 us  [tp_swap(): return lax.ppermute(x, 'tp', [(z, z ^ step) for z in range(tp_count)])]
    ppermute x10, waiting for transfers between devices: 16.1 us -> 14.8 us  [chip_move(): lax.ppermute(x, 'pool', [(p, (p // 2 + d) % chips * 2 + (p % 2 ^ e)) for...]
  transfers between devices with their start and end apart: 35 -> 35, of which waited for: 18 -> 19; matrix products, arithmetic and copies ran while one was open for 1% -> 1% of each run, Pallas kernels for 33% -> 33%
where the time goes in v10:
time: 120 us
  waiting for transfers between devices  44.2 us (37%)
  Pallas kernels  43.3 us (36%)
  starting transfers between devices  30.7 us (26%)
    pallas_call x25, Pallas kernels, local_call(): pl.pallas_call(body, in_specs=[spec for _, spec in operands] + [HBM] * le...  43.3 us
    ppermute x8, waiting for transfers between devices, tp_swap(): return lax.ppermute(x, 'tp', [(z, z ^ step) for z in range(tp_count)])  24.5 us
    ppermute x10, waiting for transfers between devices, chip_move(): lax.ppermute(x, 'pool', [(p, (p // 2 + d) % chips * 2 + (p % 2 ^ e)) for...  14.8 us
    ppermute x3, starting transfers between devices, along_tp(): return lax.ppermute(x, ('pool', 'tp'), pairs)  9.78 us
    ppermute x10, starting transfers between devices, chip_move(): lax.ppermute(x, 'pool', [(p, (p // 2 + d) % chips * 2 + (p % 2 ^ e)) for...  7.63 us
    ppermute x8, starting transfers between devices, tp_swap(): return lax.ppermute(x, 'tp', [(z, z ^ step) for z in range(tp_count)])  6.47 us
    ppermute x3, starting transfers between devices, shards(): lax.ppermute(shrunk, 'tp', [(i, (i + d) % tp_count) for i in range(tp_cou...  4.67 us
    ppermute x11, waiting for transfers between devices, core_swap(): return lax.ppermute(x, 'pool', [(p, p ^ 1) for p in range(pool_count)])  4.2 us
  transfers between devices with their start and end apart: 35, of which 19 were waited for; matrix products, arithmetic and copies ran while one was open for 1% of the time, Pallas kernels for 33%

profile of v10, /device:TPU:0, one launch (start us, length us, event | category | flops | bytes accessed | tf_op | source)
XLA Modules:
  0.0 120.2 jit_solution(7934917635006055140)
XLA Ops:
  0.6 0.5 collective-permute-start
  1.1 2.6 %collective-permute-start.1 = (s32[1,128]{1,0:T(1,128)}, s32[1,128]{1,0:T(1,128)S(1)}, u32[]{:S(2)}, u32[]{:S(2)}) collective-permute-start(s32[1,128]{1,0:T(1,128)} %bitcast.19), channel_id=1, source_target_pairs={{0,8},{4,12},{8,0},{12,4},{1,9},{5,13},{9,1},{13,5},{2,10},{6,14},... | collective-permute-start | bytes 1544 | tf_op jit(solution)/shard_map/ppermute | solution.py:75
  3.8 0.7 reshape.40.refs_1_
  4.6 1.1 slice_tp.1.refs_6_
  5.7 1.1 collective-permute-done.2.refs_5_
  6.8 0.7 collective-permute-start.4
  7.5 0.1 pad_add_fusion.refs_0_
  7.6 2.2 %slice_pool.1 = (bf16[128,2048]{1,0:T(8,128)(2,1)S(1)}, bf16[64,2048]{1,0:T(8,128)(2,1)S(1)}, bf16[64,2048]{1,0:T(8,128)(2,1)S(1)}, bf16[128,2048]{1,0:T(8,128)(2,1)S(1)}, bf16[96,2048]{1,0:T(8,128)(2,1)S(1)}) custom-call(s32[4]{0:T(128)S(1)} %pad_add_fusion.refs_0_, bf16[1,8192]{1,0:T(2,128)(2,1)S(1)} %reshape.40.refs_1_, bf16[128,8192]{1,0:T(8,128)(2,1)} %refs_0_.1), custom_call_target="tpu_custom_call" | custom-call | flops 1000 | bytes 1000 | tf_op jit(solution)/shard_map/slice_pool/pallas_call | solution.py:42
  9.8 0.1 collective-permute-start.5
  9.9 0.4 collective-permute-start.6
  10.4 0.1 pad_add_fusion.1.refs_0_
  10.4 0.1 collective-permute-start.3
  10.5 5.9 %load.1 = (bf16[512,2048]{1,0:T(8,128)(2,1)S(1)}, bf16[512,2048]{1,0:T(8,128)(2,1)S(1)}, bf16[2048,2048]{1,0:T(8,128)(2,1)S(1)}, bf16[2048,256]{1,0:T(8,128)(2,1...) custom-call(bf16[512,2048]{1,0:T(8,128)(2,1)} %bitcast.23, ...), custom_call_target="tpu_custom_call" | custom-call | flops 1000 | bytes 1000 | tf_op jit(solution)/shard_map/load/pallas_call | solution.py:42
  16.5 3.7 %project_base.1 = (f32[128,2560]{1,0:T(8,128)S(1)}, f32[128,2560]{1,0:T(8,128)S(1)}, bf16[128,2,64,128]{3,2,1,0:T(8,128)(2,1)S(1)}, bf16[128,2,64,128]{3,2,1,0:T(8,128)(2,1)S(1)}) custom-call(bf16[128,2048]{1,0:T(8,128)(2,1)S(1)} %get-tuple-element.94.refs_0_, bf16[64,2048]{1,0:T(8,128)(2,1)S(1)} %collective-permute-done.5.refs_1_, ...), custom_call_target="tpu_custom_call" | custom-call | flops 1000 | bytes 1000 | tf_op jit(solution)/shard_map/project_base/pallas_call | solution.py:42
  20.1 0.7 collective-permute-done.4.refs_8_
  20.8 1.1 collective-permute-start.12
  22.0 0.7 collective-permute-start.13
  22.8 2.4 %shrink.1 = (s32[1,512]{1,0:T(1,128)S(1)}, f32[32,512]{1,0:T(8,128)S(1)}, bf16[32,2048]{1,0:T(8,128)(2,1)S(1)}) custom-call(s32[1]{0:T(128)} %bitcast.6.refs_0_, s32[1]{0:T(128)} %bitcast.7.refs_1_, s32[1,128]{1,0:T(1,128)S(1)} %bitcast.21, s32[1,128]{1,0:T(1,128)S(1)} %collective-permute-done.refs_3_, s32[1,128]{1,0:T(1,128)S(1)} %collective-permute-done.1.refs_4_, ...), custom_call_target="tpu_custom_call" | custom-call | flops 1000 | bytes 1000 | tf_op jit(solution)/shard_map/shrink/pallas_call | solution.py:42
  25.1 3.7 %collective-permute-start.10 = (f32[32,512]{1,0:T(8,128)S(1)}, f32[32,512]{1,0:T(8,128)S(1)}, u32[]{:S(2)}, u32[]{:S(2)}) collective-permute-start(f32[32,512]{1,0:T(8,128)S(1)} %get-tuple-element.107.refs_1_.refs_2_), channel_id=1, source_target_pairs={{0,3},{1,0},{2,1},{3,2},{4,7},{5,4},{6,5},{7,6},{8,11},{9,8},{10,9... | collective-permute-start | bytes 196616 | tf_op jit(solution)/shard_map/ppermute | solution.py:648
  28.8 1.0 collective-permute-start.9
  29.8 0.8 tables.1
  30.6 0.6 collective-permute-done.10.refs_4_.refs_5_
  31.2 4.6 %collective-permute-start.14 = (bf16[32,2048]{1,0:T(8,128)(2,1)S(1)}, bf16[32,2048]{1,0:T(8,128)(2,1)S(1)}, u32[]{:S(2)}, u32[]{:S(2)}) collective-permute-start(bf16[32,2048]{1,0:T(8,128)(2,1)S(1)} %get-tuple-element.124.refs_7_), channel_id=1, source_target_pairs={{0,1},{5,6},{10,11},{15,12},{16,17},{21,22},{26,27},{31,28}} | collective-permute-start | bytes 393224 | tf_op jit(solution)/shard_map/ppermute | solution.py:658
  35.9 1.3 %collective-permute-start.15 = (bf16[32,2048]{1,0:T(8,128)(2,1)S(1)}, bf16[32,2048]{1,0:T(8,128)(2,1)S(1)}, u32[]{:S(2)}, u32[]{:S(2)}) collective-permute-start(bf16[32,2048]{1,0:T(8,128)(2,1)S(1)} %get-tuple-element.124.refs_7_), channel_id=1, source_target_pairs={{0,2},{5,7},{10,8},{15,13},{16,18},{21,23},{26,24},{31,29}} | collective-permute-start | bytes 393224 | tf_op jit(solution)/shard_map/ppermute | solution.py:658
  37.2 3.8 %collective-permute-start.16 = (bf16[32,2048]{1,0:T(8,128)(2,1)S(1)}, bf16[32,2048]{1,0:T(8,128)(2,1)S(1)}, u32[]{:S(2)}, u32[]{:S(2)}) collective-permute-start(bf16[32,2048]{1,0:T(8,128)(2,1)S(1)} %get-tuple-element.124.refs_7_), channel_id=1, source_target_pairs={{0,3},{5,4},{10,9},{15,14},{16,19},{21,20},{26,25},{31,30}} | collective-permute-start | bytes 393224 | tf_op jit(solution)/shard_map/ppermute | solution.py:658
  41.0 1.7 %add_adapters.1 = (f32[128,2560]{1,0:T(8,128)S(1)}, bf16[128,2560]{1,0:T(8,128)(2,1)S(1)}) custom-call(s32[1,512]{1,0:T(1,128)S(1)} %get-tuple-element.116.refs_0_.refs_1_, f32[32,512]{1,0:T(8,128)S(1)} %get-tuple-element.107.refs_1_.refs_2_, f32[32,512]{1,0:T(8,128)S(1)} %collective-permute-done.8.refs_2_.refs_3_, ...), custom_call_target="tpu_custom_call" | custom-call | flops 1000 | bytes 1000 | tf_op jit(solution)/shard_map/add_adapters/pallas_call | solution.py:42
  42.7 2.7 %project_1_0.1.refs_0_ = f32[128,2560]{1,0:T(8,128)S(1)} custom-call(s32[1,512]{1,0:T(1,128)S(1)} %get-tuple-element.116.refs_0_.refs_1_, f32[32,512]{1,0:T(8,128)S(1)} %get-tuple-element.107.refs_1_.refs_2_, f32[32,512]{1,0:T(8,128)S(1)} %collective-permute-done.8.refs_2_.refs_3_, f32[32,512]{1,0:T(8,128)S(1)} %collective-permute-done.9.refs_3_.refs_4_, ...), custom_call_target="tpu_custom_call" | custom-call | flops 1000 | bytes 1000 | tf_op jit(solution)/shard_map/project_1_0/pallas_call | solution.py:42
  45.5 3.0 %project_1_1.1 = (bf16[64,2560]{1,0:T(8,128)(2,1)S(1)}, bf16[64,2560]{1,0:T(8,128)(2,1)S(1)}) custom-call(s32[1]{0:T(128)} %bitcast.8.refs_0_, s32[1,512]{1,0:T(1,128)S(1)} %get-tuple-element.116.refs_0_.refs_1_, f32[32,512]{1,0:T(8,128)S(1)} %get-tuple-element.107.refs_1_.refs_2_, f32[32,512]{1,0:T(8,128)S(1)} %collective-permute-done.8.refs_2_.refs_3_, ...), custom_call_target="tpu_custom_call" | custom-call | flops 1000 | bytes 1000 | tf_op jit(solution)/shard_map/project_1_1/pallas_call | solution.py:42
  48.5 0.1 collective-permute-start.17
  48.6 0.5 collective-permute-start.11
  49.1 0.1 collective-permute-start.19
  49.2 1.0 collective-permute-done.17.refs_1_
  50.4 1.3 %collective-permute-done.19.refs_1_ = bf16[64,2560]{1,0:T(8,128)(2,1)S(1)} collective-permute-done((bf16[64,2560]{1,0:T(8,128)(2,1)S(1)}, bf16[64,2560]{1,0:T(8,128)(2,1)S(1)}, u32[]{:S(2)}, u32[]{:S(2)}) %collective-permute-start.19) | collective-permute-done | bytes 327712 | tf_op jit(solution)/shard_map/ppermute | solution.py:70
  51.7 0.8 collective-permute-start.20
  52.5 8.4 %collective-permute-done.18.refs_2_ = bf16[64,2560]{1,0:T(8,128)(2,1)S(1)} collective-permute-done((bf16[64,2560]{1,0:T(8,128)(2,1)S(1)}, bf16[64,2560]{1,0:T(8,128)(2,1)S(1)}, u32[]{:S(2)}, u32[]{:S(2)}) %collective-permute-start.18) | collective-permute-done | bytes 327712 | tf_op jit(solution)/shard_map/ppermute | solution.py:75
  60.9 5.1 %attend_0.1 = (bf16[64,2048]{1,0:T(8,128)(2,1)S(1)}, bf16[64,256]{1,0:T(8,128)(2,1)S(1)}, bf16[64,256]{1,0:T(8,128)(2,1)S(1)}, bf16[2048,2048]{1,0:T(8,128)(2,1)S(1)}) custom-call(f32[128,2560]{1,0:T(8,128)S(1)} %get-tuple-element.114.refs_0_.refs_2_, bf16[128,2560]{1,0:T(8,128)(2,1)S(1)} %collective-permute-done.11.refs_1_.refs_3_, ...), custom_call_target="tpu_custom_call" | custom-call | flops 1000 | bytes 1000 | tf_op jit(solution)/shard_map/attend_0/pallas_call | solution.py:42
  66.1 1.1 collective-permute-done.20.refs_4_
  67.1 5.5 %attend_1.1 = (bf16[64,2048]{1,0:T(8,128)(2,1)S(1)}, bf16[128,256]{1,0:T(8,128)(2,1)}, bf16[128,256]{1,0:T(8,128)(2,1)}) custom-call(bf16[64,256]{1,0:T(8,128)(2,1)S(1)} %get-tuple-element.135.refs_0_, bf16[64,256]{1,0:T(8,128)(2,1)S(1)} %get-tuple-element.136.refs_1_, f32[128,2560]{1,0:T(8,128)S(1)} %get-tuple-element.114.refs_0_.refs_2_, ...), custom_call_target="tpu_custom_call" | custom-call | flops 1000 | bytes 1000 | tf_op jit(solution)/shard_map/attend_1/pallas_call | solution.py:42
  72.6 0.1 collective-permute-done.22.refs_3_
  72.8 0.4 collective-permute-start.23
  73.1 1.0 collective-permute-start.26
  74.2 0.4 collective-permute-done.23.refs_4_
  74.5 3.5 %output_0_0_1.1 = (bf16[128,2048]{1,0:T(8,128)(2,1)S(1)}, bf16[128,2048]{1,0:T(8,128)(2,1)S(1)}) custom-call(s32[4]{0:T(128)S(1)} %pad_add_fusion.1.refs_0_, bf16[64,2048]{1,0:T(8,128)(2,1)S(1)} %get-tuple-element.138.refs_1_, bf16[64,2048]{1,0:T(8,128)(2,1)S(1)} %collective-permute-done.21.refs_2_, bf16[64,2048]{1,0:T(8,128)(2,1)S(1)} %collective-permute-done.22.refs_3_, ...), custom_call_target="tpu_custom_call" | custom-call | flops 1000 | bytes 1000 | tf_op jit(solution)/shard_map/output_0_0_1/pallas_call | solution.py:42
  78.0 0.1 collective-permute-start.24
  78.1 3.4 %collective-permute-done.26.refs_3_ = bf16[64,2048]{1,0:T(8,128)(2,1)S(1)} collective-permute-done((bf16[64,2048]{1,0:T(8,128)(2,1)S(1)}, bf16[64,2048]{1,0:T(8,128)(2,1)S(1)}, u32[]{:S(2)}, u32[]{:S(2)}) %collective-permute-start.26) | collective-permute-done | bytes 262176 | tf_op jit(solution)/shard_map/ppermute | solution.py:75
  81.5 0.5 collective-permute-start.25
  82.0 1.0 collective-permute-done.27.refs_4_
  83.0 0.4 collective-permute-done.25.refs_2_
  83.4 2.0 %output_1_0_2.1 = (bf16[128,1024]{1,0:T(8,128)(2,1)S(1)}, bf16[128,1024]{1,0:T(8,128)(2,1)S(1)}) custom-call(s32[4]{0:T(128)S(1)} %pad_add_fusion.1.refs_0_, bf16[64,2048]{1,0:T(8,128)(2,1)S(1)} %get-tuple-element.157.refs_1_, bf16[64,2048]{1,0:T(8,128)(2,1)S(1)} %collective-permute-done.25.refs_2_, bf16[64,2048]{1,0:T(8,128)(2,1)S(1)} %collective-permute-done.26.refs_3_, ...), custom_call_target="tpu_custom_call" | custom-call | flops 1000 | bytes 1000 | tf_op jit(solution)/shard_map/output_1_0_2/pallas_call | solution.py:42
  85.5 7.3 %collective-permute-done.24.refs_1_ = bf16[128,2048]{1,0:T(8,128)(2,1)S(1)} collective-permute-done((bf16[128,2048]{1,0:T(8,128)(2,1)S(1)}, bf16[128,2048]{1,0:T(8,128)(2,1)S(1)}, u32[]{:S(2)}, u32[]{:S(2)}) %collective-permute-start.24) | collective-permute-done | bytes 524320 | tf_op jit(solution)/shard_map/ppermute | solution.py:83
  92.8 0.1 halves_0_0.1
  93.0 0.8 collective-permute-start.28
  93.8 1.3 %output_1_2_4.1 = (bf16[128,512]{1,0:T(8,128)(2,1)S(1)}, bf16[128,512]{1,0:T(8,128)(2,1)S(1)}) custom-call(s32[4]{0:T(128)S(1)} %pad_add_fusion.1.refs_0_, bf16[64,2048]{1,0:T(8,128)(2,1)S(1)} %get-tuple-element.157.refs_1_, bf16[64,2048]{1,0:T(8,128)(2,1)S(1)} %collective-permute-done.25.refs_2_, bf16[64,2048]{1,0:T(8,128)(2,1)S(1)} %collective-permute-done.26.refs_3_, ...), custom_call_target="tpu_custom_call" | custom-call | flops 1000 | bytes 1000 | tf_op jit(solution)/shard_map/output_1_2_4/pallas_call | solution.py:42
  95.1 2.1 %collective-permute-start.31 = (bf16[128,512]{1,0:T(8,128)(2,1)S(1)}, bf16[128,512]{1,0:T(8,128)(2,1)S(1)}, u32[]{:S(2)}, u32[]{:S(2)}) collective-permute-start(bf16[128,512]{1,0:T(8,128)(2,1)S(1)} %get-tuple-element.159), channel_id=1, source_target_pairs={{0,1},{1,0},{2,3},{3,2},{4,5},{5,4},{6,7},{7,6},{8,9},{9,8},{10,11... | collective-permute-start | bytes 393224 | tf_op jit(solution)/shard_map/ppermute | solution.py:83
  97.2 4.5 %collective-permute-done.29.refs_1_ = bf16[128,1024]{1,0:T(8,128)(2,1)S(1)} collective-permute-done((bf16[128,1024]{1,0:T(8,128)(2,1)S(1)}, bf16[128,1024]{1,0:T(8,128)(2,1)S(1)}, u32[]{:S(2)}, u32[]{:S(2)}) %collective-permute-start.29) | collective-permute-done | bytes 262176 | tf_op jit(solution)/shard_map/ppermute | solution.py:83
  101.7 0.1 collective-permute-start.30
  101.8 1.3 %output_1_3_4.1 = (bf16[128,512]{1,0:T(8,128)(2,1)S(1)}, bf16[128,512]{1,0:T(8,128)(2,1)S(1)}) custom-call(s32[4]{0:T(128)S(1)} %pad_add_fusion.1.refs_0_, bf16[64,2048]{1,0:T(8,128)(2,1)S(1)} %get-tuple-element.157.refs_1_, bf16[64,2048]{1,0:T(8,128)(2,1)S(1)} %collective-permute-done.25.refs_2_, bf16[64,2048]{1,0:T(8,128)(2,1)S(1)} %collective-permute-done.26.refs_3_, ...), custom_call_target="tpu_custom_call" | custom-call | flops 1000 | bytes 1000 | tf_op jit(solution)/shard_map/output_1_3_4/pallas_call | solution.py:42
  103.1 2.2 %collective-permute-start.33 = (bf16[128,512]{1,0:T(8,128)(2,1)S(1)}, bf16[128,512]{1,0:T(8,128)(2,1)S(1)}, u32[]{:S(2)}, u32[]{:S(2)}) collective-permute-start(bf16[128,512]{1,0:T(8,128)(2,1)S(1)} %get-tuple-element.164), channel_id=1, source_target_pairs={{0,1},{1,0},{2,3},{3,2},{4,5},{5,4},{6,7},{7,6},{8,9},{9,8},{10,11... | collective-permute-start | bytes 393224 | tf_op jit(solution)/shard_map/ppermute | solution.py:83
  105.3 5.9 %collective-permute-done.28.refs_1_ = bf16[64,2048]{1,0:T(8,128)(2,1)S(1)} collective-permute-done((bf16[64,2048]{1,0:T(8,128)(2,1)S(1)}, bf16[64,2048]{1,0:T(8,128)(2,1)S(1)}, u32[]{:S(2)}, u32[]{:S(2)}) %collective-permute-start.28) | collective-permute-done | bytes 262176 | tf_op jit(solution)/shard_map/ppermute | solution.py:83
  111.4 1.9 %collective-permute-done.30.refs_1_ = bf16[64,1024]{1,0:T(8,128)(2,1)S(1)} collective-permute-done((bf16[64,1024]{1,0:T(8,128)(2,1)S(1)}, bf16[64,1024]{1,0:T(8,128)(2,1)S(1)}, u32[]{:S(2)}, u32[]{:S(2)}) %collective-permute-start.30) | collective-permute-done | bytes 131104 | tf_op jit(solution)/shard_map/ppermute | solution.py:83
  113.4 1.1 collective-permute-start.34
  114.5 2.4 %collective-permute-done.32.refs_1_ = bf16[64,512]{1,0:T(8,128)(2,1)S(1)} collective-permute-done((bf16[64,512]{1,0:T(8,128)(2,1)S(1)}, bf16[64,512]{1,0:T(8,128)(2,1)S(1)}, u32[]{:S(2)}, u32[]{:S(2)}) %collective-permute-start.32) | collective-permute-done | bytes 65568 | tf_op jit(solution)/shard_map/ppermute | solution.py:83
  116.9 2.5 %collective-permute-done.34.refs_4_ = bf16[64,512]{1,0:T(8,128)(2,1)S(1)} collective-permute-done((bf16[64,512]{1,0:T(8,128)(2,1)S(1)}, bf16[64,512]{1,0:T(8,128)(2,1)S(1)}, u32[]{:S(2)}, u32[]{:S(2)}) %collective-permute-start.34) | collective-permute-done | bytes 65568 | tf_op jit(solution)/shard_map/ppermute | solution.py:83
  119.4 0.8 assemble.1
  (40 shorter events, 0.9 us)
Async XLA Ops:
  0.6 5.1 %collective-permute-start = (s32[1,128]{1,0:T(1,128)}, s32[1,128]{1,0:T(1,128)S(1)}, u32[]{:S(2)}, u32[]{:S(2)}) collective-permute-start(s32[1,128]{1,0:T(1,128)} %bitcast.18), channel_id=1, source_target_pairs={{0,4},{4,0},{8,12},{12,8},{1,5},{5,1},{9,13},{13,9},{2,6},{6,2},{1... | collective-permute-start | bytes 1544 | tf_op jit(solution)/shard_map/ppermute | solution.py:75
  1.1 4.6 %collective-permute-start.1 = (s32[1,128]{1,0:T(1,128)}, s32[1,128]{1,0:T(1,128)S(1)}, u32[]{:S(2)}, u32[]{:S(2)}) collective-permute-start(s32[1,128]{1,0:T(1,128)} %bitcast.19), channel_id=1, source_target_pairs={{0,8},{4,12},{8,0},{12,4},{1,9},{5,13},{9,1},{13,5},{2,10},{6,14},... | collective-permute-start | bytes 1544 | tf_op jit(solution)/shard_map/ppermute | solution.py:75
  3.7 3.1 %collective-permute-start.2 = (s32[1,128]{1,0:T(1,128)}, s32[1,128]{1,0:T(1,128)S(1)}, u32[]{:S(2)}, u32[]{:S(2)}) collective-permute-start(s32[1,128]{1,0:T(1,128)} %bitcast.20), channel_id=1, source_target_pairs={{0,12},{4,8},{8,4},{12,0},{1,13},{5,9},{9,5},{13,1},{2,14},{6,10},... | collective-permute-start | bytes 1544 | tf_op jit(solution)/shard_map/ppermute | solution.py:75
  6.8 14.0 %collective-permute-start.4 = (bf16[128,2048]{1,0:T(8,128)(2,1)S(1)}, bf16[128,2048]{1,0:T(8,128)(2,1)S(1)}, u32[]{:S(2)}, u32[]{:S(2)}) collective-permute-start(bf16[128,2048]{1,0:T(8,128)(2,1)S(1)} %slice_tp.1.refs_6_), channel_id=1, source_target_pairs={{0,8},{4,12},{8,0},{12,4},{1,9},{5,13},{9,1},{13,5},{2,10},{6,14},... | collective-permute-start | bytes 1572872 | tf_op jit(solution)/shard_map/ppermute | solution.py:75
  9.8 6.6 %collective-permute-start.5 = (bf16[64,2048]{1,0:T(8,128)(2,1)S(1)}, bf16[64,2048]{1,0:T(8,128)(2,1)S(1)}, u32[]{:S(2)}, u32[]{:S(2)}) collective-permute-start(bf16[64,2048]{1,0:T(8,128)(2,1)S(1)} %get-tuple-element.95), channel_id=1, source_target_pairs={{0,4},{4,0},{8,12},{12,8},{1,5},{5,1},{9,13},{13,9},{2,6},{6,2},{1... | collective-permute-start | bytes 786440 | tf_op jit(solution)/shard_map/ppermute | solution.py:70
  9.9 6.5 %collective-permute-start.6 = (bf16[64,2048]{1,0:T(8,128)(2,1)S(1)}, bf16[64,2048]{1,0:T(8,128)(2,1)S(1)}, u32[]{:S(2)}, u32[]{:S(2)}) collective-permute-start(bf16[64,2048]{1,0:T(8,128)(2,1)S(1)} %get-tuple-element.96), channel_id=1, source_target_pairs={{0,4},{4,0},{8,12},{12,8},{1,5},{5,1},{9,13},{13,9},{2,6},{6,2},{1... | collective-permute-start | bytes 786440 | tf_op jit(solution)/shard_map/ppermute | solution.py:70
  10.4 12.3 %collective-permute-start.3 = (bf16[128,2048]{1,0:T(8,128)(2,1)S(1)}, bf16[128,2048]{1,0:T(8,128)(2,1)S(1)}, u32[]{:S(2)}, u32[]{:S(2)}) collective-permute-start(bf16[128,2048]{1,0:T(8,128)(2,1)S(1)} %slice_tp.1.refs_6_), channel_id=1, source_target_pairs={{0,4},{4,0},{8,12},{12,8},{1,5},{5,1},{9,13},{13,9},{2,6},{6,2},{1... | collective-permute-start | bytes 1572872 | tf_op jit(solution)/shard_map/ppermute | solution.py:70
  16.5 6.3 %copy-start.1 = (s32[128]{0:T(128)S(1)}, s32[128]{0:T(128)}, u32[]{:S(2)}) copy-start(s32[128]{0:T(128)} %param.23) | copy-start | bytes 1540
  20.8 1.9 %collective-permute-start.7 = (bf16[128,2048]{1,0:T(8,128)(2,1)S(1)}, bf16[128,2048]{1,0:T(8,128)(2,1)S(1)}, u32[]{:S(2)}, u32[]{:S(2)}) collective-permute-start(bf16[128,2048]{1,0:T(8,128)(2,1)S(1)} %collective-permute-done.4.refs_8_), channel_id=1, source_target_pairs={{0,4},{4,0},{8,12},{12,8},{1,5},{5,1},{9,13},{13,9},{2,6},{6,2},{1... | collective-permute-start | bytes 1572872 | tf_op jit(solution)/shard_map/ppermute | solution.py:70
  20.8 21.9 %collective-permute-start.12 = (bf16[128,2048]{1,0:T(8,128)(2,1)S(1)}, bf16[128,2048]{1,0:T(8,128)(2,1)S(1)}, u32[]{:S(2)}, u32[]{:S(2)}) collective-permute-start(bf16[128,2048]{1,0:T(8,128)(2,1)S(1)} %get-tuple-element.118), channel_id=1, source_target_pairs={{0,8},{4,12},{8,0},{12,4},{1,9},{5,13},{9,1},{13,5},{2,10},{6,14},... | collective-permute-start | bytes 1572872 | tf_op jit(solution)/shard_map/ppermute | solution.py:75
  22.0 23.5 %collective-permute-start.13 = (bf16[96,2048]{1,0:T(8,128)(2,1)S(1)}, bf16[96,2048]{1,0:T(8,128)(2,1)S(1)}, u32[]{:S(2)}, u32[]{:S(2)}) collective-permute-start(bf16[96,2048]{1,0:T(8,128)(2,1)S(1)} %get-tuple-element.121), channel_id=1, source_target_pairs={{0,12},{4,8},{8,4},{12,0},{1,13},{5,9},{9,5},{13,1},{2,14},{6,10},... | collective-permute-start | bytes 1179656 | tf_op jit(solution)/shard_map/ppermute | solution.py:75
  22.8 7.0 %copy-start = (bf16[128,8192]{1,0:T(8,128)(2,1)S(1)}, bf16[128,8192]{1,0:T(8,128)(2,1)}, u32[]{:S(2)}) copy-start(bf16[128,8192]{1,0:T(8,128)(2,1)} %refs_0_.1) | copy-start | bytes 6291460
  22.8 7.0 %copy-start.2 = (s32[128]{0:T(128)S(1)}, s32[128]{0:T(128)}, u32[]{:S(2)}) copy-start(s32[128]{0:T(128)} %param.22) | copy-start | bytes 1540
  25.1 6.1 %collective-permute-start.10 = (f32[32,512]{1,0:T(8,128)S(1)}, f32[32,512]{1,0:T(8,128)S(1)}, u32[]{:S(2)}, u32[]{:S(2)}) collective-permute-start(f32[32,512]{1,0:T(8,128)S(1)} %get-tuple-element.107.refs_1_.refs_2_), channel_id=1, source_target_pairs={{0,3},{1,0},{2,1},{3,2},{4,7},{5,4},{6,5},{7,6},{8,11},{9,8},{10,9... | collective-permute-start | bytes 196616 | tf_op jit(solution)/shard_map/ppermute | solution.py:648
  28.8 7.1 %collective-permute-start.8 = (f32[32,512]{1,0:T(8,128)S(1)}, f32[32,512]{1,0:T(8,128)S(1)}, u32[]{:S(2)}, u32[]{:S(2)}) collective-permute-start(f32[32,512]{1,0:T(8,128)S(1)} %get-tuple-element.107.refs_1_.refs_2_), channel_id=1, source_target_pairs={{0,1},{1,2},{2,3},{3,0},{4,5},{5,6},{6,7},{7,4},{8,9},{9,10},{10,1... | collective-permute-start | bytes 196616 | tf_op jit(solution)/shard_map/ppermute | solution.py:648
  28.8 8.4 %collective-permute-start.9 = (f32[32,512]{1,0:T(8,128)S(1)}, f32[32,512]{1,0:T(8,128)S(1)}, u32[]{:S(2)}, u32[]{:S(2)}) collective-permute-start(f32[32,512]{1,0:T(8,128)S(1)} %get-tuple-element.107.refs_1_.refs_2_), channel_id=1, source_target_pairs={{0,2},{1,3},{2,0},{3,1},{4,6},{5,7},{6,4},{7,5},{8,10},{9,11},{10,... | collective-permute-start | bytes 196616 | tf_op jit(solution)/shard_map/ppermute | solution.py:648
  31.2 14.3 %collective-permute-start.14 = (bf16[32,2048]{1,0:T(8,128)(2,1)S(1)}, bf16[32,2048]{1,0:T(8,128)(2,1)S(1)}, u32[]{:S(2)}, u32[]{:S(2)}) collective-permute-start(bf16[32,2048]{1,0:T(8,128)(2,1)S(1)} %get-tuple-element.124.refs_7_), channel_id=1, source_target_pairs={{0,1},{5,6},{10,11},{15,12},{16,17},{21,22},{26,27},{31,28}} | collective-permute-start | bytes 393224 | tf_op jit(solution)/shard_map/ppermute | solution.py:658
  35.9 9.6 %collective-permute-start.15 = (bf16[32,2048]{1,0:T(8,128)(2,1)S(1)}, bf16[32,2048]{1,0:T(8,128)(2,1)S(1)}, u32[]{:S(2)}, u32[]{:S(2)}) collective-permute-start(bf16[32,2048]{1,0:T(8,128)(2,1)S(1)} %get-tuple-element.124.refs_7_), channel_id=1, source_target_pairs={{0,2},{5,7},{10,8},{15,13},{16,18},{21,23},{26,24},{31,29}} | collective-permute-start | bytes 393224 | tf_op jit(solution)/shard_map/ppermute | solution.py:658
  37.2 8.3 %collective-permute-start.16 = (bf16[32,2048]{1,0:T(8,128)(2,1)S(1)}, bf16[32,2048]{1,0:T(8,128)(2,1)S(1)}, u32[]{:S(2)}, u32[]{:S(2)}) collective-permute-start(bf16[32,2048]{1,0:T(8,128)(2,1)S(1)} %get-tuple-element.124.refs_7_), channel_id=1, source_target_pairs={{0,3},{5,4},{10,9},{15,14},{16,19},{21,20},{26,25},{31,30}} | collective-permute-start | bytes 393224 | tf_op jit(solution)/shard_map/ppermute | solution.py:658
  48.5 1.7 %collective-permute-start.17 = (bf16[64,2560]{1,0:T(8,128)(2,1)S(1)}, bf16[64,2560]{1,0:T(8,128)(2,1)S(1)}, u32[]{:S(2)}, u32[]{:S(2)}) collective-permute-start(bf16[64,2560]{1,0:T(8,128)(2,1)S(1)} %get-tuple-element.125), channel_id=1, source_target_pairs={{0,4},{4,0},{8,12},{12,8},{1,5},{5,1},{9,13},{13,9},{2,6},{6,2},{1... | collective-permute-start | bytes 983048 | tf_op jit(solution)/shard_map/ppermute | solution.py:70
  48.6 12.3 %collective-permute-start.11 = (bf16[128,2560]{1,0:T(8,128)(2,1)S(1)}, bf16[128,2560]{1,0:T(8,128)(2,1)S(1)}, u32[]{:S(2)}, u32[]{:S(2)}) collective-permute-start(bf16[128,2560]{1,0:T(8,128)(2,1)S(1)} %get-tuple-element.115), channel_id=1, source_target_pairs={{0,4},{4,0},{8,12},{12,8},{1,5},{5,1},{9,13},{13,9},{2,6},{6,2},{1... | collective-permute-start | bytes 1966088 | tf_op jit(solution)/shard_map/ppermute | solution.py:70
  49.1 2.5 %collective-permute-start.19 = (bf16[64,2560]{1,0:T(8,128)(2,1)S(1)}, bf16[64,2560]{1,0:T(8,128)(2,1)S(1)}, u32[]{:S(2)}, u32[]{:S(2)}) collective-permute-start(bf16[64,2560]{1,0:T(8,128)(2,1)S(1)} %get-tuple-element.126), channel_id=1, source_target_pairs={{0,4},{4,0},{8,12},{12,8},{1,5},{5,1},{9,13},{13,9},{2,6},{6,2},{1... | collective-permute-start | bytes 983048 | tf_op jit(solution)/shard_map/ppermute | solution.py:70
  50.3 10.6 %collective-permute-start.18 = (bf16[64,2560]{1,0:T(8,128)(2,1)S(1)}, bf16[64,2560]{1,0:T(8,128)(2,1)S(1)}, u32[]{:S(2)}, u32[]{:S(2)}) collective-permute-start(bf16[64,2560]{1,0:T(8,128)(2,1)S(1)} %add_1_0.1), channel_id=1, source_target_pairs={{0,8},{4,12},{8,0},{12,4},{1,9},{5,13},{9,1},{13,5},{2,10},{6,14},... | collective-permute-start | bytes 983048 | tf_op jit(solution)/shard_map/ppermute | solution.py:75
  51.7 15.4 %collective-permute-start.20 = (bf16[64,2560]{1,0:T(8,128)(2,1)S(1)}, bf16[64,2560]{1,0:T(8,128)(2,1)S(1)}, u32[]{:S(2)}, u32[]{:S(2)}) collective-permute-start(bf16[64,2560]{1,0:T(8,128)(2,1)S(1)} %add_1_1.1), channel_id=1, source_target_pairs={{0,8},{4,12},{8,0},{12,4},{1,9},{5,13},{9,1},{13,5},{2,10},{6,14},... | collective-permute-start | bytes 983048 | tf_op jit(solution)/shard_map/ppermute | solution.py:75
  66.0 6.8 %collective-permute-start.22 = (bf16[64,2048]{1,0:T(8,128)(2,1)S(1)}, bf16[64,2048]{1,0:T(8,128)(2,1)S(1)}, u32[]{:S(2)}, u32[]{:S(2)}) collective-permute-start(bf16[64,2048]{1,0:T(8,128)(2,1)S(1)} %get-tuple-element.138.refs_1_), channel_id=1, source_target_pairs={{0,8},{4,12},{8,0},{12,4},{1,9},{5,13},{9,1},{13,5},{2,10},{6,14},... | collective-permute-start | bytes 786440 | tf_op jit(solution)/shard_map/ppermute | solution.py:75
  72.6 1.5 %collective-permute-start.21 = (bf16[64,2048]{1,0:T(8,128)(2,1)S(1)}, bf16[64,2048]{1,0:T(8,128)(2,1)S(1)}, u32[]{:S(2)}, u32[]{:S(2)}) collective-permute-start(bf16[64,2048]{1,0:T(8,128)(2,1)S(1)} %get-tuple-element.138.refs_1_), channel_id=1, source_target_pairs={{0,4},{4,0},{8,12},{12,8},{1,5},{5,1},{9,13},{13,9},{2,6},{6,2},{1... | collective-permute-start | bytes 786440 | tf_op jit(solution)/shard_map/ppermute | solution.py:70
  72.8 1.8 %collective-permute-start.23 = (bf16[64,2048]{1,0:T(8,128)(2,1)S(1)}, bf16[64,2048]{1,0:T(8,128)(2,1)S(1)}, u32[]{:S(2)}, u32[]{:S(2)}) collective-permute-start(bf16[64,2048]{1,0:T(8,128)(2,1)S(1)} %collective-permute-done.22.refs_3_), channel_id=1, source_target_pairs={{0,4},{4,0},{8,12},{12,8},{1,5},{5,1},{9,13},{13,9},{2,6},{6,2},{1... | collective-permute-start | bytes 786440 | tf_op jit(solution)/shard_map/ppermute | solution.py:70
  73.1 8.4 %collective-permute-start.26 = (bf16[64,2048]{1,0:T(8,128)(2,1)S(1)}, bf16[64,2048]{1,0:T(8,128)(2,1)S(1)}, u32[]{:S(2)}, u32[]{:S(2)}) collective-permute-start(bf16[64,2048]{1,0:T(8,128)(2,1)S(1)} %get-tuple-element.157.refs_1_), channel_id=1, source_target_pairs={{0,8},{4,12},{8,0},{12,4},{1,9},{5,13},{9,1},{13,5},{2,10},{6,14},... | collective-permute-start | bytes 786440 | tf_op jit(solution)/shard_map/ppermute | solution.py:75
  78.0 14.8 %collective-permute-start.24 = (bf16[128,2048]{1,0:T(8,128)(2,1)S(1)}, bf16[128,2048]{1,0:T(8,128)(2,1)S(1)}, u32[]{:S(2)}, u32[]{:S(2)}) collective-permute-start(bf16[128,2048]{1,0:T(8,128)(2,1)S(1)} %get-tuple-element.141), channel_id=1, source_target_pairs={{0,1},{1,0},{2,3},{3,2},{4,5},{5,4},{6,7},{7,6},{8,9},{9,8},{10,11... | collective-permute-start | bytes 1572872 | tf_op jit(solution)/shard_map/ppermute | solution.py:83
  81.5 1.5 %collective-permute-start.27 = (bf16[64,2048]{1,0:T(8,128)(2,1)S(1)}, bf16[64,2048]{1,0:T(8,128)(2,1)S(1)}, u32[]{:S(2)}, u32[]{:S(2)}) collective-permute-start(bf16[64,2048]{1,0:T(8,128)(2,1)S(1)} %collective-permute-done.26.refs_3_), channel_id=1, source_target_pairs={{0,4},{4,0},{8,12},{12,8},{1,5},{5,1},{9,13},{13,9},{2,6},{6,2},{1... | collective-permute-start | bytes 786440 | tf_op jit(solution)/shard_map/ppermute | solution.py:70
  81.5 1.9 %collective-permute-start.25 = (bf16[64,2048]{1,0:T(8,128)(2,1)S(1)}, bf16[64,2048]{1,0:T(8,128)(2,1)S(1)}, u32[]{:S(2)}, u32[]{:S(2)}) collective-permute-start(bf16[64,2048]{1,0:T(8,128)(2,1)S(1)} %get-tuple-element.157.refs_1_), channel_id=1, source_target_pairs={{0,4},{4,0},{8,12},{12,8},{1,5},{5,1},{9,13},{13,9},{2,6},{6,2},{1... | collective-permute-start | bytes 786440 | tf_op jit(solution)/shard_map/ppermute | solution.py:70
  85.4 16.2 %collective-permute-start.29 = (bf16[128,1024]{1,0:T(8,128)(2,1)S(1)}, bf16[128,1024]{1,0:T(8,128)(2,1)S(1)}, u32[]{:S(2)}, u32[]{:S(2)}) collective-permute-start(bf16[128,1024]{1,0:T(8,128)(2,1)S(1)} %get-tuple-element.152), channel_id=1, source_target_pairs={{0,1},{1,0},{2,3},{3,2},{4,5},{5,4},{6,7},{7,6},{8,9},{9,8},{10,11... | collective-permute-start | bytes 786440 | tf_op jit(solution)/shard_map/ppermute | solution.py:83
  93.0 18.3 %collective-permute-start.28 = (bf16[64,2048]{1,0:T(8,128)(2,1)S(1)}, bf16[64,2048]{1,0:T(8,128)(2,1)S(1)}, u32[]{:S(2)}, u32[]{:S(2)}) collective-permute-start(bf16[64,2048]{1,0:T(8,128)(2,1)S(1)} %get-tuple-element.149), channel_id=1, source_target_pairs={{0,2},{1,3},{2,0},{3,1},{4,6},{5,7},{6,4},{7,5},{8,10},{9,11},{10,... | collective-permute-start | bytes 786440 | tf_op jit(solution)/shard_map/ppermute | solution.py:83
  95.1 16.2 %collective-permute-start.31 = (bf16[128,512]{1,0:T(8,128)(2,1)S(1)}, bf16[128,512]{1,0:T(8,128)(2,1)S(1)}, u32[]{:S(2)}, u32[]{:S(2)}) collective-permute-start(bf16[128,512]{1,0:T(8,128)(2,1)S(1)} %get-tuple-element.159), channel_id=1, source_target_pairs={{0,1},{1,0},{2,3},{3,2},{4,5},{5,4},{6,7},{7,6},{8,9},{9,8},{10,11... | collective-permute-start | bytes 393224 | tf_op jit(solution)/shard_map/ppermute | solution.py:83
  101.7 11.6 %collective-permute-start.30 = (bf16[64,1024]{1,0:T(8,128)(2,1)S(1)}, bf16[64,1024]{1,0:T(8,128)(2,1)S(1)}, u32[]{:S(2)}, u32[]{:S(2)}) collective-permute-start(bf16[64,1024]{1,0:T(8,128)(2,1)S(1)} %get-tuple-element.154), channel_id=1, source_target_pairs={{0,2},{1,3},{2,0},{3,1},{4,6},{5,7},{6,4},{7,5},{8,10},{9,11},{10,... | collective-permute-start | bytes 393224 | tf_op jit(solution)/shard_map/ppermute | solution.py:83
  103.1 10.3 %collective-permute-start.33 = (bf16[128,512]{1,0:T(8,128)(2,1)S(1)}, bf16[128,512]{1,0:T(8,128)(2,1)S(1)}, u32[]{:S(2)}, u32[]{:S(2)}) collective-permute-start(bf16[128,512]{1,0:T(8,128)(2,1)S(1)} %get-tuple-element.164), channel_id=1, source_target_pairs={{0,1},{1,0},{2,3},{3,2},{4,5},{5,4},{6,7},{7,6},{8,9},{9,8},{10,11... | collective-permute-start | bytes 393224 | tf_op jit(solution)/shard_map/ppermute | solution.py:83
  111.3 5.5 %collective-permute-start.32 = (bf16[64,512]{1,0:T(8,128)(2,1)S(1)}, bf16[64,512]{1,0:T(8,128)(2,1)S(1)}, u32[]{:S(2)}, u32[]{:S(2)}) collective-permute-start(bf16[64,512]{1,0:T(8,128)(2,1)S(1)} %get-tuple-element.161), channel_id=1, source_target_pairs={{0,2},{1,3},{2,0},{3,1},{4,6},{5,7},{6,4},{7,5},{8,10},{9,11},{10,... | collective-permute-start | bytes 196616 | tf_op jit(solution)/shard_map/ppermute | solution.py:83
  113.4 5.9 %collective-permute-start.34 = (bf16[64,512]{1,0:T(8,128)(2,1)S(1)}, bf16[64,512]{1,0:T(8,128)(2,1)S(1)}, u32[]{:S(2)}, u32[]{:S(2)}) collective-permute-start(bf16[64,512]{1,0:T(8,128)(2,1)S(1)} %get-tuple-element.166), channel_id=1, source_target_pairs={{0,2},{1,3},{2,0},{3,1},{4,6},{5,7},{6,4},{7,5},{8,10},{9,11},{10,... | collective-permute-start | bytes 196616 | tf_op jit(solution)/shard_map/ppermute | solution.py:83

commit v11 on v10

--- a/solution.py
+++ b/solution.py
@@ -119,19 +119,16 @@
     )
 
 
-def shrink(first_id, at, ids, blocks, query_down, value_down, width, tail):
+def shrink(first_id, ids, blocks, query_down, value_down):
     slots, _ = query_down.shape
     rows = blocks[0].shape[0]
     adapters = slots // 16
     count = len(blocks)
 
     def kernel(ins, outs, _):
-        first_id, at, *ins = ins
+        first_id, *ins = ins
         ids, blocks, tables = ins[:count], ins[count : 2 * count], ins[2 * count :]
-        local_ids, out, *tails = outs
-        for b, tail_out in enumerate(tails):
-            columns = pl.ds(pl.multiple_of(at[0], 128), width)
-            tail_out[...] = blocks[2 * b + 3][rows - tail :, columns]
+        local_ids, out = outs
         for b in range(count):
             local_ids[:, b * rows : (b + 1) * rows] = ids[b][...] - first_id[0]
         for first in range(0, count, 2):
@@ -150,11 +147,10 @@
     return local_call(
         kernel,
         "shrink",
-        [(first_id, SMEM), (at, SMEM), *in_vmem([*ids, *blocks, query_down, value_down])],
+        [(first_id, SMEM), *in_vmem([*ids, *blocks, query_down, value_down])],
         [
             shaped((1, rows * count), jnp.int32),
             shaped((32, rows * count)),
-            *[shaped((tail, width), jnp.bfloat16)] * (count // 2 - 1),
         ],
     )
 
@@ -218,7 +214,7 @@
     return pl.ds(pl.multiple_of(start, width), width)
 
 
-def project(name, kinds, span, ids, lows, blocks, weights, which=None, options=()):
+def project(name, kinds, span, ids, lows, blocks, weights):
     wq, wk, wv, uq, uv = weights
     depth = blocks[0].shape[1]
     wide, kv, slots = wq.shape[1], wk.shape[1], uq.shape[0]
@@ -226,23 +222,14 @@
     start, total = span
 
     def kernel(ins, outs, scratch):
-        if options:
-            which, *ins = ins
         ids, *ins = ins
         wq, wk, wv, uq, uv = ins[-5:]
-        low_refs, ins = ins[: len(lows)], ins[len(lows) : -5]
-        blocks, choices = ins[: len(ins) - len(options)], ins[len(ins) - len(options) :]
+        low_refs, blocks = ins[: len(lows)], ins[len(lows) : -5]
         xs, spread_q, spread_v = scratch
         at = 0
         for block in blocks:
             xs[at : at + block.shape[0], :] = block[...]
             at += block.shape[0]
-        for j, choice in enumerate(choices):
-
-            @pl.when(which[0] == j)
-            def _():
-                xs[at:, :] = choice[...]
-
         low = low_refs[0][:, start : start + total]
         for other in low_refs[1:]:
             low = low + other[:, start : start + total]
@@ -272,8 +259,7 @@
     return local_call(
         kernel,
         name,
-        [(which, SMEM)] * bool(options)
-        + in_vmem([ids, *lows, *blocks, *options, *weights]),
+        in_vmem([ids, *lows, *blocks, *weights]),
         [shaped((count, wide + 2 * kv), dtype) for _, count, dtype in kinds],
         [pltpu.VMEM((total, depth), jnp.bfloat16), spread, spread],
     )
@@ -359,17 +345,20 @@
     )
 
 
-def add_sums(name, window, keep, other):
+def add_sums(name, window, keep, others):
     first, part = window
 
     def kernel(ins, outs, _):
-        keep, other = ins
-        outs[0][...] = (
-            keep[first : first + part, :] + other[...].astype(jnp.float32)
-        ).astype(jnp.bfloat16)
-
-    return local_call(
-        kernel, name, in_vmem([keep, other]), [shaped((part, keep.shape[1]), jnp.bfloat16)]
+        keep, *others = ins
+        at = 0
+        for other in others:
+            n = other.shape[0]
+            total = keep[first + at : first + at + n, :] + other[...].astype(jnp.float32)
+            outs[0][at : at + n, :] = total.astype(jnp.bfloat16)
+            at += n
+
+    return local_call(
+        kernel, name, in_vmem([keep, *others]), [shaped((part, keep.shape[1]), jnp.bfloat16)]
     )[0]
 
 
@@ -599,20 +588,20 @@
 
     cut = rows // 2
     chunks = [(0, cut), (cut, rows - cut)]
-    tail = rows // 4
     starts = [pool_at * base, (pool_at // 2 * 2 + 1 - core) * base]
     wanted = [(0, 0, rows), (1, 0, rows // 2), (1, rows // 2, rows // 2)]
-    places = [(d, e) for d in range(1, chips) for e in range(2)]
-    for i, (d, e) in enumerate(places):
-        starts.append(((chip + d) % chips * 2 + (core + e) % 2) * base)
-        wanted.append((2 + i, 0, rows - tail if e else rows))
+    places = []
+    for d in range(1, chips):
+        for e in range(2):
+            for c, (at, part) in enumerate(chunks if e else [(0, rows)]):
+                places.append((d, e, c))
+                wanted.append((len(starts), at, part))
+            starts.append(((chip + d) % chips * 2 + (core + e) % 2) * base)
     own, *slices = scaled_slices(
         "slice_pool", jnp.stack(starts).astype(jnp.int32), tokens, gain_1, base, wanted
     )
     partner, away = slices[:2], dict(zip(places, slices[2:]))
     first_id = (pool_at * adapters).reshape(1).astype(jnp.int32)
-    at_piece = (pool_at * base % piece).reshape(1).astype(jnp.int32)
-    which = ((tp_at - pool_at * base // piece) % tp_count).reshape(1).astype(jnp.int32)
     lengths = cache_length_per_row.reshape(1, rows)
     share = pool_count // tp_count
     order = []
@@ -626,9 +615,9 @@
 
     flat_down = [x.reshape(adapters * rank, piece) for x in (query_down_maps, value_down_maps)]
     flat_up = [x.reshape(adapters * rank, x.shape[2]) for x in (query_up_maps, value_up_maps)]
-    small = [own, first_id, at_piece, which, lengths, order]
+    small = [own, first_id, lengths, order]
     query_matrix, *small = lax.optimization_barrier((query_matrix, *small))
-    own, first_id, at_piece, which, lengths, order = small
+    own, first_id, lengths, order = small
     down_q, down_v, *weights = load(
         [*flat_down, query_matrix, key_matrix, value_matrix, *flat_up]
     )
@@ -636,65 +625,61 @@
     own_keep, own_send, keys, values = project_base(
         [own, *partner], weights[:3], [rotated_key_cache, cached_value_rows]
     )
-    remote = [[] for _ in range(chips)]
-    for (d, e), x in away.items():
-        remote[d].append(chip_move(after(x, *same_core[1:]), pool_count, d, e))
+    remote = {}
+    for (d, e, c), x in away.items():
+        remote[d, e, c] = chip_move(after(x, *same_core[1:]), pool_count, d, e)
     same_core[1:] = [after(x, own_keep) for x in same_core[1:]]
     adapter_rows = [b for x in same_core for b in (x, core_swap(x, pool_count))]
-    local_ids, shrunk, *tails = shrink(
-        first_id, at_piece, ids, adapter_rows, down_q, down_v, base, tail
-    )
+    local_ids, shrunk = shrink(first_id, ids, adapter_rows, down_q, down_v)
     lows = [shrunk] + [
         lax.ppermute(shrunk, "tp", [(i, (i + d) % tp_count) for i in range(tp_count)])
         for d in range(1, tp_count)
     ]
     rest = tables(tokens, after(lengths, shrunk), head)
 
-    def along_tp(x, k):
-        pairs = []
-        for p in range(pool_count):
-            z = p * base // piece
-            pairs.append((p * tp_count + z, p * tp_count + (z + k) % tp_count))
-        return lax.ppermute(x, ("pool", "tp"), pairs)
-
-    tails = [after(x, rest[0]) for x in tails]
-    tails = [[x] + [along_tp(x, k) for k in range(1, tp_count)] for x in tails]
     own_sums, own_send = add_adapters(
         own_keep, own_send, after(local_ids, rest[0]), lows, *weights[3:]
     )
     swapped = core_swap(own_send, pool_count)
     local_ids = after(local_ids, own_sums)
     moved = [[] for _ in chunks]
-    both = None
+    keeps, sends, last = {}, {}, own_sums
     for d in range(1, chips):
-        if both is not None:
-            remote[d][0] = after(remote[d][0], both)
         at = 2 * d * rows
-        (keep,) = project(
+        (keeps[d],) = project(
             f"project_{d}_0",
             [(0, rows, jnp.float32)],
             (at, rows),
             local_ids,
             lows,
-            remote[d][:1],
+            [after(remote[d, 0, 0], last)],
             weights,
         )
-        sends = project(
-            f"project_{d}_1",
-            [(first, part, jnp.bfloat16) for first, part in chunks],
-            (at + rows, rows),
-            local_ids,
-            lows,
-            [after(remote[d][1], keep)],
-            weights,
-            which,
-            tails[d - 1],
-        )
-        for c, window in enumerate(chunks):
-            swap = core_swap(sends[c], pool_count)
+        last = keeps[d]
+    for c, (first, part) in enumerate(chunks):
+        piece_rows = part // 2
+        kinds = [(i, piece_rows, jnp.bfloat16) for i in range(0, part, piece_rows)]
+        for d in range(1, chips):
+            sends[c, d] = project(
+                f"project_{d}_1_{c}",
+                kinds,
+                ((2 * d + 1) * rows + first, part),
+                local_ids,
+                lows,
+                [after(remote[d, 1, c], last)],
+                weights,
+            )
+            last = sends[c, d][0]
+    both = None
+    for c, window in enumerate(chunks):
+        for d in range(1, chips):
+            keep = keeps[d]
             if c:
-                swap = after(swap, both)
-            both = add_sums(f"add_{d}_{c}", window, keep, swap)
+                keep = after(keep, both)
+            else:
+                keep = after(keep, *[x for (_, _, c), x in remote.items() if c])
+            swaps = [core_swap(x, pool_count) for x in sends[c, d]]
+            both = add_sums(f"add_{d}_{c}", window, keep, swaps)
             moved[c].append(chip_move(both, pool_count, -d))
     moved[0][0] = after(moved[0][0], both)
 

time: 120 us -> 118 us (0.983)
  starting transfers between devices: 30.7 us -> 24.1 us
  Pallas kernels: 43.3 us -> 47 us
    ppermute x3 -> x0, starting transfers between devices: 9.78 us -> none  [along_tp(): return lax.ppermute(x, ('pool', 'tp'), pairs)]
    ppermute x3, waiting for transfers between devices: 0.65 us -> 6.28 us  [shards(): lax.ppermute(shrunk, 'tp', [(i, (i + d) % tp_count) for i in range(tp_cou...]
    ppermute x10 -> x11, waiting for transfers between devices: 14.8 us -> 9.46 us  [chip_move(): lax.ppermute(x, 'pool', [(p, (p // 2 + d) % chips * 2 + (p % 2 ^ e)) for...]
    pallas_call x25 -> x26, Pallas kernels: 43.3 us -> 47 us  [local_call(): pl.pallas_call(body, in_specs=[spec for _, spec in operands] + [HBM] * le...]
    ppermute x10 -> x11, starting transfers between devices: 7.63 us -> 10.5 us  [chip_move(): lax.ppermute(x, 'pool', [(p, (p // 2 + d) % chips * 2 + (p % 2 ^ e)) for...]
    ppermute x11 -> x13, starting transfers between devices: 2.19 us -> 3.01 us  [core_swap(): return lax.ppermute(x, 'pool', [(p, p ^ 1) for p in range(pool_count)])]
    ppermute x11 -> x13, waiting for transfers between devices: 4.2 us -> 3.97 us  [core_swap(): return lax.ppermute(x, 'pool', [(p, p ^ 1) for p in range(pool_count)])]
  transfers between devices with their start and end apart: 35 -> 35, of which waited for: 19 -> 25; matrix products, arithmetic and copies ran while one was open for 1% -> 1% of each run, Pallas kernels for 33% -> 39%
where the time goes in v11:
time: 118 us
  Pallas kernels  47 us (40%)
  waiting for transfers between devices  44.8 us (38%)
  starting transfers between devices  24.1 us (20%)
    pallas_call x26, Pallas kernels, local_call(): pl.pallas_call(body, in_specs=[spec for _, spec in operands] + [HBM] * le...  47 us
    ppermute x8, waiting for transfers between devices, tp_swap(): return lax.ppermute(x, 'tp', [(z, z ^ step) for z in range(tp_count)])  25.1 us
    ppermute x11, starting transfers between devices, chip_move(): lax.ppermute(x, 'pool', [(p, (p // 2 + d) % chips * 2 + (p % 2 ^ e)) for...  10.5 us
    ppermute x11, waiting for transfers between devices, chip_move(): lax.ppermute(x, 'pool', [(p, (p // 2 + d) % chips * 2 + (p % 2 ^ e)) for...  9.46 us
    ppermute x3, waiting for transfers between devices, shards(): lax.ppermute(shrunk, 'tp', [(i, (i + d) % tp_count) for i in range(tp_cou...  6.28 us
    ppermute x8, starting transfers between devices, tp_swap(): return lax.ppermute(x, 'tp', [(z, z ^ step) for z in range(tp_count)])  5.96 us
    ppermute x3, starting transfers between devices, shards(): lax.ppermute(shrunk, 'tp', [(i, (i + d) % tp_count) for i in range(tp_cou...  4.67 us
    ppermute x13, waiting for transfers between devices, core_swap(): return lax.ppermute(x, 'pool', [(p, p ^ 1) for p in range(pool_count)])  3.97 us
  transfers between devices with their start and end apart: 35, of which 25 were waited for; matrix products, arithmetic and copies ran while one was open for 1% of the time, Pallas kernels for 39%

profile of v11, /device:TPU:0, one launch (start us, length us, event | category | flops | bytes accessed | tf_op | source)
XLA Modules:
  0.0 117.7 jit_solution(4563855395912942469)
XLA Ops:
  0.6 0.5 collective-permute-start
  1.1 2.6 %collective-permute-start.1 = (s32[1,128]{1,0:T(1,128)}, s32[1,128]{1,0:T(1,128)S(1)}, u32[]{:S(2)}, u32[]{:S(2)}) collective-permute-start(s32[1,128]{1,0:T(1,128)} %bitcast.17), channel_id=1, source_target_pairs={{0,8},{4,12},{8,0},{12,4},{1,9},{5,13},{9,1},{13,5},{2,10},{6,14},... | collective-permute-start | bytes 1544 | tf_op jit(solution)/shard_map/ppermute | solution.py:75
  3.8 0.7 reshape.34.refs_1_
  4.6 1.1 slice_tp.1.refs_5_
  5.7 1.1 collective-permute-done.2.refs_4_
  6.8 0.7 collective-permute-start.4
  7.6 2.8 %slice_pool.1 = (bf16[128,2048]{1,0:T(8,128)(2,1)S(1)}, bf16[64,2048]{1,0:T(8,128)(2,1)}, bf16[64,2048]{1,0:T(8,128)(2,1)S(1)}, bf16[128,2048]{1,0:T(8,128)(2,1)...) custom-call(s32[4]{0:T(128)S(1)} %pad_add_fusion.refs_0_, bf16[1,8192]{1,0:T(2,128)(2,1)S(1)} %reshape.34.refs_1_, ...), custom_call_target="tpu_custom_call" | custom-call | flops 1000 | bytes 1000 | tf_op jit(solution)/shard_map/slice_pool/pallas_call | solution.py:42
  10.6 0.4 collective-permute-start.6
  11.2 5.9 %load.1 = (bf16[512,2048]{1,0:T(8,128)(2,1)S(1)}, bf16[512,2048]{1,0:T(8,128)(2,1)S(1)}, bf16[2048,2048]{1,0:T(8,128)(2,1)S(1)}, bf16[2048,256]{1,0:T(8,128)(2,1...) custom-call(bf16[512,2048]{1,0:T(8,128)(2,1)} %bitcast.21, ...), custom_call_target="tpu_custom_call" | custom-call | flops 1000 | bytes 1000 | tf_op jit(solution)/shard_map/load/pallas_call | solution.py:42
  17.1 3.6 %project_base.1 = (f32[128,2560]{1,0:T(8,128)S(1)}, f32[128,2560]{1,0:T(8,128)S(1)}, bf16[128,2,64,128]{3,2,1,0:T(8,128)(2,1)S(1)}, bf16[128,2,64,128]{3,2,1,0:T(8,128)(2,1)S(1)}) custom-call(bf16[128,2048]{1,0:T(8,128)(2,1)S(1)} %get-tuple-element.96.refs_0_, bf16[64,2048]{1,0:T(8,128)(2,1)S(1)} %collective-permute-done.5.refs_1_, ...), custom_call_target="tpu_custom_call" | custom-call | flops 1000 | bytes 1000 | tf_op jit(solution)/shard_map/project_base/pallas_call | solution.py:42
  20.8 0.4 collective-permute-start.7
  21.3 1.3 %collective-permute-start.12 = (bf16[128,2048]{1,0:T(8,128)(2,1)S(1)}, bf16[128,2048]{1,0:T(8,128)(2,1)S(1)}, u32[]{:S(2)}, u32[]{:S(2)}) collective-permute-start(bf16[128,2048]{1,0:T(8,128)(2,1)S(1)} %get-tuple-element.120), channel_id=1, source_target_pairs={{0,8},{4,12},{8,0},{12,4},{1,9},{5,13},{9,1},{13,5},{2,10},{6,14},... | collective-permute-start | bytes 1572872 | tf_op jit(solution)/shard_map/ppermute | solution.py:75
  22.8 2.4 %shrink.1 = (s32[1,512]{1,0:T(1,128)S(1)}, f32[32,512]{1,0:T(8,128)S(1)}) custom-call(s32[1]{0:T(128)} %bitcast.6.refs_0_, s32[1,128]{1,0:T(1,128)S(1)} %bitcast.19, s32[1,128]{1,0:T(1,128)S(1)} %collective-permute-done.refs_2_, s32[1,128]{1,0:T(1,128)S(1)} %collective-permute-done.1.refs_3_, s32[1,128]{1,0:T(1,128)S(1)} %collective-permute-done.2.refs_4_, ...), custom_call_target="tpu_custom_call" | custom-call | flops 1000 | bytes 1000 | tf_op jit(solution)/shard_map/shrink/pallas_call | solution.py:42
  25.2 3.7 %collective-permute-start.10 = (f32[32,512]{1,0:T(8,128)S(1)}, f32[32,512]{1,0:T(8,128)S(1)}, u32[]{:S(2)}, u32[]{:S(2)}) collective-permute-start(f32[32,512]{1,0:T(8,128)S(1)} %get-tuple-element.109.refs_1_), channel_id=1, source_target_pairs={{0,3},{1,0},{2,1},{3,2},{4,7},{5,4},{6,5},{7,6},{8,11},{9,8},{10,9... | collective-permute-start | bytes 196616 | tf_op jit(solution)/shard_map/ppermute | solution.py:635
  28.8 1.0 collective-permute-start.9
  29.9 0.8 tables.1
  30.6 0.7 collective-permute-done.10.refs_4_
  31.3 4.3 %collective-permute-done.8.refs_2_ = f32[32,512]{1,0:T(8,128)S(1)} collective-permute-done((f32[32,512]{1,0:T(8,128)S(1)}, f32[32,512]{1,0:T(8,128)S(1)}, u32[]{:S(2)}, u32[]{:S(2)}) %collective-permute-start.8) | collective-permute-done | bytes 65568 | tf_op jit(solution)/shard_map/ppermute | solution.py:635
  35.7 1.2 %collective-permute-done.9.refs_3_ = f32[32,512]{1,0:T(8,128)S(1)} collective-permute-done((f32[32,512]{1,0:T(8,128)S(1)}, f32[32,512]{1,0:T(8,128)S(1)}, u32[]{:S(2)}, u32[]{:S(2)}) %collective-permute-start.9) | collective-permute-done | bytes 65568 | tf_op jit(solution)/shard_map/ppermute | solution.py:635
  36.9 1.7 %add_adapters.1 = (f32[128,2560]{1,0:T(8,128)S(1)}, bf16[128,2560]{1,0:T(8,128)(2,1)S(1)}) custom-call(s32[1,512]{1,0:T(1,128)S(1)} %get-tuple-element.118.refs_0_, f32[32,512]{1,0:T(8,128)S(1)} %get-tuple-element.109.refs_1_, f32[32,512]{1,0:T(8,128)S(1)} %collective-permute-done.8.refs_2_, f32[32,512]{1,0:T(8,128)S(1)} %collective-permute-done.9.refs_3_, ...), custom_call_target="tpu_custom_call" | custom-call | flops 1000 | bytes 1000 | tf_op jit(solution)/shard_map/add_adapters/pallas_call | solution.py:42
  38.7 1.5 %collective-permute-start.13 = (bf16[64,2048]{1,0:T(8,128)(2,1)S(1)}, bf16[64,2048]{1,0:T(8,128)(2,1)S(1)}, u32[]{:S(2)}, u32[]{:S(2)}) collective-permute-start(bf16[64,2048]{1,0:T(8,128)(2,1)S(1)} %get-tuple-element.123), channel_id=1, source_target_pairs={{0,12},{4,8},{8,4},{12,0},{1,13},{5,9},{9,5},{13,1},{2,14},{6,10},... | collective-permute-start | bytes 786440 | tf_op jit(solution)/shard_map/ppermute | solution.py:75
  40.1 2.7 %project_1_0.1.refs_0_ = f32[128,2560]{1,0:T(8,128)S(1)} custom-call(s32[1,512]{1,0:T(1,128)S(1)} %get-tuple-element.118.refs_0_, f32[32,512]{1,0:T(8,128)S(1)} %get-tuple-element.109.refs_1_, f32[32,512]{1,0:T(8,128)S(1)} %collective-permute-done.8.refs_2_, f32[32,512]{1,0:T(8,128)S(1)} %collective-permute-done.9.refs_3_, ...), custom_call_target="tpu_custom_call" | custom-call | flops 1000 | bytes 1000 | tf_op jit(solution)/shard_map/project_1_0/pallas_call | solution.py:42
  42.9 3.0 %project_1_1_0.1 = (bf16[32,2560]{1,0:T(8,128)(2,1)S(1)}, bf16[32,2560]{1,0:T(8,128)(2,1)S(1)}) custom-call(s32[1,512]{1,0:T(1,128)S(1)} %get-tuple-element.118.refs_0_, f32[32,512]{1,0:T(8,128)S(1)} %get-tuple-element.109.refs_1_, f32[32,512]{1,0:T(8,128)S(1)} %collective-permute-done.8.refs_2_, f32[32,512]{1,0:T(8,128)S(1)} %collective-permute-done.9.refs_3_, ...), custom_call_target="tpu_custom_call" | custom-call | flops 1000 | bytes 1000 | tf_op jit(solution)/shard_map/project_1_1_0/pallas_call | solution.py:42
  46.0 0.4 collective-permute-start.16
  46.4 0.4 collective-permute-done.13.refs_5_
  46.8 0.5 collective-permute-done.15.refs_1_
  47.3 0.2 collective-permute-done.16.refs_2_
  47.6 0.8 collective-permute-start.17
  48.3 3.0 %project_1_1_1.1 = (bf16[32,2560]{1,0:T(8,128)(2,1)S(1)}, bf16[32,2560]{1,0:T(8,128)(2,1)S(1)}) custom-call(s32[1,512]{1,0:T(1,128)S(1)} %get-tuple-element.118.refs_0_, f32[32,512]{1,0:T(8,128)S(1)} %get-tuple-element.109.refs_1_, f32[32,512]{1,0:T(8,128)S(1)} %collective-permute-done.8.refs_2_, f32[32,512]{1,0:T(8,128)S(1)} %collective-permute-done.9.refs_3_, ...), custom_call_target="tpu_custom_call" | custom-call | flops 1000 | bytes 1000 | tf_op jit(solution)/shard_map/project_1_1_1/pallas_call | solution.py:42
  51.5 0.5 collective-permute-start.19
  52.0 0.9 collective-permute-done.18.refs_1_
  52.9 0.2 collective-permute-done.19.refs_2_
  53.1 1.4 %collective-permute-start.20 = (bf16[64,2560]{1,0:T(8,128)(2,1)S(1)}, bf16[64,2560]{1,0:T(8,128)(2,1)S(1)}, u32[]{:S(2)}, u32[]{:S(2)}) collective-permute-start(bf16[64,2560]{1,0:T(8,128)(2,1)S(1)} %add_1_1.1), channel_id=1, source_target_pairs={{0,8},{4,12},{8,0},{12,4},{1,9},{5,13},{9,1},{13,5},{2,10},{6,14},... | collective-permute-start | bytes 983048 | tf_op jit(solution)/shard_map/ppermute | solution.py:75
  54.5 3.6 %collective-permute-done.17.refs_2_ = bf16[64,2560]{1,0:T(8,128)(2,1)S(1)} collective-permute-done((bf16[64,2560]{1,0:T(8,128)(2,1)S(1)}, bf16[64,2560]{1,0:T(8,128)(2,1)S(1)}, u32[]{:S(2)}, u32[]{:S(2)}) %collective-permute-start.17) | collective-permute-done | bytes 327712 | tf_op jit(solution)/shard_map/ppermute | solution.py:75
  58.2 5.1 %attend_0.1 = (bf16[64,2048]{1,0:T(8,128)(2,1)S(1)}, bf16[64,256]{1,0:T(8,128)(2,1)S(1)}, bf16[64,256]{1,0:T(8,128)(2,1)S(1)}, bf16[2048,2048]{1,0:T(8,128)(2,1)S(1)}) custom-call(f32[128,2560]{1,0:T(8,128)S(1)} %get-tuple-element.116.refs_0_.refs_2_, bf16[128,2560]{1,0:T(8,128)(2,1)S(1)} %collective-permute-done.11.refs_1_.refs_3_, ...), custom_call_target="tpu_custom_call" | custom-call | flops 1000 | bytes 1000 | tf_op jit(solution)/shard_map/attend_0/pallas_call | solution.py:42
  63.3 0.8 collective-permute-start.22
  64.0 0.5 collective-permute-done.20.refs_4_
  64.6 5.5 %attend_1.1 = (bf16[64,2048]{1,0:T(8,128)(2,1)S(1)}, bf16[128,256]{1,0:T(8,128)(2,1)}, bf16[128,256]{1,0:T(8,128)(2,1)}) custom-call(bf16[64,256]{1,0:T(8,128)(2,1)S(1)} %get-tuple-element.141.refs_0_, bf16[64,256]{1,0:T(8,128)(2,1)S(1)} %get-tuple-element.142.refs_1_, f32[128,2560]{1,0:T(8,128)S(1)} %get-tuple-element.116.refs_0_.refs_2_, ...), custom_call_target="tpu_custom_call" | custom-call | flops 1000 | bytes 1000 | tf_op jit(solution)/shard_map/attend_1/pallas_call | solution.py:42
  70.1 0.3 collective-permute-done.22.refs_3_
  70.4 0.2 collective-permute-start.23
  70.6 0.8 collective-permute-start.26
  71.4 0.2 collective-permute-done.21.refs_2_
  71.6 0.4 collective-permute-done.23.refs_4_
  72.0 3.5 %output_0_0_1.1 = (bf16[128,2048]{1,0:T(8,128)(2,1)S(1)}, bf16[128,2048]{1,0:T(8,128)(2,1)S(1)}) custom-call(s32[4]{0:T(128)S(1)} %pad_add_fusion.1.refs_0_, bf16[64,2048]{1,0:T(8,128)(2,1)S(1)} %get-tuple-element.144.refs_1_, bf16[64,2048]{1,0:T(8,128)(2,1)S(1)} %collective-permute-done.21.refs_2_, bf16[64,2048]{1,0:T(8,128)(2,1)S(1)} %collective-permute-done.22.refs_3_, ...), custom_call_target="tpu_custom_call" | custom-call | flops 1000 | bytes 1000 | tf_op jit(solution)/shard_map/output_0_0_1/pallas_call | solution.py:42
  75.4 0.2 collective-permute-start.24
  75.7 3.4 %collective-permute-done.26.refs_3_ = bf16[64,2048]{1,0:T(8,128)(2,1)S(1)} collective-permute-done((bf16[64,2048]{1,0:T(8,128)(2,1)S(1)}, bf16[64,2048]{1,0:T(8,128)(2,1)S(1)}, u32[]{:S(2)}, u32[]{:S(2)}) %collective-permute-start.26) | collective-permute-done | bytes 262176 | tf_op jit(solution)/shard_map/ppermute | solution.py:75
  79.1 0.5 collective-permute-start.25
  79.6 1.0 collective-permute-done.27.refs_4_
  80.6 0.4 collective-permute-done.25.refs_2_
  81.0 2.0 %output_1_0_2.1 = (bf16[128,1024]{1,0:T(8,128)(2,1)S(1)}, bf16[128,1024]{1,0:T(8,128)(2,1)S(1)}) custom-call(s32[4]{0:T(128)S(1)} %pad_add_fusion.1.refs_0_, bf16[64,2048]{1,0:T(8,128)(2,1)S(1)} %get-tuple-element.163.refs_1_, bf16[64,2048]{1,0:T(8,128)(2,1)S(1)} %collective-permute-done.25.refs_2_, bf16[64,2048]{1,0:T(8,128)(2,1)S(1)} %collective-permute-done.26.refs_3_, ...), custom_call_target="tpu_custom_call" | custom-call | flops 1000 | bytes 1000 | tf_op jit(solution)/shard_map/output_1_0_2/pallas_call | solution.py:42
  83.0 0.2 collective-permute-start.29
  83.3 7.0 %collective-permute-done.24.refs_1_ = bf16[128,2048]{1,0:T(8,128)(2,1)S(1)} collective-permute-done((bf16[128,2048]{1,0:T(8,128)(2,1)S(1)}, bf16[128,2048]{1,0:T(8,128)(2,1)S(1)}, u32[]{:S(2)}, u32[]{:S(2)}) %collective-permute-start.24) | collective-permute-done | bytes 524320 | tf_op jit(solution)/shard_map/ppermute | solution.py:83
  90.4 1.4 %collective-permute-start.28 = (bf16[64,2048]{1,0:T(8,128)(2,1)S(1)}, bf16[64,2048]{1,0:T(8,128)(2,1)S(1)}, u32[]{:S(2)}, u32[]{:S(2)}) collective-permute-start(bf16[64,2048]{1,0:T(8,128)(2,1)S(1)} %get-tuple-element.155), channel_id=1, source_target_pairs={{0,2},{1,3},{2,0},{3,1},{4,6},{5,7},{6,4},{7,5},{8,10},{9,11},{10,... | collective-permute-start | bytes 786440 | tf_op jit(solution)/shard_map/ppermute | solution.py:83
  91.8 1.3 %output_1_2_4.1 = (bf16[128,512]{1,0:T(8,128)(2,1)S(1)}, bf16[128,512]{1,0:T(8,128)(2,1)S(1)}) custom-call(s32[4]{0:T(128)S(1)} %pad_add_fusion.1.refs_0_, bf16[64,2048]{1,0:T(8,128)(2,1)S(1)} %get-tuple-element.163.refs_1_, bf16[64,2048]{1,0:T(8,128)(2,1)S(1)} %collective-permute-done.25.refs_2_, bf16[64,2048]{1,0:T(8,128)(2,1)S(1)} %collective-permute-done.26.refs_3_, ...), custom_call_target="tpu_custom_call" | custom-call | flops 1000 | bytes 1000 | tf_op jit(solution)/shard_map/output_1_2_4/pallas_call | solution.py:42
  93.1 1.4 %collective-permute-start.31 = (bf16[128,512]{1,0:T(8,128)(2,1)S(1)}, bf16[128,512]{1,0:T(8,128)(2,1)S(1)}, u32[]{:S(2)}, u32[]{:S(2)}) collective-permute-start(bf16[128,512]{1,0:T(8,128)(2,1)S(1)} %get-tuple-element.165), channel_id=1, source_target_pairs={{0,1},{1,0},{2,3},{3,2},{4,5},{5,4},{6,7},{7,6},{8,9},{9,8},{10,11... | collective-permute-start | bytes 393224 | tf_op jit(solution)/shard_map/ppermute | solution.py:83
  94.5 4.9 %collective-permute-done.29.refs_1_ = bf16[128,1024]{1,0:T(8,128)(2,1)S(1)} collective-permute-done((bf16[128,1024]{1,0:T(8,128)(2,1)S(1)}, bf16[128,1024]{1,0:T(8,128)(2,1)S(1)}, u32[]{:S(2)}, u32[]{:S(2)}) %collective-permute-start.29) | collective-permute-done | bytes 262176 | tf_op jit(solution)/shard_map/ppermute | solution.py:83
  99.5 1.3 %output_1_3_4.1 = (bf16[128,512]{1,0:T(8,128)(2,1)S(1)}, bf16[128,512]{1,0:T(8,128)(2,1)S(1)}) custom-call(s32[4]{0:T(128)S(1)} %pad_add_fusion.1.refs_0_, bf16[64,2048]{1,0:T(8,128)(2,1)S(1)} %get-tuple-element.163.refs_1_, bf16[64,2048]{1,0:T(8,128)(2,1)S(1)} %collective-permute-done.25.refs_2_, bf16[64,2048]{1,0:T(8,128)(2,1)S(1)} %collective-permute-done.26.refs_3_, ...), custom_call_target="tpu_custom_call" | custom-call | flops 1000 | bytes 1000 | tf_op jit(solution)/shard_map/output_1_3_4/pallas_call | solution.py:42
  100.9 1.9 %collective-permute-start.33 = (bf16[128,512]{1,0:T(8,128)(2,1)S(1)}, bf16[128,512]{1,0:T(8,128)(2,1)S(1)}, u32[]{:S(2)}, u32[]{:S(2)}) collective-permute-start(bf16[128,512]{1,0:T(8,128)(2,1)S(1)} %get-tuple-element.170), channel_id=1, source_target_pairs={{0,1},{1,0},{2,3},{3,2},{4,5},{5,4},{6,7},{7,6},{8,9},{9,8},{10,11... | collective-permute-start | bytes 393224 | tf_op jit(solution)/shard_map/ppermute | solution.py:83
  102.7 5.6 %collective-permute-done.28.refs_1_ = bf16[64,2048]{1,0:T(8,128)(2,1)S(1)} collective-permute-done((bf16[64,2048]{1,0:T(8,128)(2,1)S(1)}, bf16[64,2048]{1,0:T(8,128)(2,1)S(1)}, u32[]{:S(2)}, u32[]{:S(2)}) %collective-permute-start.28) | collective-permute-done | bytes 262176 | tf_op jit(solution)/shard_map/ppermute | solution.py:83
  108.5 2.3 %collective-permute-done.30.refs_1_ = bf16[64,1024]{1,0:T(8,128)(2,1)S(1)} collective-permute-done((bf16[64,1024]{1,0:T(8,128)(2,1)S(1)}, bf16[64,1024]{1,0:T(8,128)(2,1)S(1)}, u32[]{:S(2)}, u32[]{:S(2)}) %collective-permute-start.30) | collective-permute-done | bytes 131104 | tf_op jit(solution)/shard_map/ppermute | solution.py:83
  110.9 0.7 collective-permute-start.34
  111.6 2.5 %collective-permute-done.32.refs_1_ = bf16[64,512]{1,0:T(8,128)(2,1)S(1)} collective-permute-done((bf16[64,512]{1,0:T(8,128)(2,1)S(1)}, bf16[64,512]{1,0:T(8,128)(2,1)S(1)}, u32[]{:S(2)}, u32[]{:S(2)}) %collective-permute-start.32) | collective-permute-done | bytes 65568 | tf_op jit(solution)/shard_map/ppermute | solution.py:83
  114.1 2.7 %collective-permute-done.34.refs_4_ = bf16[64,512]{1,0:T(8,128)(2,1)S(1)} collective-permute-done((bf16[64,512]{1,0:T(8,128)(2,1)S(1)}, bf16[64,512]{1,0:T(8,128)(2,1)S(1)}, u32[]{:S(2)}, u32[]{:S(2)}) %collective-permute-start.34) | collective-permute-done | bytes 65568 | tf_op jit(solution)/shard_map/ppermute | solution.py:83
  116.8 0.8 assemble.1
  (41 shorter events, 1.6 us)
Async XLA Ops:
  0.6 5.1 %collective-permute-start = (s32[1,128]{1,0:T(1,128)}, s32[1,128]{1,0:T(1,128)S(1)}, u32[]{:S(2)}, u32[]{:S(2)}) collective-permute-start(s32[1,128]{1,0:T(1,128)} %bitcast.16), channel_id=1, source_target_pairs={{0,4},{4,0},{8,12},{12,8},{1,5},{5,1},{9,13},{13,9},{2,6},{6,2},{1... | collective-permute-start | bytes 1544 | tf_op jit(solution)/shard_map/ppermute | solution.py:75
  1.1 4.6 %collective-permute-start.1 = (s32[1,128]{1,0:T(1,128)}, s32[1,128]{1,0:T(1,128)S(1)}, u32[]{:S(2)}, u32[]{:S(2)}) collective-permute-start(s32[1,128]{1,0:T(1,128)} %bitcast.17), channel_id=1, source_target_pairs={{0,8},{4,12},{8,0},{12,4},{1,9},{5,13},{9,1},{13,5},{2,10},{6,14},... | collective-permute-start | bytes 1544 | tf_op jit(solution)/shard_map/ppermute | solution.py:75
  3.7 3.1 %collective-permute-start.2 = (s32[1,128]{1,0:T(1,128)}, s32[1,128]{1,0:T(1,128)S(1)}, u32[]{:S(2)}, u32[]{:S(2)}) collective-permute-start(s32[1,128]{1,0:T(1,128)} %bitcast.18), channel_id=1, source_target_pairs={{0,12},{4,8},{8,4},{12,0},{1,13},{5,9},{9,5},{13,1},{2,14},{6,10},... | collective-permute-start | bytes 1544 | tf_op jit(solution)/shard_map/ppermute | solution.py:75
  6.8 14.0 %collective-permute-start.4 = (bf16[128,2048]{1,0:T(8,128)(2,1)S(1)}, bf16[128,2048]{1,0:T(8,128)(2,1)S(1)}, u32[]{:S(2)}, u32[]{:S(2)}) collective-permute-start(bf16[128,2048]{1,0:T(8,128)(2,1)S(1)} %slice_tp.1.refs_5_), channel_id=1, source_target_pairs={{0,8},{4,12},{8,0},{12,4},{1,9},{5,13},{9,1},{13,5},{2,10},{6,14},... | collective-permute-start | bytes 1572872 | tf_op jit(solution)/shard_map/ppermute | solution.py:75
  10.4 6.6 %collective-permute-start.5 = (bf16[64,2048]{1,0:T(8,128)(2,1)}, bf16[64,2048]{1,0:T(8,128)(2,1)S(1)}, u32[]{:S(2)}, u32[]{:S(2)}) collective-permute-start(bf16[64,2048]{1,0:T(8,128)(2,1)} %get-tuple-element.97), channel_id=1, source_target_pairs={{0,4},{4,0},{8,12},{12,8},{1,5},{5,1},{9,13},{13,9},{2,6},{6,2},{1... | collective-permute-start | bytes 786440 | tf_op jit(solution)/shard_map/ppermute | solution.py:70
  10.6 6.5 %collective-permute-start.6 = (bf16[64,2048]{1,0:T(8,128)(2,1)S(1)}, bf16[64,2048]{1,0:T(8,128)(2,1)S(1)}, u32[]{:S(2)}, u32[]{:S(2)}) collective-permute-start(bf16[64,2048]{1,0:T(8,128)(2,1)S(1)} %get-tuple-element.98), channel_id=1, source_target_pairs={{0,4},{4,0},{8,12},{12,8},{1,5},{5,1},{9,13},{13,9},{2,6},{6,2},{1... | collective-permute-start | bytes 786440 | tf_op jit(solution)/shard_map/ppermute | solution.py:70
  11.1 11.6 %collective-permute-start.3 = (bf16[128,2048]{1,0:T(8,128)(2,1)S(1)}, bf16[128,2048]{1,0:T(8,128)(2,1)S(1)}, u32[]{:S(2)}, u32[]{:S(2)}) collective-permute-start(bf16[128,2048]{1,0:T(8,128)(2,1)S(1)} %slice_tp.1.refs_5_), channel_id=1, source_target_pairs={{0,4},{4,0},{8,12},{12,8},{1,5},{5,1},{9,13},{13,9},{2,6},{6,2},{1... | collective-permute-start | bytes 1572872 | tf_op jit(solution)/shard_map/ppermute | solution.py:70
  17.1 5.7 %copy-start.1 = (s32[128]{0:T(128)S(1)}, s32[128]{0:T(128)}, u32[]{:S(2)}) copy-start(s32[128]{0:T(128)} %param.23) | copy-start | bytes 1540
  20.8 2.0 %collective-permute-start.7 = (bf16[128,2048]{1,0:T(8,128)(2,1)S(1)}, bf16[128,2048]{1,0:T(8,128)(2,1)S(1)}, u32[]{:S(2)}, u32[]{:S(2)}) collective-permute-start(bf16[128,2048]{1,0:T(8,128)(2,1)S(1)} %collective-permute-done.4.refs_7_), channel_id=1, source_target_pairs={{0,4},{4,0},{8,12},{12,8},{1,5},{5,1},{9,13},{13,9},{2,6},{6,2},{1... | collective-permute-start | bytes 1572872 | tf_op jit(solution)/shard_map/ppermute | solution.py:70
  21.3 18.9 %collective-permute-start.12 = (bf16[128,2048]{1,0:T(8,128)(2,1)S(1)}, bf16[128,2048]{1,0:T(8,128)(2,1)S(1)}, u32[]{:S(2)}, u32[]{:S(2)}) collective-permute-start(bf16[128,2048]{1,0:T(8,128)(2,1)S(1)} %get-tuple-element.120), channel_id=1, source_target_pairs={{0,8},{4,12},{8,0},{12,4},{1,9},{5,13},{9,1},{13,5},{2,10},{6,14},... | collective-permute-start | bytes 1572872 | tf_op jit(solution)/shard_map/ppermute | solution.py:75
  22.6 20.3 %collective-permute-start.14 = (bf16[64,2048]{1,0:T(8,128)(2,1)S(1)}, bf16[64,2048]{1,0:T(8,128)(2,1)S(1)}, u32[]{:S(2)}, u32[]{:S(2)}) collective-permute-start(bf16[64,2048]{1,0:T(8,128)(2,1)S(1)} %get-tuple-element.126), channel_id=1, source_target_pairs={{0,12},{4,8},{8,4},{12,0},{1,13},{5,9},{9,5},{13,1},{2,14},{6,10},... | collective-permute-start | bytes 786440 | tf_op jit(solution)/shard_map/ppermute | solution.py:75
  22.8 7.0 %copy-start = (bf16[128,8192]{1,0:T(8,128)(2,1)S(1)}, bf16[128,8192]{1,0:T(8,128)(2,1)}, u32[]{:S(2)}) copy-start(bf16[128,8192]{1,0:T(8,128)(2,1)} %refs_0_.1) | copy-start | bytes 6291460
  22.8 7.0 %copy-start.2 = (s32[128]{0:T(128)S(1)}, s32[128]{0:T(128)}, u32[]{:S(2)}) copy-start(s32[128]{0:T(128)} %param.22) | copy-start | bytes 1540
  25.2 6.1 %collective-permute-start.10 = (f32[32,512]{1,0:T(8,128)S(1)}, f32[32,512]{1,0:T(8,128)S(1)}, u32[]{:S(2)}, u32[]{:S(2)}) collective-permute-start(f32[32,512]{1,0:T(8,128)S(1)} %get-tuple-element.109.refs_1_), channel_id=1, source_target_pairs={{0,3},{1,0},{2,1},{3,2},{4,7},{5,4},{6,5},{7,6},{8,11},{9,8},{10,9... | collective-permute-start | bytes 196616 | tf_op jit(solution)/shard_map/ppermute | solution.py:635
  28.8 6.8 %collective-permute-start.8 = (f32[32,512]{1,0:T(8,128)S(1)}, f32[32,512]{1,0:T(8,128)S(1)}, u32[]{:S(2)}, u32[]{:S(2)}) collective-permute-start(f32[32,512]{1,0:T(8,128)S(1)} %get-tuple-element.109.refs_1_), channel_id=1, source_target_pairs={{0,1},{1,2},{2,3},{3,0},{4,5},{5,6},{6,7},{7,4},{8,9},{9,10},{10,1... | collective-permute-start | bytes 196616 | tf_op jit(solution)/shard_map/ppermute | solution.py:635
  28.8 8.1 %collective-permute-start.9 = (f32[32,512]{1,0:T(8,128)S(1)}, f32[32,512]{1,0:T(8,128)S(1)}, u32[]{:S(2)}, u32[]{:S(2)}) collective-permute-start(f32[32,512]{1,0:T(8,128)S(1)} %get-tuple-element.109.refs_1_), channel_id=1, source_target_pairs={{0,2},{1,3},{2,0},{3,1},{4,6},{5,7},{6,4},{7,5},{8,10},{9,11},{10,... | collective-permute-start | bytes 196616 | tf_op jit(solution)/shard_map/ppermute | solution.py:635
  38.6 19.6 %collective-permute-start.11 = (bf16[128,2560]{1,0:T(8,128)(2,1)S(1)}, bf16[128,2560]{1,0:T(8,128)(2,1)S(1)}, u32[]{:S(2)}, u32[]{:S(2)}) collective-permute-start(bf16[128,2560]{1,0:T(8,128)(2,1)S(1)} %get-tuple-element.117), channel_id=1, source_target_pairs={{0,4},{4,0},{8,12},{12,8},{1,5},{5,1},{9,13},{13,9},{2,6},{6,2},{1... | collective-permute-start | bytes 1966088 | tf_op jit(solution)/shard_map/ppermute | solution.py:70
  38.7 8.1 %collective-permute-start.13 = (bf16[64,2048]{1,0:T(8,128)(2,1)S(1)}, bf16[64,2048]{1,0:T(8,128)(2,1)S(1)}, u32[]{:S(2)}, u32[]{:S(2)}) collective-permute-start(bf16[64,2048]{1,0:T(8,128)(2,1)S(1)} %get-tuple-element.123), channel_id=1, source_target_pairs={{0,12},{4,8},{8,4},{12,0},{1,13},{5,9},{9,5},{13,1},{2,14},{6,10},... | collective-permute-start | bytes 786440 | tf_op jit(solution)/shard_map/ppermute | solution.py:75
  45.8 1.5 %collective-permute-start.15 = (bf16[32,2560]{1,0:T(8,128)(2,1)S(1)}, bf16[32,2560]{1,0:T(8,128)(2,1)S(1)}, u32[]{:S(2)}, u32[]{:S(2)}) collective-permute-start(bf16[32,2560]{1,0:T(8,128)(2,1)S(1)} %get-tuple-element.128), channel_id=1, source_target_pairs={{0,4},{4,0},{8,12},{12,8},{1,5},{5,1},{9,13},{13,9},{2,6},{6,2},{1... | collective-permute-start | bytes 491528 | tf_op jit(solution)/shard_map/ppermute | solution.py:70
  46.0 1.6 %collective-permute-start.16 = (bf16[32,2560]{1,0:T(8,128)(2,1)S(1)}, bf16[32,2560]{1,0:T(8,128)(2,1)S(1)}, u32[]{:S(2)}, u32[]{:S(2)}) collective-permute-start(bf16[32,2560]{1,0:T(8,128)(2,1)S(1)} %get-tuple-element.129), channel_id=1, source_target_pairs={{0,4},{4,0},{8,12},{12,8},{1,5},{5,1},{9,13},{13,9},{2,6},{6,2},{1... | collective-permute-start | bytes 491528 | tf_op jit(solution)/shard_map/ppermute | solution.py:70
  47.6 10.6 %collective-permute-start.17 = (bf16[64,2560]{1,0:T(8,128)(2,1)S(1)}, bf16[64,2560]{1,0:T(8,128)(2,1)S(1)}, u32[]{:S(2)}, u32[]{:S(2)}) collective-permute-start(bf16[64,2560]{1,0:T(8,128)(2,1)S(1)} %add_1_0.1), channel_id=1, source_target_pairs={{0,8},{4,12},{8,0},{12,4},{1,9},{5,13},{9,1},{13,5},{2,10},{6,14},... | collective-permute-start | bytes 983048 | tf_op jit(solution)/shard_map/ppermute | solution.py:75
  51.4 1.5 %collective-permute-start.18 = (bf16[32,2560]{1,0:T(8,128)(2,1)S(1)}, bf16[32,2560]{1,0:T(8,128)(2,1)S(1)}, u32[]{:S(2)}, u32[]{:S(2)}) collective-permute-start(bf16[32,2560]{1,0:T(8,128)(2,1)S(1)} %get-tuple-element.132), channel_id=1, source_target_pairs={{0,4},{4,0},{8,12},{12,8},{1,5},{5,1},{9,13},{13,9},{2,6},{6,2},{1... | collective-permute-start | bytes 491528 | tf_op jit(solution)/shard_map/ppermute | solution.py:70
  51.5 1.6 %collective-permute-start.19 = (bf16[32,2560]{1,0:T(8,128)(2,1)S(1)}, bf16[32,2560]{1,0:T(8,128)(2,1)S(1)}, u32[]{:S(2)}, u32[]{:S(2)}) collective-permute-start(bf16[32,2560]{1,0:T(8,128)(2,1)S(1)} %get-tuple-element.133), channel_id=1, source_target_pairs={{0,4},{4,0},{8,12},{12,8},{1,5},{5,1},{9,13},{13,9},{2,6},{6,2},{1... | collective-permute-start | bytes 491528 | tf_op jit(solution)/shard_map/ppermute | solution.py:70
  53.1 11.4 %collective-permute-start.20 = (bf16[64,2560]{1,0:T(8,128)(2,1)S(1)}, bf16[64,2560]{1,0:T(8,128)(2,1)S(1)}, u32[]{:S(2)}, u32[]{:S(2)}) collective-permute-start(bf16[64,2560]{1,0:T(8,128)(2,1)S(1)} %add_1_1.1), channel_id=1, source_target_pairs={{0,8},{4,12},{8,0},{12,4},{1,9},{5,13},{9,1},{13,5},{2,10},{6,14},... | collective-permute-start | bytes 983048 | tf_op jit(solution)/shard_map/ppermute | solution.py:75
  63.3 7.1 %collective-permute-start.22 = (bf16[64,2048]{1,0:T(8,128)(2,1)S(1)}, bf16[64,2048]{1,0:T(8,128)(2,1)S(1)}, u32[]{:S(2)}, u32[]{:S(2)}) collective-permute-start(bf16[64,2048]{1,0:T(8,128)(2,1)S(1)} %get-tuple-element.144.refs_1_), channel_id=1, source_target_pairs={{0,8},{4,12},{8,0},{12,4},{1,9},{5,13},{9,1},{13,5},{2,10},{6,14},... | collective-permute-start | bytes 786440 | tf_op jit(solution)/shard_map/ppermute | solution.py:75
  70.1 1.5 %collective-permute-start.21 = (bf16[64,2048]{1,0:T(8,128)(2,1)S(1)}, bf16[64,2048]{1,0:T(8,128)(2,1)S(1)}, u32[]{:S(2)}, u32[]{:S(2)}) collective-permute-start(bf16[64,2048]{1,0:T(8,128)(2,1)S(1)} %get-tuple-element.144.refs_1_), channel_id=1, source_target_pairs={{0,4},{4,0},{8,12},{12,8},{1,5},{5,1},{9,13},{13,9},{2,6},{6,2},{1... | collective-permute-start | bytes 786440 | tf_op jit(solution)/shard_map/ppermute | solution.py:70
  70.4 1.6 %collective-permute-start.23 = (bf16[64,2048]{1,0:T(8,128)(2,1)S(1)}, bf16[64,2048]{1,0:T(8,128)(2,1)S(1)}, u32[]{:S(2)}, u32[]{:S(2)}) collective-permute-start(bf16[64,2048]{1,0:T(8,128)(2,1)S(1)} %collective-permute-done.22.refs_3_), channel_id=1, source_target_pairs={{0,4},{4,0},{8,12},{12,8},{1,5},{5,1},{9,13},{13,9},{2,6},{6,2},{1... | collective-permute-start | bytes 786440 | tf_op jit(solution)/shard_map/ppermute | solution.py:70
  70.6 8.5 %collective-permute-start.26 = (bf16[64,2048]{1,0:T(8,128)(2,1)S(1)}, bf16[64,2048]{1,0:T(8,128)(2,1)S(1)}, u32[]{:S(2)}, u32[]{:S(2)}) collective-permute-start(bf16[64,2048]{1,0:T(8,128)(2,1)S(1)} %get-tuple-element.163.refs_1_), channel_id=1, source_target_pairs={{0,8},{4,12},{8,0},{12,4},{1,9},{5,13},{9,1},{13,5},{2,10},{6,14},... | collective-permute-start | bytes 786440 | tf_op jit(solution)/shard_map/ppermute | solution.py:75
  75.4 14.8 %collective-permute-start.24 = (bf16[128,2048]{1,0:T(8,128)(2,1)S(1)}, bf16[128,2048]{1,0:T(8,128)(2,1)S(1)}, u32[]{:S(2)}, u32[]{:S(2)}) collective-permute-start(bf16[128,2048]{1,0:T(8,128)(2,1)S(1)} %get-tuple-element.147), channel_id=1, source_target_pairs={{0,1},{1,0},{2,3},{3,2},{4,5},{5,4},{6,7},{7,6},{8,9},{9,8},{10,11... | collective-permute-start | bytes 1572872 | tf_op jit(solution)/shard_map/ppermute | solution.py:83
  79.1 1.5 %collective-permute-start.27 = (bf16[64,2048]{1,0:T(8,128)(2,1)S(1)}, bf16[64,2048]{1,0:T(8,128)(2,1)S(1)}, u32[]{:S(2)}, u32[]{:S(2)}) collective-permute-start(bf16[64,2048]{1,0:T(8,128)(2,1)S(1)} %collective-permute-done.26.refs_3_), channel_id=1, source_target_pairs={{0,4},{4,0},{8,12},{12,8},{1,5},{5,1},{9,13},{13,9},{2,6},{6,2},{1... | collective-permute-start | bytes 786440 | tf_op jit(solution)/shard_map/ppermute | solution.py:70
  79.1 1.9 %collective-permute-start.25 = (bf16[64,2048]{1,0:T(8,128)(2,1)S(1)}, bf16[64,2048]{1,0:T(8,128)(2,1)S(1)}, u32[]{:S(2)}, u32[]{:S(2)}) collective-permute-start(bf16[64,2048]{1,0:T(8,128)(2,1)S(1)} %get-tuple-element.163.refs_1_), channel_id=1, source_target_pairs={{0,4},{4,0},{8,12},{12,8},{1,5},{5,1},{9,13},{13,9},{2,6},{6,2},{1... | collective-permute-start | bytes 786440 | tf_op jit(solution)/shard_map/ppermute | solution.py:70
  83.0 16.4 %collective-permute-start.29 = (bf16[128,1024]{1,0:T(8,128)(2,1)S(1)}, bf16[128,1024]{1,0:T(8,128)(2,1)S(1)}, u32[]{:S(2)}, u32[]{:S(2)}) collective-permute-start(bf16[128,1024]{1,0:T(8,128)(2,1)S(1)} %get-tuple-element.158), channel_id=1, source_target_pairs={{0,1},{1,0},{2,3},{3,2},{4,5},{5,4},{6,7},{7,6},{8,9},{9,8},{10,11... | collective-permute-start | bytes 786440 | tf_op jit(solution)/shard_map/ppermute | solution.py:83
  90.4 17.9 %collective-permute-start.28 = (bf16[64,2048]{1,0:T(8,128)(2,1)S(1)}, bf16[64,2048]{1,0:T(8,128)(2,1)S(1)}, u32[]{:S(2)}, u32[]{:S(2)}) collective-permute-start(bf16[64,2048]{1,0:T(8,128)(2,1)S(1)} %get-tuple-element.155), channel_id=1, source_target_pairs={{0,2},{1,3},{2,0},{3,1},{4,6},{5,7},{6,4},{7,5},{8,10},{9,11},{10,... | collective-permute-start | bytes 786440 | tf_op jit(solution)/shard_map/ppermute | solution.py:83
  93.1 15.2 %collective-permute-start.31 = (bf16[128,512]{1,0:T(8,128)(2,1)S(1)}, bf16[128,512]{1,0:T(8,128)(2,1)S(1)}, u32[]{:S(2)}, u32[]{:S(2)}) collective-permute-start(bf16[128,512]{1,0:T(8,128)(2,1)S(1)} %get-tuple-element.165), channel_id=1, source_target_pairs={{0,1},{1,0},{2,3},{3,2},{4,5},{5,4},{6,7},{7,6},{8,9},{9,8},{10,11... | collective-permute-start | bytes 393224 | tf_op jit(solution)/shard_map/ppermute | solution.py:83
  99.5 11.3 %collective-permute-start.30 = (bf16[64,1024]{1,0:T(8,128)(2,1)S(1)}, bf16[64,1024]{1,0:T(8,128)(2,1)S(1)}, u32[]{:S(2)}, u32[]{:S(2)}) collective-permute-start(bf16[64,1024]{1,0:T(8,128)(2,1)S(1)} %get-tuple-element.160), channel_id=1, source_target_pairs={{0,2},{1,3},{2,0},{3,1},{4,6},{5,7},{6,4},{7,5},{8,10},{9,11},{10,... | collective-permute-start | bytes 393224 | tf_op jit(solution)/shard_map/ppermute | solution.py:83
  100.9 10.0 %collective-permute-start.33 = (bf16[128,512]{1,0:T(8,128)(2,1)S(1)}, bf16[128,512]{1,0:T(8,128)(2,1)S(1)}, u32[]{:S(2)}, u32[]{:S(2)}) collective-permute-start(bf16[128,512]{1,0:T(8,128)(2,1)S(1)} %get-tuple-element.170), channel_id=1, source_target_pairs={{0,1},{1,0},{2,3},{3,2},{4,5},{5,4},{6,7},{7,6},{8,9},{9,8},{10,11... | collective-permute-start | bytes 393224 | tf_op jit(solution)/shard_map/ppermute | solution.py:83
  108.4 5.7 %collective-permute-start.32 = (bf16[64,512]{1,0:T(8,128)(2,1)S(1)}, bf16[64,512]{1,0:T(8,128)(2,1)S(1)}, u32[]{:S(2)}, u32[]{:S(2)}) collective-permute-start(bf16[64,512]{1,0:T(8,128)(2,1)S(1)} %get-tuple-element.167), channel_id=1, source_target_pairs={{0,2},{1,3},{2,0},{3,1},{4,6},{5,7},{6,4},{7,5},{8,10},{9,11},{10,... | collective-permute-start | bytes 196616 | tf_op jit(solution)/shard_map/ppermute | solution.py:83
  110.9 5.9 %collective-permute-start.34 = (bf16[64,512]{1,0:T(8,128)(2,1)S(1)}, bf16[64,512]{1,0:T(8,128)(2,1)S(1)}, u32[]{:S(2)}, u32[]{:S(2)}) collective-permute-start(bf16[64,512]{1,0:T(8,128)(2,1)S(1)} %get-tuple-element.172), channel_id=1, source_target_pairs={{0,2},{1,3},{2,0},{3,1},{4,6},{5,7},{6,4},{7,5},{8,10},{9,11},{10,... | collective-permute-start | bytes 196616 | tf_op jit(solution)/shard_map/ppermute | solution.py:83

commit v12 on v11

--- a/solution.py
+++ b/solution.py
@@ -89,7 +89,7 @@
 
     def kernel(ins, outs, scratch):
         starts, gain, tokens = ins
-        held, sems = scratch
+        held, factors, sems = scratch
 
         def copy(i):
             columns = pl.ds(pl.multiple_of(starts[i], 128), width)
@@ -97,14 +97,17 @@
 
         for i in range(count):
             copy(i).start()
+        factors[...] = gain[...].astype(jnp.float32)
         for i in range(count):
             copy(i).wait()
-            columns = pl.ds(pl.multiple_of(starts[i], 128), width)
-            factor = gain[:, columns].astype(jnp.float32)
-            for out, (which, first, part) in zip(outs, wanted):
-                if which == i:
-                    values = held[i, first : first + part].astype(jnp.float32)
-                    out[...] = (values * factor).astype(jnp.bfloat16)
+            row = starts[i] // 128
+            for j in range(width // 128):
+                columns = slice(j * 128, (j + 1) * 128)
+                factor = factors[pl.ds(row + j, 1), :]
+                for out, (which, first, part) in zip(outs, wanted):
+                    if which == i:
+                        values = held[i, first : first + part, columns].astype(jnp.float32)
+                        out[:, columns] = (values * factor).astype(jnp.bfloat16)
 
     tokens = pltpu.with_memory_space_constraint(tokens, pltpu.HBM)
     return local_call(
@@ -114,6 +117,7 @@
         [shaped((part, width), jnp.bfloat16) for _, _, part in wanted],
         [
             pltpu.VMEM((count, rows, width), jnp.bfloat16),
+            pltpu.VMEM(gain.shape, jnp.float32),
             pltpu.SemaphoreType.DMA((count,)),
         ],
     )
@@ -578,7 +582,7 @@
         for d in range(chips)
         for e in range(2)
     ]
-    gain = input_norm_gain.reshape(1, -1)
+    gain = input_norm_gain.reshape(-1, 128)
     (first,) = scaled_slices(
         "slice_tp", (tp_at * piece).reshape(1), tokens, gain, piece, [(0, 0, rows)]
     )
@@ -644,32 +648,24 @@
     local_ids = after(local_ids, own_sums)
     moved = [[] for _ in chunks]
     keeps, sends, last = {}, {}, own_sums
-    for d in range(1, chips):
-        at = 2 * d * rows
-        (keeps[d],) = project(
-            f"project_{d}_0",
-            [(0, rows, jnp.float32)],
-            (at, rows),
-            local_ids,
-            lows,
-            [after(remote[d, 0, 0], last)],
-            weights,
-        )
-        last = keeps[d]
     for c, (first, part) in enumerate(chunks):
-        piece_rows = part // 2
-        kinds = [(i, piece_rows, jnp.bfloat16) for i in range(0, part, piece_rows)]
         for d in range(1, chips):
-            sends[c, d] = project(
-                f"project_{d}_1_{c}",
-                kinds,
-                ((2 * d + 1) * rows + first, part),
+            ahead = 0 if c else rows
+            sent = [(ahead + i, part // 2, jnp.bfloat16) for i in (0, part // 2)]
+            blocks = [remote[d, 1, c]] if c else [remote[d, 0, 0], remote[d, 1, 0]]
+            results = project(
+                f"project_{d}_{c}",
+                sent if c else [(0, rows, jnp.float32), *sent],
+                ((2 * d + 1) * rows + first - ahead, ahead + part),
                 local_ids,
                 lows,
-                [after(remote[d, 1, c], last)],
+                [after(blocks[0], last), *blocks[1:]],
                 weights,
             )
-            last = sends[c, d][0]
+            last = results[0]
+            if c == 0:
+                keeps[d], *results = results
+            sends[c, d] = results
     both = None
     for c, window in enumerate(chunks):
         for d in range(1, chips):

time: 118 us -> 116 us (0.983)
  starting transfers between devices: 24.1 us -> 32.1 us
  waiting for transfers between devices: 44.8 us -> 36.8 us
  Pallas kernels: 47 us -> 45 us
    ppermute x8, waiting for transfers between devices: 25.1 us -> 17.7 us  [tp_swap(): return lax.ppermute(x, 'tp', [(z, z ^ step) for z in range(tp_count)])]
    ppermute x8, starting transfers between devices: 5.96 us -> 12.8 us  [tp_swap(): return lax.ppermute(x, 'tp', [(z, z ^ step) for z in range(tp_count)])]
    pallas_call x26 -> x25, Pallas kernels: 47 us -> 45 us  [local_call(): pl.pallas_call(body, in_specs=[spec for _, spec in operands] + [HBM] * le...]
    ppermute x13, waiting for transfers between devices: 3.97 us -> 2.71 us  [core_swap(): return lax.ppermute(x, 'pool', [(p, p ^ 1) for p in range(pool_count)])]
    ppermute x11, starting transfers between devices: 10.5 us -> 11.6 us  [chip_move(): lax.ppermute(x, 'pool', [(p, (p // 2 + d) % chips * 2 + (p % 2 ^ e)) for...]
  transfers between devices with their start and end apart: 35 -> 35, of which waited for: 25 -> 20; matrix products, arithmetic and copies ran while one was open for 1% -> 0% of each run, Pallas kernels for 39% -> 38%
where the time goes in v12:
time: 116 us
  Pallas kernels  45 us (39%)
  waiting for transfers between devices  36.8 us (32%)
  starting transfers between devices  32.1 us (28%)
    pallas_call x25, Pallas kernels, local_call(): pl.pallas_call(body, in_specs=[spec for _, spec in operands] + [HBM] * le...  45 us
    ppermute x8, waiting for transfers between devices, tp_swap(): return lax.ppermute(x, 'tp', [(z, z ^ step) for z in range(tp_count)])  17.7 us
    ppermute x8, starting transfers between devices, tp_swap(): return lax.ppermute(x, 'tp', [(z, z ^ step) for z in range(tp_count)])  12.8 us
    ppermute x11, starting transfers between devices, chip_move(): lax.ppermute(x, 'pool', [(p, (p // 2 + d) % chips * 2 + (p % 2 ^ e)) for...  11.6 us
    ppermute x11, waiting for transfers between devices, chip_move(): lax.ppermute(x, 'pool', [(p, (p // 2 + d) % chips * 2 + (p % 2 ^ e)) for...  10.1 us
    ppermute x3, waiting for transfers between devices, shards(): lax.ppermute(shrunk, 'tp', [(i, (i + d) % tp_count) for i in range(tp_cou...  6.26 us
    ppermute x3, starting transfers between devices, shards(): lax.ppermute(shrunk, 'tp', [(i, (i + d) % tp_count) for i in range(tp_cou...  4.68 us
    ppermute x13, starting transfers between devices, core_swap(): return lax.ppermute(x, 'pool', [(p, p ^ 1) for p in range(pool_count)])  3.02 us
  transfers between devices with their start and end apart: 35, of which 20 were waited for; matrix products, arithmetic and copies ran while one was open for 0% of the time, Pallas kernels for 38%

profile of v12, /device:TPU:0, one launch (start us, length us, event | category | flops | bytes accessed | tf_op | source)
XLA Modules:
  0.0 115.7 jit_solution(7900897042284017526)
XLA Ops:
  0.6 0.5 collective-permute-start
  1.1 2.6 %collective-permute-start.1 = (s32[1,128]{1,0:T(1,128)}, s32[1,128]{1,0:T(1,128)S(1)}, u32[]{:S(2)}, u32[]{:S(2)}) collective-permute-start(s32[1,128]{1,0:T(1,128)} %bitcast.20), channel_id=1, source_target_pairs={{0,8},{4,12},{8,0},{12,4},{1,9},{5,13},{9,1},{13,5},{2,10},{6,14},... | collective-permute-start | bytes 1544 | tf_op jit(solution)/shard_map/ppermute | solution.py:75
  3.8 0.7 copy-done.1
  4.5 1.2 %slice_tp.1.refs_5_ = bf16[128,2048]{1,0:T(8,128)(2,1)S(1)} custom-call(s32[1]{0:T(128)} %bitcast.4.refs_0_, bf16[64,128]{1,0:T(8,128)(2,1)S(1)} %bitcast.17, bf16[128,8192]{1,0:T(8,128)(2,1)} %refs_0_.1), custom_call_target="tpu_custom_call" | custom-call | flops 1000 | bytes 1000 | tf_op jit(solution)/shard_map/slice_tp/pallas_call | solution.py:42
  5.8 1.1 collective-permute-done.2.refs_4_
  6.8 0.7 collective-permute-start.4
  7.6 2.8 %slice_pool.1 = (bf16[128,2048]{1,0:T(8,128)(2,1)S(1)}, bf16[64,2048]{1,0:T(8,128)(2,1)}, bf16[64,2048]{1,0:T(8,128)(2,1)S(1)}, bf16[128,2048]{1,0:T(8,128)(2,1)...) custom-call(s32[4]{0:T(128)S(1)} %pad_add_fusion.refs_0_, bf16[64,128]{1,0:T(8,128)(2,1)S(1)} %bitcast.18, ...), custom_call_target="tpu_custom_call" | custom-call | flops 1000 | bytes 1000 | tf_op jit(solution)/shard_map/slice_pool/pallas_call | solution.py:42
  10.4 0.1 collective-permute-start.5
  10.6 0.4 collective-permute-start.6
  11.1 0.1 collective-permute-start.3
  11.2 5.9 %load.1 = (bf16[512,2048]{1,0:T(8,128)(2,1)S(1)}, bf16[512,2048]{1,0:T(8,128)(2,1)S(1)}, bf16[2048,2048]{1,0:T(8,128)(2,1)S(1)}, bf16[2048,256]{1,0:T(8,128)(2,1...) custom-call(bf16[512,2048]{1,0:T(8,128)(2,1)} %bitcast.24, ...), custom_call_target="tpu_custom_call" | custom-call | flops 1000 | bytes 1000 | tf_op jit(solution)/shard_map/load/pallas_call | solution.py:42
  17.1 3.6 %project_base.1 = (f32[128,2560]{1,0:T(8,128)S(1)}, f32[128,2560]{1,0:T(8,128)S(1)}, bf16[128,2,64,128]{3,2,1,0:T(8,128)(2,1)S(1)}, bf16[128,2,64,128]{3,2,1,0:T(8,128)(2,1)S(1)}) custom-call(bf16[128,2048]{1,0:T(8,128)(2,1)S(1)} %get-tuple-element.96.refs_0_, bf16[64,2048]{1,0:T(8,128)(2,1)S(1)} %collective-permute-done.5.refs_1_, ...), custom_call_target="tpu_custom_call" | custom-call | flops 1000 | bytes 1000 | tf_op jit(solution)/shard_map/project_base/pallas_call | solution.py:42
  20.8 0.5 collective-permute-start.7
  21.3 1.3 %collective-permute-start.12 = (bf16[128,2048]{1,0:T(8,128)(2,1)S(1)}, bf16[128,2048]{1,0:T(8,128)(2,1)S(1)}, u32[]{:S(2)}, u32[]{:S(2)}) collective-permute-start(bf16[128,2048]{1,0:T(8,128)(2,1)S(1)} %get-tuple-element.120), channel_id=1, source_target_pairs={{0,8},{4,12},{8,0},{12,4},{1,9},{5,13},{9,1},{13,5},{2,10},{6,14},... | collective-permute-start | bytes 1572872 | tf_op jit(solution)/shard_map/ppermute | solution.py:75
  22.6 0.1 collective-permute-start.13
  22.7 0.1 collective-permute-done.7.refs_8_
  22.8 2.4 %shrink.1 = (s32[1,512]{1,0:T(1,128)S(1)}, f32[32,512]{1,0:T(8,128)S(1)}) custom-call(s32[1]{0:T(128)} %bitcast.7.refs_0_, s32[1,128]{1,0:T(1,128)S(1)} %bitcast.22, s32[1,128]{1,0:T(1,128)S(1)} %collective-permute-done.refs_2_, s32[1,128]{1,0:T(1,128)S(1)} %collective-permute-done.1.refs_3_, s32[1,128]{1,0:T(1,128)S(1)} %collective-permute-done.2.refs_4_, ...), custom_call_target="tpu_custom_call" | custom-call | flops 1000 | bytes 1000 | tf_op jit(solution)/shard_map/shrink/pallas_call | solution.py:42
  25.2 3.7 %collective-permute-start.10 = (f32[32,512]{1,0:T(8,128)S(1)}, f32[32,512]{1,0:T(8,128)S(1)}, u32[]{:S(2)}, u32[]{:S(2)}) collective-permute-start(f32[32,512]{1,0:T(8,128)S(1)} %get-tuple-element.109.refs_1_), channel_id=1, source_target_pairs={{0,3},{1,0},{2,1},{3,2},{4,7},{5,4},{6,5},{7,6},{8,11},{9,8},{10,9... | collective-permute-start | bytes 196616 | tf_op jit(solution)/shard_map/ppermute | solution.py:639
  28.9 1.0 collective-permute-start.9
  29.9 0.8 tables.1
  30.7 0.7 collective-permute-done.10.refs_4_
  31.3 4.3 %collective-permute-done.8.refs_2_ = f32[32,512]{1,0:T(8,128)S(1)} collective-permute-done((f32[32,512]{1,0:T(8,128)S(1)}, f32[32,512]{1,0:T(8,128)S(1)}, u32[]{:S(2)}, u32[]{:S(2)}) %collective-permute-start.8) | collective-permute-done | bytes 65568 | tf_op jit(solution)/shard_map/ppermute | solution.py:639
  35.7 1.2 %collective-permute-done.9.refs_3_ = f32[32,512]{1,0:T(8,128)S(1)} collective-permute-done((f32[32,512]{1,0:T(8,128)S(1)}, f32[32,512]{1,0:T(8,128)S(1)}, u32[]{:S(2)}, u32[]{:S(2)}) %collective-permute-start.9) | collective-permute-done | bytes 65568 | tf_op jit(solution)/shard_map/ppermute | solution.py:639
  36.9 1.7 %add_adapters.1 = (f32[128,2560]{1,0:T(8,128)S(1)}, bf16[128,2560]{1,0:T(8,128)(2,1)S(1)}) custom-call(s32[1,512]{1,0:T(1,128)S(1)} %get-tuple-element.118.refs_0_, f32[32,512]{1,0:T(8,128)S(1)} %get-tuple-element.109.refs_1_, f32[32,512]{1,0:T(8,128)S(1)} %collective-permute-done.8.refs_2_, f32[32,512]{1,0:T(8,128)S(1)} %collective-permute-done.9.refs_3_, ...), custom_call_target="tpu_custom_call" | custom-call | flops 1000 | bytes 1000 | tf_op jit(solution)/shard_map/add_adapters/pallas_call | solution.py:42
  38.7 1.4 %collective-permute-start.14 = (bf16[64,2048]{1,0:T(8,128)(2,1)S(1)}, bf16[64,2048]{1,0:T(8,128)(2,1)S(1)}, u32[]{:S(2)}, u32[]{:S(2)}) collective-permute-start(bf16[64,2048]{1,0:T(8,128)(2,1)S(1)} %get-tuple-element.126), channel_id=1, source_target_pairs={{0,12},{4,8},{8,4},{12,0},{1,13},{5,9},{9,5},{13,1},{2,14},{6,10},... | collective-permute-start | bytes 786440 | tf_op jit(solution)/shard_map/ppermute | solution.py:75
  40.1 3.6 %project_1_0.1 = (f32[128,2560]{1,0:T(8,128)S(1)}, bf16[32,2560]{1,0:T(8,128)(2,1)S(1)}, bf16[32,2560]{1,0:T(8,128)(2,1)S(1)}) custom-call(s32[1,512]{1,0:T(1,128)S(1)} %get-tuple-element.118.refs_0_, f32[32,512]{1,0:T(8,128)S(1)} %get-tuple-element.109.refs_1_, f32[32,512]{1,0:T(8,128)S(1)} %collective-permute-done.8.refs_2_, ...), custom_call_target="tpu_custom_call" | custom-call | flops 1000 | bytes 1000 | tf_op jit(solution)/shard_map/project_1_0/pallas_call | solution.py:42
  43.8 0.6 collective-permute-start.15
  44.4 2.4 %collective-permute-done.14.refs_5_ = bf16[64,2048]{1,0:T(8,128)(2,1)S(1)} collective-permute-done((bf16[64,2048]{1,0:T(8,128)(2,1)S(1)}, bf16[64,2048]{1,0:T(8,128)(2,1)S(1)}, u32[]{:S(2)}, u32[]{:S(2)}) %collective-permute-start.14) | collective-permute-done | bytes 262176 | tf_op jit(solution)/shard_map/ppermute | solution.py:75
  46.9 1.4 %collective-permute-start.17 = (bf16[64,2560]{1,0:T(8,128)(2,1)S(1)}, bf16[64,2560]{1,0:T(8,128)(2,1)S(1)}, u32[]{:S(2)}, u32[]{:S(2)}) collective-permute-start(bf16[64,2560]{1,0:T(8,128)(2,1)S(1)} %add_1_0.1), channel_id=1, source_target_pairs={{0,8},{4,12},{8,0},{12,4},{1,9},{5,13},{9,1},{13,5},{2,10},{6,14},... | collective-permute-start | bytes 983048 | tf_op jit(solution)/shard_map/ppermute | solution.py:75
  48.3 3.0 %project_1_1.1 = (bf16[32,2560]{1,0:T(8,128)(2,1)S(1)}, bf16[32,2560]{1,0:T(8,128)(2,1)S(1)}) custom-call(s32[1,512]{1,0:T(1,128)S(1)} %get-tuple-element.118.refs_0_, f32[32,512]{1,0:T(8,128)S(1)} %get-tuple-element.109.refs_1_, f32[32,512]{1,0:T(8,128)S(1)} %collective-permute-done.8.refs_2_, f32[32,512]{1,0:T(8,128)S(1)} %collective-permute-done.9.refs_3_, ...), custom_call_target="tpu_custom_call" | custom-call | flops 1000 | bytes 1000 | tf_op jit(solution)/shard_map/project_1_1/pallas_call | solution.py:42
  51.3 0.1 collective-permute-start.18
  51.5 0.4 collective-permute-start.19
  51.9 0.9 collective-permute-done.18.refs_1_
  52.8 0.2 collective-permute-done.19.refs_2_
  53.1 0.8 collective-permute-start.20
  53.9 3.6 %collective-permute-done.17.refs_2_ = bf16[64,2560]{1,0:T(8,128)(2,1)S(1)} collective-permute-done((bf16[64,2560]{1,0:T(8,128)(2,1)S(1)}, bf16[64,2560]{1,0:T(8,128)(2,1)S(1)}, u32[]{:S(2)}, u32[]{:S(2)}) %collective-permute-start.17) | collective-permute-done | bytes 327712 | tf_op jit(solution)/shard_map/ppermute | solution.py:75
  57.5 5.1 %attend_0.1 = (bf16[64,2048]{1,0:T(8,128)(2,1)S(1)}, bf16[64,256]{1,0:T(8,128)(2,1)S(1)}, bf16[64,256]{1,0:T(8,128)(2,1)S(1)}, bf16[2048,2048]{1,0:T(8,128)(2,1)S(1)}) custom-call(f32[128,2560]{1,0:T(8,128)S(1)} %get-tuple-element.116.refs_0_.refs_2_, bf16[128,2560]{1,0:T(8,128)(2,1)S(1)} %collective-permute-done.11.refs_1_.refs_3_, ...), custom_call_target="tpu_custom_call" | custom-call | flops 1000 | bytes 1000 | tf_op jit(solution)/shard_map/attend_0/pallas_call | solution.py:42
  62.6 1.4 %collective-permute-start.22 = (bf16[64,2048]{1,0:T(8,128)(2,1)S(1)}, bf16[64,2048]{1,0:T(8,128)(2,1)S(1)}, u32[]{:S(2)}, u32[]{:S(2)}) collective-permute-start(bf16[64,2048]{1,0:T(8,128)(2,1)S(1)} %get-tuple-element.144.refs_1_), channel_id=1, source_target_pairs={{0,8},{4,12},{8,0},{12,4},{1,9},{5,13},{9,1},{13,5},{2,10},{6,14},... | collective-permute-start | bytes 786440 | tf_op jit(solution)/shard_map/ppermute | solution.py:75
  64.0 5.5 %attend_1.1 = (bf16[64,2048]{1,0:T(8,128)(2,1)S(1)}, bf16[128,256]{1,0:T(8,128)(2,1)}, bf16[128,256]{1,0:T(8,128)(2,1)}) custom-call(bf16[64,256]{1,0:T(8,128)(2,1)S(1)} %get-tuple-element.141.refs_0_, bf16[64,256]{1,0:T(8,128)(2,1)S(1)} %get-tuple-element.142.refs_1_, f32[128,2560]{1,0:T(8,128)S(1)} %get-tuple-element.116.refs_0_.refs_2_, ...), custom_call_target="tpu_custom_call" | custom-call | flops 1000 | bytes 1000 | tf_op jit(solution)/shard_map/attend_1/pallas_call | solution.py:42
  69.5 0.4 collective-permute-done.22.refs_3_
  69.9 0.1 collective-permute-start.23
  70.0 1.3 %collective-permute-start.26 = (bf16[64,2048]{1,0:T(8,128)(2,1)S(1)}, bf16[64,2048]{1,0:T(8,128)(2,1)S(1)}, u32[]{:S(2)}, u32[]{:S(2)}) collective-permute-start(bf16[64,2048]{1,0:T(8,128)(2,1)S(1)} %get-tuple-element.163.refs_1_), channel_id=1, source_target_pairs={{0,8},{4,12},{8,0},{12,4},{1,9},{5,13},{9,1},{13,5},{2,10},{6,14},... | collective-permute-start | bytes 786440 | tf_op jit(solution)/shard_map/ppermute | solution.py:75
  71.4 3.5 %output_0_0_1.1 = (bf16[128,2048]{1,0:T(8,128)(2,1)S(1)}, bf16[128,2048]{1,0:T(8,128)(2,1)S(1)}) custom-call(s32[4]{0:T(128)S(1)} %pad_add_fusion.1.refs_0_, bf16[64,2048]{1,0:T(8,128)(2,1)S(1)} %get-tuple-element.144.refs_1_, bf16[64,2048]{1,0:T(8,128)(2,1)S(1)} %collective-permute-done.21.refs_2_, bf16[64,2048]{1,0:T(8,128)(2,1)S(1)} %collective-permute-done.22.refs_3_, ...), custom_call_target="tpu_custom_call" | custom-call | flops 1000 | bytes 1000 | tf_op jit(solution)/shard_map/output_0_0_1/pallas_call | solution.py:42
  74.9 1.2 %collective-permute-start.24 = (bf16[128,2048]{1,0:T(8,128)(2,1)S(1)}, bf16[128,2048]{1,0:T(8,128)(2,1)S(1)}, u32[]{:S(2)}, u32[]{:S(2)}) collective-permute-start(bf16[128,2048]{1,0:T(8,128)(2,1)S(1)} %get-tuple-element.147), channel_id=1, source_target_pairs={{0,1},{1,0},{2,3},{3,2},{4,5},{5,4},{6,7},{7,6},{8,9},{9,8},{10,11... | collective-permute-start | bytes 1572872 | tf_op jit(solution)/shard_map/ppermute | solution.py:83
  76.1 2.5 %collective-permute-done.26.refs_3_ = bf16[64,2048]{1,0:T(8,128)(2,1)S(1)} collective-permute-done((bf16[64,2048]{1,0:T(8,128)(2,1)S(1)}, bf16[64,2048]{1,0:T(8,128)(2,1)S(1)}, u32[]{:S(2)}, u32[]{:S(2)}) %collective-permute-start.26) | collective-permute-done | bytes 262176 | tf_op jit(solution)/shard_map/ppermute | solution.py:75
  78.6 0.5 collective-permute-start.25
  79.1 1.0 collective-permute-done.27.refs_4_
  80.1 0.4 collective-permute-done.25.refs_2_
  80.5 2.0 %output_1_0_2.1 = (bf16[128,1024]{1,0:T(8,128)(2,1)S(1)}, bf16[128,1024]{1,0:T(8,128)(2,1)S(1)}) custom-call(s32[4]{0:T(128)S(1)} %pad_add_fusion.1.refs_0_, bf16[64,2048]{1,0:T(8,128)(2,1)S(1)} %get-tuple-element.163.refs_1_, bf16[64,2048]{1,0:T(8,128)(2,1)S(1)} %collective-permute-done.25.refs_2_, bf16[64,2048]{1,0:T(8,128)(2,1)S(1)} %collective-permute-done.26.refs_3_, ...), custom_call_target="tpu_custom_call" | custom-call | flops 1000 | bytes 1000 | tf_op jit(solution)/shard_map/output_1_0_2/pallas_call | solution.py:42
  82.5 0.9 collective-permute-start.29
  83.5 6.2 %collective-permute-done.24.refs_1_ = bf16[128,2048]{1,0:T(8,128)(2,1)S(1)} collective-permute-done((bf16[128,2048]{1,0:T(8,128)(2,1)S(1)}, bf16[128,2048]{1,0:T(8,128)(2,1)S(1)}, u32[]{:S(2)}, u32[]{:S(2)}) %collective-permute-start.24) | collective-permute-done | bytes 524320 | tf_op jit(solution)/shard_map/ppermute | solution.py:83
  89.7 0.1 halves_0_0.1
  89.8 2.7 %collective-permute-start.28 = (bf16[64,2048]{1,0:T(8,128)(2,1)S(1)}, bf16[64,2048]{1,0:T(8,128)(2,1)S(1)}, u32[]{:S(2)}, u32[]{:S(2)}) collective-permute-start(bf16[64,2048]{1,0:T(8,128)(2,1)S(1)} %get-tuple-element.155), channel_id=1, source_target_pairs={{0,2},{1,3},{2,0},{3,1},{4,6},{5,7},{6,4},{7,5},{8,10},{9,11},{10,... | collective-permute-start | bytes 786440 | tf_op jit(solution)/shard_map/ppermute | solution.py:83
  92.5 1.3 %output_1_2_4.1 = (bf16[128,512]{1,0:T(8,128)(2,1)S(1)}, bf16[128,512]{1,0:T(8,128)(2,1)S(1)}) custom-call(s32[4]{0:T(128)S(1)} %pad_add_fusion.1.refs_0_, bf16[64,2048]{1,0:T(8,128)(2,1)S(1)} %get-tuple-element.163.refs_1_, bf16[64,2048]{1,0:T(8,128)(2,1)S(1)} %collective-permute-done.25.refs_2_, bf16[64,2048]{1,0:T(8,128)(2,1)S(1)} %collective-permute-done.26.refs_3_, ...), custom_call_target="tpu_custom_call" | custom-call | flops 1000 | bytes 1000 | tf_op jit(solution)/shard_map/output_1_2_4/pallas_call | solution.py:42
  93.8 1.2 %collective-permute-start.31 = (bf16[128,512]{1,0:T(8,128)(2,1)S(1)}, bf16[128,512]{1,0:T(8,128)(2,1)S(1)}, u32[]{:S(2)}, u32[]{:S(2)}) collective-permute-start(bf16[128,512]{1,0:T(8,128)(2,1)S(1)} %get-tuple-element.165), channel_id=1, source_target_pairs={{0,1},{1,0},{2,3},{3,2},{4,5},{5,4},{6,7},{7,6},{8,9},{9,8},{10,11... | collective-permute-start | bytes 393224 | tf_op jit(solution)/shard_map/ppermute | solution.py:83
  95.0 5.0 %collective-permute-done.29.refs_1_ = bf16[128,1024]{1,0:T(8,128)(2,1)S(1)} collective-permute-done((bf16[128,1024]{1,0:T(8,128)(2,1)S(1)}, bf16[128,1024]{1,0:T(8,128)(2,1)S(1)}, u32[]{:S(2)}, u32[]{:S(2)}) %collective-permute-start.29) | collective-permute-done | bytes 262176 | tf_op jit(solution)/shard_map/ppermute | solution.py:83
  100.2 1.3 %output_1_3_4.1 = (bf16[128,512]{1,0:T(8,128)(2,1)S(1)}, bf16[128,512]{1,0:T(8,128)(2,1)S(1)}) custom-call(s32[4]{0:T(128)S(1)} %pad_add_fusion.1.refs_0_, bf16[64,2048]{1,0:T(8,128)(2,1)S(1)} %get-tuple-element.163.refs_1_, bf16[64,2048]{1,0:T(8,128)(2,1)S(1)} %collective-permute-done.25.refs_2_, bf16[64,2048]{1,0:T(8,128)(2,1)S(1)} %collective-permute-done.26.refs_3_, ...), custom_call_target="tpu_custom_call" | custom-call | flops 1000 | bytes 1000 | tf_op jit(solution)/shard_map/output_1_3_4/pallas_call | solution.py:42
  101.5 1.5 %collective-permute-start.33 = (bf16[128,512]{1,0:T(8,128)(2,1)S(1)}, bf16[128,512]{1,0:T(8,128)(2,1)S(1)}, u32[]{:S(2)}, u32[]{:S(2)}) collective-permute-start(bf16[128,512]{1,0:T(8,128)(2,1)S(1)} %get-tuple-element.170), channel_id=1, source_target_pairs={{0,1},{1,0},{2,3},{3,2},{4,5},{5,4},{6,7},{7,6},{8,9},{9,8},{10,11... | collective-permute-start | bytes 393224 | tf_op jit(solution)/shard_map/ppermute | solution.py:83
  103.0 0.7 collective-permute-done.28.refs_1_
  103.8 2.7 %collective-permute-start.32 = (bf16[64,512]{1,0:T(8,128)(2,1)S(1)}, bf16[64,512]{1,0:T(8,128)(2,1)S(1)}, u32[]{:S(2)}, u32[]{:S(2)}) collective-permute-start(bf16[64,512]{1,0:T(8,128)(2,1)S(1)} %get-tuple-element.167), channel_id=1, source_target_pairs={{0,2},{1,3},{2,0},{3,1},{4,6},{5,7},{6,4},{7,5},{8,10},{9,11},{10,... | collective-permute-start | bytes 196616 | tf_op jit(solution)/shard_map/ppermute | solution.py:83
  106.5 3.0 %collective-permute-done.30.refs_1_ = bf16[64,1024]{1,0:T(8,128)(2,1)S(1)} collective-permute-done((bf16[64,1024]{1,0:T(8,128)(2,1)S(1)}, bf16[64,1024]{1,0:T(8,128)(2,1)S(1)}, u32[]{:S(2)}, u32[]{:S(2)}) %collective-permute-start.30) | collective-permute-done | bytes 131104 | tf_op jit(solution)/shard_map/ppermute | solution.py:83
  109.6 2.5 %collective-permute-start.34 = (bf16[64,512]{1,0:T(8,128)(2,1)S(1)}, bf16[64,512]{1,0:T(8,128)(2,1)S(1)}, u32[]{:S(2)}, u32[]{:S(2)}) collective-permute-start(bf16[64,512]{1,0:T(8,128)(2,1)S(1)} %get-tuple-element.172), channel_id=1, source_target_pairs={{0,2},{1,3},{2,0},{3,1},{4,6},{5,7},{6,4},{7,5},{8,10},{9,11},{10,... | collective-permute-start | bytes 196616 | tf_op jit(solution)/shard_map/ppermute | solution.py:83
  112.1 2.7 %collective-permute-done.34.refs_4_ = bf16[64,512]{1,0:T(8,128)(2,1)S(1)} collective-permute-done((bf16[64,512]{1,0:T(8,128)(2,1)S(1)}, bf16[64,512]{1,0:T(8,128)(2,1)S(1)}, u32[]{:S(2)}, u32[]{:S(2)}) %collective-permute-start.34) | collective-permute-done | bytes 65568 | tf_op jit(solution)/shard_map/ppermute | solution.py:83
  114.8 0.8 assemble.1
  (43 shorter events, 1.0 us)
Async XLA Ops:
  0.6 5.1 %collective-permute-start = (s32[1,128]{1,0:T(1,128)}, s32[1,128]{1,0:T(1,128)S(1)}, u32[]{:S(2)}, u32[]{:S(2)}) collective-permute-start(s32[1,128]{1,0:T(1,128)} %bitcast.19), channel_id=1, source_target_pairs={{0,4},{4,0},{8,12},{12,8},{1,5},{5,1},{9,13},{13,9},{2,6},{6,2},{1... | collective-permute-start | bytes 1544 | tf_op jit(solution)/shard_map/ppermute | solution.py:75
  1.1 4.6 %collective-permute-start.1 = (s32[1,128]{1,0:T(1,128)}, s32[1,128]{1,0:T(1,128)S(1)}, u32[]{:S(2)}, u32[]{:S(2)}) collective-permute-start(s32[1,128]{1,0:T(1,128)} %bitcast.20), channel_id=1, source_target_pairs={{0,8},{4,12},{8,0},{12,4},{1,9},{5,13},{9,1},{13,5},{2,10},{6,14},... | collective-permute-start | bytes 1544 | tf_op jit(solution)/shard_map/ppermute | solution.py:75
  3.7 3.1 %collective-permute-start.2 = (s32[1,128]{1,0:T(1,128)}, s32[1,128]{1,0:T(1,128)S(1)}, u32[]{:S(2)}, u32[]{:S(2)}) collective-permute-start(s32[1,128]{1,0:T(1,128)} %bitcast.21), channel_id=1, source_target_pairs={{0,12},{4,8},{8,4},{12,0},{1,13},{5,9},{9,5},{13,1},{2,14},{6,10},... | collective-permute-start | bytes 1544 | tf_op jit(solution)/shard_map/ppermute | solution.py:75
  3.8 0.7 copy-start.1
  4.5 3.1 %copy-start.2 = (bf16[8192]{0:T(1024)(128)(2,1)S(1)}, bf16[8192]{0:T(1024)(128)(2,1)}, u32[]{:S(2)}) copy-start(bf16[8192]{0:T(1024)(128)(2,1)} %param.15) | copy-start | bytes 49156
  6.8 14.0 %collective-permute-start.4 = (bf16[128,2048]{1,0:T(8,128)(2,1)S(1)}, bf16[128,2048]{1,0:T(8,128)(2,1)S(1)}, u32[]{:S(2)}, u32[]{:S(2)}) collective-permute-start(bf16[128,2048]{1,0:T(8,128)(2,1)S(1)} %slice_tp.1.refs_5_), channel_id=1, source_target_pairs={{0,8},{4,12},{8,0},{12,4},{1,9},{5,13},{9,1},{13,5},{2,10},{6,14},... | collective-permute-start | bytes 1572872 | tf_op jit(solution)/shard_map/ppermute | solution.py:75
  10.4 6.6 %collective-permute-start.5 = (bf16[64,2048]{1,0:T(8,128)(2,1)}, bf16[64,2048]{1,0:T(8,128)(2,1)S(1)}, u32[]{:S(2)}, u32[]{:S(2)}) collective-permute-start(bf16[64,2048]{1,0:T(8,128)(2,1)} %get-tuple-element.97), channel_id=1, source_target_pairs={{0,4},{4,0},{8,12},{12,8},{1,5},{5,1},{9,13},{13,9},{2,6},{6,2},{1... | collective-permute-start | bytes 786440 | tf_op jit(solution)/shard_map/ppermute | solution.py:70
  10.6 6.5 %collective-permute-start.6 = (bf16[64,2048]{1,0:T(8,128)(2,1)S(1)}, bf16[64,2048]{1,0:T(8,128)(2,1)S(1)}, u32[]{:S(2)}, u32[]{:S(2)}) collective-permute-start(bf16[64,2048]{1,0:T(8,128)(2,1)S(1)} %get-tuple-element.98), channel_id=1, source_target_pairs={{0,4},{4,0},{8,12},{12,8},{1,5},{5,1},{9,13},{13,9},{2,6},{6,2},{1... | collective-permute-start | bytes 786440 | tf_op jit(solution)/shard_map/ppermute | solution.py:70
  11.1 11.6 %collective-permute-start.3 = (bf16[128,2048]{1,0:T(8,128)(2,1)S(1)}, bf16[128,2048]{1,0:T(8,128)(2,1)S(1)}, u32[]{:S(2)}, u32[]{:S(2)}) collective-permute-start(bf16[128,2048]{1,0:T(8,128)(2,1)S(1)} %slice_tp.1.refs_5_), channel_id=1, source_target_pairs={{0,4},{4,0},{8,12},{12,8},{1,5},{5,1},{9,13},{13,9},{2,6},{6,2},{1... | collective-permute-start | bytes 1572872 | tf_op jit(solution)/shard_map/ppermute | solution.py:70
  17.1 5.7 %copy-start.3 = (s32[128]{0:T(128)S(1)}, s32[128]{0:T(128)}, u32[]{:S(2)}) copy-start(s32[128]{0:T(128)} %param.23) | copy-start | bytes 1540
  20.8 2.0 %collective-permute-start.7 = (bf16[128,2048]{1,0:T(8,128)(2,1)S(1)}, bf16[128,2048]{1,0:T(8,128)(2,1)S(1)}, u32[]{:S(2)}, u32[]{:S(2)}) collective-permute-start(bf16[128,2048]{1,0:T(8,128)(2,1)S(1)} %collective-permute-done.4.refs_7_), channel_id=1, source_target_pairs={{0,4},{4,0},{8,12},{12,8},{1,5},{5,1},{9,13},{13,9},{2,6},{6,2},{1... | collective-permute-start | bytes 1572872 | tf_op jit(solution)/shard_map/ppermute | solution.py:70
  21.3 18.8 %collective-permute-start.12 = (bf16[128,2048]{1,0:T(8,128)(2,1)S(1)}, bf16[128,2048]{1,0:T(8,128)(2,1)S(1)}, u32[]{:S(2)}, u32[]{:S(2)}) collective-permute-start(bf16[128,2048]{1,0:T(8,128)(2,1)S(1)} %get-tuple-element.120), channel_id=1, source_target_pairs={{0,8},{4,12},{8,0},{12,4},{1,9},{5,13},{9,1},{13,5},{2,10},{6,14},... | collective-permute-start | bytes 1572872 | tf_op jit(solution)/shard_map/ppermute | solution.py:75
  22.6 17.5 %collective-permute-start.13 = (bf16[64,2048]{1,0:T(8,128)(2,1)S(1)}, bf16[64,2048]{1,0:T(8,128)(2,1)S(1)}, u32[]{:S(2)}, u32[]{:S(2)}) collective-permute-start(bf16[64,2048]{1,0:T(8,128)(2,1)S(1)} %get-tuple-element.123), channel_id=1, source_target_pairs={{0,12},{4,8},{8,4},{12,0},{1,13},{5,9},{9,5},{13,1},{2,14},{6,10},... | collective-permute-start | bytes 786440 | tf_op jit(solution)/shard_map/ppermute | solution.py:75
  22.8 7.1 %copy-start = (bf16[128,8192]{1,0:T(8,128)(2,1)S(1)}, bf16[128,8192]{1,0:T(8,128)(2,1)}, u32[]{:S(2)}) copy-start(bf16[128,8192]{1,0:T(8,128)(2,1)} %refs_0_.1) | copy-start | bytes 6291460
  22.8 7.1 %copy-start.4 = (s32[128]{0:T(128)S(1)}, s32[128]{0:T(128)}, u32[]{:S(2)}) copy-start(s32[128]{0:T(128)} %param.22) | copy-start | bytes 1540
  25.2 6.1 %collective-permute-start.10 = (f32[32,512]{1,0:T(8,128)S(1)}, f32[32,512]{1,0:T(8,128)S(1)}, u32[]{:S(2)}, u32[]{:S(2)}) collective-permute-start(f32[32,512]{1,0:T(8,128)S(1)} %get-tuple-element.109.refs_1_), channel_id=1, source_target_pairs={{0,3},{1,0},{2,1},{3,2},{4,7},{5,4},{6,5},{7,6},{8,11},{9,8},{10,9... | collective-permute-start | bytes 196616 | tf_op jit(solution)/shard_map/ppermute | solution.py:639
  28.9 6.8 %collective-permute-start.8 = (f32[32,512]{1,0:T(8,128)S(1)}, f32[32,512]{1,0:T(8,128)S(1)}, u32[]{:S(2)}, u32[]{:S(2)}) collective-permute-start(f32[32,512]{1,0:T(8,128)S(1)} %get-tuple-element.109.refs_1_), channel_id=1, source_target_pairs={{0,1},{1,2},{2,3},{3,0},{4,5},{5,6},{6,7},{7,4},{8,9},{9,10},{10,1... | collective-permute-start | bytes 196616 | tf_op jit(solution)/shard_map/ppermute | solution.py:639
  28.9 8.1 %collective-permute-start.9 = (f32[32,512]{1,0:T(8,128)S(1)}, f32[32,512]{1,0:T(8,128)S(1)}, u32[]{:S(2)}, u32[]{:S(2)}) collective-permute-start(f32[32,512]{1,0:T(8,128)S(1)} %get-tuple-element.109.refs_1_), channel_id=1, source_target_pairs={{0,2},{1,3},{2,0},{3,1},{4,6},{5,7},{6,4},{7,5},{8,10},{9,11},{10,... | collective-permute-start | bytes 196616 | tf_op jit(solution)/shard_map/ppermute | solution.py:639
  38.6 18.9 %collective-permute-start.11 = (bf16[128,2560]{1,0:T(8,128)(2,1)S(1)}, bf16[128,2560]{1,0:T(8,128)(2,1)S(1)}, u32[]{:S(2)}, u32[]{:S(2)}) collective-permute-start(bf16[128,2560]{1,0:T(8,128)(2,1)S(1)} %get-tuple-element.117), channel_id=1, source_target_pairs={{0,4},{4,0},{8,12},{12,8},{1,5},{5,1},{9,13},{13,9},{2,6},{6,2},{1... | collective-permute-start | bytes 1966088 | tf_op jit(solution)/shard_map/ppermute | solution.py:70
  38.7 8.1 %collective-permute-start.14 = (bf16[64,2048]{1,0:T(8,128)(2,1)S(1)}, bf16[64,2048]{1,0:T(8,128)(2,1)S(1)}, u32[]{:S(2)}, u32[]{:S(2)}) collective-permute-start(bf16[64,2048]{1,0:T(8,128)(2,1)S(1)} %get-tuple-element.126), channel_id=1, source_target_pairs={{0,12},{4,8},{8,4},{12,0},{1,13},{5,9},{9,5},{13,1},{2,14},{6,10},... | collective-permute-start | bytes 786440 | tf_op jit(solution)/shard_map/ppermute | solution.py:75
  43.8 3.0 %collective-permute-start.15 = (bf16[32,2560]{1,0:T(8,128)(2,1)S(1)}, bf16[32,2560]{1,0:T(8,128)(2,1)S(1)}, u32[]{:S(2)}, u32[]{:S(2)}) collective-permute-start(bf16[32,2560]{1,0:T(8,128)(2,1)S(1)} %get-tuple-element.128), channel_id=1, source_target_pairs={{0,4},{4,0},{8,12},{12,8},{1,5},{5,1},{9,13},{13,9},{2,6},{6,2},{1... | collective-permute-start | bytes 491528 | tf_op jit(solution)/shard_map/ppermute | solution.py:70
  44.3 2.5 %collective-permute-start.16 = (bf16[32,2560]{1,0:T(8,128)(2,1)S(1)}, bf16[32,2560]{1,0:T(8,128)(2,1)S(1)}, u32[]{:S(2)}, u32[]{:S(2)}) collective-permute-start(bf16[32,2560]{1,0:T(8,128)(2,1)S(1)} %get-tuple-element.129), channel_id=1, source_target_pairs={{0,4},{4,0},{8,12},{12,8},{1,5},{5,1},{9,13},{13,9},{2,6},{6,2},{1... | collective-permute-start | bytes 491528 | tf_op jit(solution)/shard_map/ppermute | solution.py:70
  46.9 10.6 %collective-permute-start.17 = (bf16[64,2560]{1,0:T(8,128)(2,1)S(1)}, bf16[64,2560]{1,0:T(8,128)(2,1)S(1)}, u32[]{:S(2)}, u32[]{:S(2)}) collective-permute-start(bf16[64,2560]{1,0:T(8,128)(2,1)S(1)} %add_1_0.1), channel_id=1, source_target_pairs={{0,8},{4,12},{8,0},{12,4},{1,9},{5,13},{9,1},{13,5},{2,10},{6,14},... | collective-permute-start | bytes 983048 | tf_op jit(solution)/shard_map/ppermute | solution.py:75
  51.3 1.5 %collective-permute-start.18 = (bf16[32,2560]{1,0:T(8,128)(2,1)S(1)}, bf16[32,2560]{1,0:T(8,128)(2,1)S(1)}, u32[]{:S(2)}, u32[]{:S(2)}) collective-permute-start(bf16[32,2560]{1,0:T(8,128)(2,1)S(1)} %get-tuple-element.132), channel_id=1, source_target_pairs={{0,4},{4,0},{8,12},{12,8},{1,5},{5,1},{9,13},{13,9},{2,6},{6,2},{1... | collective-permute-start | bytes 491528 | tf_op jit(solution)/shard_map/ppermute | solution.py:70
  51.5 1.5 %collective-permute-start.19 = (bf16[32,2560]{1,0:T(8,128)(2,1)S(1)}, bf16[32,2560]{1,0:T(8,128)(2,1)S(1)}, u32[]{:S(2)}, u32[]{:S(2)}) collective-permute-start(bf16[32,2560]{1,0:T(8,128)(2,1)S(1)} %get-tuple-element.133), channel_id=1, source_target_pairs={{0,4},{4,0},{8,12},{12,8},{1,5},{5,1},{9,13},{13,9},{2,6},{6,2},{1... | collective-permute-start | bytes 491528 | tf_op jit(solution)/shard_map/ppermute | solution.py:70
  53.1 10.9 %collective-permute-start.20 = (bf16[64,2560]{1,0:T(8,128)(2,1)S(1)}, bf16[64,2560]{1,0:T(8,128)(2,1)S(1)}, u32[]{:S(2)}, u32[]{:S(2)}) collective-permute-start(bf16[64,2560]{1,0:T(8,128)(2,1)S(1)} %add_1_1.1), channel_id=1, source_target_pairs={{0,8},{4,12},{8,0},{12,4},{1,9},{5,13},{9,1},{13,5},{2,10},{6,14},... | collective-permute-start | bytes 983048 | tf_op jit(solution)/shard_map/ppermute | solution.py:75
  62.6 7.3 %collective-permute-start.22 = (bf16[64,2048]{1,0:T(8,128)(2,1)S(1)}, bf16[64,2048]{1,0:T(8,128)(2,1)S(1)}, u32[]{:S(2)}, u32[]{:S(2)}) collective-permute-start(bf16[64,2048]{1,0:T(8,128)(2,1)S(1)} %get-tuple-element.144.refs_1_), channel_id=1, source_target_pairs={{0,8},{4,12},{8,0},{12,4},{1,9},{5,13},{9,1},{13,5},{2,10},{6,14},... | collective-permute-start | bytes 786440 | tf_op jit(solution)/shard_map/ppermute | solution.py:75
  69.5 1.9 %collective-permute-start.21 = (bf16[64,2048]{1,0:T(8,128)(2,1)S(1)}, bf16[64,2048]{1,0:T(8,128)(2,1)S(1)}, u32[]{:S(2)}, u32[]{:S(2)}) collective-permute-start(bf16[64,2048]{1,0:T(8,128)(2,1)S(1)} %get-tuple-element.144.refs_1_), channel_id=1, source_target_pairs={{0,4},{4,0},{8,12},{12,8},{1,5},{5,1},{9,13},{13,9},{2,6},{6,2},{1... | collective-permute-start | bytes 786440 | tf_op jit(solution)/shard_map/ppermute | solution.py:70
  69.9 1.5 %collective-permute-start.23 = (bf16[64,2048]{1,0:T(8,128)(2,1)S(1)}, bf16[64,2048]{1,0:T(8,128)(2,1)S(1)}, u32[]{:S(2)}, u32[]{:S(2)}) collective-permute-start(bf16[64,2048]{1,0:T(8,128)(2,1)S(1)} %collective-permute-done.22.refs_3_), channel_id=1, source_target_pairs={{0,4},{4,0},{8,12},{12,8},{1,5},{5,1},{9,13},{13,9},{2,6},{6,2},{1... | collective-permute-start | bytes 786440 | tf_op jit(solution)/shard_map/ppermute | solution.py:70
  70.0 8.6 %collective-permute-start.26 = (bf16[64,2048]{1,0:T(8,128)(2,1)S(1)}, bf16[64,2048]{1,0:T(8,128)(2,1)S(1)}, u32[]{:S(2)}, u32[]{:S(2)}) collective-permute-start(bf16[64,2048]{1,0:T(8,128)(2,1)S(1)} %get-tuple-element.163.refs_1_), channel_id=1, source_target_pairs={{0,8},{4,12},{8,0},{12,4},{1,9},{5,13},{9,1},{13,5},{2,10},{6,14},... | collective-permute-start | bytes 786440 | tf_op jit(solution)/shard_map/ppermute | solution.py:75
  74.9 14.8 %collective-permute-start.24 = (bf16[128,2048]{1,0:T(8,128)(2,1)S(1)}, bf16[128,2048]{1,0:T(8,128)(2,1)S(1)}, u32[]{:S(2)}, u32[]{:S(2)}) collective-permute-start(bf16[128,2048]{1,0:T(8,128)(2,1)S(1)} %get-tuple-element.147), channel_id=1, source_target_pairs={{0,1},{1,0},{2,3},{3,2},{4,5},{5,4},{6,7},{7,6},{8,9},{9,8},{10,11... | collective-permute-start | bytes 1572872 | tf_op jit(solution)/shard_map/ppermute | solution.py:83
  78.6 1.5 %collective-permute-start.27 = (bf16[64,2048]{1,0:T(8,128)(2,1)S(1)}, bf16[64,2048]{1,0:T(8,128)(2,1)S(1)}, u32[]{:S(2)}, u32[]{:S(2)}) collective-permute-start(bf16[64,2048]{1,0:T(8,128)(2,1)S(1)} %collective-permute-done.26.refs_3_), channel_id=1, source_target_pairs={{0,4},{4,0},{8,12},{12,8},{1,5},{5,1},{9,13},{13,9},{2,6},{6,2},{1... | collective-permute-start | bytes 786440 | tf_op jit(solution)/shard_map/ppermute | solution.py:70
  78.6 1.9 %collective-permute-start.25 = (bf16[64,2048]{1,0:T(8,128)(2,1)S(1)}, bf16[64,2048]{1,0:T(8,128)(2,1)S(1)}, u32[]{:S(2)}, u32[]{:S(2)}) collective-permute-start(bf16[64,2048]{1,0:T(8,128)(2,1)S(1)} %get-tuple-element.163.refs_1_), channel_id=1, source_target_pairs={{0,4},{4,0},{8,12},{12,8},{1,5},{5,1},{9,13},{13,9},{2,6},{6,2},{1... | collective-permute-start | bytes 786440 | tf_op jit(solution)/shard_map/ppermute | solution.py:70
  82.5 17.5 %collective-permute-start.29 = (bf16[128,1024]{1,0:T(8,128)(2,1)S(1)}, bf16[128,1024]{1,0:T(8,128)(2,1)S(1)}, u32[]{:S(2)}, u32[]{:S(2)}) collective-permute-start(bf16[128,1024]{1,0:T(8,128)(2,1)S(1)} %get-tuple-element.158), channel_id=1, source_target_pairs={{0,1},{1,0},{2,3},{3,2},{4,5},{5,4},{6,7},{7,6},{8,9},{9,8},{10,11... | collective-permute-start | bytes 786440 | tf_op jit(solution)/shard_map/ppermute | solution.py:83
  89.8 13.9 %collective-permute-start.28 = (bf16[64,2048]{1,0:T(8,128)(2,1)S(1)}, bf16[64,2048]{1,0:T(8,128)(2,1)S(1)}, u32[]{:S(2)}, u32[]{:S(2)}) collective-permute-start(bf16[64,2048]{1,0:T(8,128)(2,1)S(1)} %get-tuple-element.155), channel_id=1, source_target_pairs={{0,2},{1,3},{2,0},{3,1},{4,6},{5,7},{6,4},{7,5},{8,10},{9,11},{10,... | collective-permute-start | bytes 786440 | tf_op jit(solution)/shard_map/ppermute | solution.py:83
  93.8 10.0 %collective-permute-start.31 = (bf16[128,512]{1,0:T(8,128)(2,1)S(1)}, bf16[128,512]{1,0:T(8,128)(2,1)S(1)}, u32[]{:S(2)}, u32[]{:S(2)}) collective-permute-start(bf16[128,512]{1,0:T(8,128)(2,1)S(1)} %get-tuple-element.165), channel_id=1, source_target_pairs={{0,1},{1,0},{2,3},{3,2},{4,5},{5,4},{6,7},{7,6},{8,9},{9,8},{10,11... | collective-permute-start | bytes 393224 | tf_op jit(solution)/shard_map/ppermute | solution.py:83
  100.2 9.4 %collective-permute-start.30 = (bf16[64,1024]{1,0:T(8,128)(2,1)S(1)}, bf16[64,1024]{1,0:T(8,128)(2,1)S(1)}, u32[]{:S(2)}, u32[]{:S(2)}) collective-permute-start(bf16[64,1024]{1,0:T(8,128)(2,1)S(1)} %get-tuple-element.160), channel_id=1, source_target_pairs={{0,2},{1,3},{2,0},{3,1},{4,6},{5,7},{6,4},{7,5},{8,10},{9,11},{10,... | collective-permute-start | bytes 393224 | tf_op jit(solution)/shard_map/ppermute | solution.py:83
  101.5 8.0 %collective-permute-start.33 = (bf16[128,512]{1,0:T(8,128)(2,1)S(1)}, bf16[128,512]{1,0:T(8,128)(2,1)S(1)}, u32[]{:S(2)}, u32[]{:S(2)}) collective-permute-start(bf16[128,512]{1,0:T(8,128)(2,1)S(1)} %get-tuple-element.170), channel_id=1, source_target_pairs={{0,1},{1,0},{2,3},{3,2},{4,5},{5,4},{6,7},{7,6},{8,9},{9,8},{10,11... | collective-permute-start | bytes 393224 | tf_op jit(solution)/shard_map/ppermute | solution.py:83
  103.8 8.3 %collective-permute-start.32 = (bf16[64,512]{1,0:T(8,128)(2,1)S(1)}, bf16[64,512]{1,0:T(8,128)(2,1)S(1)}, u32[]{:S(2)}, u32[]{:S(2)}) collective-permute-start(bf16[64,512]{1,0:T(8,128)(2,1)S(1)} %get-tuple-element.167), channel_id=1, source_target_pairs={{0,2},{1,3},{2,0},{3,1},{4,6},{5,7},{6,4},{7,5},{8,10},{9,11},{10,... | collective-permute-start | bytes 196616 | tf_op jit(solution)/shard_map/ppermute | solution.py:83
  109.6 5.2 %collective-permute-start.34 = (bf16[64,512]{1,0:T(8,128)(2,1)S(1)}, bf16[64,512]{1,0:T(8,128)(2,1)S(1)}, u32[]{:S(2)}, u32[]{:S(2)}) collective-permute-start(bf16[64,512]{1,0:T(8,128)(2,1)S(1)} %get-tuple-element.172), channel_id=1, source_target_pairs={{0,2},{1,3},{2,0},{3,1},{4,6},{5,7},{6,4},{7,5},{8,10},{9,11},{10,... | collective-permute-start | bytes 196616 | tf_op jit(solution)/shard_map/ppermute | solution.py:83
